TPU v7x, 32 devices: a whole 2x2x4 slice. The times are simulated.
32 devices in a mesh: azim: 4 (over z), rad: 4 (over x, core), axial: 2 (over y).
Axes of the slice: x: 2, y: 2, z: 4, core: 2. Of those that a mesh axis runs over, the one named last changes fastest.
Arguments:
- adjoint_final: float32 [4, 48, 8, 8, 512], P(None, None, 'azim', 'axial', 'rad'), may hold values from -6 to 6
- state_start: bfloat16 [4, 48, 8, 8, 512], P(None, None, 'azim', 'axial', 'rad'), may hold values from 0.099609375 to 2
- state_middle: bfloat16 [4, 48, 8, 8, 512], P(None, None, 'azim', 'axial', 'rad'), may hold values from 0.099609375 to 2
- speeds: float32 [3, 8, 8, 512], P(None, 'azim', 'axial', 'rad'), may hold values from 0.04 to 0.25
- flags: int32 [3, 8, 8, 512], P(None, 'azim', 'axial', 'rad'), may hold values from 0 to 1
- zones: int32 [8, 8, 512], P('azim', 'axial', 'rad'), may hold values from 0 to 3
- growth_rate: float32 [48], replicated, may hold values from 0.05 to 0.5
- transfer_rate: float32 [48], replicated, may hold values from 0.05 to 0.5
- nucleation_rate: float32 [4], replicated, may hold values from 0.2 to 1
Outputs:
- adjoint_start: float32 [4, 48, 8, 8, 512], P(None, None, 'azim', 'axial', 'rad')
All inputs are finite; a program needn't handle non-finite values.
Results may differ from a plain program's by a relative error of at most 0.0003.
Values sent between devices are 32-bit elements; how exact they have to be, the bound alone decides.
No kernel may reach another device: no remote copies, remote signals or barrier semaphores. Data moves between devices by JAX's collectives and lax.ppermute only.
A program may use at most 128 MiB of HBM per device.

v0:
```python
import jax
import jax.numpy as jnp
from jax import lax
from jax.sharding import PartitionSpec as P

supersat_scale = 1.5
crowding = 0.02
nucleus_moments = (1.0, 0.5, 0.25, 0.125)


def extended(x, sides, width, wrap):
    for axis, dim in sides:
        size, length = (lax.axis_size(axis), x.shape[dim])
        up = [(i, (i + 1) % size) for i in range(size if wrap else size - 1)]
        down = [(j, i) for i, j in up]
        last = lax.slice_in_dim(x, length - width, length, axis=dim)
        first = lax.slice_in_dim(x, 0, width, axis=dim)
        before = lax.ppermute(last, axis, up)
        after = lax.ppermute(first, axis, down)
        x = jnp.concatenate([before, x, after], axis=dim)
    return x


def source_term(state, growth_rate, transfer_rate, nucleation):
    extra = (1,) * (state.ndim - 2)
    growth = growth_rate.reshape((1, -1) + extra)
    transfer = transfer_rate.reshape((1, -1) + extra)
    third = state[3]
    sigma = supersat_scale / (1.0 + crowding * jnp.sum(third * third, axis=0))
    lower = jnp.concatenate([jnp.zeros_like(state[0:1]), state[:3]], axis=0)
    factors = jnp.array([0.0, 1.0, 2.0, 3.0], dtype=state.dtype).reshape((4, 1) + extra)
    outflow = transfer * state
    inflow = jnp.concatenate([jnp.zeros_like(outflow[:, 0:1]), outflow[:, :-1]], axis=1)
    first = (jnp.arange(state.shape[1]) == 0).astype(state.dtype).reshape((1, -1) + extra)
    nucleus = jnp.array(nucleus_moments, dtype=state.dtype).reshape((4, 1) + extra)
    birth = nucleus * first * (nucleation * sigma * sigma)[None, None]
    return sigma[None, None] * (factors * growth * lower + inflow - outflow) + birth


def source_adjoint(state, adjoint, growth_rate, transfer_rate, nucleation):
    _, pull = jax.vjp(
        lambda field: source_term(field, growth_rate, transfer_rate, nucleation), state
    )
    return pull(adjoint)[0]


def cut_region(field, direction, offset):
    lead = [slice(None)] * (field.ndim - 3)
    spatial = []
    for which in range(3):
        moved = offset if which == direction else 0
        length = field.shape[field.ndim - 3 + which]
        spatial.append(slice(1 + moved, length - 1 + moved))
    return field[tuple(lead + spatial)]


def transport_adjoint(adjoint_pad, coeff_pad):
    total = None
    for direction in range(3):
        centre = cut_region(adjoint_pad, direction, 0)
        higher = cut_region(adjoint_pad, direction, 1)
        lowerv = cut_region(adjoint_pad, direction, -1)
        p_high = cut_region(coeff_pad[direction], direction, 1)
        q_here = cut_region(coeff_pad[3 + direction], direction, 0)
        term = p_high * (higher - centre) + q_here * (lowerv - centre)
        total = term if total is None else total + term
    return total


def face_coefficients(speeds, flags):
    upwind = flags.astype(speeds.dtype)
    return jnp.concatenate([speeds * upwind, speeds * (1.0 - upwind)], axis=0)


def nucleation_field(zones, nucleation_rate):
    labels = jnp.arange(nucleation_rate.shape[0], dtype=jnp.int32).reshape((-1, 1, 1, 1))
    match = (zones[None] == labels).astype(nucleation_rate.dtype)
    return jnp.sum(match * nucleation_rate.reshape((-1, 1, 1, 1)), axis=0)


def shards(
    adjoint_final,
    state_start,
    state_middle,
    speeds,
    flags,
    zones,
    growth_rate,
    transfer_rate,
    nucleation_rate,
):
    coeffs = face_coefficients(speeds, flags)
    nucleation = nucleation_field(zones, nucleation_rate)
    start = state_start.astype(jnp.float32)
    middle = state_middle.astype(jnp.float32)
    dims = adjoint_final.shape
    comps = dims[0] * dims[1]
    packed = jnp.concatenate([adjoint_final.reshape((comps,) + dims[2:]), coeffs], axis=0)
    packed = extended(packed, (("azim", 1),), 1, True)
    packed = extended(packed, (("rad", 3), ("axial", 2)), 1, False)
    later_pad = packed[:comps].reshape(dims[:2] + packed.shape[1:])
    coeff_pad = packed[comps:]
    adjoint_middle = 0.5 * adjoint_final + 0.5 * (
        transport_adjoint(later_pad, coeff_pad)
        + source_adjoint(middle, adjoint_final, growth_rate, transfer_rate, nucleation)
    )
    flat = adjoint_middle.reshape((comps,) + dims[2:])
    flat = extended(flat, (("azim", 1),), 1, True)
    flat = extended(flat, (("rad", 3), ("axial", 2)), 1, False)
    middle_pad = flat.reshape(dims[:2] + flat.shape[1:])
    return (
        0.5 * adjoint_final
        + adjoint_middle
        + transport_adjoint(middle_pad, coeff_pad)
        + source_adjoint(start, adjoint_middle, growth_rate, transfer_rate, nucleation)
    )


def solution(mesh):
    return jax.shard_map(
        shards,
        mesh=mesh,
        in_specs=(
            P(None, None, "azim", "axial", "rad"),
            P(None, None, "azim", "axial", "rad"),
            P(None, None, "azim", "axial", "rad"),
            P(None, "azim", "axial", "rad"),
            P(None, "azim", "axial", "rad"),
            P("azim", "axial", "rad"),
            P(),
            P(),
            P(),
        ),
        out_specs=P(None, None, "azim", "axial", "rad"),
        check_vma=False,
    )
```

profile of v0, /device:TPU:0, one launch (start us, length us, event | category | flops | bytes accessed | tf_op | source)
XLA Modules:
  0.0 155.4 jit_solution(5066451087597288339)
XLA Ops:
  3.5 1.6 %fusion.35 = (f32[4,48,2,4,128]{4,1,0,3,2:T(8,128)S(1)}, f32[4,48,2,4,128]{4,1,0,3,2:T(8,128)}, f32[2,4,128]{2,1,0:T(4,128)S(1)}, f32[2,4,128]{2,1,0:T(4,128)S(1)}, f32[4,48,2,4,128]{4,1,0,3,2:T(8,128)}) fusion(f32[4,48,2,4,128]{4,3,2,1,0:T(4,128)S(1)} %copy-done, f32[2,4,128]{2,1,0:T(4,128)S(1)} %get-tuple-element.38, f32[4,48]{1,0:T(4,128)S(1)} %get-tuple-element.37, ...), kind=kLoop, calls=%fused_computation.98 | loop fusion | flops 2357248 | bytes 5306048 | tf_op args[0]
  5.3 5.1 %collective-permute-start.1 = (f32[198,1,4,128]{3,0,2,1:T(8,128)S(1)}, f32[198,1,4,128]{3,0,2,1:T(8,128)S(1)}, u32[]{:S(2)}, u32[]{:S(2)}) collective-permute-start(f32[198,1,4,128]{3,0,2,1:T(8,128)S(1)} %get-tuple-element.26), channel_id=1, source_target_pairs={{8,0},{16,8},{24,16},{0,24},{9,1},{17,9},{25,17},{1,25},{10,2},{18... | collective-permute-start | bytes 1216520 | tf_op jit(solution)/shard_map/ppermute | solution.py:19
  10.5 9.8 %collective-permute-done.1 = f32[198,1,4,128]{3,0,2,1:T(8,128)S(1)} collective-permute-done((f32[198,1,4,128]{3,0,2,1:T(8,128)S(1)}, f32[198,1,4,128]{3,0,2,1:T(8,128)S(1)}, u32[]{:S(2)}, u32[]{:S(2)}) %collective-permute-start.1) | collective-permute-done | bytes 405536 | tf_op jit(solution)/shard_map/ppermute | solution.py:19
  20.3 8.5 %collective-permute-done = f32[198,1,4,128]{3,0,2,1:T(8,128)S(1)} collective-permute-done((f32[198,1,4,128]{3,0,2,1:T(8,128)S(1)}, f32[198,1,4,128]{3,0,2,1:T(8,128)S(1)}, u32[]{:S(2)}, u32[]{:S(2)}) %collective-permute-start) | collective-permute-done | bytes 405536 | tf_op jit(solution)/shard_map/ppermute | solution.py:18
  29.7 1.7 %fusion.31 = (f32[198,4,4,1]{3,0,2,1:T(8,128)S(1)}, f32[198,4,4,1]{3,0,2,1:T(8,128)}) fusion(f32[198,4,4,128]{3,0,2,1:T(8,128)S(1)} %pad_maximum_fusion.2), kind=kLoop, calls=%fused_computation.94 | loop fusion | bytes 50688 | tf_op jit(solution)/shard_map/slice | solution.py:16
  31.5 2.0 %copy.130 = f32[198,4,4,1]{0,2,3,1:T(4,128)S(1)} copy(f32[198,4,4,1]{3,0,2,1:T(8,128)} %get-tuple-element.22) | data formatting | bytes 25344 | tf_op jit(solution)/shard_map/slice | solution.py:17
  33.5 1.3 collective-permute-start.3
  35.4 3.0 %collective-permute-start.2 = (f32[198,4,4,1]{0,2,3,1:T(4,128)S(1)}, f32[198,4,4,1]{0,2,3,1:T(4,128)S(1)}, u32[]{:S(2)}, u32[]{:S(2)}) collective-permute-start(f32[198,4,4,1]{0,2,3,1:T(4,128)S(1)} %copy.129), channel_id=1, source_target_pairs={{0,2},{2,4},{4,6},{1,3},{3,5},{5,7},{8,10},{10,12},{12,14},{9,11},... | collective-permute-start | bytes 38024 | tf_op jit(solution)/shard_map/ppermute | solution.py:18
  38.5 2.1 %split.16 = f32[4,47,2,4,128]{4,1,0,3,2:T(8,128)} slice(f32[4,48,2,4,128]{4,1,0,3,2:T(8,128)} %get-tuple-element.30), slice={[0:4], [1:48], [0:2], [0:4], [0:128]} | slice | bytes 1540096 | tf_op jit(solution)/shard_map/transpose(jvp())/split | solution.py:33
  41.2 1.8 %copy.131 = f32[198,4,4,1]{3,0,2,1:T(8,128)} copy(f32[198,4,4,1]{0,2,3,1:T(4,128)S(1)} %collective-permute-done.2) | data formatting | bytes 25344 | tf_op jit(solution)/shard_map/ppermute | solution.py:18
  43.0 3.1 %pad_maximum_fusion.10 = (f32[198,4,1,130]{3,0,2,1:T(8,128)}, f32[198,4,1,130]{3,0,2,1:T(8,128)}) fusion(f32[198,4,4,1]{3,0,2,1:T(8,128)S(1)} %copy.132, f32[198,4,4,1]{3,0,2,1:T(8,128)} %copy.131, f32[198,1,4,128]{3,0,2,1:T(8,128)} %copy-done.3, f32[198,1,4,128]{3,0,2,1:T(8,128)} %copy-done.4, f32[3,2,4,128]{3,0,2,1:T(4,128)S(1)} %copy.128, ...), kind=kLoop, calls=%fused_computation.10 | loop fusion | flops 1235520 | bytes 2471040 | tf_op jit(solution)/shard_map/slice | solution.py:16
  46.1 2.3 %copy.134 = f32[198,4,1,130]{0,1,3,2:T(4,128)} copy(f32[198,4,1,130]{3,0,2,1:T(8,128)} %get-tuple-element.18) | data formatting | bytes 823680 | tf_op jit(solution)/shard_map/slice | solution.py:17
  48.4 1.3 collective-permute-start.5
  49.7 2.3 %copy.133 = f32[198,4,1,130]{0,1,3,2:T(4,128)} copy(f32[198,4,1,130]{3,0,2,1:T(8,128)} %get-tuple-element.17) | data formatting | bytes 823680 | tf_op jit(solution)/shard_map/slice | solution.py:16
  51.9 6.2 %collective-permute-start.4 = (f32[198,4,1,130]{0,1,3,2:T(4,128)}, f32[198,4,1,130]{0,1,3,2:T(4,128)}, u32[]{:S(2)}, u32[]{:S(2)}) collective-permute-start(f32[198,4,1,130]{0,1,3,2:T(4,128)} %copy.133), channel_id=1, source_target_pairs={{0,1},{2,3},{4,5},{6,7},{8,9},{10,11},{12,13},{14,15},{16,17},{18,... | collective-permute-start | bytes 1235528 | tf_op jit(solution)/shard_map/ppermute | solution.py:18
  59.1 2.0 %slice_multiply_fusion.1 = f32[3,48,2,4,128]{4,1,0,3,2:T(8,128)} fusion(f32[4,48,2,4,128]{4,1,0,3,2:T(8,128)} %get-tuple-element.30, f32[3,48]{1,0:T(4,128)S(1)} %slice.228), kind=kLoop, calls=%fused_computation.61 | loop fusion | flops 147456 | bytes 1180224 | tf_op jit(solution)/shard_map/transpose(jvp())/mul | solution.py:37
  61.1 4.3 %collective-permute-done.5 = f32[198,4,1,130]{0,1,3,2:T(4,128)} collective-permute-done((f32[198,4,1,130]{0,1,3,2:T(4,128)}, f32[198,4,1,130]{0,1,3,2:T(4,128)}, u32[]{:S(2)}, u32[]{:S(2)}) %collective-permute-start.5) | collective-permute-done | bytes 411872 | tf_op jit(solution)/shard_map/ppermute | solution.py:19
  65.4 2.3 %copy.136 = f32[198,4,1,130]{3,0,2,1:T(8,128)} copy(f32[198,4,1,130]{0,1,3,2:T(4,128)} %collective-permute-done.5) | data formatting | bytes 823680 | tf_op jit(solution)/shard_map/ppermute | solution.py:19
  67.7 2.2 %collective-permute-done.4 = f32[198,4,1,130]{0,1,3,2:T(4,128)} collective-permute-done((f32[198,4,1,130]{0,1,3,2:T(4,128)}, f32[198,4,1,130]{0,1,3,2:T(4,128)}, u32[]{:S(2)}, u32[]{:S(2)}) %collective-permute-start.4) | collective-permute-done | bytes 411872 | tf_op jit(solution)/shard_map/ppermute | solution.py:18
  69.9 2.3 %copy.135 = f32[198,4,1,130]{3,0,2,1:T(8,128)} copy(f32[198,4,1,130]{0,1,3,2:T(4,128)} %collective-permute-done.4) | data formatting | bytes 823680 | tf_op jit(solution)/shard_map/ppermute | solution.py:18
  72.2 6.8 %pad_maximum_fusion = f32[198,4,6,130]{3,0,2,1:T(8,128)S(1)} fusion(f32[198,4,1,130]{3,0,2,1:T(8,128)} %copy.136, f32[198,4,4,1]{3,0,2,1:T(8,128)S(1)} %copy.132, f32[198,1,4,128]{3,0,2,1:T(8,128)} %copy-done.3, f32[3,2,4,128]{3,0,2,1:T(4,128)S(1)} %copy.128, f32[3,2,4,128]{3,0,2,1:T(4,128)S(1)} %copy.127, f32[192,2,4,128]{3,0,2,1:T(8,128)S(1)} %bitcast.33, ...), kind=kLoop, calls=%fused_computation | loop fusion | flops 4942080 | bytes 4942080 | tf_op jit(solution)/shard_map/concatenate | solution.py:20
  80.3 2.2 %broadcast_multiply_fusion = (f32[4,48,2,4,128]{4,1,0,3,2:T(8,128)}, f32[4,48,2,4,128]{4,1,0,3,2:T(8,128)S(1)}) fusion(f32[2,4,128]{2,1,0:T(4,128)S(1)} %get-tuple-element.39, f32[1,48,2,4,128]{4,1,0,3,2:T(8,128)S(1)} %add_multiply_fusion.1, f32[3,48,2,4,128]{4,1,0,3,2:T(8,128)S(1)} %copy-done.12, f32[4,47,2,4,128]{4,1,0,3,2:T(8,128)S(1)} %copy-done.9, ...), kind=kLoop, calls=%fused_computation.64 | loop fusion | flops 5505024 | bytes 9453760 | tf_op jit(solution)/shard_map/transpose(jvp())/mul | solution.py:37
  82.7 1.8 %collective-permute-start.7 = (f32[192,1,4,128]{3,0,2,1:T(8,128)S(1)}, f32[192,1,4,128]{3,0,2,1:T(8,128)S(1)}, u32[]{:S(2)}, u32[]{:S(2)}) collective-permute-start(f32[192,1,4,128]{3,0,2,1:T(8,128)S(1)} %get-tuple-element.28), channel_id=1, source_target_pairs={{8,0},{16,8},{24,16},{0,24},{9,1},{17,9},{25,17},{1,25},{10,2},{18... | collective-permute-start | bytes 1179656 | tf_op jit(solution)/shard_map/ppermute | solution.py:19
  85.8 8.7 %collective-permute-done.7 = f32[192,1,4,128]{3,0,2,1:T(8,128)S(1)} collective-permute-done((f32[192,1,4,128]{3,0,2,1:T(8,128)S(1)}, f32[192,1,4,128]{3,0,2,1:T(8,128)S(1)}, u32[]{:S(2)}, u32[]{:S(2)}) %collective-permute-start.7) | collective-permute-done | bytes 393248 | tf_op jit(solution)/shard_map/ppermute | solution.py:19
  94.5 7.9 %collective-permute-done.6 = f32[192,1,4,128]{3,0,2,1:T(8,128)S(1)} collective-permute-done((f32[192,1,4,128]{3,0,2,1:T(8,128)S(1)}, f32[192,1,4,128]{3,0,2,1:T(8,128)S(1)}, u32[]{:S(2)}, u32[]{:S(2)}) %collective-permute-start.6) | collective-permute-done | bytes 393248 | tf_op jit(solution)/shard_map/ppermute | solution.py:18
  103.3 1.7 %fusion.32 = (f32[192,4,4,1]{3,0,2,1:T(8,128)S(1)}, f32[192,4,4,1]{3,0,2,1:T(8,128)}) fusion(f32[192,4,4,128]{3,0,2,1:T(8,128)S(1)} %pad_maximum_fusion.3), kind=kLoop, calls=%fused_computation.95 | loop fusion | bytes 49152 | tf_op jit(solution)/shard_map/slice | solution.py:16
  105.0 2.6 %copy.154 = f32[192,4,4,1]{0,2,3,1:T(4,128)} copy(f32[192,4,4,1]{3,0,2,1:T(8,128)} %get-tuple-element.24) | data formatting | bytes 24576 | tf_op jit(solution)/shard_map/slice | solution.py:17
  107.6 1.3 collective-permute-start.9
  108.9 1.2 copy.153
  110.1 3.6 %collective-permute-start.8 = (f32[192,4,4,1]{0,2,3,1:T(4,128)}, f32[192,4,4,1]{0,2,3,1:T(4,128)}, u32[]{:S(2)}, u32[]{:S(2)}) collective-permute-start(f32[192,4,4,1]{0,2,3,1:T(4,128)} %copy.153), channel_id=1, source_target_pairs={{0,2},{2,4},{4,6},{1,3},{3,5},{5,7},{8,10},{10,12},{12,14},{9,11},... | collective-permute-start | bytes 36872 | tf_op jit(solution)/shard_map/ppermute | solution.py:18
  113.7 1.3 negate_multiply_fusion
  115.0 2.1 %split.18 = f32[4,47,2,4,128]{4,1,0,3,2:T(8,128)} slice(f32[4,48,2,4,128]{4,1,0,3,2:T(8,128)} %get-tuple-element.9), slice={[0:4], [1:48], [0:2], [0:4], [0:128]} | slice | bytes 1540096 | tf_op jit(solution)/shard_map/transpose(jvp())/split | solution.py:33
  117.1 1.2 copy.156
  118.4 2.4 %copy.155 = f32[192,4,4,1]{3,0,2,1:T(8,128)} copy(f32[192,4,4,1]{0,2,3,1:T(4,128)} %collective-permute-done.8) | data formatting | bytes 24576 | tf_op jit(solution)/shard_map/ppermute | solution.py:18
  120.8 3.0 %pad_maximum_fusion.16 = (f32[192,4,1,130]{3,0,2,1:T(8,128)}, f32[192,4,1,130]{3,0,2,1:T(8,128)}) fusion(f32[192,4,4,1]{3,0,2,1:T(8,128)S(1)} %copy.156, f32[192,4,4,1]{3,0,2,1:T(8,128)} %copy.155, f32[192,1,4,128]{3,0,2,1:T(8,128)S(1)} %collective-permute-done.7, f32[192,2,4,128]{3,0,2,1:T(8,128)S(1)} %bitcast.26, f32[192,1,4,128]{3,0,2,1:T(8,128)} %copy-done.5), kind=kLoop, calls=%fused_computation.35 | loop fusion | flops 798720 | bytes 2396160 | tf_op jit(solution)/shard_map/slice | solution.py:16
  123.8 2.3 %copy.158 = f32[192,4,1,130]{0,1,3,2:T(4,128)} copy(f32[192,4,1,130]{3,0,2,1:T(8,128)} %get-tuple-element.20) | data formatting | bytes 798720 | tf_op jit(solution)/shard_map/slice | solution.py:17
  126.1 1.3 collective-permute-start.11
  127.3 2.3 %copy.157 = f32[192,4,1,130]{0,1,3,2:T(4,128)} copy(f32[192,4,1,130]{3,0,2,1:T(8,128)} %get-tuple-element.19) | data formatting | bytes 798720 | tf_op jit(solution)/shard_map/slice | solution.py:16
  129.6 6.2 %collective-permute-start.10 = (f32[192,4,1,130]{0,1,3,2:T(4,128)}, f32[192,4,1,130]{0,1,3,2:T(4,128)}, u32[]{:S(2)}, u32[]{:S(2)}) collective-permute-start(f32[192,4,1,130]{0,1,3,2:T(4,128)} %copy.157), channel_id=1, source_target_pairs={{0,1},{2,3},{4,5},{6,7},{8,9},{10,11},{12,13},{14,15},{16,17},{18,... | collective-permute-start | bytes 1198088 | tf_op jit(solution)/shard_map/ppermute | solution.py:18
  135.8 1.6 %add_multiply_fusion = f32[1,48,2,4,128]{4,1,0,3,2:T(8,128)} fusion(f32[4,48,2,4,128]{4,1,0,3,2:T(8,128)} %copy-done.1, f32[2,4,128]{2,1,0:T(4,128)} %negate_multiply_fusion), kind=kLoop, calls=%fused_computation.68 | loop fusion | flops 98304 | bytes 397312 | tf_op jit(solution)/shard_map/transpose(jvp())/add_any | solution.py:29
  137.4 2.0 %slice_multiply_fusion = f32[3,48,2,4,128]{4,1,0,3,2:T(8,128)} fusion(f32[4,48,2,4,128]{4,1,0,3,2:T(8,128)} %get-tuple-element.9, f32[3,48]{1,0:T(4,128)} %copy-done.25), kind=kLoop, calls=%fused_computation.60 | loop fusion | flops 147456 | bytes 1180224 | tf_op jit(solution)/shard_map/transpose(jvp())/mul | solution.py:37
  139.4 2.7 %collective-permute-done.11 = f32[192,4,1,130]{0,1,3,2:T(4,128)} collective-permute-done((f32[192,4,1,130]{0,1,3,2:T(4,128)}, f32[192,4,1,130]{0,1,3,2:T(4,128)}, u32[]{:S(2)}, u32[]{:S(2)}) %collective-permute-start.11) | collective-permute-done | bytes 399392 | tf_op jit(solution)/shard_map/ppermute | solution.py:19
  142.1 2.3 %copy.160 = f32[192,4,1,130]{3,0,2,1:T(8,128)} copy(f32[192,4,1,130]{0,1,3,2:T(4,128)} %collective-permute-done.11) | data formatting | bytes 798720 | tf_op jit(solution)/shard_map/ppermute | solution.py:19
  144.3 2.0 %collective-permute-done.10 = f32[192,4,1,130]{0,1,3,2:T(4,128)} collective-permute-done((f32[192,4,1,130]{0,1,3,2:T(4,128)}, f32[192,4,1,130]{0,1,3,2:T(4,128)}, u32[]{:S(2)}, u32[]{:S(2)}) %collective-permute-start.10) | collective-permute-done | bytes 399392 | tf_op jit(solution)/shard_map/ppermute | solution.py:18
  146.3 2.3 %copy.159 = f32[192,4,1,130]{3,0,2,1:T(8,128)} copy(f32[192,4,1,130]{0,1,3,2:T(4,128)} %collective-permute-done.10) | data formatting | bytes 798720 | tf_op jit(solution)/shard_map/ppermute | solution.py:18
  148.6 3.9 %pad_maximum_fusion.1 = f32[192,4,6,130]{3,0,2,1:T(8,128)S(1)} fusion(f32[192,4,1,130]{3,0,2,1:T(8,128)} %copy.160, f32[192,4,4,1]{3,0,2,1:T(8,128)S(1)} %copy.156, f32[192,1,4,128]{3,0,2,1:T(8,128)S(1)} %collective-permute-done.7, f32[192,2,4,128]{3,0,2,1:T(8,128)S(1)} %bitcast.27, f32[192,1,4,128]{3,0,2,1:T(8,128)} %copy-done.5, ...), kind=kLoop, calls=%fused_computation.1 | loop fusion | flops 3594240 | bytes 4792320 | tf_op jit(solution)/shard_map/concatenate | solution.py:20
  152.6 1.4 fusion.4
  154.0 1.4 copy.162
  (126 shorter events, 10.1 us)
Async XLA Ops:
  0.0 2.1 %copy-start.7 = (bf16[4,48,2,4,128]{4,3,2,1,0:T(4,128)(2,1)S(1)}, bf16[4,48,2,4,128]{4,3,2,1,0:T(4,128)(2,1)}, u32[]{:S(2)}) copy-start(bf16[4,48,2,4,128]{4,3,2,1,0:T(4,128)(2,1)} %param.14) | copy-start | bytes 1179652
  1.1 0.9 copy-start.2
  1.1 1.3 copy-start.6
  1.1 1.3 copy-start.28
  2.0 0.8 copy-start.32
  2.1 0.7 copy-start.35
  2.1 0.7 copy-start.36
  2.1 1.5 copy-start
  2.2 0.9 copy-start.1
  2.8 77.5 %copy-start.19 = (f32[2,4,128]{2,1,0:T(4,128)}, f32[2,4,128]{2,1,0:T(4,128)S(1)}, u32[]{:S(2)}) copy-start(f32[2,4,128]{2,1,0:T(4,128)S(1)} %get-tuple-element.39) | copy-start | bytes 12292
  2.9 2.3 %copy-start.26 = (f32[4,48]{1,0:T(4,128)}, f32[4,48]{1,0:T(4,128)S(1)}, u32[]{:S(2)}) copy-start(f32[4,48]{1,0:T(4,128)S(1)} %get-tuple-element.37) | copy-start | bytes 2308
  2.9 35.6 %copy-start.23 = (f32[4,48]{1,0:T(4,128)}, f32[4,48]{1,0:T(4,128)S(1)}, u32[]{:S(2)}) copy-start(f32[4,48]{1,0:T(4,128)S(1)} %get-tuple-element.36) | copy-start | bytes 2308
  5.2 5.2 %copy-start.33 = (s32[2,4,128]{2,1,0:T(4,128)S(1)}, s32[2,4,128]{2,1,0:T(4,128)}, u32[]{:S(2)}) copy-start(s32[2,4,128]{2,1,0:T(4,128)} %param.18) | copy-start | bytes 12292
  5.2 5.2 %copy-start.34 = (f32[4]{0:T(128)S(1)}, f32[4]{0:T(128)}, u32[]{:S(2)}) copy-start(f32[4]{0:T(128)} %param.21) | copy-start | bytes 52
  5.3 15.0 %collective-permute-start.1 = (f32[198,1,4,128]{3,0,2,1:T(8,128)S(1)}, f32[198,1,4,128]{3,0,2,1:T(8,128)S(1)}, u32[]{:S(2)}, u32[]{:S(2)}) collective-permute-start(f32[198,1,4,128]{3,0,2,1:T(8,128)S(1)} %get-tuple-element.26), channel_id=1, source_target_pairs={{8,0},{16,8},{24,16},{0,24},{9,1},{17,9},{25,17},{1,25},{10,2},{18... | collective-permute-start | bytes 1216520 | tf_op jit(solution)/shard_map/ppermute | solution.py:19
  10.4 18.4 %collective-permute-start = (f32[198,1,4,128]{3,0,2,1:T(8,128)S(1)}, f32[198,1,4,128]{3,0,2,1:T(8,128)S(1)}, u32[]{:S(2)}, u32[]{:S(2)}) collective-permute-start(f32[198,1,4,128]{3,0,2,1:T(8,128)S(1)} %get-tuple-element.25), channel_id=1, source_target_pairs={{0,8},{8,16},{16,24},{24,0},{1,9},{9,17},{17,25},{25,1},{2,10},{10... | collective-permute-start | bytes 1216520 | tf_op jit(solution)/shard_map/ppermute | solution.py:18
  10.5 28.0 %copy-start.21 = (f32[2,4,128]{2,1,0:T(4,128)}, f32[2,4,128]{2,1,0:T(4,128)S(1)}, u32[]{:S(2)}) copy-start(f32[2,4,128]{2,1,0:T(4,128)S(1)} %select_reduce_fusion) | copy-start | bytes 12292
  20.3 8.5 %copy-start.3 = (f32[198,1,4,128]{3,0,2,1:T(8,128)}, f32[198,1,4,128]{3,0,2,1:T(8,128)S(1)}, u32[]{:S(2)}) copy-start(f32[198,1,4,128]{3,0,2,1:T(8,128)S(1)} %collective-permute-done.1) | copy-start | bytes 1216516
  28.8 0.7 copy-start.4
  33.5 7.1 %collective-permute-start.3 = (f32[198,4,4,1]{0,2,3,1:T(4,128)S(1)}, f32[198,4,4,1]{0,2,3,1:T(4,128)S(1)}, u32[]{:S(2)}, u32[]{:S(2)}) collective-permute-start(f32[198,4,4,1]{0,2,3,1:T(4,128)S(1)} %copy.130), channel_id=1, source_target_pairs={{2,0},{4,2},{6,4},{3,1},{5,3},{7,5},{10,8},{12,10},{14,12},{11,9},... | collective-permute-start | bytes 38024 | tf_op jit(solution)/shard_map/ppermute | solution.py:19
  35.4 5.8 %collective-permute-start.2 = (f32[198,4,4,1]{0,2,3,1:T(4,128)S(1)}, f32[198,4,4,1]{0,2,3,1:T(4,128)S(1)}, u32[]{:S(2)}, u32[]{:S(2)}) collective-permute-start(f32[198,4,4,1]{0,2,3,1:T(4,128)S(1)} %copy.129), channel_id=1, source_target_pairs={{0,2},{2,4},{4,6},{1,3},{3,5},{5,7},{8,10},{10,12},{12,14},{9,11},... | collective-permute-start | bytes 38024 | tf_op jit(solution)/shard_map/ppermute | solution.py:18
  38.5 20.6 %copy-start.25 = (f32[3,48]{1,0:T(4,128)}, f32[3,48]{1,0:T(4,128)S(1)}, u32[]{:S(2)}) copy-start(f32[3,48]{1,0:T(4,128)S(1)} %slice.228) | copy-start | bytes 1732
  48.4 17.0 %collective-permute-start.5 = (f32[198,4,1,130]{0,1,3,2:T(4,128)}, f32[198,4,1,130]{0,1,3,2:T(4,128)}, u32[]{:S(2)}, u32[]{:S(2)}) collective-permute-start(f32[198,4,1,130]{0,1,3,2:T(4,128)} %copy.134), channel_id=1, source_target_pairs={{1,0},{3,2},{5,4},{7,6},{9,8},{11,10},{13,12},{15,14},{17,16},{19,... | collective-permute-start | bytes 1235528 | tf_op jit(solution)/shard_map/ppermute | solution.py:19
  51.9 18.0 %collective-permute-start.4 = (f32[198,4,1,130]{0,1,3,2:T(4,128)}, f32[198,4,1,130]{0,1,3,2:T(4,128)}, u32[]{:S(2)}, u32[]{:S(2)}) collective-permute-start(f32[198,4,1,130]{0,1,3,2:T(4,128)} %copy.133), channel_id=1, source_target_pairs={{0,1},{2,3},{4,5},{6,7},{8,9},{10,11},{12,13},{14,15},{16,17},{18,... | collective-permute-start | bytes 1235528 | tf_op jit(solution)/shard_map/ppermute | solution.py:18
  79.0 1.3 copy-start.9
  79.0 1.3 copy-start.12
  80.2 2.4 %copy-start.15 = (f32[2,4,128]{2,1,0:T(4,128)}, f32[2,4,128]{2,1,0:T(4,128)S(1)}, u32[]{:S(2)}) copy-start(f32[2,4,128]{2,1,0:T(4,128)S(1)} %copy.140) | copy-start | bytes 12292
  80.3 2.3 %copy-start.17 = (f32[2,4,128]{2,1,0:T(4,128)}, f32[2,4,128]{2,1,0:T(4,128)S(1)}, u32[]{:S(2)}) copy-start(f32[2,4,128]{2,1,0:T(4,128)S(1)} %copy.138) | copy-start | bytes 12292
  82.6 2.2 %slice-start = ((f32[4,48,2,4,128]{4,1,0,3,2:T(8,128)}), f32[3,48,2,4,128]{4,1,0,3,2:T(8,128)S(1)}, s32[]{:S(2)}) async-start(f32[4,48,2,4,128]{4,1,0,3,2:T(8,128)} %copy-done.1), calls=%async_computation | async-start | bytes 1179648 | tf_op jit(solution)/shard_map/jvp()/slice | solution.py:30
  82.6 2.2 %copy-start.8 = (bf16[4,48,2,4,128]{4,3,2,1,0:T(4,128)(2,1)S(1)}, bf16[4,48,2,4,128]{4,3,2,1,0:T(4,128)(2,1)}, u32[]{:S(2)}) copy-start(bf16[4,48,2,4,128]{4,3,2,1,0:T(4,128)(2,1)} %param.14) | copy-start | bytes 1179652
  82.6 2.2 %copy-start.11 = (f32[4,48,2,4,128]{4,1,0,3,2:T(8,128)S(1)}, f32[4,48,2,4,128]{4,1,0,3,2:T(8,128)}, u32[]{:S(2)}) copy-start(f32[4,48,2,4,128]{4,1,0,3,2:T(8,128)} %get-tuple-element.35) | copy-start | bytes 2359300
  82.6 2.2 %copy-start.24 = (f32[4,48]{1,0:T(4,128)S(1)}, f32[4,48]{1,0:T(4,128)}, u32[]{:S(2)}) copy-start(f32[4,48]{1,0:T(4,128)} %copy-done.23) | copy-start | bytes 2308
  82.6 2.2 %copy-start.27 = (f32[4,48]{1,0:T(4,128)S(1)}, f32[4,48]{1,0:T(4,128)}, u32[]{:S(2)}) copy-start(f32[4,48]{1,0:T(4,128)} %copy-done.26) | copy-start | bytes 2308
  82.6 2.2 %copy-start.29 = (f32[48]{0:T(128)S(1)}, f32[48]{0:T(128)}, u32[]{:S(2)}) copy-start(f32[48]{0:T(128)} %param.20) | copy-start | bytes 580
  82.7 11.9 %collective-permute-start.7 = (f32[192,1,4,128]{3,0,2,1:T(8,128)S(1)}, f32[192,1,4,128]{3,0,2,1:T(8,128)S(1)}, u32[]{:S(2)}, u32[]{:S(2)}) collective-permute-start(f32[192,1,4,128]{3,0,2,1:T(8,128)S(1)} %get-tuple-element.28), channel_id=1, source_target_pairs={{8,0},{16,8},{24,16},{0,24},{9,1},{17,9},{25,17},{1,25},{10,2},{18... | collective-permute-start | bytes 1179656 | tf_op jit(solution)/shard_map/ppermute | solution.py:19
  84.5 18.0 %collective-permute-start.6 = (f32[192,1,4,128]{3,0,2,1:T(8,128)S(1)}, f32[192,1,4,128]{3,0,2,1:T(8,128)S(1)}, u32[]{:S(2)}, u32[]{:S(2)}) collective-permute-start(f32[192,1,4,128]{3,0,2,1:T(8,128)S(1)} %get-tuple-element.27), channel_id=1, source_target_pairs={{0,8},{8,16},{16,24},{24,0},{1,9},{9,17},{17,25},{25,1},{2,10},{10... | collective-permute-start | bytes 1179656 | tf_op jit(solution)/shard_map/ppermute | solution.py:18
  102.4 0.7 copy-start.5
  107.6 9.5 %collective-permute-start.9 = (f32[192,4,4,1]{0,2,3,1:T(4,128)}, f32[192,4,4,1]{0,2,3,1:T(4,128)}, u32[]{:S(2)}, u32[]{:S(2)}) collective-permute-start(f32[192,4,4,1]{0,2,3,1:T(4,128)} %copy.154), channel_id=1, source_target_pairs={{2,0},{4,2},{6,4},{3,1},{5,3},{7,5},{10,8},{12,10},{14,12},{11,9},... | collective-permute-start | bytes 36872 | tf_op jit(solution)/shard_map/ppermute | solution.py:19
  110.1 8.3 %collective-permute-start.8 = (f32[192,4,4,1]{0,2,3,1:T(4,128)}, f32[192,4,4,1]{0,2,3,1:T(4,128)}, u32[]{:S(2)}, u32[]{:S(2)}) collective-permute-start(f32[192,4,4,1]{0,2,3,1:T(4,128)} %copy.153), channel_id=1, source_target_pairs={{0,2},{2,4},{4,6},{1,3},{3,5},{5,7},{8,10},{10,12},{12,14},{9,11},... | collective-permute-start | bytes 36872 | tf_op jit(solution)/shard_map/ppermute | solution.py:18
  126.1 16.0 %collective-permute-start.11 = (f32[192,4,1,130]{0,1,3,2:T(4,128)}, f32[192,4,1,130]{0,1,3,2:T(4,128)}, u32[]{:S(2)}, u32[]{:S(2)}) collective-permute-start(f32[192,4,1,130]{0,1,3,2:T(4,128)} %copy.158), channel_id=1, source_target_pairs={{1,0},{3,2},{5,4},{7,6},{9,8},{11,10},{13,12},{15,14},{17,16},{19,... | collective-permute-start | bytes 1198088 | tf_op jit(solution)/shard_map/ppermute | solution.py:19
  129.6 16.7 %collective-permute-start.10 = (f32[192,4,1,130]{0,1,3,2:T(4,128)}, f32[192,4,1,130]{0,1,3,2:T(4,128)}, u32[]{:S(2)}, u32[]{:S(2)}) collective-permute-start(f32[192,4,1,130]{0,1,3,2:T(4,128)} %copy.157), channel_id=1, source_target_pairs={{0,1},{2,3},{4,5},{6,7},{8,9},{10,11},{12,13},{14,15},{16,17},{18,... | collective-permute-start | bytes 1198088 | tf_op jit(solution)/shard_map/ppermute | solution.py:18
  148.6 3.9 %copy-start.10 = (f32[4,47,2,4,128]{4,1,0,3,2:T(8,128)S(1)}, f32[4,47,2,4,128]{4,1,0,3,2:T(8,128)}, u32[]{:S(2)}) copy-start(f32[4,47,2,4,128]{4,1,0,3,2:T(8,128)} %split.18) | copy-start | bytes 2310148
  148.6 3.9 %copy-start.13 = (f32[3,48,2,4,128]{4,1,0,3,2:T(8,128)S(1)}, f32[3,48,2,4,128]{4,1,0,3,2:T(8,128)}, u32[]{:S(2)}) copy-start(f32[3,48,2,4,128]{4,1,0,3,2:T(8,128)} %slice_multiply_fusion) | copy-start | bytes 1769476
  148.6 3.9 %copy-start.14 = (f32[1,48,2,4,128]{4,1,0,3,2:T(8,128)S(1)}, f32[1,48,2,4,128]{4,1,0,3,2:T(8,128)}, u32[]{:S(2)}) copy-start(f32[1,48,2,4,128]{4,1,0,3,2:T(8,128)} %add_multiply_fusion) | copy-start | bytes 589828
  148.6 3.9 %copy-start.16 = (f32[2,4,128]{2,1,0:T(4,128)S(1)}, f32[2,4,128]{2,1,0:T(4,128)}, u32[]{:S(2)}) copy-start(f32[2,4,128]{2,1,0:T(4,128)} %copy-done.15) | copy-start | bytes 12292
  148.6 3.9 %copy-start.18 = (f32[2,4,128]{2,1,0:T(4,128)S(1)}, f32[2,4,128]{2,1,0:T(4,128)}, u32[]{:S(2)}) copy-start(f32[2,4,128]{2,1,0:T(4,128)} %copy-done.17) | copy-start | bytes 12292
  148.6 3.9 %copy-start.20 = (f32[2,4,128]{2,1,0:T(4,128)S(1)}, f32[2,4,128]{2,1,0:T(4,128)}, u32[]{:S(2)}) copy-start(f32[2,4,128]{2,1,0:T(4,128)} %copy-done.19) | copy-start | bytes 12292
  148.6 3.9 %copy-start.30 = (f32[48]{0:T(128)S(1)}, f32[48]{0:T(128)}, u32[]{:S(2)}) copy-start(f32[48]{0:T(128)} %param.20) | copy-start | bytes 580
  (2 other events, 1.4 us)
where the time goes:
time: 157 us; the launch traced here: 155 us
  waiting for transfers between devices  46.2 us (29%)
  local copies, waits for them, and re-layouts  44.5 us (28%)
  other arithmetic  32.8 us (21%)
  starting transfers between devices  31.3 us (20%)
    ppermute x6, waiting for transfers between devices, extended(): after = lax.ppermute(first, axis, down)  25.6 us
    ppermute x6, waiting for transfers between devices, extended(): before = lax.ppermute(last, axis, up)  20.7 us
    ppermute x6, starting transfers between devices, extended(): before = lax.ppermute(last, axis, up)  19.3 us
    ppermute x6, starting transfers between devices, extended(): after = lax.ppermute(first, axis, down)  12 us
    concatenate x4, other arithmetic, extended(): x = jnp.concatenate([before, x, after], axis=dim)  10.9 us
    slice x8, local copies, waits for them, and re-layouts, extended(): last = lax.slice_in_dim(x, length - width, length, axis=dim)  9.92 us
    slice x4, local copies, waits for them, and re-layouts, extended(): first = lax.slice_in_dim(x, 0, width, axis=dim)  9.22 us
    ppermute x4, local copies, waits for them, and re-layouts, extended(): before = lax.ppermute(last, axis, up)  8.7 us
  transfers between devices with their start and end apart: 12, of which 8 were waited for; matrix products, arithmetic and copies ran while one was open for 17% of the time, Pallas kernels for 0%

commit v1 on v0

v1 whole, which is shorter than its diff:
```python
import functools

import jax
import jax.numpy as jnp
from jax import lax
from jax.experimental import pallas as pl
from jax.experimental.pallas import tpu as pltpu
from jax.sharding import PartitionSpec as P

supersat_scale = 1.5
crowding = 0.02
nucleus_moments = (1.0, 0.5, 0.25, 0.125)
f32 = jnp.float32
exact = lax.Precision.HIGHEST


def rows_of():
    return lax.broadcasted_iota(jnp.int32, (8, 128), 0)


def lanes_of():
    return lax.broadcasted_iota(jnp.int32, (8, 128), 1)


def faces(speeds_ref, flags_ref):
    p, q = [], []
    for d in range(3):
        speed, upwind = speeds_ref[d], flags_ref[d].astype(f32)
        p.append(speed * upwind)
        q.append(speed * (1.0 - upwind))
    return p, q


class Local:
    def __init__(self, p, q):
        row, lane = rows_of(), lanes_of()
        z, top = row % 4, row >= 4
        self.azim = jnp.where(top, q[0], pltpu.roll(p[0], 4, 0))
        self.ax_up = jnp.where(z == 3, 0.0, pltpu.roll(p[1], 7, 0))
        self.ax_dn = jnp.where(z == 0, 0.0, q[1])
        self.rad_up = jnp.where(lane == 127, 0.0, pltpu.roll(p[2], 127, 1))
        self.rad_dn = jnp.where(lane == 0, 0.0, q[2])
        self.centre = self.azim + self.ax_up + q[1] + self.rad_up + q[2] + jnp.where(top, 0.0, q[0])

    def __call__(self, x):
        return (
            self.azim * pltpu.roll(x, 4, 0)
            + self.ax_up * pltpu.roll(x, 7, 0)
            + self.ax_dn * pltpu.roll(x, 1, 0)
            + self.rad_up * pltpu.roll(x, 127, 1)
            + self.rad_dn * pltpu.roll(x, 1, 1)
            - self.centre * x
        )


def pair_rows(x, first, second):
    return jnp.where(
        rows_of() % 2 == 0,
        jnp.broadcast_to(x[first : first + 1], (8, 128)),
        jnp.broadcast_to(x[second : second + 1], (8, 128)),
    )


def pack(comps, x_ref, where_ref, dn_ref, up_ref, ax_ref, radup_ref, raddn_ref):
    for c in range(comps):
        dn_ref[4 * c : 4 * c + 4] = x_ref[8 * c : 8 * c + 4]
        up_ref[4 * c : 4 * c + 4] = x_ref[8 * c + 4 : 8 * c + 8]

    @pl.when(where_ref[0] == 0)
    def _():
        ax_ref[0 : 2 * comps] = x_ref[pl.ds(3, 2 * comps, stride=4)]

    @pl.when(where_ref[0] != 0)
    def _():
        ax_ref[0 : 2 * comps] = x_ref[pl.ds(0, 2 * comps, stride=4)]

    ends = columns(x_ref[...])
    radup_ref[:, 0 : 8 * comps] = ends[0:1]
    raddn_ref[:, 0 : 8 * comps] = ends[1:2]


def columns(x):
    row, lane = rows_of(), lanes_of()
    take = jnp.where(((row == 0) & (lane == 127)) | ((row == 1) & (lane == 0)), 1.0, 0.0)
    return lax.dot_general(take, x, (((1,), (1,)), ((), ())), precision=exact, preferred_element_type=f32)


def put_columns(lower, upper):
    n = lower.shape[1]
    row, lane = rows_of(), lanes_of()
    which = lax.broadcasted_iota(jnp.int32, (8, n), 0)
    both = jnp.where(which == 0, lower, jnp.where(which == 1, upper, 0.0))
    place = jnp.where(((row == 0) & (lane == 0)) | ((row == 1) & (lane == 127)), 1.0, 0.0)
    return lax.dot_general(both, place, (((0,), (0,)), ((), ())), precision=exact, preferred_element_type=f32)


def first_pack(comps, where_ref, a_ref, speeds_ref, flags_ref, dn_ref, up_ref, ax_ref, radup_ref, raddn_ref):
    p, _ = faces(speeds_ref, flags_ref)
    pack(comps, a_ref, where_ref, dn_ref, up_ref, ax_ref, radup_ref, raddn_ref)
    dn_ref[4 * comps : 4 * comps + 8] = p[0]
    ax_ref[2 * comps : 2 * comps + 8] = pair_rows(p[1], 0, 4)
    radup_ref[:, 8 * comps :] = jnp.zeros((1, 128), f32)
    raddn_ref[:, 8 * comps :] = jnp.zeros((1, 128), f32)
    raddn_ref[:, 8 * comps : 8 * comps + 8] = columns(p[2])[1:2]


def source(sections, x_ref, u_ref, growth_ref, transfer_ref, zones_ref, rate_ref, finish):
    def inner(k, s, x):
        term = transfer_ref[s] * ((x[k][1] - x[k][0]) if s + 1 < sections else -x[k][0])
        if k < 3:
            term = term + ((k + 1.0) * growth_ref[s]) * x[k + 1][0]
        return term

    def load(s):
        got = []
        for k in range(4):
            c = k * sections + s
            here = x_ref[8 * c : 8 * c + 8]
            got.append((here, x_ref[8 * c + 8 : 8 * c + 16] if s + 1 < sections else None))
        return got

    squares = jnp.zeros((8, 128), f32)
    product = jnp.zeros((8, 128), f32)
    for s in range(sections):
        x = load(s)
        for k in range(4):
            u = u_ref[k * sections + s].astype(f32)
            product = product + u * inner(k, s, x)
        squares = squares + u * u
    sigma = supersat_scale / (1.0 + crowding * squares)
    birth = jnp.zeros((8, 128), f32)
    for k in range(4):
        c = k * sections
        birth = birth + nucleus_moments[k] * x_ref[8 * c : 8 * c + 8]
    rate = jnp.zeros((8, 128), f32)
    for label in range(rate_ref.shape[0]):
        rate = jnp.where(zones_ref[...] == label, rate_ref[label], rate)
    slope = (-2.0 * crowding / supersat_scale) * sigma * sigma * (product + 2.0 * rate * sigma * birth)
    for s in range(sections):
        x = load(s)
        for k in range(4):
            c = k * sections + s
            term = sigma * inner(k, s, x)
            if k == 3:
                term = term + u_ref[c].astype(f32) * slope
            finish(c, x[k][0], term)


def first_local(sections, a_ref, u_ref, speeds_ref, flags_ref, zones_ref, growth_ref, transfer_ref, rate_ref, out_ref):
    local = Local(*faces(speeds_ref, flags_ref))

    def finish(c, x, term):
        out_ref[8 * c : 8 * c + 8] = 0.5 * (x + local(x) + term)

    source(sections, a_ref, u_ref, growth_ref, transfer_ref, zones_ref, rate_ref, finish)


def second_local(
    sections, m_ref, a_ref, u_ref, edge_ref, speeds_ref, flags_ref, zones_ref, growth_ref, transfer_ref, rate_ref, out_ref
):
    local = Local(*faces(speeds_ref, flags_ref))
    local.centre = local.centre + (edge_ref[3] - 1.0)

    def finish(c, x, term):
        out_ref[8 * c : 8 * c + 8] = 0.5 * a_ref[8 * c : 8 * c + 8] + (local(x) + term)

    source(sections, m_ref, u_ref, growth_ref, transfer_ref, zones_ref, rate_ref, finish)


def add_halo(comps, scale, where_ref, part, below_ref, above_ref, ax_ref, hrad, azim, axial, rad, out_ref):
    top = rows_of() >= 4
    for c in range(comps):
        pair = 8 * (c // 2)
        below, above = below_ref[pair : pair + 8], above_ref[pair : pair + 8]
        if c % 2 == 0:
            halo = jnp.where(top, pltpu.roll(above, 4, 0), below)
        else:
            halo = jnp.where(top, above, pltpu.roll(below, 4, 0))
        out_ref[8 * c : 8 * c + 8] = part(c) + scale * (azim * halo + rad * hrad[8 * c : 8 * c + 8])
    several = jnp.concatenate([scale * axial] * (2 * comps // 8), axis=0)
    for start, index in ((3, 0), (0, 1)):

        @pl.when(where_ref[0] == index)
        def _():
            spots = pl.ds(start, 2 * comps, stride=4)
            out_ref[spots] = out_ref[spots] + several * ax_ref[0 : 2 * comps]


def first_halo(
    comps,
    where_ref,
    part_ref,
    a_ref,
    below_ref,
    above_ref,
    ax_ref,
    radlo_ref,
    radhi_ref,
    speeds_ref,
    flags_ref,
    m_ref,
    edge_ref,
    dn_ref,
    up_ref,
    axo_ref,
    radup_ref,
    raddn_ref,
):
    _, q = faces(speeds_ref, flags_ref)
    row, lane = rows_of(), lanes_of()
    hrad = put_columns(radlo_ref[...], radhi_ref[...])
    lower_half = where_ref[0] == 0
    p_azim = jnp.where(row >= 4, pltpu.roll(above_ref[4 * comps : 4 * comps + 8], 4, 0), 0.0)
    pairs = jnp.where(lower_half, ax_ref[2 * comps : 2 * comps + 8], 0.0)
    p_axial = jnp.where(row == 3, pairs[0:1], jnp.where(row == 7, pairs[1:2], 0.0))
    p_rad = jnp.where(lane == 127, hrad[8 * comps : 8 * comps + 8], 0.0)
    azim = jnp.where(row >= 4, p_azim, q[0])
    axial = jnp.where(lower_half, pairs, pair_rows(q[1], 0, 4))
    rad = jnp.where(lane == 0, q[2], p_rad)
    centre = p_azim + p_axial + p_rad
    edge_ref[0] = azim
    edge_ref[1] = axial
    edge_ref[2] = rad
    edge_ref[3] = centre

    def part(c):
        return part_ref[8 * c : 8 * c + 8] - (0.5 * centre) * a_ref[8 * c : 8 * c + 8]

    add_halo(comps, 0.5, where_ref, part, below_ref, above_ref, ax_ref, hrad, azim, axial, rad, m_ref)
    pack(comps, m_ref, where_ref, dn_ref, up_ref, axo_ref, radup_ref, raddn_ref)


def second_halo(comps, where_ref, part_ref, below_ref, above_ref, ax_ref, radlo_ref, radhi_ref, edge_ref, out_ref):
    hrad = put_columns(radlo_ref[...], radhi_ref[...])

    def part(c):
        return part_ref[8 * c : 8 * c + 8]

    add_halo(
        comps, 1.0, where_ref, part, below_ref, above_ref, ax_ref, hrad, edge_ref[0], edge_ref[1], edge_ref[2], out_ref
    )


VMEM = pl.BlockSpec(memory_space=pltpu.VMEM)
SMEM = pl.BlockSpec(memory_space=pltpu.SMEM)


def call(body, specs, outs, cost, *operands):
    many = isinstance(outs, list)
    return pl.pallas_call(
        body,
        in_specs=[SMEM if s == "s" else VMEM for s in specs],
        out_specs=[VMEM] * len(outs) if many else VMEM,
        out_shape=[jax.ShapeDtypeStruct(o, f32) for o in outs] if many else jax.ShapeDtypeStruct(outs, f32),
        cost_estimate=pl.CostEstimate(flops=cost, bytes_accessed=cost // 10, transcendentals=0),
        compiler_params=pltpu.CompilerParams(vmem_limit_bytes=32 * 1024 * 1024),
    )(*operands)


def exchange(dn, up, ax, radup, raddn):
    def shift(x, axis, step, wrap):
        size = lax.axis_size(axis)
        pairs = [(i, (i + step) % size) for i in range(size) if wrap or 0 <= i + step < size]
        return lax.ppermute(x, axis, pairs)

    above = shift(dn, "azim", -1, True)
    below = shift(up, "azim", 1, True)
    ax = lax.ppermute(ax, "axial", [(0, 1), (1, 0)])
    radlo = shift(radup, "rad", 1, False)
    radhi = shift(raddn, "rad", -1, False)
    return below, above, ax, radlo, radhi


def shards(adjoint_final, state_start, state_middle, speeds, flags, zones, growth_rate, transfer_rate, nucleation_rate):
    shape = adjoint_final.shape
    moments, sections = shape[:2]
    comps = moments * sections
    assert moments == 4 and shape[2:] == (2, 4, 128) and comps % 4 == 0
    assert lax.axis_size("axial") == 2
    cells = 8 * comps
    a = adjoint_final.reshape(cells, 128)
    start = state_start.reshape(comps, 8, 128)
    middle = state_middle.reshape(comps, 8, 128)
    speeds = speeds.reshape(3, 8, 128)
    flags = flags.reshape(3, 8, 128)
    zones = zones.reshape(8, 128)
    where = lax.axis_index("axial").reshape(1)
    half, rows = cells // 2, cells // 4

    first = call(
        functools.partial(first_pack, comps),
        "svvv",
        [(half + 8, 128), (half, 128), (rows + 8, 128), (1, cells + 128), (1, cells + 128)],
        2_000_000,
        where,
        a,
        speeds,
        flags,
    )
    part = call(
        functools.partial(first_local, sections),
        "vvvvvsss",
        (cells, 128),
        8_000_000,
        a,
        middle,
        speeds,
        flags,
        zones,
        growth_rate,
        transfer_rate,
        nucleation_rate,
    )
    below, above, ax, radlo, radhi = exchange(*first)
    m, edge, *second = call(
        functools.partial(first_halo, comps),
        "s" + "v" * 9,
        [
            (cells, 128),
            (4, 8, 128),
            (half, 128),
            (half, 128),
            (rows, 128),
            (1, cells),
            (1, cells),
        ],
        4_000_000,
        where,
        part,
        a,
        below,
        above,
        ax,
        radlo,
        radhi,
        speeds,
        flags,
    )
    part = call(
        functools.partial(second_local, sections),
        "vvvvvvvsss",
        (cells, 128),
        8_000_000,
        m,
        a,
        start,
        edge,
        speeds,
        flags,
        zones,
        growth_rate,
        transfer_rate,
        nucleation_rate,
    )
    below, above, ax, radlo, radhi = exchange(*second)
    out = call(
        functools.partial(second_halo, comps),
        "s" + "v" * 7,
        (cells, 128),
        3_000_000,
        where,
        part,
        below,
        above,
        ax,
        radlo,
        radhi,
        edge,
    )
    return out.reshape(shape)


def solution(mesh):
    field = P(None, None, "azim", "axial", "rad")
    faces_spec = P(None, "azim", "axial", "rad")
    return jax.shard_map(
        shards,
        mesh=mesh,
        in_specs=(field, field, field, faces_spec, faces_spec, P("azim", "axial", "rad"), P(), P(), P()),
        out_specs=field,
        check_vma=False,
    )
```

time: 157 us -> 51.6 us (0.33)
  local copies, waits for them, and re-layouts: 44.5 us -> 3.2 us
  other arithmetic: 32.8 us -> 0 us
  waiting for transfers between devices: 46.2 us -> 22 us
  starting transfers between devices: 31.3 us -> 17.1 us
  Pallas kernels: 0 us -> 8.71 us
    ppermute x12 -> x10, waiting for transfers between devices: 46.2 us -> 22 us  [the longest x8 22 us: shift(): return lax.ppermute(x, axis, pairs)]
    slice x35 -> x0, local copies, waits for them, and re-layouts: 20.4 us -> none  [the longest x8 9.92 us: extended(): last = lax.slice_in_dim(x, length - width, length, axis=dim)]
    ppermute x8 -> x0, local copies, waits for them, and re-layouts: 15 us -> none  [the longest x4 8.7 us: extended(): before = lax.ppermute(last, axis, up)]
    ppermute x12 -> x10, starting transfers between devices: 31.3 us -> 17.1 us  [the longest x8 14.1 us: shift(): return lax.ppermute(x, axis, pairs)]
    concatenate x5 -> x0, other arithmetic: 11 us -> none  [the longest x4 10.9 us: extended(): x = jnp.concatenate([before, x, after], axis=dim)]
    pallas_call x0 -> x5, Pallas kernels: none -> 8.71 us  [call(): pl.pallas_call(body, in_specs=[SMEM if s == 's' else VMEM for s in specs]...]
    mul x8 -> x0, other arithmetic: 7.75 us -> none  [the longest x3 4.06 us: source_term(): factors * growth * lower + inflow - outflow]
    slice x2 -> x0, other arithmetic: 6.12 us -> none  [extended(): last = lax.slice_in_dim(x, length - width, length, axis=dim)]
  transfers between devices with their start and end apart: 12 -> 10, of which waited for: 8 -> 5; matrix products, arithmetic and copies ran while one was open for 17% -> 0% of each run, Pallas kernels for 0% -> 5%
where the time goes in v1:
time: 51.6 us; the launch traced here: 51.2 us
  waiting for transfers between devices  22 us (43%)
  starting transfers between devices  17.1 us (33%)
  Pallas kernels  8.71 us (17%)
  local copies, waits for them, and re-layouts  3.2 us (6%)
    ppermute x8, waiting for transfers between devices, shift(): return lax.ppermute(x, axis, pairs)  22 us
    ppermute x8, starting transfers between devices, shift(): return lax.ppermute(x, axis, pairs)  14.1 us
    pallas_call x5, Pallas kernels, call(): pl.pallas_call(body, in_specs=[SMEM if s == 's' else VMEM for s in specs]...  8.71 us
    unnamed x18, local copies, waits for them, and re-layouts  3.2 us
    ppermute x2, starting transfers between devices, exchange(): ax = lax.ppermute(ax, 'axial', [(0, 1), (1, 0)])  3.04 us
  transfers between devices with their start and end apart: 10, of which 5 were waited for; matrix products, arithmetic and copies ran while one was open for 0% of the time, Pallas kernels for 5%

profile of v1, /device:TPU:0, one launch (start us, length us, event | category | flops | bytes accessed | tf_op | source)
XLA Modules:
  0.0 51.2 jit_solution(6337411142164722414)
XLA Ops:
  0.0 0.0 copy-start.3
  0.0 0.7 %copy-done.3 = f32[3,2,4,128]{3,2,1,0:T(4,128)S(1)} copy-done((f32[3,2,4,128]{3,2,1,0:T(4,128)S(1)}, f32[3,2,4,128]{3,2,1,0:T(4,128)}, u32[]{:S(2)}) %copy-start.3) | copy-done | bytes 12312
  0.7 0.0 copy-start
  0.7 1.1 %copy-done = f32[4,48,2,4,128]{4,3,2,1,0:T(4,128)S(1)} copy-done((f32[4,48,2,4,128]{4,3,2,1,0:T(4,128)S(1)}, f32[4,48,2,4,128]{4,3,2,1,0:T(4,128)}, u32[]{:S(2)}) %copy-start) | copy-done | bytes 786456
  1.8 0.0 copy-start.4
  1.8 0.7 %copy-done.4 = s32[3,2,4,128]{3,2,1,0:T(4,128)S(1)} copy-done((s32[3,2,4,128]{3,2,1,0:T(4,128)S(1)}, s32[3,2,4,128]{3,2,1,0:T(4,128)}, u32[]{:S(2)}) %copy-start.4) | copy-done | bytes 12312
  2.5 0.0 copy-start.1
  2.6 0.9 %shard_map.92 = (f32[776,128]{1,0:T(8,128)S(1)}, f32[768,128]{1,0:T(8,128)S(1)}, f32[392,128]{1,0:T(8,128)S(1)}, f32[1,1664]{1,0:T(1,128)S(1)}, f32[1,1664]{1,0:T(1,128)S(1)}) custom-call(s32[1]{0:T(128)} %bitcast.where_ref, f32[1536,128]{1,0:T(8,128)S(1)} %bitcast.8, f32[3,8,128]{2,1,0:T(8,128)S(1)} %bitcast.14, s32[3,8,128]{2,1,0:T(8,128)S(1)} %bitcast.18), custom_call_target="tpu_custom_call" | custom-call | flops 2000000 | bytes 200000 | tf_op jit(solution)/shard_map/pallas_call | solution.py:250
  3.5 5.1 %collective-permute-start.1 = (f32[776,128]{1,0:T(8,128)S(1)}, f32[776,128]{1,0:T(8,128)S(1)}, u32[]{:S(2)}, u32[]{:S(2)}) collective-permute-start(f32[776,128]{1,0:T(8,128)S(1)} %get-tuple-element.18), channel_id=1, source_target_pairs={{0,24},{8,0},{16,8},{24,16},{1,25},{9,1},{17,9},{25,17},{2,26},{10... | collective-permute-start | bytes 1191944 | tf_op jit(solution)/shard_map/ppermute | solution.py:264
  8.6 0.0 collective-permute-start
  8.6 0.0 copy-start.5
  8.6 1.5 %collective-permute-start.2 = (f32[392,128]{1,0:T(8,128)S(1)}, f32[392,128]{1,0:T(8,128)S(1)}, u32[]{:S(2)}, u32[]{:S(2)}) collective-permute-start(f32[392,128]{1,0:T(8,128)S(1)} %get-tuple-element.19), channel_id=1, source_target_pairs={{0,1},{1,0},{2,3},{3,2},{4,5},{5,4},{6,7},{7,6},{8,9},{9,8},{10,11... | collective-permute-start | bytes 602120 | tf_op jit(solution)/shard_map/ppermute | solution.py:268
  10.1 1.3 %collective-permute-start.3 = (f32[1,1664]{1,0:T(1,128)S(1)}, f32[1,1664]{1,0:T(1,128)S(1)}, u32[]{:S(2)}, u32[]{:S(2)}) collective-permute-start(f32[1,1664]{1,0:T(1,128)S(1)} %get-tuple-element.20), channel_id=1, source_target_pairs={{0,2},{2,4},{4,6},{1,3},{3,5},{5,7},{8,10},{10,12},{12,14},{9,11},... | collective-permute-start | bytes 19976 | tf_op jit(solution)/shard_map/ppermute | solution.py:264
  11.4 1.3 %collective-permute-start.4 = (f32[1,1664]{1,0:T(1,128)S(1)}, f32[1,1664]{1,0:T(1,128)S(1)}, u32[]{:S(2)}, u32[]{:S(2)}) collective-permute-start(f32[1,1664]{1,0:T(1,128)S(1)} %get-tuple-element.21), channel_id=1, source_target_pairs={{2,0},{4,2},{6,4},{3,1},{5,3},{7,5},{10,8},{12,10},{14,12},{11,9},... | collective-permute-start | bytes 19976 | tf_op jit(solution)/shard_map/ppermute | solution.py:264
  12.7 0.0 copy-start.6
  12.7 0.0 copy-start.7
  12.7 0.0 copy-start.8
  12.7 0.0 copy-done.1
  12.7 0.0 copy-done.5
  12.7 0.6 %copy-done.6 = f32[48]{0:T(128)S(1)} copy-done((f32[48]{0:T(128)S(1)}, f32[48]{0:T(128)}, u32[]{:S(2)}) %copy-start.6) | copy-done | bytes 216
  13.3 0.0 copy-done.7
  13.3 0.0 copy-done.8
  13.4 1.4 %shard_map.91.part_ref = f32[1536,128]{1,0:T(8,128)S(1)} custom-call(f32[1536,128]{1,0:T(8,128)S(1)} %bitcast.9, bf16[192,8,128]{2,1,0:T(8,128)(2,1)S(1)} %bitcast.12, f32[3,8,128]{2,1,0:T(8,128)S(1)} %bitcast.15, s32[3,8,128]{2,1,0:T(8,128)S(1)} %bitcast.19, s32[8,128]{1,0:T(8,128)S(1)} %bitcast.22, f32[48]{0:T(128)S(1)} %copy-done.6, f32[48]{0:T(128)S(1)} %copy-done.7, ...), custom_call_target="tpu_custom_call" | custom-call | flops 8000000 | bytes 800000 | tf_op jit(solution)/shard_map/pallas_call | solution.py:250
  14.7 0.0 copy-start.2
  14.8 0.0 collective-permute-done.3.radlo_ref
  14.8 1.4 %collective-permute-done.4.radhi_ref = f32[1,1664]{1,0:T(1,128)S(1)} collective-permute-done((f32[1,1664]{1,0:T(1,128)S(1)}, f32[1,1664]{1,0:T(1,128)S(1)}, u32[]{:S(2)}, u32[]{:S(2)}) %collective-permute-start.4) | collective-permute-done | bytes 6688 | tf_op jit(solution)/shard_map/ppermute | solution.py:264
  16.2 0.0 collective-permute-done.2.ax_ref
  16.2 10.2 %collective-permute-done.below_ref = f32[768,128]{1,0:T(8,128)S(1)} collective-permute-done((f32[768,128]{1,0:T(8,128)S(1)}, f32[768,128]{1,0:T(8,128)S(1)}, u32[]{:S(2)}, u32[]{:S(2)}) %collective-permute-start) | collective-permute-done | bytes 393248 | tf_op jit(solution)/shard_map/ppermute | solution.py:264
  26.4 0.0 collective-permute-done.1.above_ref
  26.4 3.3 %shard_map.93 = (f32[1536,128]{1,0:T(8,128)S(1)}, f32[4,8,128]{2,1,0:T(8,128)S(1)}, f32[768,128]{1,0:T(8,128)S(1)}, f32[768,128]{1,0:T(8,128)S(1)}, f32[384,128]...) custom-call(s32[1]{0:T(128)} %bitcast.where_ref, f32[1536,128]{1,0:T(8,128)S(1)} %shard_map.91.part_ref, ...), custom_call_target="tpu_custom_call" | custom-call | flops 4000000 | bytes 400000 | tf_op jit(solution)/shard_map/pallas_call | solution.py:250
  29.6 1.7 %collective-permute-start.5 = (f32[768,128]{1,0:T(8,128)S(1)}, f32[768,128]{1,0:T(8,128)S(1)}, u32[]{:S(2)}, u32[]{:S(2)}) collective-permute-start(f32[768,128]{1,0:T(8,128)S(1)} %get-tuple-element.24), channel_id=1, source_target_pairs={{0,8},{8,16},{16,24},{24,0},{1,9},{9,17},{17,25},{25,1},{2,10},{10... | collective-permute-start | bytes 1179656 | tf_op jit(solution)/shard_map/ppermute | solution.py:264
  31.3 2.2 %collective-permute-start.6 = (f32[768,128]{1,0:T(8,128)S(1)}, f32[768,128]{1,0:T(8,128)S(1)}, u32[]{:S(2)}, u32[]{:S(2)}) collective-permute-start(f32[768,128]{1,0:T(8,128)S(1)} %get-tuple-element.25), channel_id=1, source_target_pairs={{0,24},{8,0},{16,8},{24,16},{1,25},{9,1},{17,9},{25,17},{2,26},{10... | collective-permute-start | bytes 1179656 | tf_op jit(solution)/shard_map/ppermute | solution.py:264
  33.5 1.5 %collective-permute-start.7 = (f32[384,128]{1,0:T(8,128)S(1)}, f32[384,128]{1,0:T(8,128)S(1)}, u32[]{:S(2)}, u32[]{:S(2)}) collective-permute-start(f32[384,128]{1,0:T(8,128)S(1)} %get-tuple-element.26), channel_id=1, source_target_pairs={{0,1},{1,0},{2,3},{3,2},{4,5},{5,4},{6,7},{7,6},{8,9},{9,8},{10,11... | collective-permute-start | bytes 589832 | tf_op jit(solution)/shard_map/ppermute | solution.py:268
  35.0 1.3 %collective-permute-start.8 = (f32[1,1536]{1,0:T(1,128)S(1)}, f32[1,1536]{1,0:T(1,128)S(1)}, u32[]{:S(2)}, u32[]{:S(2)}) collective-permute-start(f32[1,1536]{1,0:T(1,128)S(1)} %get-tuple-element.27), channel_id=1, source_target_pairs={{0,2},{2,4},{4,6},{1,3},{3,5},{5,7},{8,10},{10,12},{12,14},{9,11},... | collective-permute-start | bytes 18440 | tf_op jit(solution)/shard_map/ppermute | solution.py:264
  36.3 1.3 %collective-permute-start.9 = (f32[1,1536]{1,0:T(1,128)S(1)}, f32[1,1536]{1,0:T(1,128)S(1)}, u32[]{:S(2)}, u32[]{:S(2)}) collective-permute-start(f32[1,1536]{1,0:T(1,128)S(1)} %get-tuple-element.28), channel_id=1, source_target_pairs={{2,0},{4,2},{6,4},{3,1},{5,3},{7,5},{10,8},{12,10},{14,12},{11,9},... | collective-permute-start | bytes 18440 | tf_op jit(solution)/shard_map/ppermute | solution.py:264
  37.6 0.0 copy-done.2
  37.6 1.4 %shard_map.94.part_ref = f32[1536,128]{1,0:T(8,128)S(1)} custom-call(f32[1536,128]{1,0:T(8,128)S(1)} %get-tuple-element.22.m_ref, f32[1536,128]{1,0:T(8,128)S(1)} %bitcast.11, bf16[192,8,128]{2,1,0:T(8,128)(2,1)S(1)} %bitcast.13, f32[4,8,128]{2,1,0:T(8,128)S(1)} %get-tuple-element.23.edge_ref, f32[3,8,128]{2,1,0:T(8,128)S(1)} %bitcast.17, ...), custom_call_target="tpu_custom_call" | custom-call | flops 8000000 | bytes 800000 | tf_op jit(solution)/shard_map/pallas_call | solution.py:250
  39.0 0.0 collective-permute-done.8.radlo_ref
  39.0 2.1 %collective-permute-done.9.radhi_ref = f32[1,1536]{1,0:T(1,128)S(1)} collective-permute-done((f32[1,1536]{1,0:T(1,128)S(1)}, f32[1,1536]{1,0:T(1,128)S(1)}, u32[]{:S(2)}, u32[]{:S(2)}) %collective-permute-start.9) | collective-permute-done | bytes 6176 | tf_op jit(solution)/shard_map/ppermute | solution.py:264
  41.1 0.0 collective-permute-done.7.ax_ref
  41.1 2.4 %collective-permute-done.5.below_ref = f32[768,128]{1,0:T(8,128)S(1)} collective-permute-done((f32[768,128]{1,0:T(8,128)S(1)}, f32[768,128]{1,0:T(8,128)S(1)}, u32[]{:S(2)}, u32[]{:S(2)}) %collective-permute-start.5) | collective-permute-done | bytes 393248 | tf_op jit(solution)/shard_map/ppermute | solution.py:264
  43.5 5.9 %collective-permute-done.6.above_ref = f32[768,128]{1,0:T(8,128)S(1)} collective-permute-done((f32[768,128]{1,0:T(8,128)S(1)}, f32[768,128]{1,0:T(8,128)S(1)}, u32[]{:S(2)}, u32[]{:S(2)}) %collective-permute-start.6) | collective-permute-done | bytes 393248 | tf_op jit(solution)/shard_map/ppermute | solution.py:264
  49.4 1.8 %shard_map.95 = f32[1536,128]{1,0:T(8,128)} custom-call(s32[1]{0:T(128)} %bitcast.where_ref, f32[1536,128]{1,0:T(8,128)S(1)} %shard_map.94.part_ref, f32[768,128]{1,0:T(8,128)S(1)} %collective-permute-done.5.below_ref, f32[768,128]{1,0:T(8,128)S(1)} %collective-permute-done.6.above_ref, f32[384,128]{1,0:T(8,128)S(1)} %collective-permute-done.7.ax_ref, ...), custom_call_target="tpu_custom_call" | custom-call | flops 3000000 | bytes 300000 | tf_op jit(solution)/shard_map/pallas_call | solution.py:250
Async XLA Ops:
  0.0 0.7 %copy-start.3 = (f32[3,2,4,128]{3,2,1,0:T(4,128)S(1)}, f32[3,2,4,128]{3,2,1,0:T(4,128)}, u32[]{:S(2)}) copy-start(f32[3,2,4,128]{3,2,1,0:T(4,128)} %param.12) | copy-start | bytes 36868
  0.7 1.1 %copy-start = (f32[4,48,2,4,128]{4,3,2,1,0:T(4,128)S(1)}, f32[4,48,2,4,128]{4,3,2,1,0:T(4,128)}, u32[]{:S(2)}) copy-start(f32[4,48,2,4,128]{4,3,2,1,0:T(4,128)} %param.9) | copy-start | bytes 2359300
  1.8 0.7 %copy-start.4 = (s32[3,2,4,128]{3,2,1,0:T(4,128)S(1)}, s32[3,2,4,128]{3,2,1,0:T(4,128)}, u32[]{:S(2)}) copy-start(s32[3,2,4,128]{3,2,1,0:T(4,128)} %param.13) | copy-start | bytes 36868
  2.5 10.2 %copy-start.1 = (bf16[4,48,2,4,128]{4,3,2,1,0:T(4,128)(2,1)S(1)}, bf16[4,48,2,4,128]{4,3,2,1,0:T(4,128)(2,1)}, u32[]{:S(2)}) copy-start(bf16[4,48,2,4,128]{4,3,2,1,0:T(4,128)(2,1)} %param.11) | copy-start | bytes 1179652
  3.5 22.9 %collective-permute-start.1 = (f32[776,128]{1,0:T(8,128)S(1)}, f32[776,128]{1,0:T(8,128)S(1)}, u32[]{:S(2)}, u32[]{:S(2)}) collective-permute-start(f32[776,128]{1,0:T(8,128)S(1)} %get-tuple-element.18), channel_id=1, source_target_pairs={{0,24},{8,0},{16,8},{24,16},{1,25},{9,1},{17,9},{25,17},{2,26},{10... | collective-permute-start | bytes 1191944 | tf_op jit(solution)/shard_map/ppermute | solution.py:264
  8.6 17.8 %collective-permute-start = (f32[768,128]{1,0:T(8,128)S(1)}, f32[768,128]{1,0:T(8,128)S(1)}, u32[]{:S(2)}, u32[]{:S(2)}) collective-permute-start(f32[768,128]{1,0:T(8,128)S(1)} %get-tuple-element.17), channel_id=1, source_target_pairs={{0,8},{8,16},{16,24},{24,0},{1,9},{9,17},{17,25},{25,1},{2,10},{10... | collective-permute-start | bytes 1179656 | tf_op jit(solution)/shard_map/ppermute | solution.py:264
  8.6 4.2 %copy-start.5 = (s32[2,4,128]{2,1,0:T(4,128)S(1)}, s32[2,4,128]{2,1,0:T(4,128)}, u32[]{:S(2)}) copy-start(s32[2,4,128]{2,1,0:T(4,128)} %param.14) | copy-start | bytes 12292
  8.6 7.6 %collective-permute-start.2 = (f32[392,128]{1,0:T(8,128)S(1)}, f32[392,128]{1,0:T(8,128)S(1)}, u32[]{:S(2)}, u32[]{:S(2)}) collective-permute-start(f32[392,128]{1,0:T(8,128)S(1)} %get-tuple-element.19), channel_id=1, source_target_pairs={{0,1},{1,0},{2,3},{3,2},{4,5},{5,4},{6,7},{7,6},{8,9},{9,8},{10,11... | collective-permute-start | bytes 602120 | tf_op jit(solution)/shard_map/ppermute | solution.py:268
  10.1 4.7 %collective-permute-start.3 = (f32[1,1664]{1,0:T(1,128)S(1)}, f32[1,1664]{1,0:T(1,128)S(1)}, u32[]{:S(2)}, u32[]{:S(2)}) collective-permute-start(f32[1,1664]{1,0:T(1,128)S(1)} %get-tuple-element.20), channel_id=1, source_target_pairs={{0,2},{2,4},{4,6},{1,3},{3,5},{5,7},{8,10},{10,12},{12,14},{9,11},... | collective-permute-start | bytes 19976 | tf_op jit(solution)/shard_map/ppermute | solution.py:264
  11.4 4.8 %collective-permute-start.4 = (f32[1,1664]{1,0:T(1,128)S(1)}, f32[1,1664]{1,0:T(1,128)S(1)}, u32[]{:S(2)}, u32[]{:S(2)}) collective-permute-start(f32[1,1664]{1,0:T(1,128)S(1)} %get-tuple-element.21), channel_id=1, source_target_pairs={{2,0},{4,2},{6,4},{3,1},{5,3},{7,5},{10,8},{12,10},{14,12},{11,9},... | collective-permute-start | bytes 19976 | tf_op jit(solution)/shard_map/ppermute | solution.py:264
  12.7 0.7 %copy-start.6 = (f32[48]{0:T(128)S(1)}, f32[48]{0:T(128)}, u32[]{:S(2)}) copy-start(f32[48]{0:T(128)} %growth_ref.3) | copy-start | bytes 580
  12.7 0.7 %copy-start.7 = (f32[48]{0:T(128)S(1)}, f32[48]{0:T(128)}, u32[]{:S(2)}) copy-start(f32[48]{0:T(128)} %transfer_ref.3) | copy-start | bytes 580
  12.7 0.7 %copy-start.8 = (f32[4]{0:T(128)S(1)}, f32[4]{0:T(128)}, u32[]{:S(2)}) copy-start(f32[4]{0:T(128)} %rate_ref.3) | copy-start | bytes 52
  14.7 22.8 %copy-start.2 = (bf16[4,48,2,4,128]{4,3,2,1,0:T(4,128)(2,1)S(1)}, bf16[4,48,2,4,128]{4,3,2,1,0:T(4,128)(2,1)}, u32[]{:S(2)}) copy-start(bf16[4,48,2,4,128]{4,3,2,1,0:T(4,128)(2,1)} %param.10) | copy-start | bytes 1179652
  29.6 13.9 %collective-permute-start.5 = (f32[768,128]{1,0:T(8,128)S(1)}, f32[768,128]{1,0:T(8,128)S(1)}, u32[]{:S(2)}, u32[]{:S(2)}) collective-permute-start(f32[768,128]{1,0:T(8,128)S(1)} %get-tuple-element.24), channel_id=1, source_target_pairs={{0,8},{8,16},{16,24},{24,0},{1,9},{9,17},{17,25},{25,1},{2,10},{10... | collective-permute-start | bytes 1179656 | tf_op jit(solution)/shard_map/ppermute | solution.py:264
  31.3 18.2 %collective-permute-start.6 = (f32[768,128]{1,0:T(8,128)S(1)}, f32[768,128]{1,0:T(8,128)S(1)}, u32[]{:S(2)}, u32[]{:S(2)}) collective-permute-start(f32[768,128]{1,0:T(8,128)S(1)} %get-tuple-element.25), channel_id=1, source_target_pairs={{0,24},{8,0},{16,8},{24,16},{1,25},{9,1},{17,9},{25,17},{2,26},{10... | collective-permute-start | bytes 1179656 | tf_op jit(solution)/shard_map/ppermute | solution.py:264
  33.5 7.6 %collective-permute-start.7 = (f32[384,128]{1,0:T(8,128)S(1)}, f32[384,128]{1,0:T(8,128)S(1)}, u32[]{:S(2)}, u32[]{:S(2)}) collective-permute-start(f32[384,128]{1,0:T(8,128)S(1)} %get-tuple-element.26), channel_id=1, source_target_pairs={{0,1},{1,0},{2,3},{3,2},{4,5},{5,4},{6,7},{7,6},{8,9},{9,8},{10,11... | collective-permute-start | bytes 589832 | tf_op jit(solution)/shard_map/ppermute | solution.py:268
  35.0 4.0 %collective-permute-start.8 = (f32[1,1536]{1,0:T(1,128)S(1)}, f32[1,1536]{1,0:T(1,128)S(1)}, u32[]{:S(2)}, u32[]{:S(2)}) collective-permute-start(f32[1,1536]{1,0:T(1,128)S(1)} %get-tuple-element.27), channel_id=1, source_target_pairs={{0,2},{2,4},{4,6},{1,3},{3,5},{5,7},{8,10},{10,12},{12,14},{9,11},... | collective-permute-start | bytes 18440 | tf_op jit(solution)/shard_map/ppermute | solution.py:264
  36.3 4.8 %collective-permute-start.9 = (f32[1,1536]{1,0:T(1,128)S(1)}, f32[1,1536]{1,0:T(1,128)S(1)}, u32[]{:S(2)}, u32[]{:S(2)}) collective-permute-start(f32[1,1536]{1,0:T(1,128)S(1)} %get-tuple-element.28), channel_id=1, source_target_pairs={{2,0},{4,2},{6,4},{3,1},{5,3},{7,5},{10,8},{12,10},{14,12},{11,9},... | collective-permute-start | bytes 18440 | tf_op jit(solution)/shard_map/ppermute | solution.py:264

commit v2 on v1

--- a/solution.py
+++ b/solution.py
@@ -61,11 +61,14 @@
     )
 
 
-def pack(comps, x_ref, where_ref, dn_ref, up_ref, ax_ref, radup_ref, raddn_ref):
-    for c in range(comps):
-        dn_ref[4 * c : 4 * c + 4] = x_ref[8 * c : 8 * c + 4]
-        up_ref[4 * c : 4 * c + 4] = x_ref[8 * c + 4 : 8 * c + 8]
-
+def copies(pairs, sems):
+    made = [pltpu.make_async_copy(src, dst, sems.at[i]) for i, (src, dst) in enumerate(pairs)]
+    for copy in made:
+        copy.start()
+    return made
+
+
+def pack_sides(comps, x_ref, where_ref, ax_ref, radup_ref, raddn_ref):
     @pl.when(where_ref[0] == 0)
     def _():
         ax_ref[0 : 2 * comps] = x_ref[pl.ds(3, 2 * comps, stride=4)]
@@ -94,10 +97,26 @@
     return lax.dot_general(both, place, (((0,), (0,)), ((), ())), precision=exact, preferred_element_type=f32)
 
 
-def first_pack(comps, where_ref, a_ref, speeds_ref, flags_ref, dn_ref, up_ref, ax_ref, radup_ref, raddn_ref):
+def first_down(comps, a_ref, speeds_ref, flags_ref, dn_ref, speed_ref, flag_ref, sems):
+    part = comps // 4
+    made = copies(
+        [(speeds_ref.at[0, 0], speed_ref), (flags_ref.at[0, 0], flag_ref)]
+        + [(a_ref.at[pl.ds(i * part, part), 0], dn_ref.at[pl.ds(i * part, part)]) for i in range(4)],
+        sems,
+    )
+    made[0].wait()
+    made[1].wait()
+    dn_ref[comps] = speed_ref[...] * flag_ref[...].astype(f32)
+    dn_ref[comps + 1] = jnp.zeros((4, 128), f32)
+    for copy in made[2:]:
+        copy.wait()
+
+
+def first_rest(comps, where_ref, a_ref, speeds_ref, flags_ref, up_ref, ax_ref, radup_ref, raddn_ref):
     p, _ = faces(speeds_ref, flags_ref)
-    pack(comps, a_ref, where_ref, dn_ref, up_ref, ax_ref, radup_ref, raddn_ref)
-    dn_ref[4 * comps : 4 * comps + 8] = p[0]
+    for c in range(comps):
+        up_ref[4 * c : 4 * c + 4] = a_ref[8 * c + 4 : 8 * c + 8]
+    pack_sides(comps, a_ref, where_ref, ax_ref, radup_ref, raddn_ref)
     ax_ref[2 * comps : 2 * comps + 8] = pair_rows(p[1], 0, 4)
     radup_ref[:, 8 * comps :] = jnp.zeros((1, 128), f32)
     raddn_ref[:, 8 * comps :] = jnp.zeros((1, 128), f32)
@@ -167,16 +186,17 @@
     source(sections, m_ref, u_ref, growth_ref, transfer_ref, zones_ref, rate_ref, finish)
 
 
-def add_halo(comps, scale, where_ref, part, below_ref, above_ref, ax_ref, hrad, azim, axial, rad, out_ref):
-    top = rows_of() >= 4
-    for c in range(comps):
-        pair = 8 * (c // 2)
-        below, above = below_ref[pair : pair + 8], above_ref[pair : pair + 8]
-        if c % 2 == 0:
-            halo = jnp.where(top, pltpu.roll(above, 4, 0), below)
-        else:
-            halo = jnp.where(top, above, pltpu.roll(below, 4, 0))
-        out_ref[8 * c : 8 * c + 8] = part(c) + scale * (azim * halo + rad * hrad[8 * c : 8 * c + 8])
+def from_below(c, below_ref):
+    pair = below_ref[8 * (c // 2) : 8 * (c // 2) + 8]
+    return pair if c % 2 == 0 else pltpu.roll(pair, 4, 0)
+
+
+def from_above(c, above_ref):
+    pair = above_ref[8 * (c // 2) : 8 * (c // 2) + 8]
+    return pair if c % 2 == 1 else pltpu.roll(pair, 4, 0)
+
+
+def add_axial(comps, scale, where_ref, axial, ax_ref, out_ref):
     several = jnp.concatenate([scale * axial] * (2 * comps // 8), axis=0)
     for start, index in ((3, 0), (0, 1)):
 
@@ -186,12 +206,11 @@
             out_ref[spots] = out_ref[spots] + several * ax_ref[0 : 2 * comps]
 
 
-def first_halo(
+def first_top(
     comps,
     where_ref,
     part_ref,
     a_ref,
-    below_ref,
     above_ref,
     ax_ref,
     radlo_ref,
@@ -200,75 +219,101 @@
     flags_ref,
     m_ref,
     edge_ref,
-    dn_ref,
     up_ref,
-    axo_ref,
-    radup_ref,
-    raddn_ref,
 ):
     _, q = faces(speeds_ref, flags_ref)
     row, lane = rows_of(), lanes_of()
+    top = row >= 4
     hrad = put_columns(radlo_ref[...], radhi_ref[...])
     lower_half = where_ref[0] == 0
-    p_azim = jnp.where(row >= 4, pltpu.roll(above_ref[4 * comps : 4 * comps + 8], 4, 0), 0.0)
+    p_azim = jnp.where(top, pltpu.roll(above_ref[4 * comps : 4 * comps + 8], 4, 0), 0.0)
     pairs = jnp.where(lower_half, ax_ref[2 * comps : 2 * comps + 8], 0.0)
     p_axial = jnp.where(row == 3, pairs[0:1], jnp.where(row == 7, pairs[1:2], 0.0))
     p_rad = jnp.where(lane == 127, hrad[8 * comps : 8 * comps + 8], 0.0)
-    azim = jnp.where(row >= 4, p_azim, q[0])
     axial = jnp.where(lower_half, pairs, pair_rows(q[1], 0, 4))
     rad = jnp.where(lane == 0, q[2], p_rad)
     centre = p_azim + p_axial + p_rad
-    edge_ref[0] = azim
+    edge_ref[0] = jnp.where(top, p_azim, q[0])
     edge_ref[1] = axial
     edge_ref[2] = rad
     edge_ref[3] = centre
-
-    def part(c):
-        return part_ref[8 * c : 8 * c + 8] - (0.5 * centre) * a_ref[8 * c : 8 * c + 8]
-
-    add_halo(comps, 0.5, where_ref, part, below_ref, above_ref, ax_ref, hrad, azim, axial, rad, m_ref)
-    pack(comps, m_ref, where_ref, dn_ref, up_ref, axo_ref, radup_ref, raddn_ref)
-
-
-def second_halo(comps, where_ref, part_ref, below_ref, above_ref, ax_ref, radlo_ref, radhi_ref, edge_ref, out_ref):
+    for c in range(comps):
+        spots = slice(8 * c, 8 * c + 8)
+        m_ref[spots] = part_ref[spots] + 0.5 * (
+            p_azim * from_above(c, above_ref) + rad * hrad[spots] - centre * a_ref[spots]
+        )
+    add_axial(comps, 0.5, where_ref, axial, ax_ref, m_ref)
+    for c in range(comps):
+        up_ref[4 * c : 4 * c + 4] = m_ref[8 * c + 4 : 8 * c + 8]
+
+
+def first_bottom(comps, where_ref, part_ref, below_ref, edge_ref, m_ref, dn_ref, ax_ref, radup_ref, raddn_ref):
+    azim = jnp.where(rows_of() >= 4, 0.0, 0.5 * edge_ref[0])
+    for c in range(comps):
+        m_ref[8 * c : 8 * c + 8] = part_ref[8 * c : 8 * c + 8] + azim * from_below(c, below_ref)
+        dn_ref[4 * c : 4 * c + 4] = m_ref[8 * c : 8 * c + 4]
+    pack_sides(comps, m_ref, where_ref, ax_ref, radup_ref, raddn_ref)
+
+
+def second_bottom(
+    comps, where_ref, part_ref, below_ref, ax_ref, radlo_ref, radhi_ref, edge_ref, out_ref, top_ref, full_ref, low_ref, sems
+):
     hrad = put_columns(radlo_ref[...], radhi_ref[...])
-
-    def part(c):
-        return part_ref[8 * c : 8 * c + 8]
-
-    add_halo(
-        comps, 1.0, where_ref, part, below_ref, above_ref, ax_ref, hrad, edge_ref[0], edge_ref[1], edge_ref[2], out_ref
-    )
-
-
-VMEM = pl.BlockSpec(memory_space=pltpu.VMEM)
-SMEM = pl.BlockSpec(memory_space=pltpu.SMEM)
-
-
-def call(body, specs, outs, cost, *operands):
-    many = isinstance(outs, list)
+    azim, rad = jnp.where(rows_of() >= 4, 0.0, edge_ref[0]), edge_ref[2]
+    for c in range(comps):
+        spots = slice(8 * c, 8 * c + 8)
+        full_ref[spots] = part_ref[spots] + azim * from_below(c, below_ref) + rad * hrad[spots]
+    add_axial(comps, 1.0, where_ref, edge_ref[1], ax_ref, full_ref)
+    for c in range(comps):
+        low_ref[c] = full_ref[8 * c : 8 * c + 4]
+    made = copies([(low_ref, out_ref.at[:, 0])], sems)
+    for c in range(comps):
+        top_ref[c] = full_ref[8 * c + 4 : 8 * c + 8]
+    made[0].wait()
+
+
+def second_top(comps, parts, _, top_ref, above_ref, edge_ref, out_ref, high_ref, sems):
+    azim = edge_ref[0][4:8]
+    size = comps // parts
+    made = []
+    for i in range(parts):
+        spots = pl.ds(i * size, size)
+        high_ref[spots] = top_ref[spots] + azim[None] * above_ref[spots]
+        made.append(pltpu.make_async_copy(high_ref.at[spots], out_ref.at[spots, 1], sems.at[i]))
+        made[-1].start()
+    for copy in made:
+        copy.wait()
+
+
+SPACES = {
+    "v": pl.BlockSpec(memory_space=pltpu.VMEM),
+    "s": pl.BlockSpec(memory_space=pltpu.SMEM),
+    "h": pl.BlockSpec(memory_space=pltpu.HBM),
+}
+
+
+def call(body, ins, outs, shapes, cost, *operands, scratch=(), aliases={}, room=32):
     return pl.pallas_call(
         body,
-        in_specs=[SMEM if s == "s" else VMEM for s in specs],
-        out_specs=[VMEM] * len(outs) if many else VMEM,
-        out_shape=[jax.ShapeDtypeStruct(o, f32) for o in outs] if many else jax.ShapeDtypeStruct(outs, f32),
+        in_specs=[SPACES[s] for s in ins],
+        out_specs=[SPACES[s] for s in outs],
+        out_shape=[jax.ShapeDtypeStruct(shape, f32) for shape in shapes],
+        scratch_shapes=scratch,
+        input_output_aliases=aliases,
         cost_estimate=pl.CostEstimate(flops=cost, bytes_accessed=cost // 10, transcendentals=0),
-        compiler_params=pltpu.CompilerParams(vmem_limit_bytes=32 * 1024 * 1024),
+        compiler_params=pltpu.CompilerParams(vmem_limit_bytes=room * 1024 * 1024),
     )(*operands)
 
 
-def exchange(dn, up, ax, radup, raddn):
-    def shift(x, axis, step, wrap):
-        size = lax.axis_size(axis)
-        pairs = [(i, (i + step) % size) for i in range(size) if wrap or 0 <= i + step < size]
-        return lax.ppermute(x, axis, pairs)
-
-    above = shift(dn, "azim", -1, True)
-    below = shift(up, "azim", 1, True)
+def shift(x, axis, step, wrap):
+    size = lax.axis_size(axis)
+    pairs = [(i, (i + step) % size) for i in range(size) if wrap or 0 <= i + step < size]
+    return lax.ppermute(x, axis, pairs)
+
+
+def sides(ax, radup, raddn):
     ax = lax.ppermute(ax, "axial", [(0, 1), (1, 0)])
-    radlo = shift(radup, "rad", 1, False)
-    radhi = shift(raddn, "rad", -1, False)
-    return below, above, ax, radlo, radhi
+    return ax, shift(radup, "rad", 1, False), shift(raddn, "rad", -1, False)
 
 
 def shards(adjoint_final, state_start, state_middle, speeds, flags, zones, growth_rate, transfer_rate, nucleation_rate):
@@ -278,94 +323,119 @@
     assert moments == 4 and shape[2:] == (2, 4, 128) and comps % 4 == 0
     assert lax.axis_size("axial") == 2
     cells = 8 * comps
+    half, rows = cells // 2, cells // 4
     a = adjoint_final.reshape(cells, 128)
-    start = state_start.reshape(comps, 8, 128)
-    middle = state_middle.reshape(comps, 8, 128)
-    speeds = speeds.reshape(3, 8, 128)
-    flags = flags.reshape(3, 8, 128)
-    zones = zones.reshape(8, 128)
+    speeds2 = speeds.reshape(3, 8, 128)
+    flags2 = flags.reshape(3, 8, 128)
     where = lax.axis_index("axial").reshape(1)
-    half, rows = cells // 2, cells // 4
-
-    first = call(
-        functools.partial(first_pack, comps),
+    rates = (zones.reshape(8, 128), growth_rate, transfer_rate, nucleation_rate)
+    dma = pltpu.SemaphoreType.DMA
+
+    (dn,) = call(
+        functools.partial(first_down, comps),
+        "hhh",
+        "v",
+        [(comps + 2, 4, 128)],
+        1_000_000,
+        adjoint_final.reshape(comps, 2, 4, 128),
+        speeds,
+        flags,
+        scratch=[pltpu.VMEM((4, 128), f32), pltpu.VMEM((4, 128), jnp.int32), dma((6,))],
+        room=60,
+    )
+    above = shift(dn, "azim", -1, True).reshape(half + 8, 128)
+    up, *edges = call(
+        functools.partial(first_rest, comps),
         "svvv",
-        [(half + 8, 128), (half, 128), (rows + 8, 128), (1, cells + 128), (1, cells + 128)],
+        "vvvv",
+        [(half, 128), (rows + 8, 128), (1, cells + 128), (1, cells + 128)],
         2_000_000,
         where,
         a,
-        speeds,
-        flags,
-    )
-    part = call(
+        speeds2,
+        flags2,
+    )
+    below = shift(up, "azim", 1, True)
+    edges = sides(*edges)
+    (part,) = call(
         functools.partial(first_local, sections),
         "vvvvvsss",
-        (cells, 128),
+        "v",
+        [(cells, 128)],
         8_000_000,
         a,
-        middle,
-        speeds,
-        flags,
-        zones,
-        growth_rate,
-        transfer_rate,
-        nucleation_rate,
-    )
-    below, above, ax, radlo, radhi = exchange(*first)
-    m, edge, *second = call(
-        functools.partial(first_halo, comps),
-        "s" + "v" * 9,
-        [
-            (cells, 128),
-            (4, 8, 128),
-            (half, 128),
-            (half, 128),
-            (rows, 128),
-            (1, cells),
-            (1, cells),
-        ],
+        state_middle.reshape(comps, 8, 128),
+        speeds2,
+        flags2,
+        *rates,
+    )
+    part, edge, up = call(
+        functools.partial(first_top, comps),
+        "s" + "v" * 8,
+        "vvv",
+        [(cells, 128), (4, 8, 128), (half, 128)],
         4_000_000,
         where,
         part,
         a,
+        above,
+        *edges,
+        speeds2,
+        flags2,
+    )
+    next_below = shift(up, "azim", 1, True)
+    m, dn, *edges = call(
+        functools.partial(first_bottom, comps),
+        "svvv",
+        "vvvvv",
+        [(cells, 128), (half, 128), (rows, 128), (1, cells), (1, cells)],
+        4_000_000,
+        where,
+        part,
         below,
-        above,
-        ax,
-        radlo,
-        radhi,
-        speeds,
-        flags,
-    )
-    part = call(
+        edge,
+    )
+    above = shift(dn, "azim", -1, True).reshape(comps, 4, 128)
+    edges = sides(*edges)
+    (part,) = call(
         functools.partial(second_local, sections),
         "vvvvvvvsss",
-        (cells, 128),
+        "v",
+        [(cells, 128)],
         8_000_000,
         m,
         a,
-        start,
+        state_start.reshape(comps, 8, 128),
         edge,
-        speeds,
-        flags,
-        zones,
-        growth_rate,
-        transfer_rate,
-        nucleation_rate,
-    )
-    below, above, ax, radlo, radhi = exchange(*second)
-    out = call(
-        functools.partial(second_halo, comps),
-        "s" + "v" * 7,
-        (cells, 128),
-        3_000_000,
+        speeds2,
+        flags2,
+        *rates,
+    )
+    out, top = call(
+        functools.partial(second_bottom, comps),
+        "s" + "v" * 6,
+        "hv",
+        [(comps, 2, 4, 128), (comps, 4, 128)],
+        4_000_000,
         where,
         part,
-        below,
+        next_below,
+        *edges,
+        edge,
+        scratch=[pltpu.VMEM((cells, 128), f32), pltpu.VMEM((comps, 4, 128), f32), dma((1,))],
+    )
+    (out,) = call(
+        functools.partial(second_top, comps, 4),
+        "hvvv",
+        "h",
+        [(comps, 2, 4, 128)],
+        1_000_000,
+        out,
+        top,
         above,
-        ax,
-        radlo,
-        radhi,
         edge,
+        scratch=[pltpu.VMEM((comps, 4, 128), f32), dma((4,))],
+        aliases={0: 0},
     )
     return out.reshape(shape)
 

time: 51.6 us -> 43 us (0.83)
  waiting for transfers between devices: 22 us -> 15.5 us
  local copies, waits for them, and re-layouts: 3.2 us -> 0.67 us
  Pallas kernels: 8.71 us -> 10.2 us
  starting transfers between devices: 17.1 us -> 16.2 us
    ppermute x8, waiting for transfers between devices: 22 us -> 15.5 us  [shift(): return lax.ppermute(x, axis, pairs)]
    unnamed x18, local copies, waits for them, and re-layouts: 3.2 us -> 0.67 us
    pallas_call x5 -> x8, Pallas kernels: 8.71 us -> 10.2 us  [call(): pl.pallas_call(body, in_specs=[SPACES[s] for s in ins], out_specs=[SPACES...]
    ppermute x8, starting transfers between devices: 14.1 us -> 13.1 us  [shift(): return lax.ppermute(x, axis, pairs)]
  transfers between devices with their start and end apart: 10 -> 10, of which waited for: 5 -> 5; matrix products, arithmetic and copies ran while one was open for 0% -> 0% of each run, Pallas kernels for 5% -> 17%
where the time goes in v2:
time: 43 us; the launch traced here: 42.7 us
  starting transfers between devices  16.2 us (38%)
  waiting for transfers between devices  15.5 us (36%)
  Pallas kernels  10.2 us (24%)
  local copies, waits for them, and re-layouts  0.67 us (2%)
    ppermute x8, waiting for transfers between devices, shift(): return lax.ppermute(x, axis, pairs)  15.5 us
    ppermute x8, starting transfers between devices, shift(): return lax.ppermute(x, axis, pairs)  13.1 us
    pallas_call x8, Pallas kernels, call(): pl.pallas_call(body, in_specs=[SPACES[s] for s in ins], out_specs=[SPACES...  10.2 us
    ppermute x2, starting transfers between devices, sides(): ax = lax.ppermute(ax, 'axial', [(0, 1), (1, 0)])  3.1 us
  transfers between devices with their start and end apart: 10, of which 5 were waited for; matrix products, arithmetic and copies ran while one was open for 0% of the time, Pallas kernels for 17%

profile of v2, /device:TPU:0, one launch (start us, length us, event | category | flops | bytes accessed | tf_op | source)
XLA Modules:
  0.0 42.7 jit_solution(9757541631474662980)
XLA Ops:
  0.0 0.0 copy-start
  0.0 0.0 copy-start.4
  0.0 1.9 %shard_map.92 = f32[194,4,128]{2,1,0:T(4,128)} custom-call(f32[192,2,4,128]{3,2,1,0:T(4,128)} %bitcast.11, f32[3,2,4,128]{3,2,1,0:T(4,128)} %speeds_ref.1, s32[3,2,4,128]{3,2,1,0:T(4,128)} %flags_ref.1), custom_call_target="tpu_custom_call" | custom-call | flops 1000000 | bytes 100000 | tf_op jit(solution)/shard_map/pallas_call | solution.py:296
  1.9 0.0 copy-start.3
  2.0 5.1 %collective-permute-start = (f32[194,4,128]{2,1,0:T(4,128)}, f32[194,4,128]{2,1,0:T(4,128)S(1)}, u32[]{:S(2)}, u32[]{:S(2)}) collective-permute-start(f32[194,4,128]{2,1,0:T(4,128)} %shard_map.92), channel_id=1, source_target_pairs={{0,24},{8,0},{16,8},{24,16},{1,25},{9,1},{17,9},{25,17},{2,26},{10... | collective-permute-start | bytes 1191944 | tf_op jit(solution)/shard_map/ppermute | solution.py:311
  7.1 0.0 copy-done
  7.1 0.0 copy-done.4
  7.1 0.0 copy-done.3
  7.1 0.0 copy-start.1
  7.1 0.8 %shard_map.93 = (f32[768,128]{1,0:T(8,128)S(1)}, f32[392,128]{1,0:T(8,128)S(1)}, f32[1,1664]{1,0:T(1,128)S(1)}, f32[1,1664]{1,0:T(1,128)S(1)}) custom-call(s32[1]{0:T(128)} %bitcast.where_ref, f32[1536,128]{1,0:T(8,128)S(1)} %bitcast.12, f32[3,8,128]{2,1,0:T(8,128)S(1)} %bitcast.20, s32[3,8,128]{2,1,0:T(8,128)S(1)} %bitcast.24), custom_call_target="tpu_custom_call" | custom-call | flops 2000000 | bytes 200000 | tf_op jit(solution)/shard_map/pallas_call | solution.py:296
  7.9 0.1 collective-permute-start.4
  8.0 0.0 copy-start.5
  8.0 1.6 %collective-permute-start.1 = (f32[392,128]{1,0:T(8,128)S(1)}, f32[392,128]{1,0:T(8,128)S(1)}, u32[]{:S(2)}, u32[]{:S(2)}) collective-permute-start(f32[392,128]{1,0:T(8,128)S(1)} %get-tuple-element.19), channel_id=1, source_target_pairs={{0,1},{1,0},{2,3},{3,2},{4,5},{5,4},{6,7},{7,6},{8,9},{9,8},{10,11... | collective-permute-start | bytes 602120 | tf_op jit(solution)/shard_map/ppermute | solution.py:315
  9.6 1.3 %collective-permute-start.2 = (f32[1,1664]{1,0:T(1,128)S(1)}, f32[1,1664]{1,0:T(1,128)S(1)}, u32[]{:S(2)}, u32[]{:S(2)}) collective-permute-start(f32[1,1664]{1,0:T(1,128)S(1)} %get-tuple-element.20), channel_id=1, source_target_pairs={{0,2},{2,4},{4,6},{1,3},{3,5},{5,7},{8,10},{10,12},{12,14},{9,11},... | collective-permute-start | bytes 19976 | tf_op jit(solution)/shard_map/ppermute | solution.py:311
  10.9 1.3 %collective-permute-start.3 = (f32[1,1664]{1,0:T(1,128)S(1)}, f32[1,1664]{1,0:T(1,128)S(1)}, u32[]{:S(2)}, u32[]{:S(2)}) collective-permute-start(f32[1,1664]{1,0:T(1,128)S(1)} %get-tuple-element.21), channel_id=1, source_target_pairs={{2,0},{4,2},{6,4},{3,1},{5,3},{7,5},{10,8},{12,10},{14,12},{11,9},... | collective-permute-start | bytes 19976 | tf_op jit(solution)/shard_map/ppermute | solution.py:311
  12.2 0.0 copy-start.6
  12.2 0.0 copy-start.7
  12.2 0.0 copy-start.8
  12.2 0.0 copy-done.1
  12.2 0.0 copy-done.5
  12.2 0.6 %copy-done.6 = f32[48]{0:T(128)S(1)} copy-done((f32[48]{0:T(128)S(1)}, f32[48]{0:T(128)}, u32[]{:S(2)}) %copy-start.6) | copy-done | bytes 216
  12.8 0.0 copy-done.7
  12.8 0.0 copy-done.8
  12.9 1.4 %shard_map.91.part_ref = f32[1536,128]{1,0:T(8,128)S(1)} custom-call(f32[1536,128]{1,0:T(8,128)S(1)} %bitcast.13, bf16[192,8,128]{2,1,0:T(8,128)(2,1)S(1)} %bitcast.18, f32[3,8,128]{2,1,0:T(8,128)S(1)} %bitcast.21, s32[3,8,128]{2,1,0:T(8,128)S(1)} %bitcast.25, s32[8,128]{1,0:T(8,128)S(1)} %bitcast.28, f32[48]{0:T(128)S(1)} %copy-done.6, f32[48]{0:T(128)S(1)} %copy-done.7, ...), custom_call_target="tpu_custom_call" | custom-call | flops 8000000 | bytes 800000 | tf_op jit(solution)/shard_map/pallas_call | solution.py:296
  14.2 0.0 collective-permute-done.2.radlo_ref
  14.3 1.4 %collective-permute-done.3.radhi_ref = f32[1,1664]{1,0:T(1,128)S(1)} collective-permute-done((f32[1,1664]{1,0:T(1,128)S(1)}, f32[1,1664]{1,0:T(1,128)S(1)}, u32[]{:S(2)}, u32[]{:S(2)}) %collective-permute-start.3) | collective-permute-done | bytes 6688 | tf_op jit(solution)/shard_map/ppermute | solution.py:311
  15.7 0.0 collective-permute-done.1.ax_ref
  15.7 1.3 %collective-permute-done = f32[194,4,128]{2,1,0:T(4,128)S(1)} collective-permute-done((f32[194,4,128]{2,1,0:T(4,128)}, f32[194,4,128]{2,1,0:T(4,128)S(1)}, u32[]{:S(2)}, u32[]{:S(2)}) %collective-permute-start) | collective-permute-done | bytes 397344 | tf_op jit(solution)/shard_map/ppermute | solution.py:311
  17.0 1.2 %shard_map.94 = (f32[1536,128]{1,0:T(8,128)S(1)}, f32[4,8,128]{2,1,0:T(8,128)S(1)}, f32[768,128]{1,0:T(8,128)S(1)}) custom-call(s32[1]{0:T(128)} %bitcast.where_ref, f32[1536,128]{1,0:T(8,128)S(1)} %shard_map.91.part_ref, f32[1536,128]{1,0:T(8,128)S(1)} %bitcast.14, f32[776,128]{1,0:T(8,128)S(1)} %bitcast.16, f32[392,128]{1,0:T(8,128)S(1)} %collective-permute-done.1.ax_ref, ...), custom_call_target="tpu_custom_call" | custom-call | flops 4000000 | bytes 400000 | tf_op jit(solution)/shard_map/pallas_call | solution.py:296
  18.2 0.1 collective-permute-start.5
  18.3 7.6 %collective-permute-done.4.below_ref = f32[768,128]{1,0:T(8,128)S(1)} collective-permute-done((f32[768,128]{1,0:T(8,128)S(1)}, f32[768,128]{1,0:T(8,128)S(1)}, u32[]{:S(2)}, u32[]{:S(2)}) %collective-permute-start.4) | collective-permute-done | bytes 393248 | tf_op jit(solution)/shard_map/ppermute | solution.py:311
  25.9 0.0 copy-start.2
  25.9 0.9 %shard_map.95 = (f32[1536,128]{1,0:T(8,128)S(1)}, f32[768,128]{1,0:T(8,128)S(1)}, f32[384,128]{1,0:T(8,128)S(1)}, f32[1,1536]{1,0:T(1,128)S(1)}, f32[1,1536]{1,0:T(1,128)S(1)}) custom-call(s32[1]{0:T(128)} %bitcast.where_ref, f32[1536,128]{1,0:T(8,128)S(1)} %get-tuple-element.22.part_ref, f32[768,128]{1,0:T(8,128)S(1)} %collective-permute-done.4.below_ref, ...), custom_call_target="tpu_custom_call" | custom-call | flops 4000000 | bytes 400000 | tf_op jit(solution)/shard_map/pallas_call | solution.py:296
  26.8 2.8 %collective-permute-start.9 = (f32[768,128]{1,0:T(8,128)S(1)}, f32[768,128]{1,0:T(8,128)S(1)}, u32[]{:S(2)}, u32[]{:S(2)}) collective-permute-start(f32[768,128]{1,0:T(8,128)S(1)} %get-tuple-element.32), channel_id=1, source_target_pairs={{0,24},{8,0},{16,8},{24,16},{1,25},{9,1},{17,9},{25,17},{2,26},{10... | collective-permute-start | bytes 1179656 | tf_op jit(solution)/shard_map/ppermute | solution.py:311
  29.5 1.5 %collective-permute-start.6 = (f32[384,128]{1,0:T(8,128)S(1)}, f32[384,128]{1,0:T(8,128)S(1)}, u32[]{:S(2)}, u32[]{:S(2)}) collective-permute-start(f32[384,128]{1,0:T(8,128)S(1)} %get-tuple-element.27), channel_id=1, source_target_pairs={{0,1},{1,0},{2,3},{3,2},{4,5},{5,4},{6,7},{7,6},{8,9},{9,8},{10,11... | collective-permute-start | bytes 589832 | tf_op jit(solution)/shard_map/ppermute | solution.py:315
  31.0 1.3 %collective-permute-start.7 = (f32[1,1536]{1,0:T(1,128)S(1)}, f32[1,1536]{1,0:T(1,128)S(1)}, u32[]{:S(2)}, u32[]{:S(2)}) collective-permute-start(f32[1,1536]{1,0:T(1,128)S(1)} %get-tuple-element.28), channel_id=1, source_target_pairs={{0,2},{2,4},{4,6},{1,3},{3,5},{5,7},{8,10},{10,12},{12,14},{9,11},... | collective-permute-start | bytes 18440 | tf_op jit(solution)/shard_map/ppermute | solution.py:311
  32.3 1.3 %collective-permute-start.8 = (f32[1,1536]{1,0:T(1,128)S(1)}, f32[1,1536]{1,0:T(1,128)S(1)}, u32[]{:S(2)}, u32[]{:S(2)}) collective-permute-start(f32[1,1536]{1,0:T(1,128)S(1)} %get-tuple-element.29), channel_id=1, source_target_pairs={{2,0},{4,2},{6,4},{3,1},{5,3},{7,5},{10,8},{12,10},{14,12},{11,9},... | collective-permute-start | bytes 18440 | tf_op jit(solution)/shard_map/ppermute | solution.py:311
  33.6 0.0 copy-done.2
  33.6 1.4 %shard_map.96.part_ref = f32[1536,128]{1,0:T(8,128)S(1)} custom-call(f32[1536,128]{1,0:T(8,128)S(1)} %get-tuple-element.25.m_ref, f32[1536,128]{1,0:T(8,128)S(1)} %bitcast.15, bf16[192,8,128]{2,1,0:T(8,128)(2,1)S(1)} %bitcast.19, f32[4,8,128]{2,1,0:T(8,128)S(1)} %get-tuple-element.24.edge_ref, f32[3,8,128]{2,1,0:T(8,128)S(1)} %bitcast.23, ...), custom_call_target="tpu_custom_call" | custom-call | flops 8000000 | bytes 800000 | tf_op jit(solution)/shard_map/pallas_call | solution.py:296
  35.0 0.0 collective-permute-done.7.radlo_ref
  35.0 2.1 %collective-permute-done.8.radhi_ref = f32[1,1536]{1,0:T(1,128)S(1)} collective-permute-done((f32[1,1536]{1,0:T(1,128)S(1)}, f32[1,1536]{1,0:T(1,128)S(1)}, u32[]{:S(2)}, u32[]{:S(2)}) %collective-permute-start.8) | collective-permute-done | bytes 6176 | tf_op jit(solution)/shard_map/ppermute | solution.py:311
  37.1 0.0 collective-permute-done.6.ax_ref
  37.1 0.0 collective-permute-done.5.below_ref
  37.1 1.7 %shard_map.97 = (f32[192,2,4,128]{3,2,1,0:T(4,128)}, f32[192,4,128]{2,1,0:T(4,128)S(1)}) custom-call(s32[1]{0:T(128)} %bitcast.where_ref, f32[1536,128]{1,0:T(8,128)S(1)} %shard_map.96.part_ref, f32[768,128]{1,0:T(8,128)S(1)} %collective-permute-done.5.below_ref, f32[384,128]{1,0:T(8,128)S(1)} %collective-permute-done.6.ax_ref, ...), custom_call_target="tpu_custom_call" | custom-call | flops 4000000 | bytes 400000 | tf_op jit(solution)/shard_map/pallas_call | solution.py:296
  38.8 3.1 %collective-permute-done.9 = f32[768,128]{1,0:T(8,128)S(1)} collective-permute-done((f32[768,128]{1,0:T(8,128)S(1)}, f32[768,128]{1,0:T(8,128)S(1)}, u32[]{:S(2)}, u32[]{:S(2)}) %collective-permute-start.9) | collective-permute-done | bytes 393248 | tf_op jit(solution)/shard_map/ppermute | solution.py:311
  41.9 0.8 %shard_map.98 = f32[192,2,4,128]{3,2,1,0:T(4,128)} custom-call(f32[192,2,4,128]{3,2,1,0:T(4,128)} %get-tuple-element.30._, f32[192,4,128]{2,1,0:T(4,128)S(1)} %get-tuple-element.31.top_ref, f32[192,4,128]{2,1,0:T(4,128)S(1)} %bitcast.17, f32[4,8,128]{2,1,0:T(8,128)S(1)} %get-tuple-element.24.edge_ref), custom_call_target="tpu_custom_call", output_to_operand_aliasing={{}: (0, {})} | custom-call | flops 1000000 | bytes 100000 | tf_op jit(solution)/shard_map/pallas_call | solution.py:296
Async XLA Ops:
  0.0 7.1 %copy-start = (f32[4,48,2,4,128]{4,3,2,1,0:T(4,128)S(1)}, f32[4,48,2,4,128]{4,3,2,1,0:T(4,128)}, u32[]{:S(2)}) copy-start(f32[4,48,2,4,128]{4,3,2,1,0:T(4,128)} %param.9) | copy-start | bytes 2359300
  0.0 7.1 %copy-start.4 = (s32[3,2,4,128]{3,2,1,0:T(4,128)S(1)}, s32[3,2,4,128]{3,2,1,0:T(4,128)}, u32[]{:S(2)}) copy-start(s32[3,2,4,128]{3,2,1,0:T(4,128)} %flags_ref.1) | copy-start | bytes 36868
  1.9 5.1 %copy-start.3 = (f32[3,2,4,128]{3,2,1,0:T(4,128)S(1)}, f32[3,2,4,128]{3,2,1,0:T(4,128)}, u32[]{:S(2)}) copy-start(f32[3,2,4,128]{3,2,1,0:T(4,128)} %speeds_ref.1) | copy-start | bytes 36868
  2.0 15.0 %collective-permute-start = (f32[194,4,128]{2,1,0:T(4,128)}, f32[194,4,128]{2,1,0:T(4,128)S(1)}, u32[]{:S(2)}, u32[]{:S(2)}) collective-permute-start(f32[194,4,128]{2,1,0:T(4,128)} %shard_map.92), channel_id=1, source_target_pairs={{0,24},{8,0},{16,8},{24,16},{1,25},{9,1},{17,9},{25,17},{2,26},{10... | collective-permute-start | bytes 1191944 | tf_op jit(solution)/shard_map/ppermute | solution.py:311
  7.1 5.1 %copy-start.1 = (bf16[4,48,2,4,128]{4,3,2,1,0:T(4,128)(2,1)S(1)}, bf16[4,48,2,4,128]{4,3,2,1,0:T(4,128)(2,1)}, u32[]{:S(2)}) copy-start(bf16[4,48,2,4,128]{4,3,2,1,0:T(4,128)(2,1)} %param.11) | copy-start | bytes 1179652
  7.9 17.9 %collective-permute-start.4 = (f32[768,128]{1,0:T(8,128)S(1)}, f32[768,128]{1,0:T(8,128)S(1)}, u32[]{:S(2)}, u32[]{:S(2)}) collective-permute-start(f32[768,128]{1,0:T(8,128)S(1)} %get-tuple-element.23), channel_id=1, source_target_pairs={{0,8},{8,16},{16,24},{24,0},{1,9},{9,17},{17,25},{25,1},{2,10},{10... | collective-permute-start | bytes 1179656 | tf_op jit(solution)/shard_map/ppermute | solution.py:311
  8.0 4.2 %copy-start.5 = (s32[2,4,128]{2,1,0:T(4,128)S(1)}, s32[2,4,128]{2,1,0:T(4,128)}, u32[]{:S(2)}) copy-start(s32[2,4,128]{2,1,0:T(4,128)} %param.14) | copy-start | bytes 12292
  8.0 7.7 %collective-permute-start.1 = (f32[392,128]{1,0:T(8,128)S(1)}, f32[392,128]{1,0:T(8,128)S(1)}, u32[]{:S(2)}, u32[]{:S(2)}) collective-permute-start(f32[392,128]{1,0:T(8,128)S(1)} %get-tuple-element.19), channel_id=1, source_target_pairs={{0,1},{1,0},{2,3},{3,2},{4,5},{5,4},{6,7},{7,6},{8,9},{9,8},{10,11... | collective-permute-start | bytes 602120 | tf_op jit(solution)/shard_map/ppermute | solution.py:315
  9.6 4.7 %collective-permute-start.2 = (f32[1,1664]{1,0:T(1,128)S(1)}, f32[1,1664]{1,0:T(1,128)S(1)}, u32[]{:S(2)}, u32[]{:S(2)}) collective-permute-start(f32[1,1664]{1,0:T(1,128)S(1)} %get-tuple-element.20), channel_id=1, source_target_pairs={{0,2},{2,4},{4,6},{1,3},{3,5},{5,7},{8,10},{10,12},{12,14},{9,11},... | collective-permute-start | bytes 19976 | tf_op jit(solution)/shard_map/ppermute | solution.py:311
  10.9 4.8 %collective-permute-start.3 = (f32[1,1664]{1,0:T(1,128)S(1)}, f32[1,1664]{1,0:T(1,128)S(1)}, u32[]{:S(2)}, u32[]{:S(2)}) collective-permute-start(f32[1,1664]{1,0:T(1,128)S(1)} %get-tuple-element.21), channel_id=1, source_target_pairs={{2,0},{4,2},{6,4},{3,1},{5,3},{7,5},{10,8},{12,10},{14,12},{11,9},... | collective-permute-start | bytes 19976 | tf_op jit(solution)/shard_map/ppermute | solution.py:311
  12.2 0.7 %copy-start.6 = (f32[48]{0:T(128)S(1)}, f32[48]{0:T(128)}, u32[]{:S(2)}) copy-start(f32[48]{0:T(128)} %growth_ref.3) | copy-start | bytes 580
  12.2 0.7 %copy-start.7 = (f32[48]{0:T(128)S(1)}, f32[48]{0:T(128)}, u32[]{:S(2)}) copy-start(f32[48]{0:T(128)} %transfer_ref.3) | copy-start | bytes 580
  12.2 0.7 %copy-start.8 = (f32[4]{0:T(128)S(1)}, f32[4]{0:T(128)}, u32[]{:S(2)}) copy-start(f32[4]{0:T(128)} %rate_ref.3) | copy-start | bytes 52
  18.2 18.9 %collective-permute-start.5 = (f32[768,128]{1,0:T(8,128)S(1)}, f32[768,128]{1,0:T(8,128)S(1)}, u32[]{:S(2)}, u32[]{:S(2)}) collective-permute-start(f32[768,128]{1,0:T(8,128)S(1)} %get-tuple-element.26), channel_id=1, source_target_pairs={{0,8},{8,16},{16,24},{24,0},{1,9},{9,17},{17,25},{25,1},{2,10},{10... | collective-permute-start | bytes 1179656 | tf_op jit(solution)/shard_map/ppermute | solution.py:311
  25.9 7.8 %copy-start.2 = (bf16[4,48,2,4,128]{4,3,2,1,0:T(4,128)(2,1)S(1)}, bf16[4,48,2,4,128]{4,3,2,1,0:T(4,128)(2,1)}, u32[]{:S(2)}) copy-start(bf16[4,48,2,4,128]{4,3,2,1,0:T(4,128)(2,1)} %param.10) | copy-start | bytes 1179652
  26.8 15.2 %collective-permute-start.9 = (f32[768,128]{1,0:T(8,128)S(1)}, f32[768,128]{1,0:T(8,128)S(1)}, u32[]{:S(2)}, u32[]{:S(2)}) collective-permute-start(f32[768,128]{1,0:T(8,128)S(1)} %get-tuple-element.32), channel_id=1, source_target_pairs={{0,24},{8,0},{16,8},{24,16},{1,25},{9,1},{17,9},{25,17},{2,26},{10... | collective-permute-start | bytes 1179656 | tf_op jit(solution)/shard_map/ppermute | solution.py:311
  29.5 7.6 %collective-permute-start.6 = (f32[384,128]{1,0:T(8,128)S(1)}, f32[384,128]{1,0:T(8,128)S(1)}, u32[]{:S(2)}, u32[]{:S(2)}) collective-permute-start(f32[384,128]{1,0:T(8,128)S(1)} %get-tuple-element.27), channel_id=1, source_target_pairs={{0,1},{1,0},{2,3},{3,2},{4,5},{5,4},{6,7},{7,6},{8,9},{9,8},{10,11... | collective-permute-start | bytes 589832 | tf_op jit(solution)/shard_map/ppermute | solution.py:315
  31.0 4.0 %collective-permute-start.7 = (f32[1,1536]{1,0:T(1,128)S(1)}, f32[1,1536]{1,0:T(1,128)S(1)}, u32[]{:S(2)}, u32[]{:S(2)}) collective-permute-start(f32[1,1536]{1,0:T(1,128)S(1)} %get-tuple-element.28), channel_id=1, source_target_pairs={{0,2},{2,4},{4,6},{1,3},{3,5},{5,7},{8,10},{10,12},{12,14},{9,11},... | collective-permute-start | bytes 18440 | tf_op jit(solution)/shard_map/ppermute | solution.py:311
  32.3 4.8 %collective-permute-start.8 = (f32[1,1536]{1,0:T(1,128)S(1)}, f32[1,1536]{1,0:T(1,128)S(1)}, u32[]{:S(2)}, u32[]{:S(2)}) collective-permute-start(f32[1,1536]{1,0:T(1,128)S(1)} %get-tuple-element.29), channel_id=1, source_target_pairs={{2,0},{4,2},{6,4},{3,1},{5,3},{7,5},{10,8},{12,10},{14,12},{11,9},... | collective-permute-start | bytes 18440 | tf_op jit(solution)/shard_map/ppermute | solution.py:311

commit v3 on v2

--- a/solution.py
+++ b/solution.py
@@ -95,21 +95,6 @@
     both = jnp.where(which == 0, lower, jnp.where(which == 1, upper, 0.0))
     place = jnp.where(((row == 0) & (lane == 0)) | ((row == 1) & (lane == 127)), 1.0, 0.0)
     return lax.dot_general(both, place, (((0,), (0,)), ((), ())), precision=exact, preferred_element_type=f32)
-
-
-def first_down(comps, a_ref, speeds_ref, flags_ref, dn_ref, speed_ref, flag_ref, sems):
-    part = comps // 4
-    made = copies(
-        [(speeds_ref.at[0, 0], speed_ref), (flags_ref.at[0, 0], flag_ref)]
-        + [(a_ref.at[pl.ds(i * part, part), 0], dn_ref.at[pl.ds(i * part, part)]) for i in range(4)],
-        sems,
-    )
-    made[0].wait()
-    made[1].wait()
-    dn_ref[comps] = speed_ref[...] * flag_ref[...].astype(f32)
-    dn_ref[comps + 1] = jnp.zeros((4, 128), f32)
-    for copy in made[2:]:
-        copy.wait()
 
 
 def first_rest(comps, where_ref, a_ref, speeds_ref, flags_ref, up_ref, ax_ref, radup_ref, raddn_ref):
@@ -226,7 +211,7 @@
     top = row >= 4
     hrad = put_columns(radlo_ref[...], radhi_ref[...])
     lower_half = where_ref[0] == 0
-    p_azim = jnp.where(top, pltpu.roll(above_ref[4 * comps : 4 * comps + 8], 4, 0), 0.0)
+    p_azim = jnp.concatenate([jnp.zeros((4, 128), f32), above_ref[4 * comps : 4 * comps + 4]], axis=0)
     pairs = jnp.where(lower_half, ax_ref[2 * comps : 2 * comps + 8], 0.0)
     p_axial = jnp.where(row == 3, pairs[0:1], jnp.where(row == 7, pairs[1:2], 0.0))
     p_rad = jnp.where(lane == 127, hrad[8 * comps : 8 * comps + 8], 0.0)
@@ -331,19 +316,11 @@
     rates = (zones.reshape(8, 128), growth_rate, transfer_rate, nucleation_rate)
     dma = pltpu.SemaphoreType.DMA
 
-    (dn,) = call(
-        functools.partial(first_down, comps),
-        "hhh",
-        "v",
-        [(comps + 2, 4, 128)],
-        1_000_000,
-        adjoint_final.reshape(comps, 2, 4, 128),
-        speeds,
-        flags,
-        scratch=[pltpu.VMEM((4, 128), f32), pltpu.VMEM((4, 128), jnp.int32), dma((6,))],
-        room=60,
-    )
-    above = shift(dn, "azim", -1, True).reshape(half + 8, 128)
+    keep = ((0, 1, 0), (0, -1, 0), (0, 0, 0), (0, 0, 0))
+    after = ((comps, -2, 0), (0, -1, 0), (0, 0, 0), (0, 0, 0))
+    dn = lax.pad(adjoint_final.reshape(comps, 2, 4, 128), 0.0, keep)
+    dn = dn + lax.pad(speeds, 0.0, after) * lax.pad(flags, 0, after).astype(f32)
+    above = shift(dn, "azim", -1, True).reshape(half + 4, 128)
     up, *edges = call(
         functools.partial(first_rest, comps),
         "svvv",

time: 43 us -> 42.8 us (level)
  Pallas kernels: 10.2 us -> 8.2 us
  other arithmetic: 0 us -> 1.85 us
  waiting for transfers between devices: 15.5 us -> 14.3 us
  local copies, waits for them, and re-layouts: 0.67 us -> 1.8 us
    pallas_call x8 -> x7, Pallas kernels: 10.2 us -> 8.2 us  [call(): pl.pallas_call(body, in_specs=[SPACES[s] for s in ins], out_specs=[SPACES...]
    add x0 -> x1, other arithmetic: none -> 1.85 us  [shards(): dn = dn + lax.pad(speeds, 0.0, after) * lax.pad(flags, 0, after).astype(f32)]
    ppermute x8, waiting for transfers between devices: 15.5 us -> 14.3 us  [shift(): return lax.ppermute(x, axis, pairs)]
    reshape x0 -> x1, local copies, waits for them, and re-layouts: none -> 1.13 us  [shards(): above = shift(dn, 'azim', -1, True).reshape(half + 4, 128)]
  transfers between devices with their start and end apart: 10 -> 10, of which waited for: 5 -> 4; matrix products, arithmetic and copies ran while one was open for 0% -> 3% of each run, Pallas kernels for 17% -> 17%
where the time goes in v3:
time: 42.8 us; the launch traced here: 42.5 us
  starting transfers between devices  16.2 us (38%)
  waiting for transfers between devices  14.3 us (33%)
  Pallas kernels  8.2 us (19%)
  other arithmetic  1.85 us (4%)
  local copies, waits for them, and re-layouts  1.8 us (4%)
    ppermute x8, waiting for transfers between devices, shift(): return lax.ppermute(x, axis, pairs)  14.3 us
    ppermute x8, starting transfers between devices, shift(): return lax.ppermute(x, axis, pairs)  13.1 us
    pallas_call x7, Pallas kernels, call(): pl.pallas_call(body, in_specs=[SPACES[s] for s in ins], out_specs=[SPACES...  8.2 us
    ppermute x2, starting transfers between devices, sides(): ax = lax.ppermute(ax, 'axial', [(0, 1), (1, 0)])  3.1 us
    add x1, other arithmetic, shards(): dn = dn + lax.pad(speeds, 0.0, after) * lax.pad(flags, 0, after).astype(f32)  1.85 us
    reshape x1, local copies, waits for them, and re-layouts, shards(): above = shift(dn, 'azim', -1, True).reshape(half + 4, 128)  1.13 us
  transfers between devices with their start and end apart: 10, of which 4 were waited for; matrix products, arithmetic and copies ran while one was open for 3% of the time, Pallas kernels for 17%

profile of v3, /device:TPU:0, one launch (start us, length us, event | category | flops | bytes accessed | tf_op | source)
XLA Modules:
  0.0 42.5 jit_solution(2447258543634855691)
XLA Ops:
  0.0 0.0 copy-start
  0.0 0.0 copy-start.4
  0.0 1.8 %fusion = f32[193,1,4,128]{3,2,1,0:T(4,128)} fusion(f32[192,2,4,128]{3,2,1,0:T(4,128)} %bitcast.10, f32[3,2,4,128]{3,2,1,0:T(4,128)} %param.12, s32[3,2,4,128]{3,2,1,0:T(4,128)} %param.13), kind=kLoop, calls=%fused_computation.3 | loop fusion | flops 296448 | bytes 1206272 | tf_op jit(solution)/shard_map/add | solution.py:322
  1.9 0.0 copy-start.3
  1.9 5.0 %collective-permute-start = (f32[193,1,4,128]{3,2,1,0:T(4,128)}, f32[193,1,4,128]{3,2,1,0:T(4,128)}, u32[]{:S(2)}, u32[]{:S(2)}) collective-permute-start(f32[193,1,4,128]{3,2,1,0:T(4,128)} %fusion), channel_id=1, source_target_pairs={{0,24},{8,0},{16,8},{24,16},{1,25},{9,1},{17,9},{25,17},{2,26},{10... | collective-permute-start | bytes 1185800 | tf_op jit(solution)/shard_map/ppermute | solution.py:296
  6.9 0.0 copy-done
  6.9 0.0 copy-done.4
  6.9 0.0 copy-done.3
  6.9 0.0 copy-start.1
  6.9 0.8 %shard_map.92 = (f32[768,128]{1,0:T(8,128)S(1)}, f32[392,128]{1,0:T(8,128)S(1)}, f32[1,1664]{1,0:T(1,128)S(1)}, f32[1,1664]{1,0:T(1,128)S(1)}) custom-call(s32[1]{0:T(128)} %bitcast.where_ref, f32[1536,128]{1,0:T(8,128)S(1)} %bitcast.11, f32[3,8,128]{2,1,0:T(8,128)S(1)} %bitcast.18, s32[3,8,128]{2,1,0:T(8,128)S(1)} %bitcast.22), custom_call_target="tpu_custom_call" | custom-call | flops 2000000 | bytes 200000 | tf_op jit(solution)/shard_map/pallas_call | solution.py:281
  7.8 0.1 collective-permute-start.4
  7.8 0.0 copy-start.5
  7.8 1.6 %collective-permute-start.1 = (f32[392,128]{1,0:T(8,128)S(1)}, f32[392,128]{1,0:T(8,128)S(1)}, u32[]{:S(2)}, u32[]{:S(2)}) collective-permute-start(f32[392,128]{1,0:T(8,128)S(1)} %get-tuple-element.19), channel_id=1, source_target_pairs={{0,1},{1,0},{2,3},{3,2},{4,5},{5,4},{6,7},{7,6},{8,9},{9,8},{10,11... | collective-permute-start | bytes 602120 | tf_op jit(solution)/shard_map/ppermute | solution.py:300
  9.4 1.3 %collective-permute-start.2 = (f32[1,1664]{1,0:T(1,128)S(1)}, f32[1,1664]{1,0:T(1,128)S(1)}, u32[]{:S(2)}, u32[]{:S(2)}) collective-permute-start(f32[1,1664]{1,0:T(1,128)S(1)} %get-tuple-element.20), channel_id=1, source_target_pairs={{0,2},{2,4},{4,6},{1,3},{3,5},{5,7},{8,10},{10,12},{12,14},{9,11},... | collective-permute-start | bytes 19976 | tf_op jit(solution)/shard_map/ppermute | solution.py:296
  10.7 1.3 %collective-permute-start.3 = (f32[1,1664]{1,0:T(1,128)S(1)}, f32[1,1664]{1,0:T(1,128)S(1)}, u32[]{:S(2)}, u32[]{:S(2)}) collective-permute-start(f32[1,1664]{1,0:T(1,128)S(1)} %get-tuple-element.21), channel_id=1, source_target_pairs={{2,0},{4,2},{6,4},{3,1},{5,3},{7,5},{10,8},{12,10},{14,12},{11,9},... | collective-permute-start | bytes 19976 | tf_op jit(solution)/shard_map/ppermute | solution.py:296
  12.0 0.0 copy-start.6
  12.0 0.0 copy-start.7
  12.0 0.0 copy-start.8
  12.1 0.0 copy-done.1
  12.1 0.0 copy-done.5
  12.1 0.6 %copy-done.6 = f32[48]{0:T(128)S(1)} copy-done((f32[48]{0:T(128)S(1)}, f32[48]{0:T(128)}, u32[]{:S(2)}) %copy-start.6) | copy-done | bytes 216
  12.7 0.0 copy-done.7
  12.7 0.0 copy-done.8
  12.7 1.4 %shard_map.91.part_ref = f32[1536,128]{1,0:T(8,128)S(1)} custom-call(f32[1536,128]{1,0:T(8,128)S(1)} %bitcast.12, bf16[192,8,128]{2,1,0:T(8,128)(2,1)S(1)} %bitcast.16, f32[3,8,128]{2,1,0:T(8,128)S(1)} %bitcast.19, s32[3,8,128]{2,1,0:T(8,128)S(1)} %bitcast.23, s32[8,128]{1,0:T(8,128)S(1)} %bitcast.26, f32[48]{0:T(128)S(1)} %copy-done.6, f32[48]{0:T(128)S(1)} %copy-done.7, ...), custom_call_target="tpu_custom_call" | custom-call | flops 8000000 | bytes 800000 | tf_op jit(solution)/shard_map/pallas_call | solution.py:281
  14.1 2.7 %collective-permute-done = f32[193,1,4,128]{3,2,1,0:T(4,128)} collective-permute-done((f32[193,1,4,128]{3,2,1,0:T(4,128)}, f32[193,1,4,128]{3,2,1,0:T(4,128)}, u32[]{:S(2)}, u32[]{:S(2)}) %collective-permute-start) | collective-permute-done | bytes 395296 | tf_op jit(solution)/shard_map/ppermute | solution.py:296
  16.8 1.1 %reshape.40.above_ref = f32[772,128]{1,0:T(8,128)S(1)} reshape(f32[193,1,4,128]{3,2,1,0:T(4,128)} %collective-permute-done) | data formatting | bytes 790528 | tf_op jit(solution)/shard_map/reshape | solution.py:323
  17.9 0.0 collective-permute-done.2.radlo_ref
  17.9 0.0 collective-permute-done.3.radhi_ref
  17.9 0.0 collective-permute-done.1.ax_ref
  18.0 1.2 %shard_map.93 = (f32[1536,128]{1,0:T(8,128)S(1)}, f32[4,8,128]{2,1,0:T(8,128)S(1)}, f32[768,128]{1,0:T(8,128)S(1)}) custom-call(s32[1]{0:T(128)} %bitcast.where_ref, f32[1536,128]{1,0:T(8,128)S(1)} %shard_map.91.part_ref, f32[1536,128]{1,0:T(8,128)S(1)} %bitcast.13, f32[772,128]{1,0:T(8,128)S(1)} %reshape.40.above_ref, ...), custom_call_target="tpu_custom_call" | custom-call | flops 4000000 | bytes 400000 | tf_op jit(solution)/shard_map/pallas_call | solution.py:281
  19.1 0.1 collective-permute-start.5
  19.2 6.5 %collective-permute-done.4.below_ref = f32[768,128]{1,0:T(8,128)S(1)} collective-permute-done((f32[768,128]{1,0:T(8,128)S(1)}, f32[768,128]{1,0:T(8,128)S(1)}, u32[]{:S(2)}, u32[]{:S(2)}) %collective-permute-start.4) | collective-permute-done | bytes 393248 | tf_op jit(solution)/shard_map/ppermute | solution.py:296
  25.7 0.0 copy-start.2
  25.7 0.9 %shard_map.94 = (f32[1536,128]{1,0:T(8,128)S(1)}, f32[768,128]{1,0:T(8,128)S(1)}, f32[384,128]{1,0:T(8,128)S(1)}, f32[1,1536]{1,0:T(1,128)S(1)}, f32[1,1536]{1,0:T(1,128)S(1)}) custom-call(s32[1]{0:T(128)} %bitcast.where_ref, f32[1536,128]{1,0:T(8,128)S(1)} %get-tuple-element.22.part_ref, f32[768,128]{1,0:T(8,128)S(1)} %collective-permute-done.4.below_ref, ...), custom_call_target="tpu_custom_call" | custom-call | flops 4000000 | bytes 400000 | tf_op jit(solution)/shard_map/pallas_call | solution.py:281
  26.6 2.8 %collective-permute-start.9 = (f32[768,128]{1,0:T(8,128)S(1)}, f32[768,128]{1,0:T(8,128)S(1)}, u32[]{:S(2)}, u32[]{:S(2)}) collective-permute-start(f32[768,128]{1,0:T(8,128)S(1)} %get-tuple-element.32), channel_id=1, source_target_pairs={{0,24},{8,0},{16,8},{24,16},{1,25},{9,1},{17,9},{25,17},{2,26},{10... | collective-permute-start | bytes 1179656 | tf_op jit(solution)/shard_map/ppermute | solution.py:296
  29.3 1.5 %collective-permute-start.6 = (f32[384,128]{1,0:T(8,128)S(1)}, f32[384,128]{1,0:T(8,128)S(1)}, u32[]{:S(2)}, u32[]{:S(2)}) collective-permute-start(f32[384,128]{1,0:T(8,128)S(1)} %get-tuple-element.27), channel_id=1, source_target_pairs={{0,1},{1,0},{2,3},{3,2},{4,5},{5,4},{6,7},{7,6},{8,9},{9,8},{10,11... | collective-permute-start | bytes 589832 | tf_op jit(solution)/shard_map/ppermute | solution.py:300
  30.8 1.3 %collective-permute-start.7 = (f32[1,1536]{1,0:T(1,128)S(1)}, f32[1,1536]{1,0:T(1,128)S(1)}, u32[]{:S(2)}, u32[]{:S(2)}) collective-permute-start(f32[1,1536]{1,0:T(1,128)S(1)} %get-tuple-element.28), channel_id=1, source_target_pairs={{0,2},{2,4},{4,6},{1,3},{3,5},{5,7},{8,10},{10,12},{12,14},{9,11},... | collective-permute-start | bytes 18440 | tf_op jit(solution)/shard_map/ppermute | solution.py:296
  32.1 1.3 %collective-permute-start.8 = (f32[1,1536]{1,0:T(1,128)S(1)}, f32[1,1536]{1,0:T(1,128)S(1)}, u32[]{:S(2)}, u32[]{:S(2)}) collective-permute-start(f32[1,1536]{1,0:T(1,128)S(1)} %get-tuple-element.29), channel_id=1, source_target_pairs={{2,0},{4,2},{6,4},{3,1},{5,3},{7,5},{10,8},{12,10},{14,12},{11,9},... | collective-permute-start | bytes 18440 | tf_op jit(solution)/shard_map/ppermute | solution.py:296
  33.4 0.0 copy-done.2
  33.4 1.4 %shard_map.95.part_ref = f32[1536,128]{1,0:T(8,128)S(1)} custom-call(f32[1536,128]{1,0:T(8,128)S(1)} %get-tuple-element.25.m_ref, f32[1536,128]{1,0:T(8,128)S(1)} %bitcast.14, bf16[192,8,128]{2,1,0:T(8,128)(2,1)S(1)} %bitcast.17, f32[4,8,128]{2,1,0:T(8,128)S(1)} %get-tuple-element.24.edge_ref, f32[3,8,128]{2,1,0:T(8,128)S(1)} %bitcast.21, ...), custom_call_target="tpu_custom_call" | custom-call | flops 8000000 | bytes 800000 | tf_op jit(solution)/shard_map/pallas_call | solution.py:281
  34.8 0.0 collective-permute-done.7.radlo_ref
  34.8 2.1 %collective-permute-done.8.radhi_ref = f32[1,1536]{1,0:T(1,128)S(1)} collective-permute-done((f32[1,1536]{1,0:T(1,128)S(1)}, f32[1,1536]{1,0:T(1,128)S(1)}, u32[]{:S(2)}, u32[]{:S(2)}) %collective-permute-start.8) | collective-permute-done | bytes 6176 | tf_op jit(solution)/shard_map/ppermute | solution.py:296
  36.9 0.0 collective-permute-done.6.ax_ref
  36.9 0.0 collective-permute-done.5.below_ref
  36.9 1.7 %shard_map.96 = (f32[192,2,4,128]{3,2,1,0:T(4,128)}, f32[192,4,128]{2,1,0:T(4,128)S(1)}) custom-call(s32[1]{0:T(128)} %bitcast.where_ref, f32[1536,128]{1,0:T(8,128)S(1)} %shard_map.95.part_ref, f32[768,128]{1,0:T(8,128)S(1)} %collective-permute-done.5.below_ref, f32[384,128]{1,0:T(8,128)S(1)} %collective-permute-done.6.ax_ref, ...), custom_call_target="tpu_custom_call" | custom-call | flops 4000000 | bytes 400000 | tf_op jit(solution)/shard_map/pallas_call | solution.py:281
  38.6 3.1 %collective-permute-done.9 = f32[768,128]{1,0:T(8,128)S(1)} collective-permute-done((f32[768,128]{1,0:T(8,128)S(1)}, f32[768,128]{1,0:T(8,128)S(1)}, u32[]{:S(2)}, u32[]{:S(2)}) %collective-permute-start.9) | collective-permute-done | bytes 393248 | tf_op jit(solution)/shard_map/ppermute | solution.py:296
  41.7 0.8 %shard_map.97 = f32[192,2,4,128]{3,2,1,0:T(4,128)} custom-call(f32[192,2,4,128]{3,2,1,0:T(4,128)} %get-tuple-element.30._, f32[192,4,128]{2,1,0:T(4,128)S(1)} %get-tuple-element.31.top_ref, f32[192,4,128]{2,1,0:T(4,128)S(1)} %bitcast.15, f32[4,8,128]{2,1,0:T(8,128)S(1)} %get-tuple-element.24.edge_ref), custom_call_target="tpu_custom_call", output_to_operand_aliasing={{}: (0, {})} | custom-call | flops 1000000 | bytes 100000 | tf_op jit(solution)/shard_map/pallas_call | solution.py:281
Async XLA Ops:
  0.0 6.9 %copy-start = (f32[4,48,2,4,128]{4,3,2,1,0:T(4,128)S(1)}, f32[4,48,2,4,128]{4,3,2,1,0:T(4,128)}, u32[]{:S(2)}) copy-start(f32[4,48,2,4,128]{4,3,2,1,0:T(4,128)} %param.9) | copy-start | bytes 2359300
  0.0 6.9 %copy-start.4 = (s32[3,2,4,128]{3,2,1,0:T(4,128)S(1)}, s32[3,2,4,128]{3,2,1,0:T(4,128)}, u32[]{:S(2)}) copy-start(s32[3,2,4,128]{3,2,1,0:T(4,128)} %param.13) | copy-start | bytes 36868
  1.9 5.1 %copy-start.3 = (f32[3,2,4,128]{3,2,1,0:T(4,128)S(1)}, f32[3,2,4,128]{3,2,1,0:T(4,128)}, u32[]{:S(2)}) copy-start(f32[3,2,4,128]{3,2,1,0:T(4,128)} %param.12) | copy-start | bytes 36868
  1.9 14.9 %collective-permute-start = (f32[193,1,4,128]{3,2,1,0:T(4,128)}, f32[193,1,4,128]{3,2,1,0:T(4,128)}, u32[]{:S(2)}, u32[]{:S(2)}) collective-permute-start(f32[193,1,4,128]{3,2,1,0:T(4,128)} %fusion), channel_id=1, source_target_pairs={{0,24},{8,0},{16,8},{24,16},{1,25},{9,1},{17,9},{25,17},{2,26},{10... | collective-permute-start | bytes 1185800 | tf_op jit(solution)/shard_map/ppermute | solution.py:296
  6.9 5.1 %copy-start.1 = (bf16[4,48,2,4,128]{4,3,2,1,0:T(4,128)(2,1)S(1)}, bf16[4,48,2,4,128]{4,3,2,1,0:T(4,128)(2,1)}, u32[]{:S(2)}) copy-start(bf16[4,48,2,4,128]{4,3,2,1,0:T(4,128)(2,1)} %param.11) | copy-start | bytes 1179652
  7.8 17.9 %collective-permute-start.4 = (f32[768,128]{1,0:T(8,128)S(1)}, f32[768,128]{1,0:T(8,128)S(1)}, u32[]{:S(2)}, u32[]{:S(2)}) collective-permute-start(f32[768,128]{1,0:T(8,128)S(1)} %get-tuple-element.23), channel_id=1, source_target_pairs={{0,8},{8,16},{16,24},{24,0},{1,9},{9,17},{17,25},{25,1},{2,10},{10... | collective-permute-start | bytes 1179656 | tf_op jit(solution)/shard_map/ppermute | solution.py:296
  7.8 4.2 %copy-start.5 = (s32[2,4,128]{2,1,0:T(4,128)S(1)}, s32[2,4,128]{2,1,0:T(4,128)}, u32[]{:S(2)}) copy-start(s32[2,4,128]{2,1,0:T(4,128)} %param.14) | copy-start | bytes 12292
  7.8 10.1 %collective-permute-start.1 = (f32[392,128]{1,0:T(8,128)S(1)}, f32[392,128]{1,0:T(8,128)S(1)}, u32[]{:S(2)}, u32[]{:S(2)}) collective-permute-start(f32[392,128]{1,0:T(8,128)S(1)} %get-tuple-element.19), channel_id=1, source_target_pairs={{0,1},{1,0},{2,3},{3,2},{4,5},{5,4},{6,7},{7,6},{8,9},{9,8},{10,11... | collective-permute-start | bytes 602120 | tf_op jit(solution)/shard_map/ppermute | solution.py:300
  9.4 8.5 %collective-permute-start.2 = (f32[1,1664]{1,0:T(1,128)S(1)}, f32[1,1664]{1,0:T(1,128)S(1)}, u32[]{:S(2)}, u32[]{:S(2)}) collective-permute-start(f32[1,1664]{1,0:T(1,128)S(1)} %get-tuple-element.20), channel_id=1, source_target_pairs={{0,2},{2,4},{4,6},{1,3},{3,5},{5,7},{8,10},{10,12},{12,14},{9,11},... | collective-permute-start | bytes 19976 | tf_op jit(solution)/shard_map/ppermute | solution.py:296
  10.7 7.2 %collective-permute-start.3 = (f32[1,1664]{1,0:T(1,128)S(1)}, f32[1,1664]{1,0:T(1,128)S(1)}, u32[]{:S(2)}, u32[]{:S(2)}) collective-permute-start(f32[1,1664]{1,0:T(1,128)S(1)} %get-tuple-element.21), channel_id=1, source_target_pairs={{2,0},{4,2},{6,4},{3,1},{5,3},{7,5},{10,8},{12,10},{14,12},{11,9},... | collective-permute-start | bytes 19976 | tf_op jit(solution)/shard_map/ppermute | solution.py:296
  12.0 0.7 %copy-start.6 = (f32[48]{0:T(128)S(1)}, f32[48]{0:T(128)}, u32[]{:S(2)}) copy-start(f32[48]{0:T(128)} %growth_ref.3) | copy-start | bytes 580
  12.0 0.7 %copy-start.7 = (f32[48]{0:T(128)S(1)}, f32[48]{0:T(128)}, u32[]{:S(2)}) copy-start(f32[48]{0:T(128)} %transfer_ref.3) | copy-start | bytes 580
  12.0 0.7 %copy-start.8 = (f32[4]{0:T(128)S(1)}, f32[4]{0:T(128)}, u32[]{:S(2)}) copy-start(f32[4]{0:T(128)} %rate_ref.3) | copy-start | bytes 52
  19.1 17.8 %collective-permute-start.5 = (f32[768,128]{1,0:T(8,128)S(1)}, f32[768,128]{1,0:T(8,128)S(1)}, u32[]{:S(2)}, u32[]{:S(2)}) collective-permute-start(f32[768,128]{1,0:T(8,128)S(1)} %get-tuple-element.26), channel_id=1, source_target_pairs={{0,8},{8,16},{16,24},{24,0},{1,9},{9,17},{17,25},{25,1},{2,10},{10... | collective-permute-start | bytes 1179656 | tf_op jit(solution)/shard_map/ppermute | solution.py:296
  25.7 7.8 %copy-start.2 = (bf16[4,48,2,4,128]{4,3,2,1,0:T(4,128)(2,1)S(1)}, bf16[4,48,2,4,128]{4,3,2,1,0:T(4,128)(2,1)}, u32[]{:S(2)}) copy-start(bf16[4,48,2,4,128]{4,3,2,1,0:T(4,128)(2,1)} %param.10) | copy-start | bytes 1179652
  26.6 15.2 %collective-permute-start.9 = (f32[768,128]{1,0:T(8,128)S(1)}, f32[768,128]{1,0:T(8,128)S(1)}, u32[]{:S(2)}, u32[]{:S(2)}) collective-permute-start(f32[768,128]{1,0:T(8,128)S(1)} %get-tuple-element.32), channel_id=1, source_target_pairs={{0,24},{8,0},{16,8},{24,16},{1,25},{9,1},{17,9},{25,17},{2,26},{10... | collective-permute-start | bytes 1179656 | tf_op jit(solution)/shard_map/ppermute | solution.py:296
  29.3 7.6 %collective-permute-start.6 = (f32[384,128]{1,0:T(8,128)S(1)}, f32[384,128]{1,0:T(8,128)S(1)}, u32[]{:S(2)}, u32[]{:S(2)}) collective-permute-start(f32[384,128]{1,0:T(8,128)S(1)} %get-tuple-element.27), channel_id=1, source_target_pairs={{0,1},{1,0},{2,3},{3,2},{4,5},{5,4},{6,7},{7,6},{8,9},{9,8},{10,11... | collective-permute-start | bytes 589832 | tf_op jit(solution)/shard_map/ppermute | solution.py:300
  30.8 4.0 %collective-permute-start.7 = (f32[1,1536]{1,0:T(1,128)S(1)}, f32[1,1536]{1,0:T(1,128)S(1)}, u32[]{:S(2)}, u32[]{:S(2)}) collective-permute-start(f32[1,1536]{1,0:T(1,128)S(1)} %get-tuple-element.28), channel_id=1, source_target_pairs={{0,2},{2,4},{4,6},{1,3},{3,5},{5,7},{8,10},{10,12},{12,14},{9,11},... | collective-permute-start | bytes 18440 | tf_op jit(solution)/shard_map/ppermute | solution.py:296
  32.1 4.8 %collective-permute-start.8 = (f32[1,1536]{1,0:T(1,128)S(1)}, f32[1,1536]{1,0:T(1,128)S(1)}, u32[]{:S(2)}, u32[]{:S(2)}) collective-permute-start(f32[1,1536]{1,0:T(1,128)S(1)} %get-tuple-element.29), channel_id=1, source_target_pairs={{2,0},{4,2},{6,4},{3,1},{5,3},{7,5},{10,8},{12,10},{14,12},{11,9},... | collective-permute-start | bytes 18440 | tf_op jit(solution)/shard_map/ppermute | solution.py:296

commit v4 on v3

v4 whole, which is shorter than its diff:
```python
import functools

import jax
import jax.numpy as jnp
from jax import lax
from jax.experimental import pallas as pl
from jax.experimental.pallas import tpu as pltpu
from jax.sharding import PartitionSpec as P

supersat_scale = 1.5
crowding = 0.02
nucleus_moments = (1.0, 0.5, 0.25, 0.125)
f32 = jnp.float32
bf16 = jnp.bfloat16
exact = lax.Precision.HIGHEST

slots = 320
extra = slots - 256


def rows_of():
    return lax.broadcasted_iota(jnp.int32, (8, 128), 0)


def lanes_of():
    return lax.broadcasted_iota(jnp.int32, (8, 128), 1)


def faces(speeds_ref, flags_ref):
    p, q = [], []
    for d in range(3):
        speed, upwind = speeds_ref[d], flags_ref[d].astype(f32)
        p.append(speed * upwind)
        q.append(speed * (1.0 - upwind))
    return p, q


class Local:
    def __init__(self, p, q):
        row, lane = rows_of(), lanes_of()
        z, top = row % 4, row >= 4
        self.azim = jnp.where(top, q[0], pltpu.roll(p[0], 4, 0))
        self.ax_up = jnp.where(z == 3, 0.0, pltpu.roll(p[1], 7, 0))
        self.ax_dn = jnp.where(z == 0, 0.0, q[1])
        self.rad_up = jnp.where(lane == 127, 0.0, pltpu.roll(p[2], 127, 1))
        self.rad_dn = jnp.where(lane == 0, 0.0, q[2])
        self.centre = self.azim + self.ax_up + q[1] + self.rad_up + q[2] + jnp.where(top, 0.0, q[0])

    def __call__(self, x):
        return (
            self.azim * pltpu.roll(x, 4, 0)
            + self.ax_up * pltpu.roll(x, 7, 0)
            + self.ax_dn * pltpu.roll(x, 1, 0)
            + self.rad_up * pltpu.roll(x, 127, 1)
            + self.rad_dn * pltpu.roll(x, 1, 1)
            - self.centre * x
        )


def pair_rows(x, first, second):
    return jnp.where(
        rows_of() % 2 == 0,
        jnp.broadcast_to(x[first : first + 1], (8, 128)),
        jnp.broadcast_to(x[second : second + 1], (8, 128)),
    )


def make_tables(p, where_zero, low_ref, high_ref):
    row, lane = rows_of(), lanes_of()
    taken = (p == 0.0) if where_zero else (p != 0.0)
    one = jnp.where(taken & (row < 4), 1.0, 0.0)
    before = lax.broadcasted_iota(jnp.int32, (128, 128), 0) < lax.broadcasted_iota(jnp.int32, (128, 128), 1)
    inside = jnp.dot(one.astype(bf16), jnp.where(before, 1.0, 0.0).astype(bf16), preferred_element_type=f32)
    total = jnp.sum(one, axis=1, keepdims=True)
    base = jnp.zeros((8, 1), f32)
    for step in (1, 2, 3):
        base = base + jnp.where(
            lax.broadcasted_iota(jnp.int32, (8, 1), 0) >= step, jnp.roll(total, step, axis=0), 0.0
        )
    slot = jnp.where(one > 0.0, inside + base, -1.0).astype(jnp.int32)
    here = lax.broadcasted_iota(jnp.int32, (128, 128), 0)
    first = jnp.where(here < extra, here + 256, -2)
    second = jnp.where(here >= extra, here + (256 - extra), -2)
    for z in range(4):
        cells = slice(128 * z, 128 * z + 128)
        want = jnp.broadcast_to(slot[z : z + 1], (128, 128))
        for ref, start, names in ((low_ref, 0, here), (low_ref, 128, here + 128), (high_ref, 0, first), (high_ref, 128, second)):
            ref[start : start + 128, cells] = jnp.where(names == want, 1.0, 0.0).astype(bf16)


def pieces(x):
    high = x.astype(bf16)
    rest = x - high.astype(f32)
    middle = rest.astype(bf16)
    return high, middle, (rest - middle.astype(f32)).astype(bf16)


def stacked(x, half):
    return jnp.concatenate([part[half * i : half * i + half] for i in range(2) for part in pieces(x)], axis=0)


def summed(x, half):
    parts = [x[half * i : half * i + half] for i in range(6)]
    return [parts[3 * i] + (parts[3 * i + 1] + parts[3 * i + 2]) for i in range(2)]


def encode(comps, x_ref, first_row, low_ref, high_ref, message_ref):
    half = comps // 2
    x = jnp.concatenate(
        [stacked(x_ref[pl.ds(first_row + z, comps, stride=8)], half) for z in range(4)], axis=1
    )
    over = (((1,), (1,)), ((), ()))
    low = lax.dot_general(x, low_ref[...], over, preferred_element_type=f32)
    high = [
        lax.dot_general(
            x[3 * half * i : 3 * half * (i + 1)], high_ref[128 * i : 128 * i + 128], over, preferred_element_type=f32
        )
        for i in range(2)
    ]
    tail = jnp.zeros((half, 128), f32)
    for i, part in enumerate(summed(low, half)):
        message_ref[half * i : half * i + half] = part[:, :128]
        message_ref[comps + half * i : comps + half * i + half] = part[:, 128:]
    for part in high:
        tail = tail + (part[:half] + (part[half : 2 * half] + part[2 * half :]))
    message_ref[2 * comps : 2 * comps + half] = tail


def decode(comps, message_ref, low_ref, high_ref):
    half = comps // 2
    x = jnp.concatenate([stacked(message_ref[comps * i : comps * i + comps], half) for i in range(2)], axis=1)
    low = jnp.dot(x, low_ref[...], preferred_element_type=f32)
    tail = jnp.concatenate(pieces(message_ref[2 * comps : 2 * comps + half]), axis=0)
    found = []
    for i, part in enumerate(summed(low, half)):
        high = jnp.dot(tail, high_ref[128 * i : 128 * i + 128], preferred_element_type=f32)
        found.append(part + (high[:half] + (high[half : 2 * half] + high[2 * half :])))
    return jnp.concatenate(found, axis=0)


def add_azimuthal(comps, halo, coefficient, first_row, out_ref):
    for z in range(4):
        spots = pl.ds(first_row + z, comps, stride=8)
        out_ref[spots] = out_ref[spots] + coefficient[first_row + z : first_row + z + 1] * halo[:, 128 * z : 128 * z + 128]


def pack_axial(comps, x_ref, where_ref, ax_ref):
    @pl.when(where_ref[0] == 0)
    def _():
        ax_ref[0 : 2 * comps] = x_ref[pl.ds(3, 2 * comps, stride=4)]

    @pl.when(where_ref[0] != 0)
    def _():
        ax_ref[0 : 2 * comps] = x_ref[pl.ds(0, 2 * comps, stride=4)]


def add_axial(comps, scale, where_ref, axial, ax_ref, out_ref):
    several = jnp.concatenate([scale * axial] * (2 * comps // 8), axis=0)
    for start, index in ((3, 0), (0, 1)):

        @pl.when(where_ref[0] == index)
        def _():
            spots = pl.ds(start, 2 * comps, stride=4)
            out_ref[spots] = out_ref[spots] + several * ax_ref[0 : 2 * comps]


def columns(x):
    row, lane = rows_of(), lanes_of()
    take = jnp.where(((row == 0) & (lane == 127)) | ((row == 1) & (lane == 0)), 1.0, 0.0)
    return lax.dot_general(take, x, (((1,), (1,)), ((), ())), precision=exact, preferred_element_type=f32)


def pack_radial(comps, x_ref, p, where_ref, one_ref, two_ref):
    even = where_ref[1] % 2 == 0
    used = 8 * comps
    ends = columns(x_ref[...])
    for ref, last in ((one_ref, even), (two_ref, jnp.logical_not(even))):
        ref[:, 0:used] = jnp.where(last, ends[0:1], ends[1:2])
        ref[:, used:] = jnp.zeros((1, 256), f32)
        if p is not None:
            ref[:, used : used + 8] = columns(p)[1:2]


def radial_halo(comps, where_ref, one_ref, two_ref):
    n = 8 * comps + 128
    even = where_ref[1] % 2 == 0
    one, two = one_ref[:, 0:n], two_ref[:, 0:n]
    lower = jnp.where(where_ref[1] > 0, jnp.where(even, two, one), 0.0)
    upper = jnp.where(where_ref[1] < where_ref[2] - 1, jnp.where(even, one, two), 0.0)
    row, lane = rows_of(), lanes_of()
    which = lax.broadcasted_iota(jnp.int32, (8, n), 0)
    both = jnp.where(which == 0, lower, jnp.where(which == 1, upper, 0.0))
    place = jnp.where(((row == 0) & (lane == 0)) | ((row == 1) & (lane == 127)), 1.0, 0.0)
    return lax.dot_general(both, place, (((0,), (0,)), ((), ())), precision=exact, preferred_element_type=f32)


def source(sections, x_ref, u_ref, growth_ref, transfer_ref, zones_ref, rate_ref, finish):
    def inner(k, s, x):
        term = transfer_ref[s] * ((x[k][1] - x[k][0]) if s + 1 < sections else -x[k][0])
        if k < 3:
            term = term + ((k + 1.0) * growth_ref[s]) * x[k + 1][0]
        return term

    def load(s):
        got = []
        for k in range(4):
            c = k * sections + s
            here = x_ref[8 * c : 8 * c + 8]
            got.append((here, x_ref[8 * c + 8 : 8 * c + 16] if s + 1 < sections else None))
        return got

    squares = jnp.zeros((8, 128), f32)
    product = jnp.zeros((8, 128), f32)
    for s in range(sections):
        x = load(s)
        for k in range(4):
            u = u_ref[k * sections + s].astype(f32)
            product = product + u * inner(k, s, x)
        squares = squares + u * u
    sigma = supersat_scale / (1.0 + crowding * squares)
    birth = jnp.zeros((8, 128), f32)
    for k in range(4):
        c = k * sections
        birth = birth + nucleus_moments[k] * x_ref[8 * c : 8 * c + 8]
    rate = jnp.zeros((8, 128), f32)
    for label in range(rate_ref.shape[0]):
        rate = jnp.where(zones_ref[...] == label, rate_ref[label], rate)
    slope = (-2.0 * crowding / supersat_scale) * sigma * sigma * (product + 2.0 * rate * sigma * birth)
    for s in range(sections):
        x = load(s)
        for k in range(4):
            c = k * sections + s
            term = sigma * inner(k, s, x)
            if k == 3:
                term = term + u_ref[c].astype(f32) * slope
            finish(c, x[k][0], term)


def first_down(comps, where_ref, a_ref, speeds_ref, flags_ref, dn_ref, ax_ref, low_ref, high_ref):
    p, _ = faces(speeds_ref, flags_ref)
    make_tables(p[0], False, low_ref, high_ref)
    encode(comps, a_ref, 0, low_ref, high_ref, dn_ref)
    dn_ref[5 * comps // 2 :] = jnp.zeros((8, 128), f32)
    pack_axial(comps, a_ref, where_ref, ax_ref)
    ax_ref[2 * comps : 2 * comps + 8] = pair_rows(p[1], 0, 4)


def first_up(comps, where_ref, a_ref, upper_ref, bad_ref, speeds_ref, flags_ref, up_ref, one_ref, two_ref, low_ref, high_ref):
    p, _ = faces(speeds_ref, flags_ref)
    make_tables(upper_ref[...], True, low_ref, high_ref)
    encode(comps, a_ref, 4, low_ref, high_ref, up_ref)
    up_ref[5 * comps // 2 :] = bad_ref[...]
    pack_radial(comps, a_ref, p[2], where_ref, one_ref, two_ref)


def first_local(sections, a_ref, u_ref, speeds_ref, flags_ref, zones_ref, growth_ref, transfer_ref, rate_ref, out_ref):
    local = Local(*faces(speeds_ref, flags_ref))

    def finish(c, x, term):
        out_ref[8 * c : 8 * c + 8] = 0.5 * (x + local(x) + term)

    source(sections, a_ref, u_ref, growth_ref, transfer_ref, zones_ref, rate_ref, finish)


def second_local(
    sections, m_ref, a_ref, u_ref, edge_ref, speeds_ref, flags_ref, zones_ref, growth_ref, transfer_ref, rate_ref, out_ref
):
    local = Local(*faces(speeds_ref, flags_ref))
    local.centre = local.centre + (edge_ref[3] - 1.0)

    def finish(c, x, term):
        out_ref[8 * c : 8 * c + 8] = 0.5 * a_ref[8 * c : 8 * c + 8] + (local(x) + term)

    source(sections, m_ref, u_ref, growth_ref, transfer_ref, zones_ref, rate_ref, finish)


def first_top(
    comps,
    where_ref,
    part_ref,
    a_ref,
    above_ref,
    ax_ref,
    one_ref,
    two_ref,
    upper_ref,
    speeds_ref,
    flags_ref,
    up_low_ref,
    up_high_ref,
    m_ref,
    edge_ref,
    up_ref,
    low_ref,
    high_ref,
):
    _, q = faces(speeds_ref, flags_ref)
    row, lane = rows_of(), lanes_of()
    top = row >= 4
    make_tables(upper_ref[...], False, low_ref, high_ref)
    hrad = radial_halo(comps, where_ref, one_ref, two_ref)
    lower_half = where_ref[0] == 0
    p_azim = jnp.where(top, pltpu.roll(upper_ref[...], 4, 0), 0.0)
    pairs = jnp.where(lower_half, ax_ref[2 * comps : 2 * comps + 8], 0.0)
    p_axial = jnp.where(row == 3, pairs[0:1], jnp.where(row == 7, pairs[1:2], 0.0))
    p_rad = jnp.where(lane == 127, hrad[8 * comps : 8 * comps + 8], 0.0)
    axial = jnp.where(lower_half, pairs, pair_rows(q[1], 0, 4))
    rad = jnp.where(lane == 0, q[2], p_rad)
    centre = p_azim + p_axial + p_rad
    edge_ref[0] = jnp.where(top, p_azim, q[0])
    edge_ref[1] = axial
    edge_ref[2] = rad
    edge_ref[3] = centre
    for c in range(comps):
        spots = slice(8 * c, 8 * c + 8)
        m_ref[spots] = part_ref[spots] + 0.5 * (rad * hrad[spots] - centre * a_ref[spots])
    add_axial(comps, 0.5, where_ref, axial, ax_ref, m_ref)
    add_azimuthal(comps, decode(comps, above_ref, low_ref, high_ref), 0.5 * p_azim, 4, m_ref)
    encode(comps, m_ref, 4, up_low_ref, up_high_ref, up_ref)


def first_bottom(
    comps,
    where_ref,
    part_ref,
    below_ref,
    above_ref,
    bad_ref,
    edge_ref,
    speeds_ref,
    flags_ref,
    dn_low_ref,
    dn_high_ref,
    m_ref,
    dn_ref,
    ax_ref,
    one_ref,
    two_ref,
    worse_ref,
    low_ref,
    high_ref,
):
    p, _ = faces(speeds_ref, flags_ref)
    make_tables(p[0], True, low_ref, high_ref)
    m_ref[...] = part_ref[...]
    add_azimuthal(comps, decode(comps, below_ref, low_ref, high_ref), 0.5 * edge_ref[0], 0, m_ref)
    encode(comps, m_ref, 0, dn_low_ref, dn_high_ref, dn_ref)
    pack_axial(comps, m_ref, where_ref, ax_ref)
    pack_radial(comps, m_ref, None, where_ref, one_ref, two_ref)
    worse_ref[...] = bad_ref[...] + below_ref[5 * comps // 2 :] + above_ref[5 * comps // 2 :]


def second_bottom(
    comps, where_ref, part_ref, below_ref, ax_ref, one_ref, two_ref, edge_ref, low_ref, high_ref, full_ref
):
    hrad = radial_halo(comps, where_ref, one_ref, two_ref)
    rad = edge_ref[2]
    for c in range(comps):
        spots = slice(8 * c, 8 * c + 8)
        full_ref[spots] = part_ref[spots] + rad * hrad[spots]
    add_axial(comps, 1.0, where_ref, edge_ref[1], ax_ref, full_ref)
    add_azimuthal(comps, decode(comps, below_ref, low_ref, high_ref), edge_ref[0], 0, full_ref)


def second_top(comps, parts, full_ref, above_ref, edge_ref, low_ref, high_ref, out_ref, done_ref, sems):
    halo = decode(comps, above_ref, low_ref, high_ref)
    edge = edge_ref[0]
    size = comps // parts
    made = []
    for i in range(parts):
        spots = pl.ds(8 * size * i, 8 * size)
        done_ref[spots] = full_ref[spots]
        for z in range(4):
            some = pl.ds(8 * size * i + 4 + z, size, stride=8)
            done_ref[some] = (
                done_ref[some] + edge[4 + z : 5 + z] * halo[size * i : size * i + size, 128 * z : 128 * z + 128]
            )
        made.append(pltpu.make_async_copy(done_ref.at[spots], out_ref.at[spots], sems.at[i]))
        made[-1].start()
    for copy in made:
        copy.wait()


SPACES = {
    "v": pl.BlockSpec(memory_space=pltpu.VMEM),
    "s": pl.BlockSpec(memory_space=pltpu.SMEM),
    "h": pl.BlockSpec(memory_space=pltpu.HBM),
}


def call(body, ins, outs, shapes, cost, *operands, scratch=()):
    shapes = [shape if isinstance(shape, jax.ShapeDtypeStruct) else jax.ShapeDtypeStruct(shape, f32) for shape in shapes]
    return pl.pallas_call(
        body,
        in_specs=[SPACES[s] for s in ins],
        out_specs=[SPACES[s] for s in outs],
        out_shape=shapes,
        scratch_shapes=scratch,
        cost_estimate=pl.CostEstimate(flops=cost, bytes_accessed=cost // 10, transcendentals=0),
        compiler_params=pltpu.CompilerParams(vmem_limit_bytes=32 * 1024 * 1024),
    )(*operands)


def shift(x, axis, step):
    size = lax.axis_size(axis)
    return lax.ppermute(x, axis, [(i, (i + step) % size) for i in range(size)])


def swap_axial(x):
    return lax.ppermute(x, "axial", [(0, 1), (1, 0)])


def swap_radial(x, first):
    size = lax.axis_size("rad")
    pairs = [(i, (i + 1) % size) for i in range(first, size, 2)]
    return lax.ppermute(x, "rad", pairs + [(j, i) for i, j in pairs])


def packed_step(
    adjoint_final, state_start, state_middle, speeds, flags, zones, growth_rate, transfer_rate, nucleation_rate
):
    shape = adjoint_final.shape
    moments, sections = shape[:2]
    comps = moments * sections
    assert moments == 4 and shape[2:] == (2, 4, 128) and comps % 32 == 0
    assert lax.axis_size("axial") == 2 and lax.axis_size("rad") == 4
    cells = 8 * comps
    rows, message = cells // 4, 5 * comps // 2 + 8
    a = adjoint_final.reshape(cells, 128)
    speeds = speeds.reshape(3, 8, 128)
    flags = flags.reshape(3, 8, 128)
    where = jnp.stack([lax.axis_index("axial"), lax.axis_index("rad"), lax.axis_size("rad")]).astype(jnp.int32)
    rates = (zones.reshape(8, 128), growth_rate, transfer_rate, nucleation_rate)
    tables = [jax.ShapeDtypeStruct((256, 512), bf16)] * 2

    lower = speeds[0] * flags[0].astype(f32)
    upper = shift(lower, "azim", -1)

    def crowded(p):
        taken = jnp.sum((p[:4] != 0.0).astype(f32))
        return jnp.maximum(taken - slots, 512.0 - slots - taken) > 0.0

    dn, ax, *dn_tables = call(
        functools.partial(first_down, comps),
        "svvv",
        "vvvv",
        [(message, 128), (rows + 8, 128)] + tables,
        2_000_000,
        where,
        a,
        speeds,
        flags,
    )
    bad = (crowded(lower) | crowded(upper)).astype(f32)
    if lax.axis_size("azim") > 4:
        bad = lax.pmax(bad, "azim")
    bad = jnp.broadcast_to(bad, (8, 128))
    dn = lax.dynamic_update_slice(dn, bad, (message - 8, 0))
    above = shift(dn, "azim", -1)
    up, one, two, *up_tables = call(
        functools.partial(first_up, comps),
        "s" + "v" * 5,
        "vvvvv",
        [(message, 128), (1, cells + 256), (1, cells + 256)] + tables,
        3_000_000,
        where,
        a,
        upper,
        bad,
        speeds,
        flags,
    )
    ax = swap_axial(ax)
    below = shift(up, "azim", 1)
    one, two = swap_radial(one, 0), swap_radial(two, 1)
    (part,) = call(
        functools.partial(first_local, sections),
        "vvvvvsss",
        "v",
        [(cells, 128)],
        8_000_000,
        a,
        state_middle.reshape(comps, 8, 128),
        speeds,
        flags,
        *rates,
    )
    part, edge, up, *above_tables = call(
        functools.partial(first_top, comps),
        "s" + "v" * 11,
        "vvvvv",
        [(cells, 128), (4, 8, 128), (message - 8, 128)] + tables,
        4_000_000,
        where,
        part,
        a,
        above,
        ax,
        one,
        two,
        upper,
        speeds,
        flags,
        *up_tables,
    )
    next_below = shift(up, "azim", 1)
    m, dn, ax, one, two, bad, *below_tables = call(
        functools.partial(first_bottom, comps),
        "s" + "v" * 9,
        "v" * 8,
        [(cells, 128), (message - 8, 128), (rows, 128), (1, cells + 256), (1, cells + 256), (8, 128)] + tables,
        4_000_000,
        where,
        part,
        below,
        above,
        bad,
        edge,
        speeds,
        flags,
        *dn_tables,
    )
    above = shift(dn, "azim", -1)

    def told(message_, count):
        return message_ + lax.pad(count, 0.0, ((0, 0, 0), (cells + 128, 0, 0)))

    bad = (bad + swap_axial(bad))[:1]
    ax = swap_axial(ax)
    one = swap_radial(told(one, bad), 0)
    bad = bad + one[:, cells + 128 :]
    two = swap_radial(told(two, bad), 1)
    bad = bad + two[:, cells + 128 :]
    (part,) = call(
        functools.partial(second_local, sections),
        "vvvvvvvsss",
        "v",
        [(cells, 128)],
        8_000_000,
        m,
        a,
        state_start.reshape(comps, 8, 128),
        edge,
        speeds,
        flags,
        *rates,
    )
    (full,) = call(
        functools.partial(second_bottom, comps),
        "s" + "v" * 8,
        "v",
        [(cells, 128)],
        4_000_000,
        where,
        part,
        next_below,
        ax,
        one,
        two,
        edge,
        *below_tables,
    )
    (out,) = call(
        functools.partial(second_top, comps, 4),
        "vvvvv",
        "h",
        [(cells, 128)],
        2_000_000,
        full,
        above,
        edge,
        *above_tables,
        scratch=[pltpu.VMEM((cells, 128), f32), pltpu.SemaphoreType.DMA((4,))],
    )
    return out.reshape(shape), bad[0, 0]


def extended(x, sides, width, wrap):
    for axis, dim in sides:
        size, length = (lax.axis_size(axis), x.shape[dim])
        up = [(i, (i + 1) % size) for i in range(size if wrap else size - 1)]
        down = [(j, i) for i, j in up]
        last = lax.slice_in_dim(x, length - width, length, axis=dim)
        first = lax.slice_in_dim(x, 0, width, axis=dim)
        before = lax.ppermute(last, axis, up)
        after = lax.ppermute(first, axis, down)
        x = jnp.concatenate([before, x, after], axis=dim)
    return x


def source_term(state, growth_rate, transfer_rate, nucleation):
    extra = (1,) * (state.ndim - 2)
    growth = growth_rate.reshape((1, -1) + extra)
    transfer = transfer_rate.reshape((1, -1) + extra)
    third = state[3]
    sigma = supersat_scale / (1.0 + crowding * jnp.sum(third * third, axis=0))
    lower = jnp.concatenate([jnp.zeros_like(state[0:1]), state[:3]], axis=0)
    factors = jnp.array([0.0, 1.0, 2.0, 3.0], dtype=state.dtype).reshape((4, 1) + extra)
    outflow = transfer * state
    inflow = jnp.concatenate([jnp.zeros_like(outflow[:, 0:1]), outflow[:, :-1]], axis=1)
    first = (jnp.arange(state.shape[1]) == 0).astype(state.dtype).reshape((1, -1) + extra)
    nucleus = jnp.array(nucleus_moments, dtype=state.dtype).reshape((4, 1) + extra)
    birth = nucleus * first * (nucleation * sigma * sigma)[None, None]
    return sigma[None, None] * (factors * growth * lower + inflow - outflow) + birth


def source_adjoint(state, adjoint, growth_rate, transfer_rate, nucleation):
    _, pull = jax.vjp(
        lambda field: source_term(field, growth_rate, transfer_rate, nucleation), state
    )
    return pull(adjoint)[0]


def cut_region(field, direction, offset):
    lead = [slice(None)] * (field.ndim - 3)
    spatial = []
    for which in range(3):
        moved = offset if which == direction else 0
        length = field.shape[field.ndim - 3 + which]
        spatial.append(slice(1 + moved, length - 1 + moved))
    return field[tuple(lead + spatial)]


def transport_adjoint(adjoint_pad, coeff_pad):
    total = None
    for direction in range(3):
        centre = cut_region(adjoint_pad, direction, 0)
        higher = cut_region(adjoint_pad, direction, 1)
        lowerv = cut_region(adjoint_pad, direction, -1)
        p_high = cut_region(coeff_pad[direction], direction, 1)
        q_here = cut_region(coeff_pad[3 + direction], direction, 0)
        term = p_high * (higher - centre) + q_here * (lowerv - centre)
        total = term if total is None else total + term
    return total


def face_coefficients(speeds, flags):
    upwind = flags.astype(speeds.dtype)
    return jnp.concatenate([speeds * upwind, speeds * (1.0 - upwind)], axis=0)


def nucleation_field(zones, nucleation_rate):
    labels = jnp.arange(nucleation_rate.shape[0], dtype=jnp.int32).reshape((-1, 1, 1, 1))
    match = (zones[None] == labels).astype(nucleation_rate.dtype)
    return jnp.sum(match * nucleation_rate.reshape((-1, 1, 1, 1)), axis=0)


def whole_step(
    adjoint_final,
    state_start,
    state_middle,
    speeds,
    flags,
    zones,
    growth_rate,
    transfer_rate,
    nucleation_rate,
):
    coeffs = face_coefficients(speeds, flags)
    nucleation = nucleation_field(zones, nucleation_rate)
    start = state_start.astype(jnp.float32)
    middle = state_middle.astype(jnp.float32)
    dims = adjoint_final.shape
    comps = dims[0] * dims[1]
    packed = jnp.concatenate([adjoint_final.reshape((comps,) + dims[2:]), coeffs], axis=0)
    packed = extended(packed, (("azim", 1),), 1, True)
    packed = extended(packed, (("rad", 3), ("axial", 2)), 1, False)
    later_pad = packed[:comps].reshape(dims[:2] + packed.shape[1:])
    coeff_pad = packed[comps:]
    adjoint_middle = 0.5 * adjoint_final + 0.5 * (
        transport_adjoint(later_pad, coeff_pad)
        + source_adjoint(middle, adjoint_final, growth_rate, transfer_rate, nucleation)
    )
    flat = adjoint_middle.reshape((comps,) + dims[2:])
    flat = extended(flat, (("azim", 1),), 1, True)
    flat = extended(flat, (("rad", 3), ("axial", 2)), 1, False)
    middle_pad = flat.reshape(dims[:2] + flat.shape[1:])
    return (
        0.5 * adjoint_final
        + adjoint_middle
        + transport_adjoint(middle_pad, coeff_pad)
        + source_adjoint(start, adjoint_middle, growth_rate, transfer_rate, nucleation)
    )


def shards(*arguments):
    out, bad = packed_step(*arguments)
    return lax.cond(bad > 0.0, lambda _: whole_step(*arguments), lambda quick: quick, out)


def solution(mesh):
    field = P(None, None, "azim", "axial", "rad")
    faces_spec = P(None, "azim", "axial", "rad")
    return jax.shard_map(
        shards,
        mesh=mesh,
        in_specs=(field, field, field, faces_spec, faces_spec, P("azim", "axial", "rad"), P(), P(), P()),
        out_specs=field,
        check_vma=False,
    )
```

time: 42.8 us -> 52.1 us (1.22)
  Pallas kernels: 8.2 us -> 17.2 us
  waiting for transfers between devices: 14.3 us -> 10.2 us
  between operations: 0.18 us -> 2.69 us
  starting transfers between devices: 16.2 us -> 18.5 us
  local copies, waits for them, and re-layouts: 1.8 us -> 0.93 us
    pallas_call x7 -> x8, Pallas kernels: 8.2 us -> 17.2 us  [call(): pl.pallas_call(body, in_specs=[SPACES[s] for s in ins], out_specs=[SPACES...]
    ppermute x10 -> x12, waiting for transfers between devices: 14.3 us -> 10.2 us  [the longest x3 7.69 us: swap_axial(): return lax.ppermute(x, 'axial', [(0, 1), (1, 0)])]
    ppermute x10 -> x12, starting transfers between devices: 16.2 us -> 18.5 us  [the longest x5 11.1 us: shift(): return lax.ppermute(x, axis, [(i, (i + step) % size) for i in range(size)])]
    add x1 -> x5, other arithmetic: 1.85 us -> 0.02 us  [the longest x2 0.01 us: told(): return message_ + lax.pad(count, 0.0, ((0, 0, 0), (cells + 128, 0, 0)))]
    reduce_sum x0 -> x2, other arithmetic: none -> 1.2 us  [crowded(): taken = jnp.sum((p[:4] != 0.0).astype(f32))]
    reshape x1 -> x0, local copies, waits for them, and re-layouts: 1.13 us -> none  [shards(): above = shift(dn, 'azim', -1, True).reshape(half + 4, 128)]
    mul x0 -> x1, other arithmetic: none -> 0.8 us  [packed_step(): lower = speeds[0] * flags[0].astype(f32)]
  transfers between devices with their start and end apart: 10 -> 12, of which waited for: 4 -> 4; matrix products, arithmetic and copies ran while one was open for 3% -> 1% of each run, Pallas kernels for 17% -> 25%
where the time goes in v4:
time: 52.1 us; the launch traced here: 51.8 us
  starting transfers between devices  18.5 us (36%)
  Pallas kernels  17.2 us (33%)
  waiting for transfers between devices  10.2 us (20%)
  between operations  2.69 us (5%)
  other arithmetic  2.1 us (4%)
  local copies, waits for them, and re-layouts  0.93 us (2%)
    pallas_call x8, Pallas kernels, call(): pl.pallas_call(body, in_specs=[SPACES[s] for s in ins], out_specs=[SPACES...  17.2 us
    ppermute x5, starting transfers between devices, shift(): return lax.ppermute(x, axis, [(i, (i + step) % size) for i in range(size)])  11.1 us
    ppermute x3, waiting for transfers between devices, swap_axial(): return lax.ppermute(x, 'axial', [(0, 1), (1, 0)])  7.69 us
    ppermute x3, starting transfers between devices, swap_axial(): return lax.ppermute(x, 'axial', [(0, 1), (1, 0)])  4.7 us
    ppermute x4, starting transfers between devices, swap_radial(): return lax.ppermute(x, 'rad', pairs + [(j, i) for i, j in pairs])  2.7 us
    ppermute x5, waiting for transfers between devices, shift(): return lax.ppermute(x, axis, [(i, (i + step) % size) for i in range(size)])  2.46 us
    reduce_sum x2, other arithmetic, crowded(): taken = jnp.sum((p[:4] != 0.0).astype(f32))  1.2 us
  transfers between devices with their start and end apart: 12, of which 4 were waited for; matrix products, arithmetic and copies ran while one was open for 1% of the time, Pallas kernels for 25%

profile of v4, /device:TPU:0, one launch (start us, length us, event | category | flops | bytes accessed | tf_op | source)
XLA Modules:
  0.0 51.8 jit_solution(15323904482248603850)
XLA Ops:
  0.0 0.0 copy-start.42
  0.0 0.0 copy-start.33
  0.0 0.0 copy-start.43
  0.0 0.8 %convert_multiply_fusion = f32[1,2,4,128]{3,2,1,0:T(4,128)S(1)} fusion(s32[3,2,4,128]{3,2,1,0:T(4,128)} %param.19, f32[3,2,4,128]{3,2,1,0:T(4,128)} %param.18), kind=kLoop, calls=%fused_computation.97 | loop fusion | flops 2048 | bytes 12288 | tf_op jit(solution)/shard_map/mul | solution.py:436
  0.8 5.1 %collective-permute-start.12 = (f32[8,128]{1,0:T(8,128)S(1)}, f32[8,128]{1,0:T(8,128)S(1)}, u32[]{:S(2)}, u32[]{:S(2)}) collective-permute-start(f32[8,128]{1,0:T(8,128)S(1)} %bitcast.76), channel_id=1, source_target_pairs={{0,24},{8,0},{16,8},{24,16},{1,25},{9,1},{17,9},{25,17},{2,26},{10... | collective-permute-start | bytes 12296 | tf_op jit(solution)/shard_map/ppermute | solution.py:406
  5.9 0.6 %convert_reduce_fusion.1 = f32[]{:T(128)} fusion(f32[1,2,4,128]{3,2,1,0:T(4,128)S(1)} %convert_multiply_fusion), kind=kLoop, calls=%fused_computation.102 | loop fusion | flops 1535 | bytes 2052 | tf_op jit(solution)/shard_map/reduce_sum | solution.py:440
  6.5 0.1 pad_add_fusion.2.where_ref
  7.7 1.9 %shard_map.132 = (f32[488,128]{1,0:T(8,128)S(1)}, f32[392,128]{1,0:T(8,128)S(1)}, bf16[256,512]{1,0:T(8,128)(2,1)S(1)}, bf16[256,512]{1,0:T(8,128)(2,1)S(1)}) custom-call(s32[3]{0:T(128)S(1)} %pad_add_fusion.2.where_ref, f32[1536,128]{1,0:T(8,128)} %bitcast.36, f32[3,8,128]{2,1,0:T(8,128)} %bitcast.56, s32[3,8,128]{2,1,0:T(8,128)} %bitcast.62), custom_call_target="tpu_custom_call" | custom-call | flops 2000000 | bytes 200000 | tf_op jit(solution)/shard_map/pallas_call | solution.py:393
  9.6 0.0 collective-permute-done.12.upper_ref
  9.6 0.6 %convert_reduce_fusion = f32[]{:T(128)} fusion(f32[8,128]{1,0:T(8,128)S(1)} %collective-permute-done.12.upper_ref), kind=kLoop, calls=%fused_computation.100 | loop fusion | flops 1535 | bytes 2052 | tf_op jit(solution)/shard_map/reduce_sum | solution.py:440
  11.5 1.8 %collective-permute-start.13 = (f32[488,128]{1,0:T(8,128)S(1)}, f32[488,128]{1,0:T(8,128)S(1)}, u32[]{:S(2)}, u32[]{:S(2)}) collective-permute-start(f32[488,128]{1,0:T(8,128)S(1)} %broadcast_dynamic-update-slice_fusion), channel_id=1, source_target_pairs={{0,24},{8,0},{16,8},{24,16},{1,25},{9,1},{17,9},{25,17},{2,26},{10... | collective-permute-start | bytes 749576 | tf_op jit(solution)/shard_map/ppermute | solution.py:406
  13.3 2.4 %shard_map.133 = (f32[488,128]{1,0:T(8,128)S(1)}, f32[1,1792]{1,0:T(1,128)S(1)}, f32[1,1792]{1,0:T(1,128)S(1)}, bf16[256,512]{1,0:T(8,128)(2,1)S(1)}, bf16[256,512]{1,0:T(8,128)(2,1)S(1)}) custom-call(s32[3]{0:T(128)S(1)} %pad_add_fusion.2.where_ref, f32[1536,128]{1,0:T(8,128)} %bitcast.37, f32[8,128]{1,0:T(8,128)S(1)} %collective-permute-done.12.upper_ref, ...), custom_call_target="tpu_custom_call" | custom-call | flops 3000000 | bytes 300000 | tf_op jit(solution)/shard_map/pallas_call | solution.py:393
  15.7 0.4 collective-permute-start.17
  16.1 1.5 %collective-permute-start.14 = (f32[392,128]{1,0:T(8,128)S(1)}, f32[392,128]{1,0:T(8,128)S(1)}, u32[]{:S(2)}, u32[]{:S(2)}) collective-permute-start(f32[392,128]{1,0:T(8,128)S(1)} %get-tuple-element.73), channel_id=1, source_target_pairs={{0,1},{1,0},{2,3},{3,2},{4,5},{5,4},{6,7},{7,6},{8,9},{9,8},{10,11... | collective-permute-start | bytes 602120 | tf_op jit(solution)/shard_map/ppermute | solution.py:410
  17.6 0.0 collective-permute-start.15
  17.6 1.6 %collective-permute-start.16 = (f32[1,1792]{1,0:T(1,128)S(1)}, f32[1,1792]{1,0:T(1,128)S(1)}, u32[]{:S(2)}, u32[]{:S(2)}) collective-permute-start(f32[1,1792]{1,0:T(1,128)S(1)} %get-tuple-element.75), channel_id=1, source_target_pairs={{2,4},{6,0},{4,2},{0,6},{3,5},{7,1},{5,3},{1,7},{10,12},{14,8},{12... | collective-permute-start | bytes 21512 | tf_op jit(solution)/shard_map/ppermute | solution.py:416
  19.2 0.0 copy-done.18
  19.2 0.0 copy-done.19
  19.2 0.0 copy-done
  19.2 0.0 copy-done.26
  19.2 0.0 copy-done.1
  19.2 0.0 copy-done.42
  19.3 1.4 %shard_map.131.part_ref = f32[1536,128]{1,0:T(8,128)S(1)} custom-call(f32[1536,128]{1,0:T(8,128)S(1)} %bitcast.38, bf16[192,8,128]{2,1,0:T(8,128)(2,1)S(1)} %bitcast.51, f32[3,8,128]{2,1,0:T(8,128)S(1)} %bitcast.58, s32[3,8,128]{2,1,0:T(8,128)S(1)} %bitcast.64, s32[8,128]{1,0:T(8,128)S(1)} %bitcast.68, f32[48]{0:T(128)S(1)} %copy-done.42, f32[48]{0:T(128)S(1)} %copy-done.33, ...), custom_call_target="tpu_custom_call" | custom-call | flops 8000000 | bytes 800000 | tf_op jit(solution)/shard_map/pallas_call | solution.py:393
  20.7 0.0 collective-permute-done.15.one_ref
  20.7 0.0 collective-permute-done.16.two_ref
  20.7 1.3 %collective-permute-done.14.ax_ref = f32[392,128]{1,0:T(8,128)S(1)} collective-permute-done((f32[392,128]{1,0:T(8,128)S(1)}, f32[392,128]{1,0:T(8,128)S(1)}, u32[]{:S(2)}, u32[]{:S(2)}) %collective-permute-start.14) | collective-permute-done | bytes 200736 | tf_op jit(solution)/shard_map/ppermute | solution.py:410
  22.0 2.4 %collective-permute-done.13.above_ref = f32[488,128]{1,0:T(8,128)S(1)} collective-permute-done((f32[488,128]{1,0:T(8,128)S(1)}, f32[488,128]{1,0:T(8,128)S(1)}, u32[]{:S(2)}, u32[]{:S(2)}) %collective-permute-start.13) | collective-permute-done | bytes 249888 | tf_op jit(solution)/shard_map/ppermute | solution.py:406
  24.4 3.6 %shard_map.134 = (f32[1536,128]{1,0:T(8,128)S(1)}, f32[4,8,128]{2,1,0:T(8,128)S(1)}, f32[480,128]{1,0:T(8,128)S(1)}, bf16[256,512]{1,0:T(8,128)(2,1)S(1)}, bf16[256,512]{1,0:T(8,128)(2,1)S(1)}) custom-call(s32[3]{0:T(128)S(1)} %pad_add_fusion.2.where_ref, f32[1536,128]{1,0:T(8,128)S(1)} %shard_map.131.part_ref, f32[1536,128]{1,0:T(8,128)S(1)} %bitcast.39, ...), custom_call_target="tpu_custom_call" | custom-call | flops 4000000 | bytes 400000 | tf_op jit(solution)/shard_map/pallas_call | solution.py:393
  28.0 0.0 collective-permute-done.17.below_ref
  28.0 2.4 %shard_map.135 = (f32[1536,128]{1,0:T(8,128)S(1)}, f32[480,128]{1,0:T(8,128)S(1)}, f32[384,128]{1,0:T(8,128)S(1)}, f32[1,1792]{1,0:T(1,128)S(1)}, f32[1,1792]{1,...) custom-call(s32[3]{0:T(128)S(1)} %pad_add_fusion.2.where_ref, ...), custom_call_target="tpu_custom_call" | custom-call | flops 4000000 | bytes 400000 | tf_op jit(solution)/shard_map/pallas_call | solution.py:393
  30.4 1.6 %collective-permute-start.18 = (f32[8,128]{1,0:T(8,128)S(1)}, f32[8,128]{1,0:T(8,128)S(1)}, u32[]{:S(2)}, u32[]{:S(2)}) collective-permute-start(f32[8,128]{1,0:T(8,128)S(1)} %get-tuple-element.83), channel_id=1, source_target_pairs={{0,1},{1,0},{2,3},{3,2},{4,5},{5,4},{6,7},{7,6},{8,9},{9,8},{10,11... | collective-permute-start | bytes 12296 | tf_op jit(solution)/shard_map/ppermute | solution.py:410
  32.0 2.0 %collective-permute-done.18 = f32[8,128]{1,0:T(8,128)S(1)} collective-permute-done((f32[8,128]{1,0:T(8,128)S(1)}, f32[8,128]{1,0:T(8,128)S(1)}, u32[]{:S(2)}, u32[]{:S(2)}) %collective-permute-start.18) | collective-permute-done | bytes 4128 | tf_op jit(solution)/shard_map/ppermute | solution.py:410
  34.1 0.1 collective-permute-start.19
  34.2 0.1 collective-permute-start.21
  34.2 3.8 %collective-permute-start.23 = (f32[480,128]{1,0:T(8,128)S(1)}, f32[480,128]{1,0:T(8,128)S(1)}, u32[]{:S(2)}, u32[]{:S(2)}) collective-permute-start(f32[480,128]{1,0:T(8,128)S(1)} %get-tuple-element.91), channel_id=1, source_target_pairs={{0,24},{8,0},{16,8},{24,16},{1,25},{9,1},{17,9},{25,17},{2,26},{10... | collective-permute-start | bytes 737288 | tf_op jit(solution)/shard_map/ppermute | solution.py:406
  38.0 0.0 collective-permute-done.19.one_ref
  38.0 1.0 %collective-permute-start.20 = (f32[1,1792]{1,0:T(1,128)S(1)}, f32[1,1792]{1,0:T(1,128)S(1)}, u32[]{:S(2)}, u32[]{:S(2)}) collective-permute-start(f32[1,1792]{1,0:T(1,128)S(1)} %pad_add_fusion), channel_id=1, source_target_pairs={{2,4},{6,0},{4,2},{0,6},{3,5},{7,1},{5,3},{1,7},{10,12},{14,8},{12... | collective-permute-start | bytes 21512 | tf_op jit(solution)/shard_map/ppermute | solution.py:416
  39.1 1.6 %collective-permute-start.22 = (f32[384,128]{1,0:T(8,128)S(1)}, f32[384,128]{1,0:T(8,128)S(1)}, u32[]{:S(2)}, u32[]{:S(2)}) collective-permute-start(f32[384,128]{1,0:T(8,128)S(1)} %get-tuple-element.88), channel_id=1, source_target_pairs={{0,1},{1,0},{2,3},{3,2},{4,5},{5,4},{6,7},{7,6},{8,9},{9,8},{10,11... | collective-permute-start | bytes 589832 | tf_op jit(solution)/shard_map/ppermute | solution.py:410
  40.7 1.4 %shard_map.136.part_ref = f32[1536,128]{1,0:T(8,128)S(1)} custom-call(f32[1536,128]{1,0:T(8,128)S(1)} %get-tuple-element.86.m_ref, f32[1536,128]{1,0:T(8,128)S(1)} %bitcast.40, bf16[192,8,128]{2,1,0:T(8,128)(2,1)S(1)} %bitcast.52, f32[4,8,128]{2,1,0:T(8,128)S(1)} %get-tuple-element.80.edge_ref, f32[3,8,128]{2,1,0:T(8,128)S(1)} %bitcast.61, ...), custom_call_target="tpu_custom_call" | custom-call | flops 8000000 | bytes 800000 | tf_op jit(solution)/shard_map/pallas_call | solution.py:393
  42.1 0.0 collective-permute-done.20.two_ref
  42.1 4.4 %collective-permute-done.22.ax_ref = f32[384,128]{1,0:T(8,128)S(1)} collective-permute-done((f32[384,128]{1,0:T(8,128)S(1)}, f32[384,128]{1,0:T(8,128)S(1)}, u32[]{:S(2)}, u32[]{:S(2)}) %collective-permute-start.22) | collective-permute-done | bytes 196640 | tf_op jit(solution)/shard_map/ppermute | solution.py:410
  46.5 0.0 collective-permute-done.21.below_ref
  46.5 2.5 %shard_map.137.full_ref = f32[1536,128]{1,0:T(8,128)S(1)} custom-call(s32[3]{0:T(128)S(1)} %pad_add_fusion.2.where_ref, f32[1536,128]{1,0:T(8,128)S(1)} %shard_map.136.part_ref, f32[480,128]{1,0:T(8,128)S(1)} %collective-permute-done.21.below_ref, f32[384,128]{1,0:T(8,128)S(1)} %collective-permute-done.22.ax_ref, ...), custom_call_target="tpu_custom_call" | custom-call | flops 4000000 | bytes 400000 | tf_op jit(solution)/shard_map/pallas_call | solution.py:393
  49.1 0.0 collective-permute-done.23.above_ref
  49.1 1.6 %shard_map.138 = f32[1536,128]{1,0:T(8,128)S(1)} custom-call(f32[1536,128]{1,0:T(8,128)S(1)} %shard_map.137.full_ref, f32[480,128]{1,0:T(8,128)S(1)} %collective-permute-done.23.above_ref, f32[4,8,128]{2,1,0:T(8,128)S(1)} %get-tuple-element.80.edge_ref, bf16[256,512]{1,0:T(8,128)(2,1)S(1)} %get-tuple-element.92.low_ref, ...), custom_call_target="tpu_custom_call" | custom-call | flops 2000000 | bytes 200000 | tf_op jit(solution)/shard_map/pallas_call | solution.py:393
  50.7 0.2 conditional.1
  51.0 0.0 copy-start.16
  51.0 0.9 %copy-done.16 = f32[4,48,2,4,128]{4,3,2,1,0:T(4,128)} copy-done((f32[4,48,2,4,128]{4,3,2,1,0:T(4,128)}, f32[4,48,2,4,128]{4,3,2,1,0:T(4,128)S(1)}, u32[]{:S(2)}) %copy-start.16) | copy-done | bytes 786456
  (18 shorter events, 0.1 us)
Async XLA Ops:
  0.0 19.2 %copy-start.18 = (f32[3,2,4,128]{3,2,1,0:T(4,128)S(1)}, f32[3,2,4,128]{3,2,1,0:T(4,128)}, u32[]{:S(2)}) copy-start(f32[3,2,4,128]{3,2,1,0:T(4,128)} %param.18) | copy-start | bytes 36868
  0.0 19.2 %copy-start.19 = (s32[3,2,4,128]{3,2,1,0:T(4,128)S(1)}, s32[3,2,4,128]{3,2,1,0:T(4,128)}, u32[]{:S(2)}) copy-start(s32[3,2,4,128]{3,2,1,0:T(4,128)} %param.19) | copy-start | bytes 36868
  0.0 19.2 %copy-start = (f32[4,48,2,4,128]{4,3,2,1,0:T(4,128)S(1)}, f32[4,48,2,4,128]{4,3,2,1,0:T(4,128)}, u32[]{:S(2)}) copy-start(f32[4,48,2,4,128]{4,3,2,1,0:T(4,128)} %param.15) | copy-start | bytes 2359300
  0.0 19.2 %copy-start.26 = (s32[2,4,128]{2,1,0:T(4,128)S(1)}, s32[2,4,128]{2,1,0:T(4,128)}, u32[]{:S(2)}) copy-start(s32[2,4,128]{2,1,0:T(4,128)} %param.20) | copy-start | bytes 12292
  0.0 19.2 %copy-start.1 = (bf16[4,48,2,4,128]{4,3,2,1,0:T(4,128)(2,1)S(1)}, bf16[4,48,2,4,128]{4,3,2,1,0:T(4,128)(2,1)}, u32[]{:S(2)}) copy-start(bf16[4,48,2,4,128]{4,3,2,1,0:T(4,128)(2,1)} %param.17) | copy-start | bytes 1179652
  0.0 19.2 %copy-start.42 = (f32[48]{0:T(128)S(1)}, f32[48]{0:T(128)}, u32[]{:S(2)}) copy-start(f32[48]{0:T(128)} %growth_ref.3) | copy-start | bytes 580
  0.0 19.2 %copy-start.33 = (f32[48]{0:T(128)S(1)}, f32[48]{0:T(128)}, u32[]{:S(2)}) copy-start(f32[48]{0:T(128)} %transfer_ref.3) | copy-start | bytes 580
  0.0 19.2 %copy-start.43 = (f32[4]{0:T(128)S(1)}, f32[4]{0:T(128)}, u32[]{:S(2)}) copy-start(f32[4]{0:T(128)} %rate_ref.3) | copy-start | bytes 52
  0.8 8.7 %collective-permute-start.12 = (f32[8,128]{1,0:T(8,128)S(1)}, f32[8,128]{1,0:T(8,128)S(1)}, u32[]{:S(2)}, u32[]{:S(2)}) collective-permute-start(f32[8,128]{1,0:T(8,128)S(1)} %bitcast.76), channel_id=1, source_target_pairs={{0,24},{8,0},{16,8},{24,16},{1,25},{9,1},{17,9},{25,17},{2,26},{10... | collective-permute-start | bytes 12296 | tf_op jit(solution)/shard_map/ppermute | solution.py:406
  11.5 12.9 %collective-permute-start.13 = (f32[488,128]{1,0:T(8,128)S(1)}, f32[488,128]{1,0:T(8,128)S(1)}, u32[]{:S(2)}, u32[]{:S(2)}) collective-permute-start(f32[488,128]{1,0:T(8,128)S(1)} %broadcast_dynamic-update-slice_fusion), channel_id=1, source_target_pairs={{0,24},{8,0},{16,8},{24,16},{1,25},{9,1},{17,9},{25,17},{2,26},{10... | collective-permute-start | bytes 749576 | tf_op jit(solution)/shard_map/ppermute | solution.py:406
  15.7 12.3 %collective-permute-start.17 = (f32[488,128]{1,0:T(8,128)S(1)}, f32[488,128]{1,0:T(8,128)S(1)}, u32[]{:S(2)}, u32[]{:S(2)}) collective-permute-start(f32[488,128]{1,0:T(8,128)S(1)} %get-tuple-element.79), channel_id=1, source_target_pairs={{0,8},{8,16},{16,24},{24,0},{1,9},{9,17},{17,25},{25,1},{2,10},{10... | collective-permute-start | bytes 749576 | tf_op jit(solution)/shard_map/ppermute | solution.py:406
  16.1 5.9 %collective-permute-start.14 = (f32[392,128]{1,0:T(8,128)S(1)}, f32[392,128]{1,0:T(8,128)S(1)}, u32[]{:S(2)}, u32[]{:S(2)}) collective-permute-start(f32[392,128]{1,0:T(8,128)S(1)} %get-tuple-element.73), channel_id=1, source_target_pairs={{0,1},{1,0},{2,3},{3,2},{4,5},{5,4},{6,7},{7,6},{8,9},{9,8},{10,11... | collective-permute-start | bytes 602120 | tf_op jit(solution)/shard_map/ppermute | solution.py:410
  17.6 3.0 %collective-permute-start.15 = (f32[1,1792]{1,0:T(1,128)S(1)}, f32[1,1792]{1,0:T(1,128)S(1)}, u32[]{:S(2)}, u32[]{:S(2)}) collective-permute-start(f32[1,1792]{1,0:T(1,128)S(1)} %get-tuple-element.74), channel_id=1, source_target_pairs={{0,2},{4,6},{2,0},{6,4},{1,3},{5,7},{3,1},{7,5},{8,10},{12,14},{10... | collective-permute-start | bytes 21512 | tf_op jit(solution)/shard_map/ppermute | solution.py:416
  17.6 3.1 %collective-permute-start.16 = (f32[1,1792]{1,0:T(1,128)S(1)}, f32[1,1792]{1,0:T(1,128)S(1)}, u32[]{:S(2)}, u32[]{:S(2)}) collective-permute-start(f32[1,1792]{1,0:T(1,128)S(1)} %get-tuple-element.75), channel_id=1, source_target_pairs={{2,4},{6,0},{4,2},{0,6},{3,5},{7,1},{5,3},{1,7},{10,12},{14,8},{12... | collective-permute-start | bytes 21512 | tf_op jit(solution)/shard_map/ppermute | solution.py:416
  24.4 16.3 %copy-start.2 = (bf16[4,48,2,4,128]{4,3,2,1,0:T(4,128)(2,1)S(1)}, bf16[4,48,2,4,128]{4,3,2,1,0:T(4,128)(2,1)}, u32[]{:S(2)}) copy-start(bf16[4,48,2,4,128]{4,3,2,1,0:T(4,128)(2,1)} %param.16) | copy-start | bytes 1179652
  30.4 3.6 %collective-permute-start.18 = (f32[8,128]{1,0:T(8,128)S(1)}, f32[8,128]{1,0:T(8,128)S(1)}, u32[]{:S(2)}, u32[]{:S(2)}) collective-permute-start(f32[8,128]{1,0:T(8,128)S(1)} %get-tuple-element.83), channel_id=1, source_target_pairs={{0,1},{1,0},{2,3},{3,2},{4,5},{5,4},{6,7},{7,6},{8,9},{9,8},{10,11... | collective-permute-start | bytes 12296 | tf_op jit(solution)/shard_map/ppermute | solution.py:410
  34.1 4.0 %collective-permute-start.19 = (f32[1,1792]{1,0:T(1,128)S(1)}, f32[1,1792]{1,0:T(1,128)S(1)}, u32[]{:S(2)}, u32[]{:S(2)}) collective-permute-start(f32[1,1792]{1,0:T(1,128)S(1)} %pad_add_fusion.1), channel_id=1, source_target_pairs={{0,2},{4,6},{2,0},{6,4},{1,3},{5,7},{3,1},{7,5},{8,10},{12,14},{10... | collective-permute-start | bytes 21512 | tf_op jit(solution)/shard_map/ppermute | solution.py:416
  34.2 12.4 %collective-permute-start.21 = (f32[480,128]{1,0:T(8,128)S(1)}, f32[480,128]{1,0:T(8,128)S(1)}, u32[]{:S(2)}, u32[]{:S(2)}) collective-permute-start(f32[480,128]{1,0:T(8,128)S(1)} %get-tuple-element.87), channel_id=1, source_target_pairs={{0,8},{8,16},{16,24},{24,0},{1,9},{9,17},{17,25},{25,1},{2,10},{10... | collective-permute-start | bytes 737288 | tf_op jit(solution)/shard_map/ppermute | solution.py:406
  34.2 14.9 %collective-permute-start.23 = (f32[480,128]{1,0:T(8,128)S(1)}, f32[480,128]{1,0:T(8,128)S(1)}, u32[]{:S(2)}, u32[]{:S(2)}) collective-permute-start(f32[480,128]{1,0:T(8,128)S(1)} %get-tuple-element.91), channel_id=1, source_target_pairs={{0,24},{8,0},{16,8},{24,16},{1,25},{9,1},{17,9},{25,17},{2,26},{10... | collective-permute-start | bytes 737288 | tf_op jit(solution)/shard_map/ppermute | solution.py:406
  38.0 4.0 %collective-permute-start.20 = (f32[1,1792]{1,0:T(1,128)S(1)}, f32[1,1792]{1,0:T(1,128)S(1)}, u32[]{:S(2)}, u32[]{:S(2)}) collective-permute-start(f32[1,1792]{1,0:T(1,128)S(1)} %pad_add_fusion), channel_id=1, source_target_pairs={{2,4},{6,0},{4,2},{0,6},{3,5},{7,1},{5,3},{1,7},{10,12},{14,8},{12... | collective-permute-start | bytes 21512 | tf_op jit(solution)/shard_map/ppermute | solution.py:416
  39.1 7.4 %collective-permute-start.22 = (f32[384,128]{1,0:T(8,128)S(1)}, f32[384,128]{1,0:T(8,128)S(1)}, u32[]{:S(2)}, u32[]{:S(2)}) collective-permute-start(f32[384,128]{1,0:T(8,128)S(1)} %get-tuple-element.88), channel_id=1, source_target_pairs={{0,1},{1,0},{2,3},{3,2},{4,5},{5,4},{6,7},{7,6},{8,9},{9,8},{10,11... | collective-permute-start | bytes 589832 | tf_op jit(solution)/shard_map/ppermute | solution.py:410
  51.0 0.9 %copy-start.16 = (f32[4,48,2,4,128]{4,3,2,1,0:T(4,128)}, f32[4,48,2,4,128]{4,3,2,1,0:T(4,128)S(1)}, u32[]{:S(2)}) copy-start(f32[4,48,2,4,128]{4,3,2,1,0:T(4,128)S(1)} %get-tuple-element.202) | copy-start | bytes 2359300

commit v5 on v4

--- a/solution.py
+++ b/solution.py
@@ -65,10 +65,9 @@
     )
 
 
-def make_tables(p, where_zero, low_ref, high_ref):
+def make_tables(p, low_ref, high_ref):
     row, lane = rows_of(), lanes_of()
-    taken = (p == 0.0) if where_zero else (p != 0.0)
-    one = jnp.where(taken & (row < 4), 1.0, 0.0)
+    one = jnp.where((p != 0.0) & (row < 4), 1.0, 0.0)
     before = lax.broadcasted_iota(jnp.int32, (128, 128), 0) < lax.broadcasted_iota(jnp.int32, (128, 128), 1)
     inside = jnp.dot(one.astype(bf16), jnp.where(before, 1.0, 0.0).astype(bf16), preferred_element_type=f32)
     total = jnp.sum(one, axis=1, keepdims=True)
@@ -86,6 +85,11 @@
         want = jnp.broadcast_to(slot[z : z + 1], (128, 128))
         for ref, start, names in ((low_ref, 0, here), (low_ref, 128, here + 128), (high_ref, 0, first), (high_ref, 128, second)):
             ref[start : start + 128, cells] = jnp.where(names == want, 1.0, 0.0).astype(bf16)
+    return jnp.sum(total, axis=0, keepdims=True)
+
+
+def crowded(count):
+    return jnp.where(jnp.broadcast_to(count, (8, 128)) > slots, 1.0, 0.0)
 
 
 def pieces(x):
@@ -144,21 +148,21 @@
         out_ref[spots] = out_ref[spots] + coefficient[first_row + z : first_row + z + 1] * halo[:, 128 * z : 128 * z + 128]
 
 
-def pack_axial(comps, x_ref, where_ref, ax_ref):
-    @pl.when(where_ref[0] == 0)
+def pack_axial(comps, x_ref, axial_ref, ax_ref):
+    @pl.when(axial_ref[0] == 0)
     def _():
         ax_ref[0 : 2 * comps] = x_ref[pl.ds(3, 2 * comps, stride=4)]
 
-    @pl.when(where_ref[0] != 0)
+    @pl.when(axial_ref[0] != 0)
     def _():
         ax_ref[0 : 2 * comps] = x_ref[pl.ds(0, 2 * comps, stride=4)]
 
 
-def add_axial(comps, scale, where_ref, axial, ax_ref, out_ref):
+def add_axial(comps, scale, axial_ref, axial, ax_ref, out_ref):
     several = jnp.concatenate([scale * axial] * (2 * comps // 8), axis=0)
     for start, index in ((3, 0), (0, 1)):
 
-        @pl.when(where_ref[0] == index)
+        @pl.when(axial_ref[0] == index)
         def _():
             spots = pl.ds(start, 2 * comps, stride=4)
             out_ref[spots] = out_ref[spots] + several * ax_ref[0 : 2 * comps]
@@ -170,8 +174,8 @@
     return lax.dot_general(take, x, (((1,), (1,)), ((), ())), precision=exact, preferred_element_type=f32)
 
 
-def pack_radial(comps, x_ref, p, where_ref, one_ref, two_ref):
-    even = where_ref[1] % 2 == 0
+def pack_radial(comps, x_ref, p, rad_ref, one_ref, two_ref):
+    even = rad_ref[0] % 2 == 0
     used = 8 * comps
     ends = columns(x_ref[...])
     for ref, last in ((one_ref, even), (two_ref, jnp.logical_not(even))):
@@ -181,12 +185,12 @@
             ref[:, used : used + 8] = columns(p)[1:2]
 
 
-def radial_halo(comps, where_ref, one_ref, two_ref):
+def radial_halo(comps, rad_ref, one_ref, two_ref):
     n = 8 * comps + 128
-    even = where_ref[1] % 2 == 0
+    even = rad_ref[0] % 2 == 0
     one, two = one_ref[:, 0:n], two_ref[:, 0:n]
-    lower = jnp.where(where_ref[1] > 0, jnp.where(even, two, one), 0.0)
-    upper = jnp.where(where_ref[1] < where_ref[2] - 1, jnp.where(even, one, two), 0.0)
+    lower = jnp.where(rad_ref[0] > 0, jnp.where(even, two, one), 0.0)
+    upper = jnp.where(rad_ref[0] < 3, jnp.where(even, one, two), 0.0)
     row, lane = rows_of(), lanes_of()
     which = lax.broadcasted_iota(jnp.int32, (8, n), 0)
     both = jnp.where(which == 0, lower, jnp.where(which == 1, upper, 0.0))
@@ -236,21 +240,17 @@
             finish(c, x[k][0], term)
 
 
-def first_down(comps, where_ref, a_ref, speeds_ref, flags_ref, dn_ref, ax_ref, low_ref, high_ref):
+def first_down(
+    comps, axial_ref, rad_ref, a_ref, speeds_ref, flags_ref, dn_ref, ax_ref, one_ref, two_ref, bad_ref, low_ref, high_ref
+):
     p, _ = faces(speeds_ref, flags_ref)
-    make_tables(p[0], False, low_ref, high_ref)
+    count = make_tables(p[0], low_ref, high_ref)
+    bad_ref[...] = crowded(count)
     encode(comps, a_ref, 0, low_ref, high_ref, dn_ref)
-    dn_ref[5 * comps // 2 :] = jnp.zeros((8, 128), f32)
-    pack_axial(comps, a_ref, where_ref, ax_ref)
+    dn_ref[5 * comps // 2 :] = p[0]
+    pack_axial(comps, a_ref, axial_ref, ax_ref)
     ax_ref[2 * comps : 2 * comps + 8] = pair_rows(p[1], 0, 4)
-
-
-def first_up(comps, where_ref, a_ref, upper_ref, bad_ref, speeds_ref, flags_ref, up_ref, one_ref, two_ref, low_ref, high_ref):
-    p, _ = faces(speeds_ref, flags_ref)
-    make_tables(upper_ref[...], True, low_ref, high_ref)
-    encode(comps, a_ref, 4, low_ref, high_ref, up_ref)
-    up_ref[5 * comps // 2 :] = bad_ref[...]
-    pack_radial(comps, a_ref, p[2], where_ref, one_ref, two_ref)
+    pack_radial(comps, a_ref, p[2], rad_ref, one_ref, two_ref)
 
 
 def first_local(sections, a_ref, u_ref, speeds_ref, flags_ref, zones_ref, growth_ref, transfer_ref, rate_ref, out_ref):
@@ -263,76 +263,101 @@
 
 
 def second_local(
-    sections, m_ref, a_ref, u_ref, edge_ref, speeds_ref, flags_ref, zones_ref, growth_ref, transfer_ref, rate_ref, out_ref
+    sections,
+    m_ref,
+    a_ref,
+    u_ref,
+    above_ref,
+    edge_ref,
+    low_ref,
+    high_ref,
+    bad_ref,
+    axial_bad_ref,
+    speeds_ref,
+    flags_ref,
+    zones_ref,
+    growth_ref,
+    transfer_ref,
+    rate_ref,
+    out_ref,
+    worse_ref,
 ):
     local = Local(*faces(speeds_ref, flags_ref))
     local.centre = local.centre + (edge_ref[3] - 1.0)
+    worse_ref[...] = (bad_ref[...] + axial_bad_ref[...])[0:1]
 
     def finish(c, x, term):
         out_ref[8 * c : 8 * c + 8] = 0.5 * a_ref[8 * c : 8 * c + 8] + (local(x) + term)
 
     source(sections, m_ref, u_ref, growth_ref, transfer_ref, zones_ref, rate_ref, finish)
-
-
-def first_top(
+    add_azimuthal(4 * sections, decode(4 * sections, above_ref, low_ref, high_ref), edge_ref[0], 4, out_ref)
+
+
+def from_below(c, below_ref):
+    pair = below_ref[8 * (c // 2) : 8 * (c // 2) + 8]
+    return pair if c % 2 == 0 else pltpu.roll(pair, 4, 0)
+
+
+def first_bottom(
     comps,
-    where_ref,
+    axial_ref,
+    rad_ref,
     part_ref,
     a_ref,
-    above_ref,
+    below_ref,
     ax_ref,
     one_ref,
     two_ref,
-    upper_ref,
+    bad_ref,
     speeds_ref,
     flags_ref,
-    up_low_ref,
-    up_high_ref,
+    low_ref,
+    high_ref,
     m_ref,
     edge_ref,
-    up_ref,
-    low_ref,
-    high_ref,
+    dn_ref,
+    worse_ref,
 ):
     _, q = faces(speeds_ref, flags_ref)
     row, lane = rows_of(), lanes_of()
-    top = row >= 4
-    make_tables(upper_ref[...], False, low_ref, high_ref)
-    hrad = radial_halo(comps, where_ref, one_ref, two_ref)
-    lower_half = where_ref[0] == 0
-    p_azim = jnp.where(top, pltpu.roll(upper_ref[...], 4, 0), 0.0)
+    hrad = radial_halo(comps, rad_ref, one_ref, two_ref)
+    lower_half = axial_ref[0] == 0
     pairs = jnp.where(lower_half, ax_ref[2 * comps : 2 * comps + 8], 0.0)
     p_axial = jnp.where(row == 3, pairs[0:1], jnp.where(row == 7, pairs[1:2], 0.0))
     p_rad = jnp.where(lane == 127, hrad[8 * comps : 8 * comps + 8], 0.0)
     axial = jnp.where(lower_half, pairs, pair_rows(q[1], 0, 4))
     rad = jnp.where(lane == 0, q[2], p_rad)
-    centre = p_azim + p_axial + p_rad
-    edge_ref[0] = jnp.where(top, p_azim, q[0])
+    centre = p_axial + p_rad
+    azim = jnp.where(row >= 4, 0.0, q[0])
+    edge_ref[0] = azim
     edge_ref[1] = axial
     edge_ref[2] = rad
     edge_ref[3] = centre
     for c in range(comps):
         spots = slice(8 * c, 8 * c + 8)
-        m_ref[spots] = part_ref[spots] + 0.5 * (rad * hrad[spots] - centre * a_ref[spots])
-    add_axial(comps, 0.5, where_ref, axial, ax_ref, m_ref)
-    add_azimuthal(comps, decode(comps, above_ref, low_ref, high_ref), 0.5 * p_azim, 4, m_ref)
-    encode(comps, m_ref, 4, up_low_ref, up_high_ref, up_ref)
-
-
-def first_bottom(
+        m_ref[spots] = part_ref[spots] + 0.5 * (
+            azim * from_below(c, below_ref) + rad * hrad[spots] - centre * a_ref[spots]
+        )
+    add_axial(comps, 0.5, axial_ref, axial, ax_ref, m_ref)
+    encode(comps, m_ref, 0, low_ref, high_ref, dn_ref)
+    below_p = jnp.where((row < 4) & (below_ref[4 * comps :] != 0.0), 1.0, 0.0)
+    count = jnp.sum(jnp.sum(below_p, axis=1, keepdims=True), axis=0, keepdims=True)
+    worse_ref[...] = bad_ref[...] + crowded(count)
+
+
+def first_top(
     comps,
-    where_ref,
+    axial_ref,
+    rad_ref,
     part_ref,
-    below_ref,
+    a_ref,
     above_ref,
+    edge_ref,
     bad_ref,
-    edge_ref,
-    speeds_ref,
-    flags_ref,
-    dn_low_ref,
-    dn_high_ref,
+    far_ref,
     m_ref,
-    dn_ref,
+    edges_ref,
+    up_ref,
     ax_ref,
     one_ref,
     two_ref,
@@ -340,42 +365,68 @@
     low_ref,
     high_ref,
 ):
-    p, _ = faces(speeds_ref, flags_ref)
-    make_tables(p[0], True, low_ref, high_ref)
-    m_ref[...] = part_ref[...]
-    add_azimuthal(comps, decode(comps, below_ref, low_ref, high_ref), 0.5 * edge_ref[0], 0, m_ref)
-    encode(comps, m_ref, 0, dn_low_ref, dn_high_ref, dn_ref)
-    pack_axial(comps, m_ref, where_ref, ax_ref)
-    pack_radial(comps, m_ref, None, where_ref, one_ref, two_ref)
-    worse_ref[...] = bad_ref[...] + below_ref[5 * comps // 2 :] + above_ref[5 * comps // 2 :]
-
-
-def second_bottom(
-    comps, where_ref, part_ref, below_ref, ax_ref, one_ref, two_ref, edge_ref, low_ref, high_ref, full_ref
+    upper = above_ref[5 * comps // 2 :]
+    count = make_tables(upper, low_ref, high_ref)
+    worse_ref[...] = bad_ref[...] + far_ref[...] + crowded(count)
+    azim = jnp.where(rows_of() >= 4, pltpu.roll(upper, 4, 0), 0.0)
+    edges_ref[0] = edge_ref[0] + azim
+    edges_ref[1] = edge_ref[1]
+    edges_ref[2] = edge_ref[2]
+    edges_ref[3] = edge_ref[3] + azim
+    half_azim = 0.5 * azim
+    for c in range(comps):
+        spots = slice(8 * c, 8 * c + 8)
+        m_ref[spots] = part_ref[spots] - half_azim * a_ref[spots]
+    add_azimuthal(comps, decode(comps, above_ref, low_ref, high_ref), half_azim, 4, m_ref)
+    for c in range(comps):
+        up_ref[4 * c : 4 * c + 4] = m_ref[8 * c + 4 : 8 * c + 8]
+    pack_axial(comps, m_ref, axial_ref, ax_ref)
+    pack_radial(comps, m_ref, None, rad_ref, one_ref, two_ref)
+
+
+def second_top(
+    comps,
+    axial_ref,
+    rad_ref,
+    part_ref,
+    ax_ref,
+    one_ref,
+    two_ref,
+    edge_ref,
+    bad_ref,
+    far_ref,
+    out_ref,
+    bottom_ref,
+    worse_ref,
+    full_ref,
+    high_half_ref,
+    sems,
 ):
-    hrad = radial_halo(comps, where_ref, one_ref, two_ref)
+    hrad = radial_halo(comps, rad_ref, one_ref, two_ref)
     rad = edge_ref[2]
     for c in range(comps):
         spots = slice(8 * c, 8 * c + 8)
         full_ref[spots] = part_ref[spots] + rad * hrad[spots]
-    add_axial(comps, 1.0, where_ref, edge_ref[1], ax_ref, full_ref)
-    add_azimuthal(comps, decode(comps, below_ref, low_ref, high_ref), edge_ref[0], 0, full_ref)
-
-
-def second_top(comps, parts, full_ref, above_ref, edge_ref, low_ref, high_ref, out_ref, done_ref, sems):
-    halo = decode(comps, above_ref, low_ref, high_ref)
-    edge = edge_ref[0]
+    add_axial(comps, 1.0, axial_ref, edge_ref[1], ax_ref, full_ref)
+    for c in range(comps):
+        high_half_ref[c] = full_ref[8 * c + 4 : 8 * c + 8]
+    copy = pltpu.make_async_copy(high_half_ref, out_ref.at[:, 1], sems.at[0])
+    copy.start()
+    for c in range(comps):
+        bottom_ref[c] = full_ref[8 * c : 8 * c + 4]
+    ends = slice(8 * comps + 128, 8 * comps + 256)
+    worse_ref[...] = bad_ref[...] + far_ref[...] + (one_ref[:, ends] + two_ref[:, ends])
+    copy.wait()
+
+
+def second_bottom(comps, parts, _, bottom_ref, below_ref, edge_ref, out_ref, low_half_ref, sems):
+    azim = edge_ref[0][0:4]
     size = comps // parts
     made = []
     for i in range(parts):
-        spots = pl.ds(8 * size * i, 8 * size)
-        done_ref[spots] = full_ref[spots]
-        for z in range(4):
-            some = pl.ds(8 * size * i + 4 + z, size, stride=8)
-            done_ref[some] = (
-                done_ref[some] + edge[4 + z : 5 + z] * halo[size * i : size * i + size, 128 * z : 128 * z + 128]
-            )
-        made.append(pltpu.make_async_copy(done_ref.at[spots], out_ref.at[spots], sems.at[i]))
+        spots = pl.ds(i * size, size)
+        low_half_ref[spots] = bottom_ref[spots] + azim[None] * below_ref[spots]
+        made.append(pltpu.make_async_copy(low_half_ref.at[spots], out_ref.at[spots, 0], sems.at[i]))
         made[-1].start()
     for copy in made:
         copy.wait()
@@ -388,7 +439,7 @@
 }
 
 
-def call(body, ins, outs, shapes, cost, *operands, scratch=()):
+def call(body, ins, outs, shapes, *operands, scratch=(), aliases={}):
     shapes = [shape if isinstance(shape, jax.ShapeDtypeStruct) else jax.ShapeDtypeStruct(shape, f32) for shape in shapes]
     return pl.pallas_call(
         body,
@@ -396,7 +447,8 @@
         out_specs=[SPACES[s] for s in outs],
         out_shape=shapes,
         scratch_shapes=scratch,
-        cost_estimate=pl.CostEstimate(flops=cost, bytes_accessed=cost // 10, transcendentals=0),
+        input_output_aliases=aliases,
+        cost_estimate=pl.CostEstimate(flops=4000000, bytes_accessed=400000, transcendentals=0),
         compiler_params=pltpu.CompilerParams(vmem_limit_bytes=32 * 1024 * 1024),
     )(*operands)
 
@@ -425,154 +477,143 @@
     assert moments == 4 and shape[2:] == (2, 4, 128) and comps % 32 == 0
     assert lax.axis_size("axial") == 2 and lax.axis_size("rad") == 4
     cells = 8 * comps
-    rows, message = cells // 4, 5 * comps // 2 + 8
+    half, rows, message = cells // 2, cells // 4, 5 * comps // 2 + 8
     a = adjoint_final.reshape(cells, 128)
-    speeds = speeds.reshape(3, 8, 128)
-    flags = flags.reshape(3, 8, 128)
-    where = jnp.stack([lax.axis_index("axial"), lax.axis_index("rad"), lax.axis_size("rad")]).astype(jnp.int32)
+    speeds_, speeds = speeds, speeds.reshape(3, 8, 128)
+    flags_, flags = flags, flags.reshape(3, 8, 128)
+    place = (lax.axis_index("axial").reshape(1), lax.axis_index("rad").reshape(1))
     rates = (zones.reshape(8, 128), growth_rate, transfer_rate, nucleation_rate)
     tables = [jax.ShapeDtypeStruct((256, 512), bf16)] * 2
 
-    lower = speeds[0] * flags[0].astype(f32)
-    upper = shift(lower, "azim", -1)
-
-    def crowded(p):
-        taken = jnp.sum((p[:4] != 0.0).astype(f32))
-        return jnp.maximum(taken - slots, 512.0 - slots - taken) > 0.0
-
-    dn, ax, *dn_tables = call(
+    keep = ((0, 2, 0), (-1, 0, 0), (0, 0, 0), (0, 0, 0))
+    after = ((comps, 1, 0), (0, -1, 0), (0, 0, 0), (0, 0, 0))
+    up = lax.pad(adjoint_final.reshape(comps, 2, 4, 128), 0.0, keep)
+    up = up + lax.pad(speeds_[:1], 0.0, after) * lax.pad(flags_[:1], 0, after).astype(f32)
+    below = shift(up.reshape(half + 8, 128), "azim", 1)
+    dn, ax, one, two, bad, *dn_tables = call(
         functools.partial(first_down, comps),
-        "svvv",
-        "vvvv",
-        [(message, 128), (rows + 8, 128)] + tables,
-        2_000_000,
-        where,
+        "ssvvv",
+        "v" * 7,
+        [(message, 128), (rows + 8, 128), (1, cells + 256), (1, cells + 256), (8, 128)] + tables,
+        *place,
         a,
         speeds,
         flags,
     )
-    bad = (crowded(lower) | crowded(upper)).astype(f32)
+    above = shift(dn, "azim", -1)
+    far = shift(bad, "azim", 2)
     if lax.axis_size("azim") > 4:
-        bad = lax.pmax(bad, "azim")
-    bad = jnp.broadcast_to(bad, (8, 128))
-    dn = lax.dynamic_update_slice(dn, bad, (message - 8, 0))
-    above = shift(dn, "azim", -1)
-    up, one, two, *up_tables = call(
-        functools.partial(first_up, comps),
-        "s" + "v" * 5,
-        "vvvvv",
-        [(message, 128), (1, cells + 256), (1, cells + 256)] + tables,
-        3_000_000,
-        where,
-        a,
-        upper,
-        bad,
-        speeds,
-        flags,
-    )
+        far = lax.pmax(far, "azim")
     ax = swap_axial(ax)
-    below = shift(up, "azim", 1)
     one, two = swap_radial(one, 0), swap_radial(two, 1)
     (part,) = call(
         functools.partial(first_local, sections),
         "vvvvvsss",
         "v",
         [(cells, 128)],
-        8_000_000,
         a,
         state_middle.reshape(comps, 8, 128),
         speeds,
         flags,
         *rates,
     )
-    part, edge, up, *above_tables = call(
+    part, edge, dn, bad = call(
+        functools.partial(first_bottom, comps),
+        "ss" + "v" * 11,
+        "vvvv",
+        [(cells, 128), (4, 8, 128), (message - 8, 128), (8, 128)],
+        *place,
+        part,
+        a,
+        below,
+        ax,
+        one,
+        two,
+        bad,
+        speeds,
+        flags,
+        *dn_tables,
+    )
+    next_above = shift(dn, "azim", -1)
+    m, edge, up, ax, one, two, bad, *tables = call(
         functools.partial(first_top, comps),
-        "s" + "v" * 11,
-        "vvvvv",
-        [(cells, 128), (4, 8, 128), (message - 8, 128)] + tables,
-        4_000_000,
-        where,
+        "ss" + "v" * 6,
+        "v" * 9,
+        [
+            (cells, 128),
+            (4, 8, 128),
+            (half, 128),
+            (rows, 128),
+            (1, cells + 256),
+            (1, cells + 256),
+            (8, 128),
+        ]
+        + tables,
+        *place,
         part,
         a,
         above,
-        ax,
-        one,
-        two,
-        upper,
-        speeds,
-        flags,
-        *up_tables,
-    )
-    next_below = shift(up, "azim", 1)
-    m, dn, ax, one, two, bad, *below_tables = call(
-        functools.partial(first_bottom, comps),
-        "s" + "v" * 9,
-        "v" * 8,
-        [(cells, 128), (message - 8, 128), (rows, 128), (1, cells + 256), (1, cells + 256), (8, 128)] + tables,
-        4_000_000,
-        where,
-        part,
-        below,
-        above,
+        edge,
         bad,
-        edge,
-        speeds,
-        flags,
-        *dn_tables,
-    )
-    above = shift(dn, "azim", -1)
-
-    def told(message_, count):
-        return message_ + lax.pad(count, 0.0, ((0, 0, 0), (cells + 128, 0, 0)))
-
-    bad = (bad + swap_axial(bad))[:1]
+        far,
+    )
+    below = shift(up, "azim", 1).reshape(comps, 4, 128)
     ax = swap_axial(ax)
-    one = swap_radial(told(one, bad), 0)
-    bad = bad + one[:, cells + 128 :]
-    two = swap_radial(told(two, bad), 1)
-    bad = bad + two[:, cells + 128 :]
-    (part,) = call(
+    part, bad = call(
         functools.partial(second_local, sections),
-        "vvvvvvvsss",
-        "v",
-        [(cells, 128)],
-        8_000_000,
+        "v" * 12 + "sss",
+        "vv",
+        [(cells, 128), (1, 128)],
         m,
         a,
         state_start.reshape(comps, 8, 128),
+        next_above,
         edge,
+        *tables,
+        bad,
+        swap_axial(bad),
         speeds,
         flags,
         *rates,
     )
-    (full,) = call(
-        functools.partial(second_bottom, comps),
-        "s" + "v" * 8,
-        "v",
-        [(cells, 128)],
-        4_000_000,
-        where,
+
+    def told(columns_):
+        return columns_ + lax.pad(bad, 0.0, ((0, 0, 0), (cells + 128, 0, 0)))
+
+    one, two = swap_radial(told(one), 0), swap_radial(told(two), 1)
+    far = shift(bad, "rad", 2)
+    out, bottom, bad = call(
+        functools.partial(second_top, comps),
+        "ss" + "v" * 7,
+        "hvv",
+        [(comps, 2, 4, 128), (comps, 4, 128), (1, 128)],
+        *place,
         part,
-        next_below,
         ax,
         one,
         two,
         edge,
-        *below_tables,
-    )
-    (out,) = call(
-        functools.partial(second_top, comps, 4),
-        "vvvvv",
-        "h",
-        [(cells, 128)],
-        2_000_000,
-        full,
-        above,
-        edge,
-        *above_tables,
-        scratch=[pltpu.VMEM((cells, 128), f32), pltpu.SemaphoreType.DMA((4,))],
-    )
-    return out.reshape(shape), bad[0, 0]
+        bad,
+        far,
+        scratch=[pltpu.VMEM((cells, 128), f32), pltpu.VMEM((comps, 4, 128), f32), pltpu.SemaphoreType.DMA((1,))],
+    )
+
+    def finish():
+        (whole,) = call(
+            functools.partial(second_bottom, comps, 4),
+            "hvvv",
+            "h",
+            [(comps, 2, 4, 128)],
+            out,
+            bottom,
+            below,
+            edge,
+            scratch=[pltpu.VMEM((comps, 4, 128), f32), pltpu.SemaphoreType.DMA((4,))],
+            aliases={0: 0},
+        )
+        return whole.reshape(shape)
+
+    return finish, bad[0, 0]
 
 
 def extended(x, sides, width, wrap):
@@ -684,8 +725,8 @@
 
 
 def shards(*arguments):
-    out, bad = packed_step(*arguments)
-    return lax.cond(bad > 0.0, lambda _: whole_step(*arguments), lambda quick: quick, out)
+    finish, bad = packed_step(*arguments)
+    return lax.cond(bad > 0.0, lambda: whole_step(*arguments), finish)
 
 
 def solution(mesh):

time: 52.1 us -> 46.5 us (0.89)
  Pallas kernels: 17.2 us -> 10.3 us
  waiting for transfers between devices: 10.2 us -> 12.8 us
  between operations: 2.69 us -> 0.19 us
  local copies, waits for them, and re-layouts: 0.93 us -> 2.38 us
  other arithmetic: 2.1 us -> 1.03 us
  starting transfers between devices: 18.5 us -> 19.1 us
    ppermute x5 -> x6, waiting for transfers between devices: 2.46 us -> 11.2 us  [shift(): return lax.ppermute(x, axis, [(i, (i + step) % size) for i in range(size)])]
    pallas_call x8 -> x7, Pallas kernels: 17.2 us -> 10.3 us  [call(): pl.pallas_call(body, in_specs=[SPACES[s] for s in ins], out_specs=[SPACES...]
    ppermute x3, waiting for transfers between devices: 7.69 us -> 1.58 us  [swap_axial(): return lax.ppermute(x, 'axial', [(0, 1), (1, 0)])]
    slice x1 -> x2, local copies, waits for them, and re-layouts: 0.01 us -> 1.47 us  [the longest x1 0.78 us: packed_step(): speeds_[:1]]
    reduce_sum x2 -> x0, other arithmetic: 1.2 us -> none  [crowded(): taken = jnp.sum((p[:4] != 0.0).astype(f32))]
    ppermute x5 -> x6, starting transfers between devices: 11.1 us -> 12.2 us  [shift(): return lax.ppermute(x, axis, [(i, (i + step) % size) for i in range(size)])]
    ppermute x3, starting transfers between devices: 4.7 us -> 3.65 us  [swap_axial(): return lax.ppermute(x, 'axial', [(0, 1), (1, 0)])]
    add x5 -> x2, other arithmetic: 0.02 us -> 1.03 us  [the longest x1 1.02 us: packed_step(): up + lax.pad(speeds_[:1], 0.0, after) * lax.pad(flags_[:1], 0, after).ast...]
  transfers between devices with their start and end apart: 12 -> 13, of which waited for: 4 -> 4; matrix products, arithmetic and copies ran while one was open for 1% -> 0% of each run, Pallas kernels for 25% -> 22%
where the time goes in v5:
time: 46.5 us; the launch traced here: 46.1 us
  starting transfers between devices  19.1 us (41%)
  waiting for transfers between devices  12.8 us (28%)
  Pallas kernels  10.3 us (22%)
  local copies, waits for them, and re-layouts  2.38 us (5%)
  other arithmetic  1.03 us (2%)
    ppermute x6, starting transfers between devices, shift(): return lax.ppermute(x, axis, [(i, (i + step) % size) for i in range(size)])  12.2 us
    ppermute x6, waiting for transfers between devices, shift(): return lax.ppermute(x, axis, [(i, (i + step) % size) for i in range(size)])  11.2 us
    pallas_call x7, Pallas kernels, call(): pl.pallas_call(body, in_specs=[SPACES[s] for s in ins], out_specs=[SPACES...  10.3 us
    ppermute x3, starting transfers between devices, swap_axial(): return lax.ppermute(x, 'axial', [(0, 1), (1, 0)])  3.65 us
    ppermute x4, starting transfers between devices, swap_radial(): return lax.ppermute(x, 'rad', pairs + [(j, i) for i, j in pairs])  3.28 us
    ppermute x3, waiting for transfers between devices, swap_axial(): return lax.ppermute(x, 'axial', [(0, 1), (1, 0)])  1.58 us
    add x1, other arithmetic, packed_step(): up + lax.pad(speeds_[:1], 0.0, after) * lax.pad(flags_[:1], 0, after).ast...  1.02 us
  transfers between devices with their start and end apart: 13, of which 4 were waited for; matrix products, arithmetic and copies ran while one was open for 0% of the time, Pallas kernels for 22%

profile of v5, /device:TPU:0, one launch (start us, length us, event | category | flops | bytes accessed | tf_op | source)
XLA Modules:
  0.0 46.1 jit_solution(9199365490037512604)
XLA Ops:
  0.0 0.0 copy-start.42
  0.0 0.0 copy-start.33
  0.0 0.0 copy-start.43
  0.0 0.8 %slice.168 = f32[1,2,4,128]{3,2,1,0:T(4,128)S(1)} slice(f32[3,2,4,128]{3,2,1,0:T(4,128)} %param.18), slice={[0:1], [0:2], [0:4], [0:128]} | slice | bytes 8192 | tf_op jit(solution)/shard_map/slice | solution.py:491
  0.8 0.7 %slice.169 = s32[1,2,4,128]{3,2,1,0:T(4,128)S(1)} slice(s32[3,2,4,128]{3,2,1,0:T(4,128)} %param.19), slice={[0:1], [0:2], [0:4], [0:128]} | slice | bytes 8192 | tf_op jit(solution)/shard_map/slice | solution.py:491
  1.5 1.0 %fusion.30 = f32[194,1,4,128]{3,2,1,0:T(4,128)S(1)} fusion(f32[192,2,4,128]{3,2,1,0:T(4,128)} %bitcast.39, f32[1,2,4,128]{3,2,1,0:T(4,128)S(1)} %slice.168, s32[1,2,4,128]{3,2,1,0:T(4,128)S(1)} %slice.169), kind=kLoop, calls=%fused_computation.98 | loop fusion | flops 297984 | bytes 1191936 | tf_op jit(solution)/shard_map/add | solution.py:491
  2.5 3.1 %collective-permute-start.12 = (f32[776,128]{1,0:T(8,128)S(1)}, f32[776,128]{1,0:T(8,128)S(1)}, u32[]{:S(2)}, u32[]{:S(2)}) collective-permute-start(f32[776,128]{1,0:T(8,128)S(1)} %bitcast.60), channel_id=1, source_target_pairs={{0,8},{8,16},{16,24},{24,0},{1,9},{9,17},{17,25},{25,1},{2,10},{10... | collective-permute-start | bytes 1191944 | tf_op jit(solution)/shard_map/ppermute | solution.py:458
  5.6 0.0 copy-done
  5.6 2.2 %shard_map.132 = (f32[488,128]{1,0:T(8,128)S(1)}, f32[392,128]{1,0:T(8,128)S(1)}, f32[1,1792]{1,0:T(1,128)S(1)}, f32[1,1792]{1,0:T(1,128)S(1)}, f32[8,128]{1,0:T...) custom-call(s32[1]{0:T(128)} %bitcast.12.axial_ref, s32[1]{0:T(128)} %bitcast.13.rad_ref, ...), custom_call_target="tpu_custom_call" | custom-call | flops 4000000 | bytes 400000 | tf_op jit(solution)/shard_map/pallas_call | solution.py:444
  7.8 1.6 %collective-permute-start.13 = (f32[392,128]{1,0:T(8,128)S(1)}, f32[392,128]{1,0:T(8,128)S(1)}, u32[]{:S(2)}, u32[]{:S(2)}) collective-permute-start(f32[392,128]{1,0:T(8,128)S(1)} %get-tuple-element.85), channel_id=1, source_target_pairs={{0,1},{1,0},{2,3},{3,2},{4,5},{5,4},{6,7},{7,6},{8,9},{9,8},{10,11... | collective-permute-start | bytes 602120 | tf_op jit(solution)/shard_map/ppermute | solution.py:462
  9.4 2.2 %collective-permute-start.16 = (f32[488,128]{1,0:T(8,128)S(1)}, f32[488,128]{1,0:T(8,128)S(1)}, u32[]{:S(2)}, u32[]{:S(2)}) collective-permute-start(f32[488,128]{1,0:T(8,128)S(1)} %get-tuple-element.92), channel_id=1, source_target_pairs={{0,24},{8,0},{16,8},{24,16},{1,25},{9,1},{17,9},{25,17},{2,26},{10... | collective-permute-start | bytes 749576 | tf_op jit(solution)/shard_map/ppermute | solution.py:458
  11.7 0.0 collective-permute-start.14
  11.7 1.6 %collective-permute-start.15 = (f32[1,1792]{1,0:T(1,128)S(1)}, f32[1,1792]{1,0:T(1,128)S(1)}, u32[]{:S(2)}, u32[]{:S(2)}) collective-permute-start(f32[1,1792]{1,0:T(1,128)S(1)} %get-tuple-element.87), channel_id=1, source_target_pairs={{2,4},{6,0},{4,2},{0,6},{3,5},{7,1},{5,3},{1,7},{10,12},{14,8},{12... | collective-permute-start | bytes 21512 | tf_op jit(solution)/shard_map/ppermute | solution.py:468
  13.3 0.0 copy-done.18
  13.3 0.0 copy-done.19
  13.3 0.0 copy-done.26
  13.3 0.0 copy-done.1
  13.3 0.0 copy-done.42
  13.3 1.4 %shard_map.131.part_ref = f32[1536,128]{1,0:T(8,128)S(1)} custom-call(f32[1536,128]{1,0:T(8,128)S(1)} %bitcast.41, bf16[192,8,128]{2,1,0:T(8,128)(2,1)S(1)} %bitcast.55, f32[3,8,128]{2,1,0:T(8,128)S(1)} %bitcast.63, s32[3,8,128]{2,1,0:T(8,128)S(1)} %bitcast.67, s32[8,128]{1,0:T(8,128)S(1)} %bitcast.70, f32[48]{0:T(128)S(1)} %copy-done.42, f32[48]{0:T(128)S(1)} %copy-done.33, ...), custom_call_target="tpu_custom_call" | custom-call | flops 4000000 | bytes 400000 | tf_op jit(solution)/shard_map/pallas_call | solution.py:444
  14.7 0.0 collective-permute-done.14.one_ref
  14.7 0.0 collective-permute-done.15.two_ref
  14.7 0.0 collective-permute-done.13.ax_ref
  14.7 3.0 %collective-permute-done.12.below_ref = f32[776,128]{1,0:T(8,128)S(1)} collective-permute-done((f32[776,128]{1,0:T(8,128)S(1)}, f32[776,128]{1,0:T(8,128)S(1)}, u32[]{:S(2)}, u32[]{:S(2)}) %collective-permute-start.12) | collective-permute-done | bytes 397344 | tf_op jit(solution)/shard_map/ppermute | solution.py:458
  17.7 2.2 %shard_map.133 = (f32[1536,128]{1,0:T(8,128)S(1)}, f32[4,8,128]{2,1,0:T(8,128)S(1)}, f32[480,128]{1,0:T(8,128)S(1)}, f32[8,128]{1,0:T(8,128)S(1)}) custom-call(s32[1]{0:T(128)} %bitcast.12.axial_ref, s32[1]{0:T(128)} %bitcast.13.rad_ref, f32[1536,128]{1,0:T(8,128)S(1)} %shard_map.131.part_ref, f32[1536,128]{1,0:T(8,128)S(1)} %bitcast.42, ...), custom_call_target="tpu_custom_call" | custom-call | flops 4000000 | bytes 400000 | tf_op jit(solution)/shard_map/pallas_call | solution.py:444
  19.9 6.3 %collective-permute-start.18 = (f32[480,128]{1,0:T(8,128)S(1)}, f32[480,128]{1,0:T(8,128)S(1)}, u32[]{:S(2)}, u32[]{:S(2)}) collective-permute-start(f32[480,128]{1,0:T(8,128)S(1)} %get-tuple-element.96), channel_id=1, source_target_pairs={{0,24},{8,0},{16,8},{24,16},{1,25},{9,1},{17,9},{25,17},{2,26},{10... | collective-permute-start | bytes 737288 | tf_op jit(solution)/shard_map/ppermute | solution.py:458
  26.2 0.0 collective-permute-start.17
  26.2 5.2 %collective-permute-done.17.far_ref = f32[8,128]{1,0:T(8,128)S(1)} collective-permute-done((f32[8,128]{1,0:T(8,128)S(1)}, f32[8,128]{1,0:T(8,128)S(1)}, u32[]{:S(2)}, u32[]{:S(2)}) %collective-permute-start.17) | collective-permute-done | bytes 4128 | tf_op jit(solution)/shard_map/ppermute | solution.py:458
  31.5 0.0 collective-permute-done.16.above_ref
  31.5 1.6 %shard_map.134 = (f32[1536,128]{1,0:T(8,128)S(1)}, f32[4,8,128]{2,1,0:T(8,128)S(1)}, f32[768,128]{1,0:T(8,128)S(1)}, f32[384,128]{1,0:T(8,128)S(1)}, f32[1,1792]...) custom-call(s32[1]{0:T(128)} %bitcast.12.axial_ref, ...), custom_call_target="tpu_custom_call" | custom-call | flops 4000000 | bytes 400000 | tf_op jit(solution)/shard_map/pallas_call | solution.py:444
  33.0 1.6 %collective-permute-start.19 = (f32[8,128]{1,0:T(8,128)S(1)}, f32[8,128]{1,0:T(8,128)S(1)}, u32[]{:S(2)}, u32[]{:S(2)}) collective-permute-start(f32[8,128]{1,0:T(8,128)S(1)} %get-tuple-element.100.bad_ref), channel_id=1, source_target_pairs={{0,1},{1,0},{2,3},{3,2},{4,5},{5,4},{6,7},{7,6},{8,9},{9,8},{10,11... | collective-permute-start | bytes 12296 | tf_op jit(solution)/shard_map/ppermute | solution.py:462
  34.6 0.5 %collective-permute-start.20 = (f32[384,128]{1,0:T(8,128)S(1)}, f32[384,128]{1,0:T(8,128)S(1)}, u32[]{:S(2)}, u32[]{:S(2)}) collective-permute-start(f32[384,128]{1,0:T(8,128)S(1)} %get-tuple-element.102), channel_id=1, source_target_pairs={{0,1},{1,0},{2,3},{3,2},{4,5},{5,4},{6,7},{7,6},{8,9},{9,8},{10,11... | collective-permute-start | bytes 589832 | tf_op jit(solution)/shard_map/ppermute | solution.py:462
  35.1 0.0 collective-permute-start.24
  35.1 1.6 %collective-permute-done.19.axial_bad_ref = f32[8,128]{1,0:T(8,128)S(1)} collective-permute-done((f32[8,128]{1,0:T(8,128)S(1)}, f32[8,128]{1,0:T(8,128)S(1)}, u32[]{:S(2)}, u32[]{:S(2)}) %collective-permute-start.19) | collective-permute-done | bytes 4128 | tf_op jit(solution)/shard_map/ppermute | solution.py:462
  36.7 0.0 collective-permute-done.18.above_ref
  36.7 1.6 %shard_map.135 = (f32[1536,128]{1,0:T(8,128)S(1)}, f32[1,128]{1,0:T(1,128)S(1)}) custom-call(f32[1536,128]{1,0:T(8,128)S(1)} %get-tuple-element.95.m_ref, f32[1536,128]{1,0:T(8,128)S(1)} %bitcast.44, bf16[192,8,128]{2,1,0:T(8,128)(2,1)S(1)} %bitcast.56, f32[480,128]{1,0:T(8,128)S(1)} %collective-permute-done.18.above_ref, ...), custom_call_target="tpu_custom_call" | custom-call | flops 4000000 | bytes 400000 | tf_op jit(solution)/shard_map/pallas_call | solution.py:444
  38.3 0.1 collective-permute-start.21
  38.4 1.6 %collective-permute-start.22 = (f32[1,1792]{1,0:T(1,128)S(1)}, f32[1,1792]{1,0:T(1,128)S(1)}, u32[]{:S(2)}, u32[]{:S(2)}) collective-permute-start(f32[1,1792]{1,0:T(1,128)S(1)} %get-tuple-element.193), channel_id=1, source_target_pairs={{2,4},{6,0},{4,2},{0,6},{3,5},{7,1},{5,3},{1,7},{10,12},{14,8},{12... | collective-permute-start | bytes 21512 | tf_op jit(solution)/shard_map/ppermute | solution.py:468
  40.0 0.5 %collective-permute-start.23 = (f32[1,128]{1,0:T(1,128)S(1)}, f32[1,128]{1,0:T(1,128)S(1)}, u32[]{:S(2)}, u32[]{:S(2)}) collective-permute-start(f32[1,128]{1,0:T(1,128)S(1)} %get-tuple-element.104.bad_ref), channel_id=1, source_target_pairs={{0,4},{2,6},{4,0},{6,2},{1,5},{3,7},{5,1},{7,3},{8,12},{10,14},{12... | collective-permute-start | bytes 1544 | tf_op jit(solution)/shard_map/ppermute | solution.py:458
  40.5 0.0 collective-permute-done.20.ax_ref
  40.5 3.0 %collective-permute-done.23.far_ref = f32[1,128]{1,0:T(1,128)S(1)} collective-permute-done((f32[1,128]{1,0:T(1,128)S(1)}, f32[1,128]{1,0:T(1,128)S(1)}, u32[]{:S(2)}, u32[]{:S(2)}) %collective-permute-start.23) | collective-permute-done | bytes 544 | tf_op jit(solution)/shard_map/ppermute | solution.py:458
  43.5 0.0 collective-permute-done.21.one_ref
  43.5 0.0 collective-permute-done.22.two_ref
  43.5 1.1 %shard_map.136 = (f32[192,2,4,128]{3,2,1,0:T(4,128)S(1)}, f32[192,4,128]{2,1,0:T(4,128)S(1)}, f32[1,128]{1,0:T(1,128)S(1)}) custom-call(s32[1]{0:T(128)} %bitcast.12.axial_ref, s32[1]{0:T(128)} %bitcast.13.rad_ref, f32[1536,128]{1,0:T(8,128)S(1)} %get-tuple-element.101.part_ref, f32[384,128]{1,0:T(8,128)S(1)} %collective-permute-done.20.ax_ref, ...), custom_call_target="tpu_custom_call" | custom-call | flops 4000000 | bytes 400000 | tf_op jit(solution)/shard_map/pallas_call | solution.py:444
  44.7 0.0 collective-permute-done.24
  44.7 0.5 %conditional.1 = (f32[4,48,2,4,128]{4,3,2,1,0:T(4,128)S(1)}) conditional(s32[]{:T(128)} %bitcast.22, (f32[768,128]{1,0:T(8,128)S(1)}, f32[192,2,4,128]{3,2,1,0:T(4,128)S(1)}, f32[192,4,128]{2,1,0:T(4,128)S(1)}, f32[4,8,128]{2,1,0:T(8,128)S(1)}) %tuple.50, (f32[4,48,2,4,128]{4,3,2,1,0:T(4,128)S(1)}, s32[3,2,4,128]{3,2,1,0:T(4,128)S(1)}, ...), branch_computations={%region_0.0_spmd, %region_1.9_spmd} | conditional | flops 29856032 | bytes 121131808 | solution.py:729
  44.7 0.2 branch_0_fun.1
  45.2 0.0 copy-start.16
  45.2 0.9 %copy-done.16 = f32[4,48,2,4,128]{4,3,2,1,0:T(4,128)} copy-done((f32[4,48,2,4,128]{4,3,2,1,0:T(4,128)}, f32[4,48,2,4,128]{4,3,2,1,0:T(4,128)S(1)}, u32[]{:S(2)}) %copy-start.16) | copy-done | bytes 786456
  (11 shorter events, 0.0 us)
Async XLA Ops:
  0.0 13.3 %copy-start.18 = (f32[3,2,4,128]{3,2,1,0:T(4,128)S(1)}, f32[3,2,4,128]{3,2,1,0:T(4,128)}, u32[]{:S(2)}) copy-start(f32[3,2,4,128]{3,2,1,0:T(4,128)} %param.18) | copy-start | bytes 36868
  0.0 13.3 %copy-start.19 = (s32[3,2,4,128]{3,2,1,0:T(4,128)S(1)}, s32[3,2,4,128]{3,2,1,0:T(4,128)}, u32[]{:S(2)}) copy-start(s32[3,2,4,128]{3,2,1,0:T(4,128)} %param.19) | copy-start | bytes 36868
  0.0 5.6 %copy-start = (f32[4,48,2,4,128]{4,3,2,1,0:T(4,128)S(1)}, f32[4,48,2,4,128]{4,3,2,1,0:T(4,128)}, u32[]{:S(2)}) copy-start(f32[4,48,2,4,128]{4,3,2,1,0:T(4,128)} %param.15) | copy-start | bytes 2359300
  0.0 13.3 %copy-start.26 = (s32[2,4,128]{2,1,0:T(4,128)S(1)}, s32[2,4,128]{2,1,0:T(4,128)}, u32[]{:S(2)}) copy-start(s32[2,4,128]{2,1,0:T(4,128)} %param.20) | copy-start | bytes 12292
  0.0 13.3 %copy-start.1 = (bf16[4,48,2,4,128]{4,3,2,1,0:T(4,128)(2,1)S(1)}, bf16[4,48,2,4,128]{4,3,2,1,0:T(4,128)(2,1)}, u32[]{:S(2)}) copy-start(bf16[4,48,2,4,128]{4,3,2,1,0:T(4,128)(2,1)} %param.17) | copy-start | bytes 1179652
  0.0 13.3 %copy-start.42 = (f32[48]{0:T(128)S(1)}, f32[48]{0:T(128)}, u32[]{:S(2)}) copy-start(f32[48]{0:T(128)} %growth_ref.3) | copy-start | bytes 580
  0.0 13.3 %copy-start.33 = (f32[48]{0:T(128)S(1)}, f32[48]{0:T(128)}, u32[]{:S(2)}) copy-start(f32[48]{0:T(128)} %transfer_ref.3) | copy-start | bytes 580
  0.0 13.3 %copy-start.43 = (f32[4]{0:T(128)S(1)}, f32[4]{0:T(128)}, u32[]{:S(2)}) copy-start(f32[4]{0:T(128)} %rate_ref.3) | copy-start | bytes 52
  2.5 15.2 %collective-permute-start.12 = (f32[776,128]{1,0:T(8,128)S(1)}, f32[776,128]{1,0:T(8,128)S(1)}, u32[]{:S(2)}, u32[]{:S(2)}) collective-permute-start(f32[776,128]{1,0:T(8,128)S(1)} %bitcast.60), channel_id=1, source_target_pairs={{0,8},{8,16},{16,24},{24,0},{1,9},{9,17},{17,25},{25,1},{2,10},{10... | collective-permute-start | bytes 1191944 | tf_op jit(solution)/shard_map/ppermute | solution.py:458
  7.8 6.9 %collective-permute-start.13 = (f32[392,128]{1,0:T(8,128)S(1)}, f32[392,128]{1,0:T(8,128)S(1)}, u32[]{:S(2)}, u32[]{:S(2)}) collective-permute-start(f32[392,128]{1,0:T(8,128)S(1)} %get-tuple-element.85), channel_id=1, source_target_pairs={{0,1},{1,0},{2,3},{3,2},{4,5},{5,4},{6,7},{7,6},{8,9},{9,8},{10,11... | collective-permute-start | bytes 602120 | tf_op jit(solution)/shard_map/ppermute | solution.py:462
  9.4 22.1 %collective-permute-start.16 = (f32[488,128]{1,0:T(8,128)S(1)}, f32[488,128]{1,0:T(8,128)S(1)}, u32[]{:S(2)}, u32[]{:S(2)}) collective-permute-start(f32[488,128]{1,0:T(8,128)S(1)} %get-tuple-element.92), channel_id=1, source_target_pairs={{0,24},{8,0},{16,8},{24,16},{1,25},{9,1},{17,9},{25,17},{2,26},{10... | collective-permute-start | bytes 749576 | tf_op jit(solution)/shard_map/ppermute | solution.py:458
  11.7 3.0 %collective-permute-start.14 = (f32[1,1792]{1,0:T(1,128)S(1)}, f32[1,1792]{1,0:T(1,128)S(1)}, u32[]{:S(2)}, u32[]{:S(2)}) collective-permute-start(f32[1,1792]{1,0:T(1,128)S(1)} %get-tuple-element.86), channel_id=1, source_target_pairs={{0,2},{4,6},{2,0},{6,4},{1,3},{5,7},{3,1},{7,5},{8,10},{12,14},{10... | collective-permute-start | bytes 21512 | tf_op jit(solution)/shard_map/ppermute | solution.py:468
  11.7 3.1 %collective-permute-start.15 = (f32[1,1792]{1,0:T(1,128)S(1)}, f32[1,1792]{1,0:T(1,128)S(1)}, u32[]{:S(2)}, u32[]{:S(2)}) collective-permute-start(f32[1,1792]{1,0:T(1,128)S(1)} %get-tuple-element.87), channel_id=1, source_target_pairs={{2,4},{6,0},{4,2},{0,6},{3,5},{7,1},{5,3},{1,7},{10,12},{14,8},{12... | collective-permute-start | bytes 21512 | tf_op jit(solution)/shard_map/ppermute | solution.py:468
  17.7 18.9 %copy-start.2 = (bf16[4,48,2,4,128]{4,3,2,1,0:T(4,128)(2,1)S(1)}, bf16[4,48,2,4,128]{4,3,2,1,0:T(4,128)(2,1)}, u32[]{:S(2)}) copy-start(bf16[4,48,2,4,128]{4,3,2,1,0:T(4,128)(2,1)} %param.16) | copy-start | bytes 1179652
  19.9 16.8 %collective-permute-start.18 = (f32[480,128]{1,0:T(8,128)S(1)}, f32[480,128]{1,0:T(8,128)S(1)}, u32[]{:S(2)}, u32[]{:S(2)}) collective-permute-start(f32[480,128]{1,0:T(8,128)S(1)} %get-tuple-element.96), channel_id=1, source_target_pairs={{0,24},{8,0},{16,8},{24,16},{1,25},{9,1},{17,9},{25,17},{2,26},{10... | collective-permute-start | bytes 737288 | tf_op jit(solution)/shard_map/ppermute | solution.py:458
  26.2 5.2 %collective-permute-start.17 = (f32[8,128]{1,0:T(8,128)S(1)}, f32[8,128]{1,0:T(8,128)S(1)}, u32[]{:S(2)}, u32[]{:S(2)}) collective-permute-start(f32[8,128]{1,0:T(8,128)S(1)} %get-tuple-element.88.bad_ref), channel_id=1, source_target_pairs={{0,16},{8,24},{16,0},{24,8},{1,17},{9,25},{17,1},{25,9},{2,18},{10... | collective-permute-start | bytes 12296 | tf_op jit(solution)/shard_map/ppermute | solution.py:458
  33.0 3.6 %collective-permute-start.19 = (f32[8,128]{1,0:T(8,128)S(1)}, f32[8,128]{1,0:T(8,128)S(1)}, u32[]{:S(2)}, u32[]{:S(2)}) collective-permute-start(f32[8,128]{1,0:T(8,128)S(1)} %get-tuple-element.100.bad_ref), channel_id=1, source_target_pairs={{0,1},{1,0},{2,3},{3,2},{4,5},{5,4},{6,7},{7,6},{8,9},{9,8},{10,11... | collective-permute-start | bytes 12296 | tf_op jit(solution)/shard_map/ppermute | solution.py:462
  34.6 5.9 %collective-permute-start.20 = (f32[384,128]{1,0:T(8,128)S(1)}, f32[384,128]{1,0:T(8,128)S(1)}, u32[]{:S(2)}, u32[]{:S(2)}) collective-permute-start(f32[384,128]{1,0:T(8,128)S(1)} %get-tuple-element.102), channel_id=1, source_target_pairs={{0,1},{1,0},{2,3},{3,2},{4,5},{5,4},{6,7},{7,6},{8,9},{9,8},{10,11... | collective-permute-start | bytes 589832 | tf_op jit(solution)/shard_map/ppermute | solution.py:462
  35.1 9.6 %collective-permute-start.24 = (f32[768,128]{1,0:T(8,128)S(1)}, f32[768,128]{1,0:T(8,128)S(1)}, u32[]{:S(2)}, u32[]{:S(2)}) collective-permute-start(f32[768,128]{1,0:T(8,128)S(1)} %get-tuple-element.107), channel_id=1, source_target_pairs={{0,8},{8,16},{16,24},{24,0},{1,9},{9,17},{17,25},{25,1},{2,10},{10... | collective-permute-start | bytes 1179656 | tf_op jit(solution)/shard_map/ppermute | solution.py:458
  38.3 5.2 %collective-permute-start.21 = (f32[1,1792]{1,0:T(1,128)S(1)}, f32[1,1792]{1,0:T(1,128)S(1)}, u32[]{:S(2)}, u32[]{:S(2)}) collective-permute-start(f32[1,1792]{1,0:T(1,128)S(1)} %get-tuple-element.194), channel_id=1, source_target_pairs={{0,2},{4,6},{2,0},{6,4},{1,3},{5,7},{3,1},{7,5},{8,10},{12,14},{10... | collective-permute-start | bytes 21512 | tf_op jit(solution)/shard_map/ppermute | solution.py:468
  38.4 5.2 %collective-permute-start.22 = (f32[1,1792]{1,0:T(1,128)S(1)}, f32[1,1792]{1,0:T(1,128)S(1)}, u32[]{:S(2)}, u32[]{:S(2)}) collective-permute-start(f32[1,1792]{1,0:T(1,128)S(1)} %get-tuple-element.193), channel_id=1, source_target_pairs={{2,4},{6,0},{4,2},{0,6},{3,5},{7,1},{5,3},{1,7},{10,12},{14,8},{12... | collective-permute-start | bytes 21512 | tf_op jit(solution)/shard_map/ppermute | solution.py:468
  40.0 3.5 %collective-permute-start.23 = (f32[1,128]{1,0:T(1,128)S(1)}, f32[1,128]{1,0:T(1,128)S(1)}, u32[]{:S(2)}, u32[]{:S(2)}) collective-permute-start(f32[1,128]{1,0:T(1,128)S(1)} %get-tuple-element.104.bad_ref), channel_id=1, source_target_pairs={{0,4},{2,6},{4,0},{6,2},{1,5},{3,7},{5,1},{7,3},{8,12},{10,14},{12... | collective-permute-start | bytes 1544 | tf_op jit(solution)/shard_map/ppermute | solution.py:458
  45.2 0.9 %copy-start.16 = (f32[4,48,2,4,128]{4,3,2,1,0:T(4,128)}, f32[4,48,2,4,128]{4,3,2,1,0:T(4,128)S(1)}, u32[]{:S(2)}) copy-start(f32[4,48,2,4,128]{4,3,2,1,0:T(4,128)S(1)} %get-tuple-element.227) | copy-start | bytes 2359300

commit v6 on v5

--- a/solution.py
+++ b/solution.py
@@ -85,10 +85,11 @@
         want = jnp.broadcast_to(slot[z : z + 1], (128, 128))
         for ref, start, names in ((low_ref, 0, here), (low_ref, 128, here + 128), (high_ref, 0, first), (high_ref, 128, second)):
             ref[start : start + 128, cells] = jnp.where(names == want, 1.0, 0.0).astype(bf16)
-    return jnp.sum(total, axis=0, keepdims=True)
-
-
-def crowded(count):
+
+
+def crowded(p):
+    taken = jnp.where((rows_of() < 4) & (p != 0.0), 1.0, 0.0)
+    count = jnp.sum(jnp.sum(taken, axis=1, keepdims=True), axis=0, keepdims=True)
     return jnp.where(jnp.broadcast_to(count, (8, 128)) > slots, 1.0, 0.0)
 
 
@@ -244,10 +245,11 @@
     comps, axial_ref, rad_ref, a_ref, speeds_ref, flags_ref, dn_ref, ax_ref, one_ref, two_ref, bad_ref, low_ref, high_ref
 ):
     p, _ = faces(speeds_ref, flags_ref)
-    count = make_tables(p[0], low_ref, high_ref)
-    bad_ref[...] = crowded(count)
+    make_tables(p[0], low_ref, high_ref)
+    bad_ref[...] = crowded(p[0])
     encode(comps, a_ref, 0, low_ref, high_ref, dn_ref)
-    dn_ref[5 * comps // 2 :] = p[0]
+    dn_ref[5 * comps // 2 : 5 * comps // 2 + 8] = p[0]
+    dn_ref[5 * comps // 2 + 8 :] = jnp.zeros((8, 128), f32)
     pack_axial(comps, a_ref, axial_ref, ax_ref)
     ax_ref[2 * comps : 2 * comps + 8] = pair_rows(p[1], 0, 4)
     pack_radial(comps, a_ref, p[2], rad_ref, one_ref, two_ref)
@@ -340,9 +342,7 @@
         )
     add_axial(comps, 0.5, axial_ref, axial, ax_ref, m_ref)
     encode(comps, m_ref, 0, low_ref, high_ref, dn_ref)
-    below_p = jnp.where((row < 4) & (below_ref[4 * comps :] != 0.0), 1.0, 0.0)
-    count = jnp.sum(jnp.sum(below_p, axis=1, keepdims=True), axis=0, keepdims=True)
-    worse_ref[...] = bad_ref[...] + crowded(count)
+    worse_ref[...] = bad_ref[...] + crowded(below_ref[4 * comps :])
 
 
 def first_top(
@@ -354,7 +354,6 @@
     above_ref,
     edge_ref,
     bad_ref,
-    far_ref,
     m_ref,
     edges_ref,
     up_ref,
@@ -365,9 +364,9 @@
     low_ref,
     high_ref,
 ):
-    upper = above_ref[5 * comps // 2 :]
-    count = make_tables(upper, low_ref, high_ref)
-    worse_ref[...] = bad_ref[...] + far_ref[...] + crowded(count)
+    upper = above_ref[5 * comps // 2 : 5 * comps // 2 + 8]
+    make_tables(upper, low_ref, high_ref)
+    worse_ref[...] = bad_ref[...] + crowded(upper) + crowded(above_ref[5 * comps // 2 + 8 :])
     azim = jnp.where(rows_of() >= 4, pltpu.roll(upper, 4, 0), 0.0)
     edges_ref[0] = edge_ref[0] + azim
     edges_ref[1] = edge_ref[1]
@@ -439,7 +438,7 @@
 }
 
 
-def call(body, ins, outs, shapes, *operands, scratch=(), aliases={}):
+def call(body, ins, outs, shapes, *operands, scratch=(), aliases={}, room=32):
     shapes = [shape if isinstance(shape, jax.ShapeDtypeStruct) else jax.ShapeDtypeStruct(shape, f32) for shape in shapes]
     return pl.pallas_call(
         body,
@@ -449,7 +448,7 @@
         scratch_shapes=scratch,
         input_output_aliases=aliases,
         cost_estimate=pl.CostEstimate(flops=4000000, bytes_accessed=400000, transcendentals=0),
-        compiler_params=pltpu.CompilerParams(vmem_limit_bytes=32 * 1024 * 1024),
+        compiler_params=pltpu.CompilerParams(vmem_limit_bytes=room * 1024 * 1024),
     )(*operands)
 
 
@@ -477,7 +476,7 @@
     assert moments == 4 and shape[2:] == (2, 4, 128) and comps % 32 == 0
     assert lax.axis_size("axial") == 2 and lax.axis_size("rad") == 4
     cells = 8 * comps
-    half, rows, message = cells // 2, cells // 4, 5 * comps // 2 + 8
+    half, rows, message = cells // 2, cells // 4, 5 * comps // 2
     a = adjoint_final.reshape(cells, 128)
     speeds_, speeds = speeds, speeds.reshape(3, 8, 128)
     flags_, flags = flags, flags.reshape(3, 8, 128)
@@ -486,24 +485,24 @@
     tables = [jax.ShapeDtypeStruct((256, 512), bf16)] * 2
 
     keep = ((0, 2, 0), (-1, 0, 0), (0, 0, 0), (0, 0, 0))
-    after = ((comps, 1, 0), (0, -1, 0), (0, 0, 0), (0, 0, 0))
+    after = ((comps, -1, 0), (0, -1, 0), (0, 0, 0), (0, 0, 0))
     up = lax.pad(adjoint_final.reshape(comps, 2, 4, 128), 0.0, keep)
-    up = up + lax.pad(speeds_[:1], 0.0, after) * lax.pad(flags_[:1], 0, after).astype(f32)
+    up = up + lax.pad(speeds_, 0.0, after) * lax.pad(flags_, 0, after).astype(f32)
     below = shift(up.reshape(half + 8, 128), "azim", 1)
+    upper = shift(speeds[0] * flags[0].astype(f32), "azim", -1)
     dn, ax, one, two, bad, *dn_tables = call(
         functools.partial(first_down, comps),
         "ssvvv",
         "v" * 7,
-        [(message, 128), (rows + 8, 128), (1, cells + 256), (1, cells + 256), (8, 128)] + tables,
+        [(message + 16, 128), (rows + 8, 128), (1, cells + 256), (1, cells + 256), (8, 128)] + tables,
         *place,
         a,
         speeds,
         flags,
     )
-    above = shift(dn, "azim", -1)
-    far = shift(bad, "azim", 2)
+    above = shift(lax.dynamic_update_slice(dn, upper, (message + 8, 0)), "azim", -1)
     if lax.axis_size("azim") > 4:
-        far = lax.pmax(far, "azim")
+        bad = lax.pmax(bad, "azim")
     ax = swap_axial(ax)
     one, two = swap_radial(one, 0), swap_radial(two, 1)
     (part,) = call(
@@ -521,7 +520,7 @@
         functools.partial(first_bottom, comps),
         "ss" + "v" * 11,
         "vvvv",
-        [(cells, 128), (4, 8, 128), (message - 8, 128), (8, 128)],
+        [(cells, 128), (4, 8, 128), (message, 128), (8, 128)],
         *place,
         part,
         a,
@@ -537,7 +536,7 @@
     next_above = shift(dn, "azim", -1)
     m, edge, up, ax, one, two, bad, *tables = call(
         functools.partial(first_top, comps),
-        "ss" + "v" * 6,
+        "ss" + "v" * 5,
         "v" * 9,
         [
             (cells, 128),
@@ -555,7 +554,6 @@
         above,
         edge,
         bad,
-        far,
     )
     below = shift(up, "azim", 1).reshape(comps, 4, 128)
     ax = swap_axial(ax)
@@ -610,6 +608,7 @@
             edge,
             scratch=[pltpu.VMEM((comps, 4, 128), f32), pltpu.SemaphoreType.DMA((4,))],
             aliases={0: 0},
+            room=63,
         )
         return whole.reshape(shape)
 

time: 46.5 us -> 52.5 us (1.13)
  waiting for transfers between devices: 12.8 us -> 16.9 us
  Pallas kernels: 10.3 us -> 13.4 us
  local copies, waits for them, and re-layouts: 2.38 us -> 0.8 us
    ppermute x6, waiting for transfers between devices: 11.2 us -> 16.9 us  [shift(): return lax.ppermute(x, axis, [(i, (i + step) % size) for i in range(size)])]
    pallas_call x7, Pallas kernels: 10.3 us -> 13.4 us  [call(): pl.pallas_call(body, in_specs=[SPACES[s] for s in ins], out_specs=[SPACES...]
    ppermute x3, waiting for transfers between devices: 1.58 us -> 0.03 us  [swap_axial(): return lax.ppermute(x, 'axial', [(0, 1), (1, 0)])]
    slice x2 -> x0, local copies, waits for them, and re-layouts: 1.47 us -> none  [the longest x1 0.78 us: packed_step(): speeds_[:1]]
    unnamed x20 -> x18, local copies, waits for them, and re-layouts: 0.91 us -> 0.03 us
    cond x0 -> x2, local copies, waits for them, and re-layouts: none -> 0.76 us
  transfers between devices with their start and end apart: 13 -> 13, of which waited for: 4 -> 3; matrix products, arithmetic and copies ran while one was open for 0% -> 0% of each run, Pallas kernels for 22% -> 22%
where the time goes in v6:
time: 52.5 us; the launch traced here: 52.2 us
  starting transfers between devices  19.3 us (37%)
  waiting for transfers between devices  16.9 us (32%)
  Pallas kernels  13.4 us (26%)
  other arithmetic  1.13 us (2%)
  local copies, waits for them, and re-layouts  0.8 us (2%)
    ppermute x6, waiting for transfers between devices, shift(): return lax.ppermute(x, axis, [(i, (i + step) % size) for i in range(size)])  16.9 us
    pallas_call x7, Pallas kernels, call(): pl.pallas_call(body, in_specs=[SPACES[s] for s in ins], out_specs=[SPACES...  13.4 us
    ppermute x6, starting transfers between devices, shift(): return lax.ppermute(x, axis, [(i, (i + step) % size) for i in range(size)])  12.4 us
    ppermute x3, starting transfers between devices, swap_axial(): return lax.ppermute(x, 'axial', [(0, 1), (1, 0)])  3.68 us
    ppermute x4, starting transfers between devices, swap_radial(): return lax.ppermute(x, 'rad', pairs + [(j, i) for i, j in pairs])  3.29 us
    add x1, other arithmetic, packed_step(): up + lax.pad(speeds_, 0.0, after) * lax.pad(flags_, 0, after).astype(f32)  1.12 us
  transfers between devices with their start and end apart: 13, of which 3 were waited for; matrix products, arithmetic and copies ran while one was open for 0% of the time, Pallas kernels for 22%

profile of v6, /device:TPU:0, one launch (start us, length us, event | category | flops | bytes accessed | tf_op | source)
XLA Modules:
  0.0 52.2 jit_solution(3928833473093871906)
XLA Ops:
  0.0 0.0 copy-start.43
  0.0 0.0 copy-start.34
  0.0 0.0 copy-start.44
  0.0 1.1 %fusion.30 = f32[194,1,4,128]{3,2,1,0:T(4,128)S(1)} fusion(f32[192,2,4,128]{3,2,1,0:T(4,128)} %bitcast.40, f32[3,2,4,128]{3,2,1,0:T(4,128)} %param.18, s32[3,2,4,128]{3,2,1,0:T(4,128)} %param.19), kind=kLoop, calls=%fused_computation.98 | loop fusion | flops 297984 | bytes 1208320 | tf_op jit(solution)/shard_map/add | solution.py:490
  1.2 3.1 %collective-permute-start.12 = (f32[776,128]{1,0:T(8,128)S(1)}, f32[776,128]{1,0:T(8,128)S(1)}, u32[]{:S(2)}, u32[]{:S(2)}) collective-permute-start(f32[776,128]{1,0:T(8,128)S(1)} %bitcast.69), channel_id=1, source_target_pairs={{0,8},{8,16},{16,24},{24,0},{1,9},{9,17},{17,25},{25,1},{2,10},{10... | collective-permute-start | bytes 1191944 | tf_op jit(solution)/shard_map/ppermute | solution.py:457
  4.3 0.0 copy-done
  4.3 2.2 %shard_map.132 = (f32[496,128]{1,0:T(8,128)S(1)}, f32[392,128]{1,0:T(8,128)S(1)}, f32[1,1792]{1,0:T(1,128)S(1)}, f32[1,1792]{1,0:T(1,128)S(1)}, f32[8,128]{1,0:T...) custom-call(s32[1]{0:T(128)} %bitcast.12.axial_ref, s32[1]{0:T(128)} %bitcast.13.rad_ref, ...), custom_call_target="tpu_custom_call" | custom-call | flops 4000000 | bytes 400000 | tf_op jit(solution)/shard_map/pallas_call | solution.py:443
  6.4 1.6 %collective-permute-start.13 = (f32[392,128]{1,0:T(8,128)S(1)}, f32[392,128]{1,0:T(8,128)S(1)}, u32[]{:S(2)}, u32[]{:S(2)}) collective-permute-start(f32[392,128]{1,0:T(8,128)S(1)} %get-tuple-element.85), channel_id=1, source_target_pairs={{0,1},{1,0},{2,3},{3,2},{4,5},{5,4},{6,7},{7,6},{8,9},{9,8},{10,11... | collective-permute-start | bytes 602120 | tf_op jit(solution)/shard_map/ppermute | solution.py:461
  8.0 0.0 copy-done.18
  8.0 0.0 copy-done.19
  8.1 2.3 %collective-permute-start.16 = (f32[8,128]{1,0:T(8,128)S(1)}, f32[8,128]{1,0:T(8,128)S(1)}, u32[]{:S(2)}, u32[]{:S(2)}) collective-permute-start(f32[8,128]{1,0:T(8,128)S(1)} %bitcast.79), channel_id=1, source_target_pairs={{0,24},{8,0},{16,8},{24,16},{1,25},{9,1},{17,9},{25,17},{2,26},{10... | collective-permute-start | bytes 12296 | tf_op jit(solution)/shard_map/ppermute | solution.py:457
  10.4 2.5 %collective-permute-done.16 = f32[8,128]{1,0:T(8,128)S(1)} collective-permute-done((f32[8,128]{1,0:T(8,128)S(1)}, f32[8,128]{1,0:T(8,128)S(1)}, u32[]{:S(2)}, u32[]{:S(2)}) %collective-permute-start.16) | collective-permute-done | bytes 4128 | tf_op jit(solution)/shard_map/ppermute | solution.py:457
  12.8 4.4 %collective-permute-start.17 = (f32[496,128]{1,0:T(8,128)S(1)}, f32[496,128]{1,0:T(8,128)S(1)}, u32[]{:S(2)}, u32[]{:S(2)}) collective-permute-start(f32[496,128]{1,0:T(8,128)S(1)} %constant_dynamic-update-slice_fusion), channel_id=1, source_target_pairs={{0,24},{8,0},{16,8},{24,16},{1,25},{9,1},{17,9},{25,17},{2,26},{10... | collective-permute-start | bytes 761864 | tf_op jit(solution)/shard_map/ppermute | solution.py:457
  17.2 0.0 collective-permute-start.14
  17.2 1.6 %collective-permute-start.15 = (f32[1,1792]{1,0:T(1,128)S(1)}, f32[1,1792]{1,0:T(1,128)S(1)}, u32[]{:S(2)}, u32[]{:S(2)}) collective-permute-start(f32[1,1792]{1,0:T(1,128)S(1)} %get-tuple-element.87), channel_id=1, source_target_pairs={{2,4},{6,0},{4,2},{0,6},{3,5},{7,1},{5,3},{1,7},{10,12},{14,8},{12... | collective-permute-start | bytes 21512 | tf_op jit(solution)/shard_map/ppermute | solution.py:467
  18.8 0.0 copy-done.27
  18.8 0.0 copy-done.1
  18.8 0.0 copy-done.43
  18.8 0.0 copy-done.34
  18.8 0.0 copy-done.44
  18.8 1.4 %shard_map.131.part_ref = f32[1536,128]{1,0:T(8,128)S(1)} custom-call(f32[1536,128]{1,0:T(8,128)S(1)} %bitcast.42, bf16[192,8,128]{2,1,0:T(8,128)(2,1)S(1)} %bitcast.56, f32[3,8,128]{2,1,0:T(8,128)S(1)} %bitcast.62, s32[3,8,128]{2,1,0:T(8,128)S(1)} %bitcast.66, s32[8,128]{1,0:T(8,128)S(1)} %bitcast.71, f32[48]{0:T(128)S(1)} %copy-done.43, f32[48]{0:T(128)S(1)} %copy-done.34, ...), custom_call_target="tpu_custom_call" | custom-call | flops 4000000 | bytes 400000 | tf_op jit(solution)/shard_map/pallas_call | solution.py:443
  20.2 0.0 collective-permute-done.14.one_ref
  20.2 0.0 collective-permute-done.15.two_ref
  20.3 0.0 collective-permute-done.13.ax_ref
  20.3 0.0 collective-permute-done.12.below_ref
  20.3 2.2 %shard_map.133 = (f32[1536,128]{1,0:T(8,128)S(1)}, f32[4,8,128]{2,1,0:T(8,128)S(1)}, f32[480,128]{1,0:T(8,128)S(1)}, f32[8,128]{1,0:T(8,128)S(1)}) custom-call(s32[1]{0:T(128)} %bitcast.12.axial_ref, s32[1]{0:T(128)} %bitcast.13.rad_ref, f32[1536,128]{1,0:T(8,128)S(1)} %shard_map.131.part_ref, f32[1536,128]{1,0:T(8,128)S(1)} %bitcast.43, ...), custom_call_target="tpu_custom_call" | custom-call | flops 4000000 | bytes 400000 | tf_op jit(solution)/shard_map/pallas_call | solution.py:443
  22.5 0.5 collective-permute-start.18
  23.0 0.0 collective-permute-done.17.above_ref
  23.0 1.6 %shard_map.134 = (f32[1536,128]{1,0:T(8,128)S(1)}, f32[4,8,128]{2,1,0:T(8,128)S(1)}, f32[768,128]{1,0:T(8,128)S(1)}, f32[384,128]{1,0:T(8,128)S(1)}, f32[1,1792]...) custom-call(s32[1]{0:T(128)} %bitcast.12.axial_ref, ...), custom_call_target="tpu_custom_call" | custom-call | flops 4000000 | bytes 400000 | tf_op jit(solution)/shard_map/pallas_call | solution.py:443
  24.6 1.6 %collective-permute-start.19 = (f32[8,128]{1,0:T(8,128)S(1)}, f32[8,128]{1,0:T(8,128)S(1)}, u32[]{:S(2)}, u32[]{:S(2)}) collective-permute-start(f32[8,128]{1,0:T(8,128)S(1)} %get-tuple-element.100.bad_ref), channel_id=1, source_target_pairs={{0,1},{1,0},{2,3},{3,2},{4,5},{5,4},{6,7},{7,6},{8,9},{9,8},{10,11... | collective-permute-start | bytes 12296 | tf_op jit(solution)/shard_map/ppermute | solution.py:461
  26.2 0.5 collective-permute-start.20
  26.7 1.6 %collective-permute-start.24 = (f32[768,128]{1,0:T(8,128)S(1)}, f32[768,128]{1,0:T(8,128)S(1)}, u32[]{:S(2)}, u32[]{:S(2)}) collective-permute-start(f32[768,128]{1,0:T(8,128)S(1)} %get-tuple-element.107), channel_id=1, source_target_pairs={{0,8},{8,16},{16,24},{24,0},{1,9},{9,17},{17,25},{25,1},{2,10},{10... | collective-permute-start | bytes 1179656 | tf_op jit(solution)/shard_map/ppermute | solution.py:457
  28.2 0.0 collective-permute-done.19.axial_bad_ref
  28.2 11.4 %collective-permute-done.18.above_ref = f32[480,128]{1,0:T(8,128)S(1)} collective-permute-done((f32[480,128]{1,0:T(8,128)S(1)}, f32[480,128]{1,0:T(8,128)S(1)}, u32[]{:S(2)}, u32[]{:S(2)}) %collective-permute-start.18) | collective-permute-done | bytes 245792 | tf_op jit(solution)/shard_map/ppermute | solution.py:457
  39.7 0.0 copy-done.3
  39.7 1.6 %shard_map.135 = (f32[1536,128]{1,0:T(8,128)S(1)}, f32[1,128]{1,0:T(1,128)S(1)}) custom-call(f32[1536,128]{1,0:T(8,128)S(1)} %get-tuple-element.95.m_ref, f32[1536,128]{1,0:T(8,128)S(1)} %bitcast.45, bf16[192,8,128]{2,1,0:T(8,128)(2,1)S(1)} %bitcast.57, f32[480,128]{1,0:T(8,128)S(1)} %collective-permute-done.18.above_ref, ...), custom_call_target="tpu_custom_call" | custom-call | flops 4000000 | bytes 400000 | tf_op jit(solution)/shard_map/pallas_call | solution.py:443
  41.3 0.1 collective-permute-start.21
  41.3 1.6 %collective-permute-start.22 = (f32[1,1792]{1,0:T(1,128)S(1)}, f32[1,1792]{1,0:T(1,128)S(1)}, u32[]{:S(2)}, u32[]{:S(2)}) collective-permute-start(f32[1,1792]{1,0:T(1,128)S(1)} %get-tuple-element.193), channel_id=1, source_target_pairs={{2,4},{6,0},{4,2},{0,6},{3,5},{7,1},{5,3},{1,7},{10,12},{14,8},{12... | collective-permute-start | bytes 21512 | tf_op jit(solution)/shard_map/ppermute | solution.py:467
  43.0 0.5 %collective-permute-start.23 = (f32[1,128]{1,0:T(1,128)S(1)}, f32[1,128]{1,0:T(1,128)S(1)}, u32[]{:S(2)}, u32[]{:S(2)}) collective-permute-start(f32[1,128]{1,0:T(1,128)S(1)} %get-tuple-element.104.bad_ref), channel_id=1, source_target_pairs={{0,4},{2,6},{4,0},{6,2},{1,5},{3,7},{5,1},{7,3},{8,12},{10,14},{12... | collective-permute-start | bytes 1544 | tf_op jit(solution)/shard_map/ppermute | solution.py:457
  43.5 0.0 collective-permute-done.20.ax_ref
  43.5 3.0 %collective-permute-done.23.far_ref = f32[1,128]{1,0:T(1,128)S(1)} collective-permute-done((f32[1,128]{1,0:T(1,128)S(1)}, f32[1,128]{1,0:T(1,128)S(1)}, u32[]{:S(2)}, u32[]{:S(2)}) %collective-permute-start.23) | collective-permute-done | bytes 544 | tf_op jit(solution)/shard_map/ppermute | solution.py:457
  46.5 0.0 collective-permute-done.21.one_ref
  46.5 0.0 collective-permute-done.22.two_ref
  46.5 2.5 %shard_map.136 = (f32[192,2,4,128]{3,2,1,0:T(4,128)}, f32[192,4,128]{2,1,0:T(4,128)}, f32[1,128]{1,0:T(1,128)S(1)}) custom-call(s32[1]{0:T(128)} %bitcast.12.axial_ref, s32[1]{0:T(128)} %bitcast.13.rad_ref, f32[1536,128]{1,0:T(8,128)S(1)} %get-tuple-element.101.part_ref, f32[384,128]{1,0:T(8,128)S(1)} %collective-permute-done.20.ax_ref, ...), custom_call_target="tpu_custom_call" | custom-call | flops 4000000 | bytes 400000 | tf_op jit(solution)/shard_map/pallas_call | solution.py:443
  49.1 0.0 collective-permute-done.24
  49.1 2.9 %conditional.1 = (f32[4,48,2,4,128]{4,3,2,1,0:T(4,128)}) conditional(s32[]{:T(128)} %bitcast.23, (f32[768,128]{1,0:T(8,128)S(1)}, f32[192,2,4,128]{3,2,1,0:T(4,128)}, f32[192,4,128]{2,1,0:T(4,128)}, f32[4,8,128]{2,1,0:T(8,128)S(1)}) %tuple.50, (f32[4,48,2,4,128]{4,3,2,1,0:T(4,128)S(1)}, s32[3,2,4,128]{3,2,1,0:T(4,128)S(1)}, ...), branch_computations={%region_0.0_spmd, %region_1.9_spmd} | conditional | flops 29856032 | bytes 122704704 | solution.py:728
  49.1 0.8 %copy-done.20 = f32[768,128]{1,0:T(8,128)} copy-done((f32[768,128]{1,0:T(8,128)}, f32[768,128]{1,0:T(8,128)S(1)}, u32[]{:S(2)}) %copy-start.20) | copy-done | bytes 393240 | tf_op jit(solution)/shard_map/cond
  49.9 1.9 %branch_0_fun.1 = f32[192,2,4,128]{3,2,1,0:T(4,128)} custom-call(f32[192,2,4,128]{3,2,1,0:T(4,128)} %get-tuple-element.43._, f32[192,4,128]{2,1,0:T(4,128)} %get-tuple-element.44.bottom_ref, f32[192,4,128]{2,1,0:T(4,128)} %bitcast.70, f32[4,8,128]{2,1,0:T(8,128)S(1)} %get-tuple-element.46.edge_ref), custom_call_target="tpu_custom_call", output_to_operand_aliasing={{}: (0, {})} | custom-call | flops 4000000 | bytes 400000 | tf_op jit(solution)/shard_map/cond/branch_0_fun/pallas_call | solution.py:443
  (11 shorter events, 0.0 us)
Async XLA Ops:
  0.0 8.0 %copy-start.18 = (f32[3,2,4,128]{3,2,1,0:T(4,128)S(1)}, f32[3,2,4,128]{3,2,1,0:T(4,128)}, u32[]{:S(2)}) copy-start(f32[3,2,4,128]{3,2,1,0:T(4,128)} %param.18) | copy-start | bytes 36868
  0.0 8.0 %copy-start.19 = (s32[3,2,4,128]{3,2,1,0:T(4,128)S(1)}, s32[3,2,4,128]{3,2,1,0:T(4,128)}, u32[]{:S(2)}) copy-start(s32[3,2,4,128]{3,2,1,0:T(4,128)} %param.19) | copy-start | bytes 36868
  0.0 4.3 %copy-start = (f32[4,48,2,4,128]{4,3,2,1,0:T(4,128)S(1)}, f32[4,48,2,4,128]{4,3,2,1,0:T(4,128)}, u32[]{:S(2)}) copy-start(f32[4,48,2,4,128]{4,3,2,1,0:T(4,128)} %param.15) | copy-start | bytes 2359300
  0.0 18.8 %copy-start.27 = (s32[2,4,128]{2,1,0:T(4,128)S(1)}, s32[2,4,128]{2,1,0:T(4,128)}, u32[]{:S(2)}) copy-start(s32[2,4,128]{2,1,0:T(4,128)} %param.20) | copy-start | bytes 12292
  0.0 18.8 %copy-start.1 = (bf16[4,48,2,4,128]{4,3,2,1,0:T(4,128)(2,1)S(1)}, bf16[4,48,2,4,128]{4,3,2,1,0:T(4,128)(2,1)}, u32[]{:S(2)}) copy-start(bf16[4,48,2,4,128]{4,3,2,1,0:T(4,128)(2,1)} %param.17) | copy-start | bytes 1179652
  0.0 18.8 %copy-start.43 = (f32[48]{0:T(128)S(1)}, f32[48]{0:T(128)}, u32[]{:S(2)}) copy-start(f32[48]{0:T(128)} %growth_ref.3) | copy-start | bytes 580
  0.0 18.8 %copy-start.34 = (f32[48]{0:T(128)S(1)}, f32[48]{0:T(128)}, u32[]{:S(2)}) copy-start(f32[48]{0:T(128)} %transfer_ref.3) | copy-start | bytes 580
  0.0 18.8 %copy-start.44 = (f32[4]{0:T(128)S(1)}, f32[4]{0:T(128)}, u32[]{:S(2)}) copy-start(f32[4]{0:T(128)} %rate_ref.3) | copy-start | bytes 52
  1.2 19.1 %collective-permute-start.12 = (f32[776,128]{1,0:T(8,128)S(1)}, f32[776,128]{1,0:T(8,128)S(1)}, u32[]{:S(2)}, u32[]{:S(2)}) collective-permute-start(f32[776,128]{1,0:T(8,128)S(1)} %bitcast.69), channel_id=1, source_target_pairs={{0,8},{8,16},{16,24},{24,0},{1,9},{9,17},{17,25},{25,1},{2,10},{10... | collective-permute-start | bytes 1191944 | tf_op jit(solution)/shard_map/ppermute | solution.py:457
  6.4 13.8 %collective-permute-start.13 = (f32[392,128]{1,0:T(8,128)S(1)}, f32[392,128]{1,0:T(8,128)S(1)}, u32[]{:S(2)}, u32[]{:S(2)}) collective-permute-start(f32[392,128]{1,0:T(8,128)S(1)} %get-tuple-element.85), channel_id=1, source_target_pairs={{0,1},{1,0},{2,3},{3,2},{4,5},{5,4},{6,7},{7,6},{8,9},{9,8},{10,11... | collective-permute-start | bytes 602120 | tf_op jit(solution)/shard_map/ppermute | solution.py:461
  8.1 4.8 %collective-permute-start.16 = (f32[8,128]{1,0:T(8,128)S(1)}, f32[8,128]{1,0:T(8,128)S(1)}, u32[]{:S(2)}, u32[]{:S(2)}) collective-permute-start(f32[8,128]{1,0:T(8,128)S(1)} %bitcast.79), channel_id=1, source_target_pairs={{0,24},{8,0},{16,8},{24,16},{1,25},{9,1},{17,9},{25,17},{2,26},{10... | collective-permute-start | bytes 12296 | tf_op jit(solution)/shard_map/ppermute | solution.py:457
  12.8 10.2 %collective-permute-start.17 = (f32[496,128]{1,0:T(8,128)S(1)}, f32[496,128]{1,0:T(8,128)S(1)}, u32[]{:S(2)}, u32[]{:S(2)}) collective-permute-start(f32[496,128]{1,0:T(8,128)S(1)} %constant_dynamic-update-slice_fusion), channel_id=1, source_target_pairs={{0,24},{8,0},{16,8},{24,16},{1,25},{9,1},{17,9},{25,17},{2,26},{10... | collective-permute-start | bytes 761864 | tf_op jit(solution)/shard_map/ppermute | solution.py:457
  17.2 3.0 %collective-permute-start.14 = (f32[1,1792]{1,0:T(1,128)S(1)}, f32[1,1792]{1,0:T(1,128)S(1)}, u32[]{:S(2)}, u32[]{:S(2)}) collective-permute-start(f32[1,1792]{1,0:T(1,128)S(1)} %get-tuple-element.86), channel_id=1, source_target_pairs={{0,2},{4,6},{2,0},{6,4},{1,3},{5,7},{3,1},{7,5},{8,10},{12,14},{10... | collective-permute-start | bytes 21512 | tf_op jit(solution)/shard_map/ppermute | solution.py:467
  17.2 3.1 %collective-permute-start.15 = (f32[1,1792]{1,0:T(1,128)S(1)}, f32[1,1792]{1,0:T(1,128)S(1)}, u32[]{:S(2)}, u32[]{:S(2)}) collective-permute-start(f32[1,1792]{1,0:T(1,128)S(1)} %get-tuple-element.87), channel_id=1, source_target_pairs={{2,4},{6,0},{4,2},{0,6},{3,5},{7,1},{5,3},{1,7},{10,12},{14,8},{12... | collective-permute-start | bytes 21512 | tf_op jit(solution)/shard_map/ppermute | solution.py:467
  20.3 19.4 %copy-start.3 = (bf16[4,48,2,4,128]{4,3,2,1,0:T(4,128)(2,1)S(1)}, bf16[4,48,2,4,128]{4,3,2,1,0:T(4,128)(2,1)}, u32[]{:S(2)}) copy-start(bf16[4,48,2,4,128]{4,3,2,1,0:T(4,128)(2,1)} %param.16) | copy-start | bytes 1179652
  22.5 17.1 %collective-permute-start.18 = (f32[480,128]{1,0:T(8,128)S(1)}, f32[480,128]{1,0:T(8,128)S(1)}, u32[]{:S(2)}, u32[]{:S(2)}) collective-permute-start(f32[480,128]{1,0:T(8,128)S(1)} %get-tuple-element.96), channel_id=1, source_target_pairs={{0,24},{8,0},{16,8},{24,16},{1,25},{9,1},{17,9},{25,17},{2,26},{10... | collective-permute-start | bytes 737288 | tf_op jit(solution)/shard_map/ppermute | solution.py:457
  24.6 3.7 %collective-permute-start.19 = (f32[8,128]{1,0:T(8,128)S(1)}, f32[8,128]{1,0:T(8,128)S(1)}, u32[]{:S(2)}, u32[]{:S(2)}) collective-permute-start(f32[8,128]{1,0:T(8,128)S(1)} %get-tuple-element.100.bad_ref), channel_id=1, source_target_pairs={{0,1},{1,0},{2,3},{3,2},{4,5},{5,4},{6,7},{7,6},{8,9},{9,8},{10,11... | collective-permute-start | bytes 12296 | tf_op jit(solution)/shard_map/ppermute | solution.py:461
  26.2 17.3 %collective-permute-start.20 = (f32[384,128]{1,0:T(8,128)S(1)}, f32[384,128]{1,0:T(8,128)S(1)}, u32[]{:S(2)}, u32[]{:S(2)}) collective-permute-start(f32[384,128]{1,0:T(8,128)S(1)} %get-tuple-element.102), channel_id=1, source_target_pairs={{0,1},{1,0},{2,3},{3,2},{4,5},{5,4},{6,7},{7,6},{8,9},{9,8},{10,11... | collective-permute-start | bytes 589832 | tf_op jit(solution)/shard_map/ppermute | solution.py:461
  26.7 22.4 %collective-permute-start.24 = (f32[768,128]{1,0:T(8,128)S(1)}, f32[768,128]{1,0:T(8,128)S(1)}, u32[]{:S(2)}, u32[]{:S(2)}) collective-permute-start(f32[768,128]{1,0:T(8,128)S(1)} %get-tuple-element.107), channel_id=1, source_target_pairs={{0,8},{8,16},{16,24},{24,0},{1,9},{9,17},{17,25},{25,1},{2,10},{10... | collective-permute-start | bytes 1179656 | tf_op jit(solution)/shard_map/ppermute | solution.py:457
  41.3 5.2 %collective-permute-start.21 = (f32[1,1792]{1,0:T(1,128)S(1)}, f32[1,1792]{1,0:T(1,128)S(1)}, u32[]{:S(2)}, u32[]{:S(2)}) collective-permute-start(f32[1,1792]{1,0:T(1,128)S(1)} %get-tuple-element.194), channel_id=1, source_target_pairs={{0,2},{4,6},{2,0},{6,4},{1,3},{5,7},{3,1},{7,5},{8,10},{12,14},{10... | collective-permute-start | bytes 21512 | tf_op jit(solution)/shard_map/ppermute | solution.py:467
  41.3 5.2 %collective-permute-start.22 = (f32[1,1792]{1,0:T(1,128)S(1)}, f32[1,1792]{1,0:T(1,128)S(1)}, u32[]{:S(2)}, u32[]{:S(2)}) collective-permute-start(f32[1,1792]{1,0:T(1,128)S(1)} %get-tuple-element.193), channel_id=1, source_target_pairs={{2,4},{6,0},{4,2},{0,6},{3,5},{7,1},{5,3},{1,7},{10,12},{14,8},{12... | collective-permute-start | bytes 21512 | tf_op jit(solution)/shard_map/ppermute | solution.py:467
  43.0 3.5 %collective-permute-start.23 = (f32[1,128]{1,0:T(1,128)S(1)}, f32[1,128]{1,0:T(1,128)S(1)}, u32[]{:S(2)}, u32[]{:S(2)}) collective-permute-start(f32[1,128]{1,0:T(1,128)S(1)} %get-tuple-element.104.bad_ref), channel_id=1, source_target_pairs={{0,4},{2,6},{4,0},{6,2},{1,5},{3,7},{5,1},{7,3},{8,12},{10,14},{12... | collective-permute-start | bytes 1544 | tf_op jit(solution)/shard_map/ppermute | solution.py:457
  49.1 0.8 %copy-start.20 = (f32[768,128]{1,0:T(8,128)}, f32[768,128]{1,0:T(8,128)S(1)}, u32[]{:S(2)}) copy-start(f32[768,128]{1,0:T(8,128)S(1)} %get-tuple-element.45) | copy-start | bytes 1179652 | tf_op jit(solution)/shard_map/cond

commit v7 on v3

--- a/solution.py
+++ b/solution.py
@@ -11,7 +11,11 @@
 crowding = 0.02
 nucleus_moments = (1.0, 0.5, 0.25, 0.125)
 f32 = jnp.float32
+bf16 = jnp.bfloat16
 exact = lax.Precision.HIGHEST
+
+slots = 320
+extra = slots - 256
 
 
 def rows_of():
@@ -61,11 +65,90 @@
     )
 
 
-def copies(pairs, sems):
-    made = [pltpu.make_async_copy(src, dst, sems.at[i]) for i, (src, dst) in enumerate(pairs)]
-    for copy in made:
-        copy.start()
-    return made
+def make_tables(p, where_zero, low_ref, high_ref):
+    row, lane = rows_of(), lanes_of()
+    taken = (p == 0.0) if where_zero else (p != 0.0)
+    one = jnp.where(taken & (row < 4), 1.0, 0.0)
+    before = lax.broadcasted_iota(jnp.int32, (128, 128), 0) < lax.broadcasted_iota(jnp.int32, (128, 128), 1)
+    inside = jnp.dot(one.astype(bf16), jnp.where(before, 1.0, 0.0).astype(bf16), preferred_element_type=f32)
+    total = jnp.sum(one, axis=1, keepdims=True)
+    base = jnp.zeros((8, 1), f32)
+    for step in (1, 2, 3):
+        base = base + jnp.where(
+            lax.broadcasted_iota(jnp.int32, (8, 1), 0) >= step, jnp.roll(total, step, axis=0), 0.0
+        )
+    slot = jnp.where(one > 0.0, inside + base, -1.0).astype(jnp.int32)
+    here = lax.broadcasted_iota(jnp.int32, (128, 128), 0)
+    first = jnp.where(here < extra, here + 256, -2)
+    second = jnp.where(here >= extra, here + (256 - extra), -2)
+    for z in range(4):
+        cells = slice(128 * z, 128 * z + 128)
+        want = jnp.broadcast_to(slot[z : z + 1], (128, 128))
+        for ref, start, names in ((low_ref, 0, here), (low_ref, 128, here + 128), (high_ref, 0, first), (high_ref, 128, second)):
+            ref[start : start + 128, cells] = jnp.where(names == want, 1.0, 0.0).astype(bf16)
+
+
+def crowded(p):
+    taken = jnp.where((rows_of() < 4) & (p != 0.0), 1.0, 0.0)
+    count = jnp.sum(jnp.sum(taken, axis=1, keepdims=True), axis=0, keepdims=True)
+    count = jnp.broadcast_to(count, (8, 128))
+    return jnp.where(jnp.maximum(count, 512.0 - count) > slots, 1.0, 0.0)
+
+
+def pieces(x):
+    high = x.astype(bf16)
+    rest = x - high.astype(f32)
+    middle = rest.astype(bf16)
+    return high, middle, (rest - middle.astype(f32)).astype(bf16)
+
+
+def stacked(x, half):
+    return jnp.concatenate([part[half * i : half * i + half] for i in range(2) for part in pieces(x)], axis=0)
+
+
+def summed(x, half):
+    parts = [x[half * i : half * i + half] for i in range(6)]
+    return [parts[3 * i] + (parts[3 * i + 1] + parts[3 * i + 2]) for i in range(2)]
+
+
+def encode(comps, x_ref, first_row, low_ref, high_ref, message_ref):
+    half = comps // 2
+    x = jnp.concatenate(
+        [stacked(x_ref[pl.ds(first_row + z, comps, stride=8)], half) for z in range(4)], axis=1
+    )
+    over = (((1,), (1,)), ((), ()))
+    low = lax.dot_general(x, low_ref[...], over, preferred_element_type=f32)
+    high = [
+        lax.dot_general(
+            x[3 * half * i : 3 * half * (i + 1)], high_ref[128 * i : 128 * i + 128], over, preferred_element_type=f32
+        )
+        for i in range(2)
+    ]
+    tail = jnp.zeros((half, 128), f32)
+    for i, part in enumerate(summed(low, half)):
+        message_ref[half * i : half * i + half] = part[:, :128]
+        message_ref[comps + half * i : comps + half * i + half] = part[:, 128:]
+    for part in high:
+        tail = tail + (part[:half] + (part[half : 2 * half] + part[2 * half :]))
+    message_ref[2 * comps : 2 * comps + half] = tail
+
+
+def decode(comps, message_ref, low_ref, high_ref):
+    half = comps // 2
+    x = jnp.concatenate([stacked(message_ref[comps * i : comps * i + comps], half) for i in range(2)], axis=1)
+    low = jnp.dot(x, low_ref[...], preferred_element_type=f32)
+    tail = jnp.concatenate(pieces(message_ref[2 * comps : 2 * comps + half]), axis=0)
+    found = []
+    for i, part in enumerate(summed(low, half)):
+        high = jnp.dot(tail, high_ref[128 * i : 128 * i + 128], preferred_element_type=f32)
+        found.append(part + (high[:half] + (high[half : 2 * half] + high[2 * half :])))
+    return jnp.concatenate(found, axis=0)
+
+
+def add_azimuthal(comps, halo, coefficient, first_row, out_ref):
+    for z in range(4):
+        spots = pl.ds(first_row + z, comps, stride=8)
+        out_ref[spots] = out_ref[spots] + coefficient[first_row + z : first_row + z + 1] * halo[:, 128 * z : 128 * z + 128]
 
 
 def pack_sides(comps, x_ref, where_ref, ax_ref, radup_ref, raddn_ref):
@@ -101,6 +184,7 @@
     p, _ = faces(speeds_ref, flags_ref)
     for c in range(comps):
         up_ref[4 * c : 4 * c + 4] = a_ref[8 * c + 4 : 8 * c + 8]
+    up_ref[4 * comps :] = p[0]
     pack_sides(comps, a_ref, where_ref, ax_ref, radup_ref, raddn_ref)
     ax_ref[2 * comps : 2 * comps + 8] = pair_rows(p[1], 0, 4)
     radup_ref[:, 8 * comps :] = jnp.zeros((1, 128), f32)
@@ -150,8 +234,26 @@
             finish(c, x[k][0], term)
 
 
-def first_local(sections, a_ref, u_ref, speeds_ref, flags_ref, zones_ref, growth_ref, transfer_ref, rate_ref, out_ref):
-    local = Local(*faces(speeds_ref, flags_ref))
+def first_local(
+    sections,
+    a_ref,
+    u_ref,
+    speeds_ref,
+    flags_ref,
+    zones_ref,
+    growth_ref,
+    transfer_ref,
+    rate_ref,
+    out_ref,
+    dn_low_ref,
+    dn_high_ref,
+    up_low_ref,
+    up_high_ref,
+):
+    p, q = faces(speeds_ref, flags_ref)
+    local = Local(p, q)
+    make_tables(p[0], False, dn_low_ref, dn_high_ref)
+    make_tables(p[0], True, up_low_ref, up_high_ref)
 
     def finish(c, x, term):
         out_ref[8 * c : 8 * c + 8] = 0.5 * (x + local(x) + term)
@@ -200,25 +302,34 @@
     ax_ref,
     radlo_ref,
     radhi_ref,
+    far_ref,
     speeds_ref,
     flags_ref,
     m_ref,
     edge_ref,
     up_ref,
+    bad_ref,
+    dn_low_ref,
+    dn_high_ref,
+    up_low_ref,
+    up_high_ref,
 ):
-    _, q = faces(speeds_ref, flags_ref)
+    p, q = faces(speeds_ref, flags_ref)
     row, lane = rows_of(), lanes_of()
-    top = row >= 4
+    upper = above_ref[4 * comps :]
+    make_tables(upper, True, up_low_ref, up_high_ref)
+    make_tables(upper, False, dn_low_ref, dn_high_ref)
+    bad_ref[...] = crowded(p[0]) + crowded(upper) + crowded(far_ref[...])
     hrad = put_columns(radlo_ref[...], radhi_ref[...])
     lower_half = where_ref[0] == 0
-    p_azim = jnp.concatenate([jnp.zeros((4, 128), f32), above_ref[4 * comps : 4 * comps + 4]], axis=0)
+    p_azim = jnp.where(row >= 4, pltpu.roll(upper, 4, 0), 0.0)
     pairs = jnp.where(lower_half, ax_ref[2 * comps : 2 * comps + 8], 0.0)
     p_axial = jnp.where(row == 3, pairs[0:1], jnp.where(row == 7, pairs[1:2], 0.0))
     p_rad = jnp.where(lane == 127, hrad[8 * comps : 8 * comps + 8], 0.0)
     axial = jnp.where(lower_half, pairs, pair_rows(q[1], 0, 4))
     rad = jnp.where(lane == 0, q[2], p_rad)
     centre = p_azim + p_axial + p_rad
-    edge_ref[0] = jnp.where(top, p_azim, q[0])
+    edge_ref[0] = jnp.where(row >= 4, p_azim, q[0])
     edge_ref[1] = axial
     edge_ref[2] = rad
     edge_ref[3] = centre
@@ -228,46 +339,49 @@
             p_azim * from_above(c, above_ref) + rad * hrad[spots] - centre * a_ref[spots]
         )
     add_axial(comps, 0.5, where_ref, axial, ax_ref, m_ref)
-    for c in range(comps):
-        up_ref[4 * c : 4 * c + 4] = m_ref[8 * c + 4 : 8 * c + 8]
-
-
-def first_bottom(comps, where_ref, part_ref, below_ref, edge_ref, m_ref, dn_ref, ax_ref, radup_ref, raddn_ref):
+    encode(comps, m_ref, 4, up_low_ref, up_high_ref, up_ref)
+
+
+def first_bottom(
+    comps,
+    where_ref,
+    part_ref,
+    below_ref,
+    edge_ref,
+    bad_ref,
+    low_ref,
+    high_ref,
+    m_ref,
+    dn_ref,
+    ax_ref,
+    radup_ref,
+    raddn_ref,
+    worse_ref,
+):
     azim = jnp.where(rows_of() >= 4, 0.0, 0.5 * edge_ref[0])
     for c in range(comps):
         m_ref[8 * c : 8 * c + 8] = part_ref[8 * c : 8 * c + 8] + azim * from_below(c, below_ref)
-        dn_ref[4 * c : 4 * c + 4] = m_ref[8 * c : 8 * c + 4]
+    encode(comps, m_ref, 0, low_ref, high_ref, dn_ref)
+    worse_ref[...] = bad_ref[...] + crowded(below_ref[4 * comps :])
     pack_sides(comps, m_ref, where_ref, ax_ref, radup_ref, raddn_ref)
 
 
 def second_bottom(
-    comps, where_ref, part_ref, below_ref, ax_ref, radlo_ref, radhi_ref, edge_ref, out_ref, top_ref, full_ref, low_ref, sems
+    comps, where_ref, part_ref, below_ref, ax_ref, radlo_ref, radhi_ref, edge_ref, low_ref, high_ref, base_ref, full_ref
 ):
     hrad = put_columns(radlo_ref[...], radhi_ref[...])
-    azim, rad = jnp.where(rows_of() >= 4, 0.0, edge_ref[0]), edge_ref[2]
+    rad = edge_ref[2]
     for c in range(comps):
         spots = slice(8 * c, 8 * c + 8)
-        full_ref[spots] = part_ref[spots] + azim * from_below(c, below_ref) + rad * hrad[spots]
-    add_axial(comps, 1.0, where_ref, edge_ref[1], ax_ref, full_ref)
-    for c in range(comps):
-        low_ref[c] = full_ref[8 * c : 8 * c + 4]
-    made = copies([(low_ref, out_ref.at[:, 0])], sems)
-    for c in range(comps):
-        top_ref[c] = full_ref[8 * c + 4 : 8 * c + 8]
-    made[0].wait()
-
-
-def second_top(comps, parts, _, top_ref, above_ref, edge_ref, out_ref, high_ref, sems):
-    azim = edge_ref[0][4:8]
-    size = comps // parts
-    made = []
-    for i in range(parts):
-        spots = pl.ds(i * size, size)
-        high_ref[spots] = top_ref[spots] + azim[None] * above_ref[spots]
-        made.append(pltpu.make_async_copy(high_ref.at[spots], out_ref.at[spots, 1], sems.at[i]))
-        made[-1].start()
-    for copy in made:
-        copy.wait()
+        base_ref[spots] = part_ref[spots] + rad * hrad[spots]
+    add_axial(comps, 1.0, where_ref, edge_ref[1], ax_ref, base_ref)
+    full_ref[...] = base_ref[...]
+    add_azimuthal(comps, decode(comps, below_ref, low_ref, high_ref), edge_ref[0], 0, full_ref)
+
+
+def second_top(comps, full_ref, above_ref, edge_ref, low_ref, high_ref, out_ref):
+    out_ref[...] = full_ref[...]
+    add_azimuthal(comps, decode(comps, above_ref, low_ref, high_ref), edge_ref[0], 4, out_ref)
 
 
 SPACES = {
@@ -277,16 +391,14 @@
 }
 
 
-def call(body, ins, outs, shapes, cost, *operands, scratch=(), aliases={}, room=32):
+def call(body, ins, outs, shapes, cost, *operands):
     return pl.pallas_call(
         body,
         in_specs=[SPACES[s] for s in ins],
         out_specs=[SPACES[s] for s in outs],
-        out_shape=[jax.ShapeDtypeStruct(shape, f32) for shape in shapes],
-        scratch_shapes=scratch,
-        input_output_aliases=aliases,
+        out_shape=[s if isinstance(s, jax.ShapeDtypeStruct) else jax.ShapeDtypeStruct(s, f32) for s in shapes],
         cost_estimate=pl.CostEstimate(flops=cost, bytes_accessed=cost // 10, transcendentals=0),
-        compiler_params=pltpu.CompilerParams(vmem_limit_bytes=room * 1024 * 1024),
+        compiler_params=pltpu.CompilerParams(vmem_limit_bytes=32 * 1024 * 1024),
     )(*operands)
 
 
@@ -314,18 +426,19 @@
     flags2 = flags.reshape(3, 8, 128)
     where = lax.axis_index("axial").reshape(1)
     rates = (zones.reshape(8, 128), growth_rate, transfer_rate, nucleation_rate)
-    dma = pltpu.SemaphoreType.DMA
-
-    keep = ((0, 1, 0), (0, -1, 0), (0, 0, 0), (0, 0, 0))
-    after = ((comps, -2, 0), (0, -1, 0), (0, 0, 0), (0, 0, 0))
+    message = 5 * comps // 2
+    tables = [jax.ShapeDtypeStruct((256, 512), bf16)] * 2
+
+    keep = ((0, 2, 0), (0, -1, 0), (0, 0, 0), (0, 0, 0))
+    after = ((comps, -1, 0), (0, -1, 0), (0, 0, 0), (0, 0, 0))
     dn = lax.pad(adjoint_final.reshape(comps, 2, 4, 128), 0.0, keep)
     dn = dn + lax.pad(speeds, 0.0, after) * lax.pad(flags, 0, after).astype(f32)
-    above = shift(dn, "azim", -1, True).reshape(half + 4, 128)
+    above = shift(dn.reshape(half + 8, 128), "azim", -1, True)
     up, *edges = call(
         functools.partial(first_rest, comps),
         "svvv",
         "vvvv",
-        [(half, 128), (rows + 8, 128), (1, cells + 128), (1, cells + 128)],
+        [(half + 8, 128), (rows + 8, 128), (1, cells + 128), (1, cells + 128)],
         2_000_000,
         where,
         a,
@@ -333,12 +446,13 @@
         flags2,
     )
     below = shift(up, "azim", 1, True)
+    far = shift(speeds2[0] * flags2[0].astype(f32), "azim", 2, True)
     edges = sides(*edges)
-    (part,) = call(
+    part, *lower_tables = call(
         functools.partial(first_local, sections),
         "vvvvvsss",
-        "v",
-        [(cells, 128)],
+        "vvvvv",
+        [(cells, 128)] + 2 * tables,
         8_000_000,
         a,
         state_middle.reshape(comps, 8, 128),
@@ -346,33 +460,36 @@
         flags2,
         *rates,
     )
-    part, edge, up = call(
+    part, edge, up, bad, *upper_tables = call(
         functools.partial(first_top, comps),
-        "s" + "v" * 8,
-        "vvv",
-        [(cells, 128), (4, 8, 128), (half, 128)],
+        "s" + "v" * 9,
+        "v" * 8,
+        [(cells, 128), (4, 8, 128), (message, 128), (8, 128)] + 2 * tables,
         4_000_000,
         where,
         part,
         a,
         above,
         *edges,
+        far,
         speeds2,
         flags2,
     )
     next_below = shift(up, "azim", 1, True)
-    m, dn, *edges = call(
+    m, dn, *edges, bad = call(
         functools.partial(first_bottom, comps),
-        "svvv",
-        "vvvvv",
-        [(cells, 128), (half, 128), (rows, 128), (1, cells), (1, cells)],
+        "s" + "v" * 6,
+        "v" * 6,
+        [(cells, 128), (message, 128), (rows, 128), (1, cells), (1, cells), (8, 128)],
         4_000_000,
         where,
         part,
         below,
         edge,
-    )
-    above = shift(dn, "azim", -1, True).reshape(comps, 4, 128)
+        bad,
+        *lower_tables[:2],
+    )
+    next_above = shift(dn, "azim", -1, True)
     edges = sides(*edges)
     (part,) = call(
         functools.partial(second_local, sections),
@@ -388,33 +505,43 @@
         flags2,
         *rates,
     )
-    out, top = call(
+    base, full = call(
         functools.partial(second_bottom, comps),
-        "s" + "v" * 6,
-        "hv",
-        [(comps, 2, 4, 128), (comps, 4, 128)],
+        "s" + "v" * 8,
+        "vv",
+        [(cells, 128), (cells, 128)],
         4_000_000,
         where,
         part,
         next_below,
         *edges,
         edge,
-        scratch=[pltpu.VMEM((cells, 128), f32), pltpu.VMEM((comps, 4, 128), f32), dma((1,))],
-    )
-    (out,) = call(
-        functools.partial(second_top, comps, 4),
-        "hvvv",
-        "h",
-        [(comps, 2, 4, 128)],
-        1_000_000,
-        out,
-        top,
-        above,
-        edge,
-        scratch=[pltpu.VMEM((comps, 4, 128), f32), dma((4,))],
-        aliases={0: 0},
-    )
-    return out.reshape(shape)
+        *lower_tables[2:],
+    )
+
+    def quick():
+        (out,) = call(
+            functools.partial(second_top, comps),
+            "vvvvv",
+            "v",
+            [(cells, 128)],
+            1_000_000,
+            full,
+            next_above,
+            edge,
+            *upper_tables[:2],
+        )
+        return out
+
+    def whole():
+        rows_ = m.reshape(comps, 2, 4, 128)
+        halo = jnp.stack([shift(rows_[:, 1], "azim", 1, True), shift(rows_[:, 0], "azim", -1, True)], axis=1)
+        return base + (edge[0].reshape(1, 2, 4, 128) * halo).reshape(cells, 128)
+
+    worst = bad[0, 0]
+    if lax.axis_size("azim") != 4:
+        worst = lax.pmax(worst, "azim")
+    return lax.cond(worst > 0.0, whole, quick).reshape(shape)
 
 
 def solution(mesh):

time: 42.8 us -> 48.7 us (1.14)
  the two profiles are of different devices: /device:TPU:0 before, /device:TPU:1 now
where the time goes in v7:
time: 48.7 us; the launch traced here: 48.4 us
  starting transfers between devices  24.9 us (51%)
  Pallas kernels  9.85 us (20%)
  waiting for transfers between devices  9.69 us (20%)
  local copies, waits for them, and re-layouts  2.06 us (4%)
  other arithmetic  1.1 us (2%)
  between operations  0.83 us (2%)
    ppermute x9, starting transfers between devices, shift(): return lax.ppermute(x, axis, pairs)  22.3 us
    pallas_call x7, Pallas kernels, call(): pl.pallas_call(body, in_specs=[SPACES[s] for s in ins], out_specs=[SPACES...  9.85 us
    ppermute x9, waiting for transfers between devices, shift(): return lax.ppermute(x, axis, pairs)  9.68 us
    ppermute x2, starting transfers between devices, sides(): ax = lax.ppermute(ax, 'axial', [(0, 1), (1, 0)])  2.57 us
    unnamed x20, local copies, waits for them, and re-layouts  1.54 us
    add x1, other arithmetic, shards(): dn = dn + lax.pad(speeds, 0.0, after) * lax.pad(flags, 0, after).astype(f32)  1.1 us
  transfers between devices with their start and end apart: 11, of which 3 were waited for; matrix products, arithmetic and copies ran while one was open for 1% of the time, Pallas kernels for 19%

profile of v7, /device:TPU:1, one launch (start us, length us, event | category | flops | bytes accessed | tf_op | source)
XLA Modules:
  0.0 48.4 jit_solution(3264800972780899533)
XLA Ops:
  0.0 0.0 copy-start
  0.0 1.1 %fusion = f32[194,1,4,128]{3,2,1,0:T(4,128)S(1)} fusion(f32[192,2,4,128]{3,2,1,0:T(4,128)} %bitcast.26, f32[3,2,4,128]{3,2,1,0:T(4,128)} %param.14, s32[3,2,4,128]{3,2,1,0:T(4,128)} %param.15), kind=kLoop, calls=%fused_computation.6 | loop fusion | flops 297984 | bytes 1208320 | tf_op jit(solution)/shard_map/add | solution.py:435
  1.1 0.0 copy-start.3
  1.1 4.2 %collective-permute-start.2 = (f32[776,128]{1,0:T(8,128)S(1)}, f32[776,128]{1,0:T(8,128)S(1)}, u32[]{:S(2)}, u32[]{:S(2)}) collective-permute-start(f32[776,128]{1,0:T(8,128)S(1)} %bitcast.47), channel_id=1, source_target_pairs={{0,24},{8,0},{16,8},{24,16},{1,25},{9,1},{17,9},{25,17},{2,26},{10... | collective-permute-start | bytes 1191944 | tf_op jit(solution)/shard_map/ppermute | solution.py:408
  5.3 0.0 copy-done
  5.3 0.0 copy-done.4
  5.3 0.0 copy-done.3
  5.3 0.8 %shard_map.94 = (f32[776,128]{1,0:T(8,128)S(1)}, f32[392,128]{1,0:T(8,128)S(1)}, f32[1,1664]{1,0:T(1,128)S(1)}, f32[1,1664]{1,0:T(1,128)S(1)}) custom-call(s32[1]{0:T(128)} %bitcast.9.where_ref, f32[1536,128]{1,0:T(8,128)S(1)} %bitcast.27, f32[3,8,128]{2,1,0:T(8,128)S(1)} %bitcast.33, s32[3,8,128]{2,1,0:T(8,128)S(1)} %bitcast.37), custom_call_target="tpu_custom_call" | custom-call | flops 2000000 | bytes 200000 | tf_op jit(solution)/shard_map/pallas_call | solution.py:395
  6.2 0.1 collective-permute-start.7
  6.3 1.3 %collective-permute-start.3 = (f32[392,128]{1,0:T(8,128)S(1)}, f32[392,128]{1,0:T(8,128)S(1)}, u32[]{:S(2)}, u32[]{:S(2)}) collective-permute-start(f32[392,128]{1,0:T(8,128)S(1)} %get-tuple-element.57), channel_id=1, source_target_pairs={{0,1},{1,0},{2,3},{3,2},{4,5},{5,4},{6,7},{7,6},{8,9},{9,8},{10,11... | collective-permute-start | bytes 602120 | tf_op jit(solution)/shard_map/ppermute | solution.py:412
  7.6 0.9 %collective-permute-start.6 = (f32[8,128]{1,0:T(8,128)S(1)}, f32[8,128]{1,0:T(8,128)S(1)}, u32[]{:S(2)}, u32[]{:S(2)}) collective-permute-start(f32[8,128]{1,0:T(8,128)S(1)} %bitcast.51), channel_id=1, source_target_pairs={{0,16},{8,24},{16,0},{24,8},{1,17},{9,25},{17,1},{25,9},{2,18},{10... | collective-permute-start | bytes 12296 | tf_op jit(solution)/shard_map/ppermute | solution.py:408
  8.4 4.5 %collective-permute-start.4 = (f32[1,1664]{1,0:T(1,128)S(1)}, f32[1,1664]{1,0:T(1,128)S(1)}, u32[]{:S(2)}, u32[]{:S(2)}) collective-permute-start(f32[1,1664]{1,0:T(1,128)S(1)} %get-tuple-element.58), channel_id=1, source_target_pairs={{0,2},{2,4},{4,6},{1,3},{3,5},{5,7},{8,10},{10,12},{12,14},{9,11},... | collective-permute-start | bytes 19976 | tf_op jit(solution)/shard_map/ppermute | solution.py:408
  13.0 8.9 %collective-permute-done.6.far_ref = f32[8,128]{1,0:T(8,128)S(1)} collective-permute-done((f32[8,128]{1,0:T(8,128)S(1)}, f32[8,128]{1,0:T(8,128)S(1)}, u32[]{:S(2)}, u32[]{:S(2)}) %collective-permute-start.6) | collective-permute-done | bytes 4128 | tf_op jit(solution)/shard_map/ppermute | solution.py:408
  21.9 3.4 %collective-permute-start.5 = (f32[1,1664]{1,0:T(1,128)S(1)}, f32[1,1664]{1,0:T(1,128)S(1)}, u32[]{:S(2)}, u32[]{:S(2)}) collective-permute-start(f32[1,1664]{1,0:T(1,128)S(1)} %get-tuple-element.59), channel_id=1, source_target_pairs={{2,0},{4,2},{6,4},{3,1},{5,3},{7,5},{10,8},{12,10},{14,12},{11,9},... | collective-permute-start | bytes 19976 | tf_op jit(solution)/shard_map/ppermute | solution.py:408
  25.3 0.0 copy-start.6
  25.3 0.0 copy-start.7
  25.3 0.0 copy-start.8
  25.3 0.0 copy-done.1
  25.3 0.0 copy-done.5
  25.3 0.6 %copy-done.6 = f32[48]{0:T(128)S(1)} copy-done((f32[48]{0:T(128)S(1)}, f32[48]{0:T(128)}, u32[]{:S(2)}) %copy-start.6) | copy-done | bytes 216
  26.0 0.0 copy-done.7
  26.0 0.0 copy-done.8
  26.0 1.6 %shard_map.93 = (f32[1536,128]{1,0:T(8,128)S(1)}, bf16[256,512]{1,0:T(8,128)(2,1)S(1)}, bf16[256,512]{1,0:T(8,128)(2,1)S(1)}, bf16[256,512]{1,0:T(8,128)(2,1)S(1)}, bf16[256,512]{1,0:T(8,128)(2,1)S(1)}) custom-call(f32[1536,128]{1,0:T(8,128)S(1)} %bitcast.28, bf16[192,8,128]{2,1,0:T(8,128)(2,1)S(1)} %bitcast.31, f32[3,8,128]{2,1,0:T(8,128)S(1)} %bitcast.34, ...), custom_call_target="tpu_custom_call" | custom-call | flops 8000000 | bytes 800000 | tf_op jit(solution)/shard_map/pallas_call | solution.py:395
  27.6 0.0 collective-permute-done.4.radlo_ref
  27.6 0.1 collective-permute-done.5.radhi_ref
  27.7 0.0 collective-permute-done.3.ax_ref
  27.7 0.0 collective-permute-done.2.above_ref
  27.7 2.3 %shard_map.95 = (f32[1536,128]{1,0:T(8,128)S(1)}, f32[4,8,128]{2,1,0:T(8,128)S(1)}, f32[480,128]{1,0:T(8,128)S(1)}, f32[8,128]{1,0:T(8,128)S(1)}, bf16[256,512]{...) custom-call(s32[1]{0:T(128)} %bitcast.9.where_ref, ...), custom_call_target="tpu_custom_call" | custom-call | flops 4000000 | bytes 400000 | tf_op jit(solution)/shard_map/pallas_call | solution.py:395
  30.0 1.2 %collective-permute-start.8 = (f32[480,128]{1,0:T(8,128)S(1)}, f32[480,128]{1,0:T(8,128)S(1)}, u32[]{:S(2)}, u32[]{:S(2)}) collective-permute-start(f32[480,128]{1,0:T(8,128)S(1)} %get-tuple-element.68), channel_id=1, source_target_pairs={{0,8},{8,16},{16,24},{24,0},{1,9},{9,17},{17,25},{25,1},{2,10},{10... | collective-permute-start | bytes 737288 | tf_op jit(solution)/shard_map/ppermute | solution.py:408
  31.2 0.0 collective-permute-done.7.below_ref
  31.2 1.2 %shard_map.96 = (f32[1536,128]{1,0:T(8,128)S(1)}, f32[480,128]{1,0:T(8,128)S(1)}, f32[384,128]{1,0:T(8,128)S(1)}, f32[1,1536]{1,0:T(1,128)S(1)}, f32[1,1536]{1,0:T(1,128)S(1)}, /*index=5*/f32[8,128]{1,0:T(8,128)S(1)}) custom-call(s32[1]{0:T(128)} %bitcast.9.where_ref, f32[1536,128]{1,0:T(8,128)S(1)} %get-tuple-element.60.part_ref, ...), custom_call_target="tpu_custom_call" | custom-call | flops 4000000 | bytes 400000 | tf_op jit(solution)/shard_map/pallas_call | solution.py:395
  32.4 2.6 %collective-permute-start.12 = (f32[480,128]{1,0:T(8,128)S(1)}, f32[480,128]{1,0:T(8,128)S(1)}, u32[]{:S(2)}, u32[]{:S(2)}) collective-permute-start(f32[480,128]{1,0:T(8,128)S(1)} %get-tuple-element.75), channel_id=1, source_target_pairs={{0,24},{8,0},{16,8},{24,16},{1,25},{9,1},{17,9},{25,17},{2,26},{10... | collective-permute-start | bytes 737288 | tf_op jit(solution)/shard_map/ppermute | solution.py:408
  35.1 1.3 %collective-permute-start.9 = (f32[384,128]{1,0:T(8,128)S(1)}, f32[384,128]{1,0:T(8,128)S(1)}, u32[]{:S(2)}, u32[]{:S(2)}) collective-permute-start(f32[384,128]{1,0:T(8,128)S(1)} %get-tuple-element.69), channel_id=1, source_target_pairs={{0,1},{1,0},{2,3},{3,2},{4,5},{5,4},{6,7},{7,6},{8,9},{9,8},{10,11... | collective-permute-start | bytes 589832 | tf_op jit(solution)/shard_map/ppermute | solution.py:412
  36.3 3.5 %collective-permute-start.10 = (f32[1,1536]{1,0:T(1,128)S(1)}, f32[1,1536]{1,0:T(1,128)S(1)}, u32[]{:S(2)}, u32[]{:S(2)}) collective-permute-start(f32[1,1536]{1,0:T(1,128)S(1)} %get-tuple-element.70), channel_id=1, source_target_pairs={{0,2},{2,4},{4,6},{1,3},{3,5},{5,7},{8,10},{10,12},{12,14},{9,11},... | collective-permute-start | bytes 18440 | tf_op jit(solution)/shard_map/ppermute | solution.py:408
  39.9 1.9 %collective-permute-start.11 = (f32[1,1536]{1,0:T(1,128)S(1)}, f32[1,1536]{1,0:T(1,128)S(1)}, u32[]{:S(2)}, u32[]{:S(2)}) collective-permute-start(f32[1,1536]{1,0:T(1,128)S(1)} %get-tuple-element.71), channel_id=1, source_target_pairs={{2,0},{4,2},{6,4},{3,1},{5,3},{7,5},{10,8},{12,10},{14,12},{11,9},... | collective-permute-start | bytes 18440 | tf_op jit(solution)/shard_map/ppermute | solution.py:408
  41.8 0.5 %slice.25 = f32[1,1]{1,0:T(1,128)} slice(f32[8,128]{1,0:T(8,128)S(1)} %get-tuple-element.66), slice={[0:1], [0:1]} | slice | bytes 8 | tf_op jit(solution)/shard_map/slice | solution.py:541
  43.0 0.0 copy-done.2
  43.0 1.4 %shard_map.97.part_ref = f32[1536,128]{1,0:T(8,128)S(1)} custom-call(f32[1536,128]{1,0:T(8,128)S(1)} %get-tuple-element.67.m_ref, f32[1536,128]{1,0:T(8,128)S(1)} %bitcast.30, bf16[192,8,128]{2,1,0:T(8,128)(2,1)S(1)} %bitcast.32, f32[4,8,128]{2,1,0:T(8,128)S(1)} %get-tuple-element.62.edge_ref, f32[3,8,128]{2,1,0:T(8,128)S(1)} %bitcast.36, ...), custom_call_target="tpu_custom_call" | custom-call | flops 8000000 | bytes 800000 | tf_op jit(solution)/shard_map/pallas_call | solution.py:395
  44.4 0.0 collective-permute-done.10.radlo_ref
  44.4 0.6 %collective-permute-done.11.radhi_ref = f32[1,1536]{1,0:T(1,128)S(1)} collective-permute-done((f32[1,1536]{1,0:T(1,128)S(1)}, f32[1,1536]{1,0:T(1,128)S(1)}, u32[]{:S(2)}, u32[]{:S(2)}) %collective-permute-start.11) | collective-permute-done | bytes 6176 | tf_op jit(solution)/shard_map/ppermute | solution.py:408
  45.0 0.0 collective-permute-done.9.ax_ref
  45.1 0.0 collective-permute-done.8.below_ref
  45.1 2.0 %shard_map.98 = (f32[1536,128]{1,0:T(8,128)S(1)}, f32[1536,128]{1,0:T(8,128)S(1)}) custom-call(s32[1]{0:T(128)} %bitcast.9.where_ref, f32[1536,128]{1,0:T(8,128)S(1)} %shard_map.97.part_ref, f32[480,128]{1,0:T(8,128)S(1)} %collective-permute-done.8.below_ref, f32[384,128]{1,0:T(8,128)S(1)} %collective-permute-done.9.ax_ref, ...), custom_call_target="tpu_custom_call" | custom-call | flops 4000000 | bytes 400000 | tf_op jit(solution)/shard_map/pallas_call | solution.py:395
  47.0 0.0 collective-permute-done.12
  47.0 0.5 %conditional.1 = (f32[4,48,2,4,128]{4,3,2,1,0:T(4,128)S(1)}) conditional(s32[]{:T(128)} %bitcast.18, (f32[1536,128]{1,0:T(8,128)S(1)}, f32[480,128]{1,0:T(8,128)S(1)}, f32[4,8,128]{2,1,0:T(8,128)S(1)}, bf16[256,512]{1,0:T(8,128)(2,1)S(1)}, bf16[256,512]{1,0:T(8,128)(2,1)S(1)}) %tuple.13, (f32[4,8,128]{2,1,0:T(8,128)S(1)}, f32[1536,128]{1,0:T(8,128)S(1)}, ...), branch_computations={%region_0.0_spmd, %region_1.0_spmd} | conditional | flops 1000000 | bytes 8663128 | solution.py:544
  47.0 0.5 %branch_0_fun.1 = f32[1536,128]{1,0:T(8,128)S(1)} custom-call(f32[1536,128]{1,0:T(8,128)S(1)} %get-tuple-element.25.full_ref, f32[480,128]{1,0:T(8,128)S(1)} %get-tuple-element.26.above_ref, f32[4,8,128]{2,1,0:T(8,128)S(1)} %get-tuple-element.27.edge_ref, bf16[256,512]{1,0:T(8,128)(2,1)S(1)} %get-tuple-element.28.low_ref, ...), custom_call_target="tpu_custom_call" | custom-call | flops 1000000 | bytes 100000 | tf_op jit(solution)/shard_map/cond/branch_0_fun/pallas_call | solution.py:395
  47.6 0.0 copy-start.9
  47.6 0.9 %copy-done.9 = f32[4,48,2,4,128]{4,3,2,1,0:T(4,128)} copy-done((f32[4,48,2,4,128]{4,3,2,1,0:T(4,128)}, f32[4,48,2,4,128]{4,3,2,1,0:T(4,128)S(1)}, u32[]{:S(2)}) %copy-start.9) | copy-done | bytes 786456
  (5 shorter events, 0.0 us)
Async XLA Ops:
  0.0 5.3 %copy-start = (f32[4,48,2,4,128]{4,3,2,1,0:T(4,128)S(1)}, f32[4,48,2,4,128]{4,3,2,1,0:T(4,128)}, u32[]{:S(2)}) copy-start(f32[4,48,2,4,128]{4,3,2,1,0:T(4,128)} %param.11) | copy-start | bytes 2359300
  0.0 5.3 %copy-start.4 = (s32[3,2,4,128]{3,2,1,0:T(4,128)S(1)}, s32[3,2,4,128]{3,2,1,0:T(4,128)}, u32[]{:S(2)}) copy-start(s32[3,2,4,128]{3,2,1,0:T(4,128)} %param.15) | copy-start | bytes 36868
  1.1 4.2 %copy-start.3 = (f32[3,2,4,128]{3,2,1,0:T(4,128)S(1)}, f32[3,2,4,128]{3,2,1,0:T(4,128)}, u32[]{:S(2)}) copy-start(f32[3,2,4,128]{3,2,1,0:T(4,128)} %param.14) | copy-start | bytes 36868
  1.1 26.6 %collective-permute-start.2 = (f32[776,128]{1,0:T(8,128)S(1)}, f32[776,128]{1,0:T(8,128)S(1)}, u32[]{:S(2)}, u32[]{:S(2)}) collective-permute-start(f32[776,128]{1,0:T(8,128)S(1)} %bitcast.47), channel_id=1, source_target_pairs={{0,24},{8,0},{16,8},{24,16},{1,25},{9,1},{17,9},{25,17},{2,26},{10... | collective-permute-start | bytes 1191944 | tf_op jit(solution)/shard_map/ppermute | solution.py:408
  5.3 20.0 %copy-start.1 = (bf16[4,48,2,4,128]{4,3,2,1,0:T(4,128)(2,1)S(1)}, bf16[4,48,2,4,128]{4,3,2,1,0:T(4,128)(2,1)}, u32[]{:S(2)}) copy-start(bf16[4,48,2,4,128]{4,3,2,1,0:T(4,128)(2,1)} %param.13) | copy-start | bytes 1179652
  6.2 25.0 %collective-permute-start.7 = (f32[776,128]{1,0:T(8,128)S(1)}, f32[776,128]{1,0:T(8,128)S(1)}, u32[]{:S(2)}, u32[]{:S(2)}) collective-permute-start(f32[776,128]{1,0:T(8,128)S(1)} %get-tuple-element.61), channel_id=1, source_target_pairs={{0,8},{8,16},{16,24},{24,0},{1,9},{9,17},{17,25},{25,1},{2,10},{10... | collective-permute-start | bytes 1191944 | tf_op jit(solution)/shard_map/ppermute | solution.py:408
  6.3 21.4 %collective-permute-start.3 = (f32[392,128]{1,0:T(8,128)S(1)}, f32[392,128]{1,0:T(8,128)S(1)}, u32[]{:S(2)}, u32[]{:S(2)}) collective-permute-start(f32[392,128]{1,0:T(8,128)S(1)} %get-tuple-element.57), channel_id=1, source_target_pairs={{0,1},{1,0},{2,3},{3,2},{4,5},{5,4},{6,7},{7,6},{8,9},{9,8},{10,11... | collective-permute-start | bytes 602120 | tf_op jit(solution)/shard_map/ppermute | solution.py:412
  7.6 17.8 %copy-start.5 = (s32[2,4,128]{2,1,0:T(4,128)S(1)}, s32[2,4,128]{2,1,0:T(4,128)}, u32[]{:S(2)}) copy-start(s32[2,4,128]{2,1,0:T(4,128)} %param.16) | copy-start | bytes 12292
  7.6 14.3 %collective-permute-start.6 = (f32[8,128]{1,0:T(8,128)S(1)}, f32[8,128]{1,0:T(8,128)S(1)}, u32[]{:S(2)}, u32[]{:S(2)}) collective-permute-start(f32[8,128]{1,0:T(8,128)S(1)} %bitcast.51), channel_id=1, source_target_pairs={{0,16},{8,24},{16,0},{24,8},{1,17},{9,25},{17,1},{25,9},{2,18},{10... | collective-permute-start | bytes 12296 | tf_op jit(solution)/shard_map/ppermute | solution.py:408
  8.4 19.2 %collective-permute-start.4 = (f32[1,1664]{1,0:T(1,128)S(1)}, f32[1,1664]{1,0:T(1,128)S(1)}, u32[]{:S(2)}, u32[]{:S(2)}) collective-permute-start(f32[1,1664]{1,0:T(1,128)S(1)} %get-tuple-element.58), channel_id=1, source_target_pairs={{0,2},{2,4},{4,6},{1,3},{3,5},{5,7},{8,10},{10,12},{12,14},{9,11},... | collective-permute-start | bytes 19976 | tf_op jit(solution)/shard_map/ppermute | solution.py:408
  21.9 5.8 %collective-permute-start.5 = (f32[1,1664]{1,0:T(1,128)S(1)}, f32[1,1664]{1,0:T(1,128)S(1)}, u32[]{:S(2)}, u32[]{:S(2)}) collective-permute-start(f32[1,1664]{1,0:T(1,128)S(1)} %get-tuple-element.59), channel_id=1, source_target_pairs={{2,0},{4,2},{6,4},{3,1},{5,3},{7,5},{10,8},{12,10},{14,12},{11,9},... | collective-permute-start | bytes 19976 | tf_op jit(solution)/shard_map/ppermute | solution.py:408
  25.3 0.7 %copy-start.6 = (f32[48]{0:T(128)S(1)}, f32[48]{0:T(128)}, u32[]{:S(2)}) copy-start(f32[48]{0:T(128)} %growth_ref.3) | copy-start | bytes 580
  25.3 0.7 %copy-start.7 = (f32[48]{0:T(128)S(1)}, f32[48]{0:T(128)}, u32[]{:S(2)}) copy-start(f32[48]{0:T(128)} %transfer_ref.3) | copy-start | bytes 580
  25.3 0.7 %copy-start.8 = (f32[4]{0:T(128)S(1)}, f32[4]{0:T(128)}, u32[]{:S(2)}) copy-start(f32[4]{0:T(128)} %rate_ref.3) | copy-start | bytes 52
  30.0 15.1 %collective-permute-start.8 = (f32[480,128]{1,0:T(8,128)S(1)}, f32[480,128]{1,0:T(8,128)S(1)}, u32[]{:S(2)}, u32[]{:S(2)}) collective-permute-start(f32[480,128]{1,0:T(8,128)S(1)} %get-tuple-element.68), channel_id=1, source_target_pairs={{0,8},{8,16},{16,24},{24,0},{1,9},{9,17},{17,25},{25,1},{2,10},{10... | collective-permute-start | bytes 737288 | tf_op jit(solution)/shard_map/ppermute | solution.py:408
  31.2 11.8 %copy-start.2 = (bf16[4,48,2,4,128]{4,3,2,1,0:T(4,128)(2,1)S(1)}, bf16[4,48,2,4,128]{4,3,2,1,0:T(4,128)(2,1)}, u32[]{:S(2)}) copy-start(bf16[4,48,2,4,128]{4,3,2,1,0:T(4,128)(2,1)} %param.12) | copy-start | bytes 1179652
  32.4 14.6 %collective-permute-start.12 = (f32[480,128]{1,0:T(8,128)S(1)}, f32[480,128]{1,0:T(8,128)S(1)}, u32[]{:S(2)}, u32[]{:S(2)}) collective-permute-start(f32[480,128]{1,0:T(8,128)S(1)} %get-tuple-element.75), channel_id=1, source_target_pairs={{0,24},{8,0},{16,8},{24,16},{1,25},{9,1},{17,9},{25,17},{2,26},{10... | collective-permute-start | bytes 737288 | tf_op jit(solution)/shard_map/ppermute | solution.py:408
  35.1 10.0 %collective-permute-start.9 = (f32[384,128]{1,0:T(8,128)S(1)}, f32[384,128]{1,0:T(8,128)S(1)}, u32[]{:S(2)}, u32[]{:S(2)}) collective-permute-start(f32[384,128]{1,0:T(8,128)S(1)} %get-tuple-element.69), channel_id=1, source_target_pairs={{0,1},{1,0},{2,3},{3,2},{4,5},{5,4},{6,7},{7,6},{8,9},{9,8},{10,11... | collective-permute-start | bytes 589832 | tf_op jit(solution)/shard_map/ppermute | solution.py:412
  36.3 8.0 %collective-permute-start.10 = (f32[1,1536]{1,0:T(1,128)S(1)}, f32[1,1536]{1,0:T(1,128)S(1)}, u32[]{:S(2)}, u32[]{:S(2)}) collective-permute-start(f32[1,1536]{1,0:T(1,128)S(1)} %get-tuple-element.70), channel_id=1, source_target_pairs={{0,2},{2,4},{4,6},{1,3},{3,5},{5,7},{8,10},{10,12},{12,14},{9,11},... | collective-permute-start | bytes 18440 | tf_op jit(solution)/shard_map/ppermute | solution.py:408
  39.9 5.2 %collective-permute-start.11 = (f32[1,1536]{1,0:T(1,128)S(1)}, f32[1,1536]{1,0:T(1,128)S(1)}, u32[]{:S(2)}, u32[]{:S(2)}) collective-permute-start(f32[1,1536]{1,0:T(1,128)S(1)} %get-tuple-element.71), channel_id=1, source_target_pairs={{2,0},{4,2},{6,4},{3,1},{5,3},{7,5},{10,8},{12,10},{14,12},{11,9},... | collective-permute-start | bytes 18440 | tf_op jit(solution)/shard_map/ppermute | solution.py:408
  47.6 0.9 %copy-start.9 = (f32[4,48,2,4,128]{4,3,2,1,0:T(4,128)}, f32[4,48,2,4,128]{4,3,2,1,0:T(4,128)S(1)}, u32[]{:S(2)}) copy-start(f32[4,48,2,4,128]{4,3,2,1,0:T(4,128)S(1)} %get-tuple-element.103) | copy-start | bytes 2359300

commit v8 on v7

--- a/solution.py
+++ b/solution.py
@@ -302,7 +302,6 @@
     ax_ref,
     radlo_ref,
     radhi_ref,
-    far_ref,
     speeds_ref,
     flags_ref,
     m_ref,
@@ -319,7 +318,7 @@
     upper = above_ref[4 * comps :]
     make_tables(upper, True, up_low_ref, up_high_ref)
     make_tables(upper, False, dn_low_ref, dn_high_ref)
-    bad_ref[...] = crowded(p[0]) + crowded(upper) + crowded(far_ref[...])
+    bad_ref[...] = crowded(p[0]) + crowded(upper)
     hrad = put_columns(radlo_ref[...], radhi_ref[...])
     lower_half = where_ref[0] == 0
     p_azim = jnp.where(row >= 4, pltpu.roll(upper, 4, 0), 0.0)
@@ -363,6 +362,7 @@
         m_ref[8 * c : 8 * c + 8] = part_ref[8 * c : 8 * c + 8] + azim * from_below(c, below_ref)
     encode(comps, m_ref, 0, low_ref, high_ref, dn_ref)
     worse_ref[...] = bad_ref[...] + crowded(below_ref[4 * comps :])
+    dn_ref[5 * comps // 2 :] = worse_ref[...]
     pack_sides(comps, m_ref, where_ref, ax_ref, radup_ref, raddn_ref)
 
 
@@ -379,7 +379,8 @@
     add_azimuthal(comps, decode(comps, below_ref, low_ref, high_ref), edge_ref[0], 0, full_ref)
 
 
-def second_top(comps, full_ref, above_ref, edge_ref, low_ref, high_ref, out_ref):
+def second_top(comps, full_ref, above_ref, edge_ref, bad_ref, low_ref, high_ref, out_ref, again_ref):
+    again_ref[0] = (jnp.max(bad_ref[...] + above_ref[5 * comps // 2 :]) > 0.0).astype(jnp.int32)
     out_ref[...] = full_ref[...]
     add_azimuthal(comps, decode(comps, above_ref, low_ref, high_ref), edge_ref[0], 4, out_ref)
 
@@ -446,7 +447,6 @@
         flags2,
     )
     below = shift(up, "azim", 1, True)
-    far = shift(speeds2[0] * flags2[0].astype(f32), "azim", 2, True)
     edges = sides(*edges)
     part, *lower_tables = call(
         functools.partial(first_local, sections),
@@ -462,7 +462,7 @@
     )
     part, edge, up, bad, *upper_tables = call(
         functools.partial(first_top, comps),
-        "s" + "v" * 9,
+        "s" + "v" * 8,
         "v" * 8,
         [(cells, 128), (4, 8, 128), (message, 128), (8, 128)] + 2 * tables,
         4_000_000,
@@ -471,7 +471,6 @@
         a,
         above,
         *edges,
-        far,
         speeds2,
         flags2,
     )
@@ -480,7 +479,7 @@
         functools.partial(first_bottom, comps),
         "s" + "v" * 6,
         "v" * 6,
-        [(cells, 128), (message, 128), (rows, 128), (1, cells), (1, cells), (8, 128)],
+        [(cells, 128), (message + 8, 128), (rows, 128), (1, cells), (1, cells), (8, 128)],
         4_000_000,
         where,
         part,
@@ -519,29 +518,28 @@
         *lower_tables[2:],
     )
 
-    def quick():
-        (out,) = call(
-            functools.partial(second_top, comps),
-            "vvvvv",
-            "v",
-            [(cells, 128)],
-            1_000_000,
-            full,
-            next_above,
-            edge,
-            *upper_tables[:2],
-        )
-        return out
+    out, again = call(
+        functools.partial(second_top, comps),
+        "vvvvvv",
+        "vs",
+        [(cells, 128), jax.ShapeDtypeStruct((1,), jnp.int32)],
+        1_000_000,
+        full,
+        next_above,
+        edge,
+        bad,
+        *upper_tables[:2],
+    )
 
     def whole():
         rows_ = m.reshape(comps, 2, 4, 128)
         halo = jnp.stack([shift(rows_[:, 1], "azim", 1, True), shift(rows_[:, 0], "azim", -1, True)], axis=1)
         return base + (edge[0].reshape(1, 2, 4, 128) * halo).reshape(cells, 128)
 
-    worst = bad[0, 0]
+    again = again[0]
     if lax.axis_size("azim") != 4:
-        worst = lax.pmax(worst, "azim")
-    return lax.cond(worst > 0.0, whole, quick).reshape(shape)
+        again = lax.pmax(again.astype(f32), "azim").astype(jnp.int32)
+    return lax.cond(again > 0, whole, lambda: out).reshape(shape)
 
 
 def solution(mesh):

time: 48.7 us -> 44.6 us (0.916)
  the two profiles are of different devices: /device:TPU:1 before, /device:TPU:0 now
where the time goes in v8:
time: 44.6 us; the launch traced here: 44.3 us
  starting transfers between devices  16.6 us (37%)
  waiting for transfers between devices  13.9 us (31%)
  Pallas kernels  10.3 us (23%)
  local copies, waits for them, and re-layouts  1.55 us (3%)
  other arithmetic  1.1 us (2%)
  between operations  0.84 us (2%)
    ppermute x8, waiting for transfers between devices, shift(): return lax.ppermute(x, axis, pairs)  13.9 us
    ppermute x8, starting transfers between devices, shift(): return lax.ppermute(x, axis, pairs)  13.5 us
    pallas_call x7, Pallas kernels, call(): pl.pallas_call(body, in_specs=[SPACES[s] for s in ins], out_specs=[SPACES...  10.3 us
    ppermute x2, starting transfers between devices, sides(): ax = lax.ppermute(ax, 'axial', [(0, 1), (1, 0)])  3.12 us
    unnamed x20, local copies, waits for them, and re-layouts  1.55 us
    add x1, other arithmetic, shards(): dn = dn + lax.pad(speeds, 0.0, after) * lax.pad(flags, 0, after).astype(f32)  1.1 us
  transfers between devices with their start and end apart: 10, of which 5 were waited for; matrix products, arithmetic and copies ran while one was open for 0% of the time, Pallas kernels for 18%

profile of v8, /device:TPU:0, one launch (start us, length us, event | category | flops | bytes accessed | tf_op | source)
XLA Modules:
  0.0 44.3 jit_solution(1739236521135316179)
XLA Ops:
  0.0 0.0 copy-start
  0.0 0.0 copy-start.4
  0.0 1.1 %fusion = f32[194,1,4,128]{3,2,1,0:T(4,128)S(1)} fusion(f32[192,2,4,128]{3,2,1,0:T(4,128)} %bitcast.25, f32[3,2,4,128]{3,2,1,0:T(4,128)} %param.14, s32[3,2,4,128]{3,2,1,0:T(4,128)} %param.15), kind=kLoop, calls=%fused_computation.6 | loop fusion | flops 297984 | bytes 1208320 | tf_op jit(solution)/shard_map/add | solution.py:436
  1.1 0.0 copy-start.3
  1.1 5.1 %collective-permute-start.2 = (f32[776,128]{1,0:T(8,128)S(1)}, f32[776,128]{1,0:T(8,128)S(1)}, u32[]{:S(2)}, u32[]{:S(2)}) collective-permute-start(f32[776,128]{1,0:T(8,128)S(1)} %bitcast.44), channel_id=1, source_target_pairs={{0,24},{8,0},{16,8},{24,16},{1,25},{9,1},{17,9},{25,17},{2,26},{10... | collective-permute-start | bytes 1191944 | tf_op jit(solution)/shard_map/ppermute | solution.py:409
  6.2 0.0 copy-done
  6.2 0.0 copy-done.4
  6.2 0.0 copy-done.3
  6.2 0.0 copy-start.1
  6.2 0.8 %shard_map.94 = (f32[776,128]{1,0:T(8,128)S(1)}, f32[392,128]{1,0:T(8,128)S(1)}, f32[1,1664]{1,0:T(1,128)S(1)}, f32[1,1664]{1,0:T(1,128)S(1)}) custom-call(s32[1]{0:T(128)} %bitcast.9.where_ref, f32[1536,128]{1,0:T(8,128)S(1)} %bitcast.26, f32[3,8,128]{2,1,0:T(8,128)S(1)} %bitcast.32, s32[3,8,128]{2,1,0:T(8,128)S(1)} %bitcast.36), custom_call_target="tpu_custom_call" | custom-call | flops 2000000 | bytes 200000 | tf_op jit(solution)/shard_map/pallas_call | solution.py:396
  7.1 0.1 collective-permute-start.6
  7.2 0.0 copy-start.5
  7.2 1.6 %collective-permute-start.3 = (f32[392,128]{1,0:T(8,128)S(1)}, f32[392,128]{1,0:T(8,128)S(1)}, u32[]{:S(2)}, u32[]{:S(2)}) collective-permute-start(f32[392,128]{1,0:T(8,128)S(1)} %get-tuple-element.46), channel_id=1, source_target_pairs={{0,1},{1,0},{2,3},{3,2},{4,5},{5,4},{6,7},{7,6},{8,9},{9,8},{10,11... | collective-permute-start | bytes 602120 | tf_op jit(solution)/shard_map/ppermute | solution.py:413
  8.7 1.3 %collective-permute-start.4 = (f32[1,1664]{1,0:T(1,128)S(1)}, f32[1,1664]{1,0:T(1,128)S(1)}, u32[]{:S(2)}, u32[]{:S(2)}) collective-permute-start(f32[1,1664]{1,0:T(1,128)S(1)} %get-tuple-element.47), channel_id=1, source_target_pairs={{0,2},{2,4},{4,6},{1,3},{3,5},{5,7},{8,10},{10,12},{12,14},{9,11},... | collective-permute-start | bytes 19976 | tf_op jit(solution)/shard_map/ppermute | solution.py:409
  10.0 1.3 %collective-permute-start.5 = (f32[1,1664]{1,0:T(1,128)S(1)}, f32[1,1664]{1,0:T(1,128)S(1)}, u32[]{:S(2)}, u32[]{:S(2)}) collective-permute-start(f32[1,1664]{1,0:T(1,128)S(1)} %get-tuple-element.48), channel_id=1, source_target_pairs={{2,0},{4,2},{6,4},{3,1},{5,3},{7,5},{10,8},{12,10},{14,12},{11,9},... | collective-permute-start | bytes 19976 | tf_op jit(solution)/shard_map/ppermute | solution.py:409
  11.3 0.0 copy-start.6
  11.3 0.0 copy-start.7
  11.4 0.0 copy-start.8
  11.4 0.0 copy-done.1
  11.4 0.0 copy-done.5
  11.4 0.6 %copy-done.6 = f32[48]{0:T(128)S(1)} copy-done((f32[48]{0:T(128)S(1)}, f32[48]{0:T(128)}, u32[]{:S(2)}) %copy-start.6) | copy-done | bytes 216
  12.0 0.0 copy-done.7
  12.0 0.0 copy-done.8
  12.0 1.6 %shard_map.93 = (f32[1536,128]{1,0:T(8,128)S(1)}, bf16[256,512]{1,0:T(8,128)(2,1)S(1)}, bf16[256,512]{1,0:T(8,128)(2,1)S(1)}, bf16[256,512]{1,0:T(8,128)(2,1)S(1)}, bf16[256,512]{1,0:T(8,128)(2,1)S(1)}) custom-call(f32[1536,128]{1,0:T(8,128)S(1)} %bitcast.27, bf16[192,8,128]{2,1,0:T(8,128)(2,1)S(1)} %bitcast.30, f32[3,8,128]{2,1,0:T(8,128)S(1)} %bitcast.33, ...), custom_call_target="tpu_custom_call" | custom-call | flops 8000000 | bytes 800000 | tf_op jit(solution)/shard_map/pallas_call | solution.py:396
  13.6 0.0 collective-permute-done.4.radlo_ref
  13.6 1.2 %collective-permute-done.5.radhi_ref = f32[1,1664]{1,0:T(1,128)S(1)} collective-permute-done((f32[1,1664]{1,0:T(1,128)S(1)}, f32[1,1664]{1,0:T(1,128)S(1)}, u32[]{:S(2)}, u32[]{:S(2)}) %collective-permute-start.5) | collective-permute-done | bytes 6688 | tf_op jit(solution)/shard_map/ppermute | solution.py:409
  14.8 0.0 collective-permute-done.3.ax_ref
  14.8 1.0 %collective-permute-done.2.above_ref = f32[776,128]{1,0:T(8,128)S(1)} collective-permute-done((f32[776,128]{1,0:T(8,128)S(1)}, f32[776,128]{1,0:T(8,128)S(1)}, u32[]{:S(2)}, u32[]{:S(2)}) %collective-permute-start.2) | collective-permute-done | bytes 397344 | tf_op jit(solution)/shard_map/ppermute | solution.py:409
  15.8 2.3 %shard_map.95 = (f32[1536,128]{1,0:T(8,128)S(1)}, f32[4,8,128]{2,1,0:T(8,128)S(1)}, f32[480,128]{1,0:T(8,128)S(1)}, f32[8,128]{1,0:T(8,128)S(1)}, bf16[256,512]{...) custom-call(s32[1]{0:T(128)} %bitcast.9.where_ref, ...), custom_call_target="tpu_custom_call" | custom-call | flops 4000000 | bytes 400000 | tf_op jit(solution)/shard_map/pallas_call | solution.py:396
  18.1 6.0 %collective-permute-done.6.below_ref = f32[776,128]{1,0:T(8,128)S(1)} collective-permute-done((f32[776,128]{1,0:T(8,128)S(1)}, f32[776,128]{1,0:T(8,128)S(1)}, u32[]{:S(2)}, u32[]{:S(2)}) %collective-permute-start.6) | collective-permute-done | bytes 397344 | tf_op jit(solution)/shard_map/ppermute | solution.py:409
  24.1 0.0 copy-start.2
  24.1 1.3 %shard_map.96 = (f32[1536,128]{1,0:T(8,128)S(1)}, f32[488,128]{1,0:T(8,128)S(1)}, f32[384,128]{1,0:T(8,128)S(1)}, f32[1,1536]{1,0:T(1,128)S(1)}, f32[1,1536]{1,0:T(1,128)S(1)}, /*index=5*/f32[8,128]{1,0:T(8,128)S(1)}) custom-call(s32[1]{0:T(128)} %bitcast.9.where_ref, f32[1536,128]{1,0:T(8,128)S(1)} %get-tuple-element.49.part_ref, ...), custom_call_target="tpu_custom_call" | custom-call | flops 4000000 | bytes 400000 | tf_op jit(solution)/shard_map/pallas_call | solution.py:396
  25.4 3.2 %collective-permute-start.11 = (f32[488,128]{1,0:T(8,128)S(1)}, f32[488,128]{1,0:T(8,128)S(1)}, u32[]{:S(2)}, u32[]{:S(2)}) collective-permute-start(f32[488,128]{1,0:T(8,128)S(1)} %get-tuple-element.63), channel_id=1, source_target_pairs={{0,24},{8,0},{16,8},{24,16},{1,25},{9,1},{17,9},{25,17},{2,26},{10... | collective-permute-start | bytes 749576 | tf_op jit(solution)/shard_map/ppermute | solution.py:409
  28.5 0.0 collective-permute-start.7
  28.5 1.5 %collective-permute-start.8 = (f32[384,128]{1,0:T(8,128)S(1)}, f32[384,128]{1,0:T(8,128)S(1)}, u32[]{:S(2)}, u32[]{:S(2)}) collective-permute-start(f32[384,128]{1,0:T(8,128)S(1)} %get-tuple-element.57), channel_id=1, source_target_pairs={{0,1},{1,0},{2,3},{3,2},{4,5},{5,4},{6,7},{7,6},{8,9},{9,8},{10,11... | collective-permute-start | bytes 589832 | tf_op jit(solution)/shard_map/ppermute | solution.py:413
  30.1 1.3 %collective-permute-start.9 = (f32[1,1536]{1,0:T(1,128)S(1)}, f32[1,1536]{1,0:T(1,128)S(1)}, u32[]{:S(2)}, u32[]{:S(2)}) collective-permute-start(f32[1,1536]{1,0:T(1,128)S(1)} %get-tuple-element.58), channel_id=1, source_target_pairs={{0,2},{2,4},{4,6},{1,3},{3,5},{5,7},{8,10},{10,12},{12,14},{9,11},... | collective-permute-start | bytes 18440 | tf_op jit(solution)/shard_map/ppermute | solution.py:409
  31.4 1.3 %collective-permute-start.10 = (f32[1,1536]{1,0:T(1,128)S(1)}, f32[1,1536]{1,0:T(1,128)S(1)}, u32[]{:S(2)}, u32[]{:S(2)}) collective-permute-start(f32[1,1536]{1,0:T(1,128)S(1)} %get-tuple-element.59), channel_id=1, source_target_pairs={{2,0},{4,2},{6,4},{3,1},{5,3},{7,5},{10,8},{12,10},{14,12},{11,9},... | collective-permute-start | bytes 18440 | tf_op jit(solution)/shard_map/ppermute | solution.py:409
  32.7 0.0 copy-done.2
  32.7 1.4 %shard_map.97.part_ref = f32[1536,128]{1,0:T(8,128)S(1)} custom-call(f32[1536,128]{1,0:T(8,128)S(1)} %get-tuple-element.55.m_ref, f32[1536,128]{1,0:T(8,128)S(1)} %bitcast.29, bf16[192,8,128]{2,1,0:T(8,128)(2,1)S(1)} %bitcast.31, f32[4,8,128]{2,1,0:T(8,128)S(1)} %get-tuple-element.51.edge_ref, f32[3,8,128]{2,1,0:T(8,128)S(1)} %bitcast.35, ...), custom_call_target="tpu_custom_call" | custom-call | flops 8000000 | bytes 800000 | tf_op jit(solution)/shard_map/pallas_call | solution.py:396
  34.1 0.0 collective-permute-done.9.radlo_ref
  34.1 2.0 %collective-permute-done.10.radhi_ref = f32[1,1536]{1,0:T(1,128)S(1)} collective-permute-done((f32[1,1536]{1,0:T(1,128)S(1)}, f32[1,1536]{1,0:T(1,128)S(1)}, u32[]{:S(2)}, u32[]{:S(2)}) %collective-permute-start.10) | collective-permute-done | bytes 6176 | tf_op jit(solution)/shard_map/ppermute | solution.py:409
  36.2 0.0 collective-permute-done.8.ax_ref
  36.2 3.7 %collective-permute-done.7.below_ref = f32[480,128]{1,0:T(8,128)S(1)} collective-permute-done((f32[480,128]{1,0:T(8,128)S(1)}, f32[480,128]{1,0:T(8,128)S(1)}, u32[]{:S(2)}, u32[]{:S(2)}) %collective-permute-start.7) | collective-permute-done | bytes 245792 | tf_op jit(solution)/shard_map/ppermute | solution.py:409
  39.8 2.0 %shard_map.98 = (f32[1536,128]{1,0:T(8,128)S(1)}, f32[1536,128]{1,0:T(8,128)S(1)}) custom-call(s32[1]{0:T(128)} %bitcast.9.where_ref, f32[1536,128]{1,0:T(8,128)S(1)} %shard_map.97.part_ref, f32[480,128]{1,0:T(8,128)S(1)} %collective-permute-done.7.below_ref, f32[384,128]{1,0:T(8,128)S(1)} %collective-permute-done.8.ax_ref, ...), custom_call_target="tpu_custom_call" | custom-call | flops 4000000 | bytes 400000 | tf_op jit(solution)/shard_map/pallas_call | solution.py:396
  41.8 0.0 collective-permute-done.11.above_ref
  41.8 1.0 %shard_map.99 = (f32[1536,128]{1,0:T(8,128)S(1)}, s32[1]{0:T(128)}) custom-call(f32[1536,128]{1,0:T(8,128)S(1)} %get-tuple-element.62.full_ref, f32[488,128]{1,0:T(8,128)S(1)} %collective-permute-done.11.above_ref, f32[4,8,128]{2,1,0:T(8,128)S(1)} %get-tuple-element.51.edge_ref, f32[8,128]{1,0:T(8,128)S(1)} %get-tuple-element.64.bad_ref, ...), custom_call_target="tpu_custom_call" | custom-call | flops 1000000 | bytes 100000 | tf_op jit(solution)/shard_map/pallas_call | solution.py:396
  43.4 0.0 copy-start.9
  43.5 0.9 %copy-done.9 = f32[4,48,2,4,128]{4,3,2,1,0:T(4,128)} copy-done((f32[4,48,2,4,128]{4,3,2,1,0:T(4,128)}, f32[4,48,2,4,128]{4,3,2,1,0:T(4,128)S(1)}, u32[]{:S(2)}) %copy-start.9) | copy-done | bytes 786456
  (1 shorter events, 0.0 us)
Async XLA Ops:
  0.0 6.2 %copy-start = (f32[4,48,2,4,128]{4,3,2,1,0:T(4,128)S(1)}, f32[4,48,2,4,128]{4,3,2,1,0:T(4,128)}, u32[]{:S(2)}) copy-start(f32[4,48,2,4,128]{4,3,2,1,0:T(4,128)} %param.11) | copy-start | bytes 2359300
  0.0 6.2 %copy-start.4 = (s32[3,2,4,128]{3,2,1,0:T(4,128)S(1)}, s32[3,2,4,128]{3,2,1,0:T(4,128)}, u32[]{:S(2)}) copy-start(s32[3,2,4,128]{3,2,1,0:T(4,128)} %param.15) | copy-start | bytes 36868
  1.1 5.1 %copy-start.3 = (f32[3,2,4,128]{3,2,1,0:T(4,128)S(1)}, f32[3,2,4,128]{3,2,1,0:T(4,128)}, u32[]{:S(2)}) copy-start(f32[3,2,4,128]{3,2,1,0:T(4,128)} %param.14) | copy-start | bytes 36868
  1.1 14.7 %collective-permute-start.2 = (f32[776,128]{1,0:T(8,128)S(1)}, f32[776,128]{1,0:T(8,128)S(1)}, u32[]{:S(2)}, u32[]{:S(2)}) collective-permute-start(f32[776,128]{1,0:T(8,128)S(1)} %bitcast.44), channel_id=1, source_target_pairs={{0,24},{8,0},{16,8},{24,16},{1,25},{9,1},{17,9},{25,17},{2,26},{10... | collective-permute-start | bytes 1191944 | tf_op jit(solution)/shard_map/ppermute | solution.py:409
  6.2 5.1 %copy-start.1 = (bf16[4,48,2,4,128]{4,3,2,1,0:T(4,128)(2,1)S(1)}, bf16[4,48,2,4,128]{4,3,2,1,0:T(4,128)(2,1)}, u32[]{:S(2)}) copy-start(bf16[4,48,2,4,128]{4,3,2,1,0:T(4,128)(2,1)} %param.13) | copy-start | bytes 1179652
  7.1 17.0 %collective-permute-start.6 = (f32[776,128]{1,0:T(8,128)S(1)}, f32[776,128]{1,0:T(8,128)S(1)}, u32[]{:S(2)}, u32[]{:S(2)}) collective-permute-start(f32[776,128]{1,0:T(8,128)S(1)} %get-tuple-element.50), channel_id=1, source_target_pairs={{0,8},{8,16},{16,24},{24,0},{1,9},{9,17},{17,25},{25,1},{2,10},{10... | collective-permute-start | bytes 1191944 | tf_op jit(solution)/shard_map/ppermute | solution.py:409
  7.2 4.2 %copy-start.5 = (s32[2,4,128]{2,1,0:T(4,128)S(1)}, s32[2,4,128]{2,1,0:T(4,128)}, u32[]{:S(2)}) copy-start(s32[2,4,128]{2,1,0:T(4,128)} %param.16) | copy-start | bytes 12292
  7.2 7.7 %collective-permute-start.3 = (f32[392,128]{1,0:T(8,128)S(1)}, f32[392,128]{1,0:T(8,128)S(1)}, u32[]{:S(2)}, u32[]{:S(2)}) collective-permute-start(f32[392,128]{1,0:T(8,128)S(1)} %get-tuple-element.46), channel_id=1, source_target_pairs={{0,1},{1,0},{2,3},{3,2},{4,5},{5,4},{6,7},{7,6},{8,9},{9,8},{10,11... | collective-permute-start | bytes 602120 | tf_op jit(solution)/shard_map/ppermute | solution.py:413
  8.7 4.9 %collective-permute-start.4 = (f32[1,1664]{1,0:T(1,128)S(1)}, f32[1,1664]{1,0:T(1,128)S(1)}, u32[]{:S(2)}, u32[]{:S(2)}) collective-permute-start(f32[1,1664]{1,0:T(1,128)S(1)} %get-tuple-element.47), channel_id=1, source_target_pairs={{0,2},{2,4},{4,6},{1,3},{3,5},{5,7},{8,10},{10,12},{12,14},{9,11},... | collective-permute-start | bytes 19976 | tf_op jit(solution)/shard_map/ppermute | solution.py:409
  10.0 4.8 %collective-permute-start.5 = (f32[1,1664]{1,0:T(1,128)S(1)}, f32[1,1664]{1,0:T(1,128)S(1)}, u32[]{:S(2)}, u32[]{:S(2)}) collective-permute-start(f32[1,1664]{1,0:T(1,128)S(1)} %get-tuple-element.48), channel_id=1, source_target_pairs={{2,0},{4,2},{6,4},{3,1},{5,3},{7,5},{10,8},{12,10},{14,12},{11,9},... | collective-permute-start | bytes 19976 | tf_op jit(solution)/shard_map/ppermute | solution.py:409
  11.3 0.7 %copy-start.6 = (f32[48]{0:T(128)S(1)}, f32[48]{0:T(128)}, u32[]{:S(2)}) copy-start(f32[48]{0:T(128)} %growth_ref.3) | copy-start | bytes 580
  11.3 0.7 %copy-start.7 = (f32[48]{0:T(128)S(1)}, f32[48]{0:T(128)}, u32[]{:S(2)}) copy-start(f32[48]{0:T(128)} %transfer_ref.3) | copy-start | bytes 580
  11.4 0.7 %copy-start.8 = (f32[4]{0:T(128)S(1)}, f32[4]{0:T(128)}, u32[]{:S(2)}) copy-start(f32[4]{0:T(128)} %rate_ref.3) | copy-start | bytes 52
  24.1 8.6 %copy-start.2 = (bf16[4,48,2,4,128]{4,3,2,1,0:T(4,128)(2,1)S(1)}, bf16[4,48,2,4,128]{4,3,2,1,0:T(4,128)(2,1)}, u32[]{:S(2)}) copy-start(bf16[4,48,2,4,128]{4,3,2,1,0:T(4,128)(2,1)} %param.12) | copy-start | bytes 1179652
  25.4 16.5 %collective-permute-start.11 = (f32[488,128]{1,0:T(8,128)S(1)}, f32[488,128]{1,0:T(8,128)S(1)}, u32[]{:S(2)}, u32[]{:S(2)}) collective-permute-start(f32[488,128]{1,0:T(8,128)S(1)} %get-tuple-element.63), channel_id=1, source_target_pairs={{0,24},{8,0},{16,8},{24,16},{1,25},{9,1},{17,9},{25,17},{2,26},{10... | collective-permute-start | bytes 749576 | tf_op jit(solution)/shard_map/ppermute | solution.py:409
  28.5 11.3 %collective-permute-start.7 = (f32[480,128]{1,0:T(8,128)S(1)}, f32[480,128]{1,0:T(8,128)S(1)}, u32[]{:S(2)}, u32[]{:S(2)}) collective-permute-start(f32[480,128]{1,0:T(8,128)S(1)} %get-tuple-element.56), channel_id=1, source_target_pairs={{0,8},{8,16},{16,24},{24,0},{1,9},{9,17},{17,25},{25,1},{2,10},{10... | collective-permute-start | bytes 737288 | tf_op jit(solution)/shard_map/ppermute | solution.py:409
  28.5 7.6 %collective-permute-start.8 = (f32[384,128]{1,0:T(8,128)S(1)}, f32[384,128]{1,0:T(8,128)S(1)}, u32[]{:S(2)}, u32[]{:S(2)}) collective-permute-start(f32[384,128]{1,0:T(8,128)S(1)} %get-tuple-element.57), channel_id=1, source_target_pairs={{0,1},{1,0},{2,3},{3,2},{4,5},{5,4},{6,7},{7,6},{8,9},{9,8},{10,11... | collective-permute-start | bytes 589832 | tf_op jit(solution)/shard_map/ppermute | solution.py:413
  30.1 4.0 %collective-permute-start.9 = (f32[1,1536]{1,0:T(1,128)S(1)}, f32[1,1536]{1,0:T(1,128)S(1)}, u32[]{:S(2)}, u32[]{:S(2)}) collective-permute-start(f32[1,1536]{1,0:T(1,128)S(1)} %get-tuple-element.58), channel_id=1, source_target_pairs={{0,2},{2,4},{4,6},{1,3},{3,5},{5,7},{8,10},{10,12},{12,14},{9,11},... | collective-permute-start | bytes 18440 | tf_op jit(solution)/shard_map/ppermute | solution.py:409
  31.4 4.8 %collective-permute-start.10 = (f32[1,1536]{1,0:T(1,128)S(1)}, f32[1,1536]{1,0:T(1,128)S(1)}, u32[]{:S(2)}, u32[]{:S(2)}) collective-permute-start(f32[1,1536]{1,0:T(1,128)S(1)} %get-tuple-element.59), channel_id=1, source_target_pairs={{2,0},{4,2},{6,4},{3,1},{5,3},{7,5},{10,8},{12,10},{14,12},{11,9},... | collective-permute-start | bytes 18440 | tf_op jit(solution)/shard_map/ppermute | solution.py:409
  43.4 0.9 %copy-start.9 = (f32[4,48,2,4,128]{4,3,2,1,0:T(4,128)}, f32[4,48,2,4,128]{4,3,2,1,0:T(4,128)S(1)}, u32[]{:S(2)}) copy-start(f32[4,48,2,4,128]{4,3,2,1,0:T(4,128)S(1)} %get-tuple-element.99) | copy-start | bytes 2359300

commit v9 on v8

--- a/solution.py
+++ b/solution.py
@@ -262,7 +262,22 @@
 
 
 def second_local(
-    sections, m_ref, a_ref, u_ref, edge_ref, speeds_ref, flags_ref, zones_ref, growth_ref, transfer_ref, rate_ref, out_ref
+    sections,
+    m_ref,
+    a_ref,
+    u_ref,
+    below_ref,
+    edge_ref,
+    low_ref,
+    high_ref,
+    speeds_ref,
+    flags_ref,
+    zones_ref,
+    growth_ref,
+    transfer_ref,
+    rate_ref,
+    out_ref,
+    bottom_ref,
 ):
     local = Local(*faces(speeds_ref, flags_ref))
     local.centre = local.centre + (edge_ref[3] - 1.0)
@@ -271,6 +286,8 @@
         out_ref[8 * c : 8 * c + 8] = 0.5 * a_ref[8 * c : 8 * c + 8] + (local(x) + term)
 
     source(sections, m_ref, u_ref, growth_ref, transfer_ref, zones_ref, rate_ref, finish)
+    bottom_ref[...] = out_ref[...]
+    add_azimuthal(4 * sections, decode(4 * sections, below_ref, low_ref, high_ref), edge_ref[0], 0, bottom_ref)
 
 
 def from_below(c, below_ref):
@@ -366,17 +383,18 @@
     pack_sides(comps, m_ref, where_ref, ax_ref, radup_ref, raddn_ref)
 
 
-def second_bottom(
-    comps, where_ref, part_ref, below_ref, ax_ref, radlo_ref, radhi_ref, edge_ref, low_ref, high_ref, base_ref, full_ref
+def second_sides(
+    comps, where_ref, part_ref, bottom_ref, ax_ref, radlo_ref, radhi_ref, edge_ref, base_ref, full_ref
 ):
     hrad = put_columns(radlo_ref[...], radhi_ref[...])
     rad = edge_ref[2]
     for c in range(comps):
         spots = slice(8 * c, 8 * c + 8)
-        base_ref[spots] = part_ref[spots] + rad * hrad[spots]
-    add_axial(comps, 1.0, where_ref, edge_ref[1], ax_ref, base_ref)
-    full_ref[...] = base_ref[...]
-    add_azimuthal(comps, decode(comps, below_ref, low_ref, high_ref), edge_ref[0], 0, full_ref)
+        halo = rad * hrad[spots]
+        base_ref[spots] = part_ref[spots] + halo
+        full_ref[spots] = bottom_ref[spots] + halo
+    for ref in (base_ref, full_ref):
+        add_axial(comps, 1.0, where_ref, edge_ref[1], ax_ref, ref)
 
 
 def second_top(comps, full_ref, above_ref, edge_ref, bad_ref, low_ref, high_ref, out_ref, again_ref):
@@ -480,7 +498,7 @@
         "s" + "v" * 6,
         "v" * 6,
         [(cells, 128), (message + 8, 128), (rows, 128), (1, cells), (1, cells), (8, 128)],
-        4_000_000,
+        10_000,
         where,
         part,
         below,
@@ -490,32 +508,33 @@
     )
     next_above = shift(dn, "azim", -1, True)
     edges = sides(*edges)
-    (part,) = call(
+    part, bottom = call(
         functools.partial(second_local, sections),
-        "vvvvvvvsss",
-        "v",
-        [(cells, 128)],
-        8_000_000,
+        "v" * 10 + "sss",
+        "vv",
+        [(cells, 128), (cells, 128)],
+        300_000_000,
         m,
         a,
         state_start.reshape(comps, 8, 128),
+        next_below,
         edge,
+        *lower_tables[2:],
         speeds2,
         flags2,
         *rates,
     )
     base, full = call(
-        functools.partial(second_bottom, comps),
-        "s" + "v" * 8,
+        functools.partial(second_sides, comps),
+        "s" + "v" * 6,
         "vv",
         [(cells, 128), (cells, 128)],
-        4_000_000,
+        10_000,
         where,
         part,
-        next_below,
+        bottom,
         *edges,
         edge,
-        *lower_tables[2:],
     )
 
     out, again = call(

time: 44.6 us -> 42.2 us (0.946)
  the two profiles are of different devices: /device:TPU:0 before, /device:TPU:1 now
where the time goes in v9:
time: 42.2 us; the launch traced here: 41.9 us
  starting transfers between devices  23.3 us (55%)
  Pallas kernels  9.49 us (22%)
  waiting for transfers between devices  5.6 us (13%)
  local copies, waits for them, and re-layouts  1.55 us (4%)
  other arithmetic  1.1 us (3%)
  between operations  0.86 us (2%)
    ppermute x8, starting transfers between devices, shift(): return lax.ppermute(x, axis, pairs)  20.8 us
    pallas_call x7, Pallas kernels, call(): pl.pallas_call(body, in_specs=[SPACES[s] for s in ins], out_specs=[SPACES...  9.49 us
    ppermute x8, waiting for transfers between devices, shift(): return lax.ppermute(x, axis, pairs)  5.6 us
    ppermute x2, starting transfers between devices, sides(): ax = lax.ppermute(ax, 'axial', [(0, 1), (1, 0)])  2.56 us
    unnamed x20, local copies, waits for them, and re-layouts  1.55 us
    add x1, other arithmetic, shards(): dn = dn + lax.pad(speeds, 0.0, after) * lax.pad(flags, 0, after).astype(f32)  1.1 us
  transfers between devices with their start and end apart: 10, of which 3 were waited for; matrix products, arithmetic and copies ran while one was open for 0% of the time, Pallas kernels for 20%

profile of v9, /device:TPU:1, one launch (start us, length us, event | category | flops | bytes accessed | tf_op | source)
XLA Modules:
  0.0 41.9 jit_solution(1372164385650262752)
XLA Ops:
  0.0 0.0 copy-start
  0.0 0.0 copy-start.4
  0.0 1.1 %fusion = f32[194,1,4,128]{3,2,1,0:T(4,128)S(1)} fusion(f32[192,2,4,128]{3,2,1,0:T(4,128)} %bitcast.25, f32[3,2,4,128]{3,2,1,0:T(4,128)} %param.14, s32[3,2,4,128]{3,2,1,0:T(4,128)} %param.15), kind=kLoop, calls=%fused_computation.6 | loop fusion | flops 297984 | bytes 1208320 | tf_op jit(solution)/shard_map/add | solution.py:454
  1.1 0.0 copy-start.3
  1.1 4.2 %collective-permute-start.2 = (f32[776,128]{1,0:T(8,128)S(1)}, f32[776,128]{1,0:T(8,128)S(1)}, u32[]{:S(2)}, u32[]{:S(2)}) collective-permute-start(f32[776,128]{1,0:T(8,128)S(1)} %bitcast.44), channel_id=1, source_target_pairs={{0,24},{8,0},{16,8},{24,16},{1,25},{9,1},{17,9},{25,17},{2,26},{10... | collective-permute-start | bytes 1191944 | tf_op jit(solution)/shard_map/ppermute | solution.py:427
  5.3 0.0 copy-done
  5.3 0.0 copy-done.4
  5.3 0.0 copy-done.3
  5.3 0.0 copy-start.1
  5.3 0.8 %shard_map.94 = (f32[776,128]{1,0:T(8,128)S(1)}, f32[392,128]{1,0:T(8,128)S(1)}, f32[1,1664]{1,0:T(1,128)S(1)}, f32[1,1664]{1,0:T(1,128)S(1)}) custom-call(s32[1]{0:T(128)} %bitcast.9.where_ref, f32[1536,128]{1,0:T(8,128)S(1)} %bitcast.26, f32[3,8,128]{2,1,0:T(8,128)S(1)} %bitcast.32, s32[3,8,128]{2,1,0:T(8,128)S(1)} %bitcast.36), custom_call_target="tpu_custom_call" | custom-call | flops 2000000 | bytes 200000 | tf_op jit(solution)/shard_map/pallas_call | solution.py:414
  6.2 0.1 collective-permute-start.6
  6.3 0.0 copy-start.5
  6.3 1.3 %collective-permute-start.3 = (f32[392,128]{1,0:T(8,128)S(1)}, f32[392,128]{1,0:T(8,128)S(1)}, u32[]{:S(2)}, u32[]{:S(2)}) collective-permute-start(f32[392,128]{1,0:T(8,128)S(1)} %get-tuple-element.48), channel_id=1, source_target_pairs={{0,1},{1,0},{2,3},{3,2},{4,5},{5,4},{6,7},{7,6},{8,9},{9,8},{10,11... | collective-permute-start | bytes 602120 | tf_op jit(solution)/shard_map/ppermute | solution.py:431
  7.6 4.2 %collective-permute-start.4 = (f32[1,1664]{1,0:T(1,128)S(1)}, f32[1,1664]{1,0:T(1,128)S(1)}, u32[]{:S(2)}, u32[]{:S(2)}) collective-permute-start(f32[1,1664]{1,0:T(1,128)S(1)} %get-tuple-element.49), channel_id=1, source_target_pairs={{0,2},{2,4},{4,6},{1,3},{3,5},{5,7},{8,10},{10,12},{12,14},{9,11},... | collective-permute-start | bytes 19976 | tf_op jit(solution)/shard_map/ppermute | solution.py:427
  11.8 1.9 %collective-permute-start.5 = (f32[1,1664]{1,0:T(1,128)S(1)}, f32[1,1664]{1,0:T(1,128)S(1)}, u32[]{:S(2)}, u32[]{:S(2)}) collective-permute-start(f32[1,1664]{1,0:T(1,128)S(1)} %get-tuple-element.50), channel_id=1, source_target_pairs={{2,0},{4,2},{6,4},{3,1},{5,3},{7,5},{10,8},{12,10},{14,12},{11,9},... | collective-permute-start | bytes 19976 | tf_op jit(solution)/shard_map/ppermute | solution.py:427
  13.7 0.0 copy-start.6
  13.7 0.0 copy-start.7
  13.8 0.0 copy-start.8
  13.8 0.0 copy-done.1
  13.8 0.0 copy-done.5
  13.8 0.6 %copy-done.6 = f32[48]{0:T(128)S(1)} copy-done((f32[48]{0:T(128)S(1)}, f32[48]{0:T(128)}, u32[]{:S(2)}) %copy-start.6) | copy-done | bytes 216
  14.4 0.0 copy-done.7
  14.4 0.0 copy-done.8
  14.4 1.6 %shard_map.93 = (f32[1536,128]{1,0:T(8,128)S(1)}, bf16[256,512]{1,0:T(8,128)(2,1)S(1)}, bf16[256,512]{1,0:T(8,128)(2,1)S(1)}, bf16[256,512]{1,0:T(8,128)(2,1)S(1)}, bf16[256,512]{1,0:T(8,128)(2,1)S(1)}) custom-call(f32[1536,128]{1,0:T(8,128)S(1)} %bitcast.27, bf16[192,8,128]{2,1,0:T(8,128)(2,1)S(1)} %bitcast.30, f32[3,8,128]{2,1,0:T(8,128)S(1)} %bitcast.33, ...), custom_call_target="tpu_custom_call" | custom-call | flops 8000000 | bytes 800000 | tf_op jit(solution)/shard_map/pallas_call | solution.py:414
  16.0 0.0 collective-permute-done.4.radlo_ref
  16.0 1.0 %collective-permute-done.5.radhi_ref = f32[1,1664]{1,0:T(1,128)S(1)} collective-permute-done((f32[1,1664]{1,0:T(1,128)S(1)}, f32[1,1664]{1,0:T(1,128)S(1)}, u32[]{:S(2)}, u32[]{:S(2)}) %collective-permute-start.5) | collective-permute-done | bytes 6688 | tf_op jit(solution)/shard_map/ppermute | solution.py:427
  17.1 0.0 collective-permute-done.3.ax_ref
  17.1 0.0 collective-permute-done.2.above_ref
  17.1 2.3 %shard_map.95 = (f32[1536,128]{1,0:T(8,128)S(1)}, f32[4,8,128]{2,1,0:T(8,128)S(1)}, f32[480,128]{1,0:T(8,128)S(1)}, f32[8,128]{1,0:T(8,128)S(1)}, bf16[256,512]{...) custom-call(s32[1]{0:T(128)} %bitcast.9.where_ref, ...), custom_call_target="tpu_custom_call" | custom-call | flops 4000000 | bytes 400000 | tf_op jit(solution)/shard_map/pallas_call | solution.py:414
  19.3 0.1 collective-permute-start.7
  19.4 3.2 %collective-permute-done.6.below_ref = f32[776,128]{1,0:T(8,128)S(1)} collective-permute-done((f32[776,128]{1,0:T(8,128)S(1)}, f32[776,128]{1,0:T(8,128)S(1)}, u32[]{:S(2)}, u32[]{:S(2)}) %collective-permute-start.6) | collective-permute-done | bytes 397344 | tf_op jit(solution)/shard_map/ppermute | solution.py:427
  22.6 0.0 copy-start.2
  22.6 1.3 %shard_map.96 = (f32[1536,128]{1,0:T(8,128)S(1)}, f32[488,128]{1,0:T(8,128)S(1)}, f32[384,128]{1,0:T(8,128)S(1)}, f32[1,1536]{1,0:T(1,128)S(1)}, f32[1,1536]{1,0:T(1,128)S(1)}, /*index=5*/f32[8,128]{1,0:T(8,128)S(1)}) custom-call(s32[1]{0:T(128)} %bitcast.9.where_ref, f32[1536,128]{1,0:T(8,128)S(1)} %get-tuple-element.51.part_ref, ...), custom_call_target="tpu_custom_call" | custom-call | flops 10000 | bytes 1000 | tf_op jit(solution)/shard_map/pallas_call | solution.py:414
  23.9 3.7 %collective-permute-start.11 = (f32[488,128]{1,0:T(8,128)S(1)}, f32[488,128]{1,0:T(8,128)S(1)}, u32[]{:S(2)}, u32[]{:S(2)}) collective-permute-start(f32[488,128]{1,0:T(8,128)S(1)} %get-tuple-element.67), channel_id=1, source_target_pairs={{0,24},{8,0},{16,8},{24,16},{1,25},{9,1},{17,9},{25,17},{2,26},{10... | collective-permute-start | bytes 749576 | tf_op jit(solution)/shard_map/ppermute | solution.py:427
  27.5 1.3 %collective-permute-start.8 = (f32[384,128]{1,0:T(8,128)S(1)}, f32[384,128]{1,0:T(8,128)S(1)}, u32[]{:S(2)}, u32[]{:S(2)}) collective-permute-start(f32[384,128]{1,0:T(8,128)S(1)} %get-tuple-element.63), channel_id=1, source_target_pairs={{0,1},{1,0},{2,3},{3,2},{4,5},{5,4},{6,7},{7,6},{8,9},{9,8},{10,11... | collective-permute-start | bytes 589832 | tf_op jit(solution)/shard_map/ppermute | solution.py:431
  28.8 4.7 %collective-permute-start.9 = (f32[1,1536]{1,0:T(1,128)S(1)}, f32[1,1536]{1,0:T(1,128)S(1)}, u32[]{:S(2)}, u32[]{:S(2)}) collective-permute-start(f32[1,1536]{1,0:T(1,128)S(1)} %get-tuple-element.64), channel_id=1, source_target_pairs={{0,2},{2,4},{4,6},{1,3},{3,5},{5,7},{8,10},{10,12},{12,14},{9,11},... | collective-permute-start | bytes 18440 | tf_op jit(solution)/shard_map/ppermute | solution.py:427
  33.5 1.9 %collective-permute-start.10 = (f32[1,1536]{1,0:T(1,128)S(1)}, f32[1,1536]{1,0:T(1,128)S(1)}, u32[]{:S(2)}, u32[]{:S(2)}) collective-permute-start(f32[1,1536]{1,0:T(1,128)S(1)} %get-tuple-element.65), channel_id=1, source_target_pairs={{2,0},{4,2},{6,4},{3,1},{5,3},{7,5},{10,8},{12,10},{14,12},{11,9},... | collective-permute-start | bytes 18440 | tf_op jit(solution)/shard_map/ppermute | solution.py:427
  35.4 0.0 collective-permute-done.7.below_ref
  35.5 0.0 copy-done.2
  35.5 1.6 %shard_map.97 = (f32[1536,128]{1,0:T(8,128)S(1)}, f32[1536,128]{1,0:T(8,128)S(1)}) custom-call(f32[1536,128]{1,0:T(8,128)S(1)} %get-tuple-element.57.m_ref, f32[1536,128]{1,0:T(8,128)S(1)} %bitcast.29, bf16[192,8,128]{2,1,0:T(8,128)(2,1)S(1)} %bitcast.31, f32[480,128]{1,0:T(8,128)S(1)} %collective-permute-done.7.below_ref, ...), custom_call_target="tpu_custom_call" | custom-call | flops 300000000 | bytes 30000000 | tf_op jit(solution)/shard_map/pallas_call | solution.py:414
  37.1 0.0 collective-permute-done.9.radlo_ref
  37.1 1.4 %collective-permute-done.10.radhi_ref = f32[1,1536]{1,0:T(1,128)S(1)} collective-permute-done((f32[1,1536]{1,0:T(1,128)S(1)}, f32[1,1536]{1,0:T(1,128)S(1)}, u32[]{:S(2)}, u32[]{:S(2)}) %collective-permute-start.10) | collective-permute-done | bytes 6176 | tf_op jit(solution)/shard_map/ppermute | solution.py:427
  38.5 0.0 collective-permute-done.8.ax_ref
  38.5 0.9 %shard_map.98 = (f32[1536,128]{1,0:T(8,128)S(1)}, f32[1536,128]{1,0:T(8,128)S(1)}) custom-call(s32[1]{0:T(128)} %bitcast.9.where_ref, f32[1536,128]{1,0:T(8,128)S(1)} %get-tuple-element.61.part_ref, f32[1536,128]{1,0:T(8,128)S(1)} %get-tuple-element.62.bottom_ref, f32[384,128]{1,0:T(8,128)S(1)} %collective-permute-done.8.ax_ref, ...), custom_call_target="tpu_custom_call" | custom-call | flops 10000 | bytes 1000 | tf_op jit(solution)/shard_map/pallas_call | solution.py:414
  39.4 0.0 collective-permute-done.11.above_ref
  39.4 0.9 %shard_map.99 = (f32[1536,128]{1,0:T(8,128)S(1)}, s32[1]{0:T(128)}) custom-call(f32[1536,128]{1,0:T(8,128)S(1)} %get-tuple-element.66.full_ref, f32[488,128]{1,0:T(8,128)S(1)} %collective-permute-done.11.above_ref, f32[4,8,128]{2,1,0:T(8,128)S(1)} %get-tuple-element.53.edge_ref, f32[8,128]{1,0:T(8,128)S(1)} %get-tuple-element.68.bad_ref, ...), custom_call_target="tpu_custom_call" | custom-call | flops 1000000 | bytes 100000 | tf_op jit(solution)/shard_map/pallas_call | solution.py:414
  41.1 0.0 copy-start.9
  41.1 0.9 %copy-done.9 = f32[4,48,2,4,128]{4,3,2,1,0:T(4,128)} copy-done((f32[4,48,2,4,128]{4,3,2,1,0:T(4,128)}, f32[4,48,2,4,128]{4,3,2,1,0:T(4,128)S(1)}, u32[]{:S(2)}) %copy-start.9) | copy-done | bytes 786456
  (1 shorter events, 0.0 us)
Async XLA Ops:
  0.0 5.3 %copy-start = (f32[4,48,2,4,128]{4,3,2,1,0:T(4,128)S(1)}, f32[4,48,2,4,128]{4,3,2,1,0:T(4,128)}, u32[]{:S(2)}) copy-start(f32[4,48,2,4,128]{4,3,2,1,0:T(4,128)} %param.11) | copy-start | bytes 2359300
  0.0 5.3 %copy-start.4 = (s32[3,2,4,128]{3,2,1,0:T(4,128)S(1)}, s32[3,2,4,128]{3,2,1,0:T(4,128)}, u32[]{:S(2)}) copy-start(s32[3,2,4,128]{3,2,1,0:T(4,128)} %param.15) | copy-start | bytes 36868
  1.1 4.2 %copy-start.3 = (f32[3,2,4,128]{3,2,1,0:T(4,128)S(1)}, f32[3,2,4,128]{3,2,1,0:T(4,128)}, u32[]{:S(2)}) copy-start(f32[3,2,4,128]{3,2,1,0:T(4,128)} %param.14) | copy-start | bytes 36868
  1.1 15.9 %collective-permute-start.2 = (f32[776,128]{1,0:T(8,128)S(1)}, f32[776,128]{1,0:T(8,128)S(1)}, u32[]{:S(2)}, u32[]{:S(2)}) collective-permute-start(f32[776,128]{1,0:T(8,128)S(1)} %bitcast.44), channel_id=1, source_target_pairs={{0,24},{8,0},{16,8},{24,16},{1,25},{9,1},{17,9},{25,17},{2,26},{10... | collective-permute-start | bytes 1191944 | tf_op jit(solution)/shard_map/ppermute | solution.py:427
  5.3 8.4 %copy-start.1 = (bf16[4,48,2,4,128]{4,3,2,1,0:T(4,128)(2,1)S(1)}, bf16[4,48,2,4,128]{4,3,2,1,0:T(4,128)(2,1)}, u32[]{:S(2)}) copy-start(bf16[4,48,2,4,128]{4,3,2,1,0:T(4,128)(2,1)} %param.13) | copy-start | bytes 1179652
  6.2 16.4 %collective-permute-start.6 = (f32[776,128]{1,0:T(8,128)S(1)}, f32[776,128]{1,0:T(8,128)S(1)}, u32[]{:S(2)}, u32[]{:S(2)}) collective-permute-start(f32[776,128]{1,0:T(8,128)S(1)} %get-tuple-element.52), channel_id=1, source_target_pairs={{0,8},{8,16},{16,24},{24,0},{1,9},{9,17},{17,25},{25,1},{2,10},{10... | collective-permute-start | bytes 1191944 | tf_op jit(solution)/shard_map/ppermute | solution.py:427
  6.3 7.5 %copy-start.5 = (s32[2,4,128]{2,1,0:T(4,128)S(1)}, s32[2,4,128]{2,1,0:T(4,128)}, u32[]{:S(2)}) copy-start(s32[2,4,128]{2,1,0:T(4,128)} %param.16) | copy-start | bytes 12292
  6.3 10.8 %collective-permute-start.3 = (f32[392,128]{1,0:T(8,128)S(1)}, f32[392,128]{1,0:T(8,128)S(1)}, u32[]{:S(2)}, u32[]{:S(2)}) collective-permute-start(f32[392,128]{1,0:T(8,128)S(1)} %get-tuple-element.48), channel_id=1, source_target_pairs={{0,1},{1,0},{2,3},{3,2},{4,5},{5,4},{6,7},{7,6},{8,9},{9,8},{10,11... | collective-permute-start | bytes 602120 | tf_op jit(solution)/shard_map/ppermute | solution.py:431
  7.6 8.5 %collective-permute-start.4 = (f32[1,1664]{1,0:T(1,128)S(1)}, f32[1,1664]{1,0:T(1,128)S(1)}, u32[]{:S(2)}, u32[]{:S(2)}) collective-permute-start(f32[1,1664]{1,0:T(1,128)S(1)} %get-tuple-element.49), channel_id=1, source_target_pairs={{0,2},{2,4},{4,6},{1,3},{3,5},{5,7},{8,10},{10,12},{12,14},{9,11},... | collective-permute-start | bytes 19976 | tf_op jit(solution)/shard_map/ppermute | solution.py:427
  11.8 5.2 %collective-permute-start.5 = (f32[1,1664]{1,0:T(1,128)S(1)}, f32[1,1664]{1,0:T(1,128)S(1)}, u32[]{:S(2)}, u32[]{:S(2)}) collective-permute-start(f32[1,1664]{1,0:T(1,128)S(1)} %get-tuple-element.50), channel_id=1, source_target_pairs={{2,0},{4,2},{6,4},{3,1},{5,3},{7,5},{10,8},{12,10},{14,12},{11,9},... | collective-permute-start | bytes 19976 | tf_op jit(solution)/shard_map/ppermute | solution.py:427
  13.7 0.7 %copy-start.6 = (f32[48]{0:T(128)S(1)}, f32[48]{0:T(128)}, u32[]{:S(2)}) copy-start(f32[48]{0:T(128)} %growth_ref.3) | copy-start | bytes 580
  13.7 0.7 %copy-start.7 = (f32[48]{0:T(128)S(1)}, f32[48]{0:T(128)}, u32[]{:S(2)}) copy-start(f32[48]{0:T(128)} %transfer_ref.3) | copy-start | bytes 580
  13.8 0.7 %copy-start.8 = (f32[4]{0:T(128)S(1)}, f32[4]{0:T(128)}, u32[]{:S(2)}) copy-start(f32[4]{0:T(128)} %rate_ref.3) | copy-start | bytes 52
  19.3 16.1 %collective-permute-start.7 = (f32[480,128]{1,0:T(8,128)S(1)}, f32[480,128]{1,0:T(8,128)S(1)}, u32[]{:S(2)}, u32[]{:S(2)}) collective-permute-start(f32[480,128]{1,0:T(8,128)S(1)} %get-tuple-element.58), channel_id=1, source_target_pairs={{0,8},{8,16},{16,24},{24,0},{1,9},{9,17},{17,25},{25,1},{2,10},{10... | collective-permute-start | bytes 737288 | tf_op jit(solution)/shard_map/ppermute | solution.py:427
  22.6 12.8 %copy-start.2 = (bf16[4,48,2,4,128]{4,3,2,1,0:T(4,128)(2,1)S(1)}, bf16[4,48,2,4,128]{4,3,2,1,0:T(4,128)(2,1)}, u32[]{:S(2)}) copy-start(bf16[4,48,2,4,128]{4,3,2,1,0:T(4,128)(2,1)} %param.12) | copy-start | bytes 1179652
  23.9 15.6 %collective-permute-start.11 = (f32[488,128]{1,0:T(8,128)S(1)}, f32[488,128]{1,0:T(8,128)S(1)}, u32[]{:S(2)}, u32[]{:S(2)}) collective-permute-start(f32[488,128]{1,0:T(8,128)S(1)} %get-tuple-element.67), channel_id=1, source_target_pairs={{0,24},{8,0},{16,8},{24,16},{1,25},{9,1},{17,9},{25,17},{2,26},{10... | collective-permute-start | bytes 749576 | tf_op jit(solution)/shard_map/ppermute | solution.py:427
  27.5 10.9 %collective-permute-start.8 = (f32[384,128]{1,0:T(8,128)S(1)}, f32[384,128]{1,0:T(8,128)S(1)}, u32[]{:S(2)}, u32[]{:S(2)}) collective-permute-start(f32[384,128]{1,0:T(8,128)S(1)} %get-tuple-element.63), channel_id=1, source_target_pairs={{0,1},{1,0},{2,3},{3,2},{4,5},{5,4},{6,7},{7,6},{8,9},{9,8},{10,11... | collective-permute-start | bytes 589832 | tf_op jit(solution)/shard_map/ppermute | solution.py:431
  28.8 8.3 %collective-permute-start.9 = (f32[1,1536]{1,0:T(1,128)S(1)}, f32[1,1536]{1,0:T(1,128)S(1)}, u32[]{:S(2)}, u32[]{:S(2)}) collective-permute-start(f32[1,1536]{1,0:T(1,128)S(1)} %get-tuple-element.64), channel_id=1, source_target_pairs={{0,2},{2,4},{4,6},{1,3},{3,5},{5,7},{8,10},{10,12},{12,14},{9,11},... | collective-permute-start | bytes 18440 | tf_op jit(solution)/shard_map/ppermute | solution.py:427
  33.5 4.9 %collective-permute-start.10 = (f32[1,1536]{1,0:T(1,128)S(1)}, f32[1,1536]{1,0:T(1,128)S(1)}, u32[]{:S(2)}, u32[]{:S(2)}) collective-permute-start(f32[1,1536]{1,0:T(1,128)S(1)} %get-tuple-element.65), channel_id=1, source_target_pairs={{2,0},{4,2},{6,4},{3,1},{5,3},{7,5},{10,8},{12,10},{14,12},{11,9},... | collective-permute-start | bytes 18440 | tf_op jit(solution)/shard_map/ppermute | solution.py:427
  41.1 0.9 %copy-start.9 = (f32[4,48,2,4,128]{4,3,2,1,0:T(4,128)}, f32[4,48,2,4,128]{4,3,2,1,0:T(4,128)S(1)}, u32[]{:S(2)}) copy-start(f32[4,48,2,4,128]{4,3,2,1,0:T(4,128)S(1)} %get-tuple-element.103) | copy-start | bytes 2359300

commit v10 on v9

--- a/solution.py
+++ b/solution.py
@@ -187,6 +187,7 @@
     up_ref[4 * comps :] = p[0]
     pack_sides(comps, a_ref, where_ref, ax_ref, radup_ref, raddn_ref)
     ax_ref[2 * comps : 2 * comps + 8] = pair_rows(p[1], 0, 4)
+    ax_ref[2 * comps + 8 :] = jnp.zeros((8, 128), f32)
     radup_ref[:, 8 * comps :] = jnp.zeros((1, 128), f32)
     raddn_ref[:, 8 * comps :] = jnp.zeros((1, 128), f32)
     raddn_ref[:, 8 * comps : 8 * comps + 8] = columns(p[2])[1:2]
@@ -238,6 +239,8 @@
     sections,
     a_ref,
     u_ref,
+    radlo_ref,
+    radhi_ref,
     speeds_ref,
     flags_ref,
     zones_ref,
@@ -245,6 +248,7 @@
     transfer_ref,
     rate_ref,
     out_ref,
+    rad_ref,
     dn_low_ref,
     dn_high_ref,
     up_low_ref,
@@ -252,11 +256,16 @@
 ):
     p, q = faces(speeds_ref, flags_ref)
     local = Local(p, q)
+    hrad = put_columns(radlo_ref[...], radhi_ref[...])
+    p_rad = jnp.where(lanes_of() == 127, hrad[32 * sections : 32 * sections + 8], 0.0)
+    rad = jnp.where(lanes_of() == 0, q[2], p_rad)
+    rad_ref[...] = rad
+    local.centre = local.centre + p_rad
     make_tables(p[0], False, dn_low_ref, dn_high_ref)
     make_tables(p[0], True, up_low_ref, up_high_ref)
 
     def finish(c, x, term):
-        out_ref[8 * c : 8 * c + 8] = 0.5 * (x + local(x) + term)
+        out_ref[8 * c : 8 * c + 8] = 0.5 * (x + local(x) + rad * hrad[8 * c : 8 * c + 8] + term)
 
     source(sections, a_ref, u_ref, growth_ref, transfer_ref, zones_ref, rate_ref, finish)
 
@@ -267,6 +276,8 @@
     a_ref,
     u_ref,
     below_ref,
+    radlo_ref,
+    radhi_ref,
     edge_ref,
     low_ref,
     high_ref,
@@ -281,9 +292,12 @@
 ):
     local = Local(*faces(speeds_ref, flags_ref))
     local.centre = local.centre + (edge_ref[3] - 1.0)
+    hrad = put_columns(radlo_ref[...], radhi_ref[...])
+    rad = edge_ref[2]
 
     def finish(c, x, term):
-        out_ref[8 * c : 8 * c + 8] = 0.5 * a_ref[8 * c : 8 * c + 8] + (local(x) + term)
+        spots = slice(8 * c, 8 * c + 8)
+        out_ref[spots] = 0.5 * a_ref[spots] + (local(x) + rad * hrad[spots] + term)
 
     source(sections, m_ref, u_ref, growth_ref, transfer_ref, zones_ref, rate_ref, finish)
     bottom_ref[...] = out_ref[...]
@@ -317,8 +331,7 @@
     a_ref,
     above_ref,
     ax_ref,
-    radlo_ref,
-    radhi_ref,
+    rad_ref,
     speeds_ref,
     flags_ref,
     m_ref,
@@ -336,23 +349,20 @@
     make_tables(upper, True, up_low_ref, up_high_ref)
     make_tables(upper, False, dn_low_ref, dn_high_ref)
     bad_ref[...] = crowded(p[0]) + crowded(upper)
-    hrad = put_columns(radlo_ref[...], radhi_ref[...])
     lower_half = where_ref[0] == 0
     p_azim = jnp.where(row >= 4, pltpu.roll(upper, 4, 0), 0.0)
     pairs = jnp.where(lower_half, ax_ref[2 * comps : 2 * comps + 8], 0.0)
     p_axial = jnp.where(row == 3, pairs[0:1], jnp.where(row == 7, pairs[1:2], 0.0))
-    p_rad = jnp.where(lane == 127, hrad[8 * comps : 8 * comps + 8], 0.0)
     axial = jnp.where(lower_half, pairs, pair_rows(q[1], 0, 4))
-    rad = jnp.where(lane == 0, q[2], p_rad)
-    centre = p_azim + p_axial + p_rad
+    centre = p_azim + p_axial
     edge_ref[0] = jnp.where(row >= 4, p_azim, q[0])
     edge_ref[1] = axial
-    edge_ref[2] = rad
-    edge_ref[3] = centre
+    edge_ref[2] = rad_ref[...]
+    edge_ref[3] = centre + jnp.where(lane == 127, rad_ref[...], 0.0)
     for c in range(comps):
         spots = slice(8 * c, 8 * c + 8)
         m_ref[spots] = part_ref[spots] + 0.5 * (
-            p_azim * from_above(c, above_ref) + rad * hrad[spots] - centre * a_ref[spots]
+            p_azim * from_above(c, above_ref) - centre * a_ref[spots]
         )
     add_axial(comps, 0.5, where_ref, axial, ax_ref, m_ref)
     encode(comps, m_ref, 4, up_low_ref, up_high_ref, up_ref)
@@ -379,27 +389,15 @@
         m_ref[8 * c : 8 * c + 8] = part_ref[8 * c : 8 * c + 8] + azim * from_below(c, below_ref)
     encode(comps, m_ref, 0, low_ref, high_ref, dn_ref)
     worse_ref[...] = bad_ref[...] + crowded(below_ref[4 * comps :])
+    ax_ref[2 * comps :] = jnp.zeros((8, 128), f32)
     dn_ref[5 * comps // 2 :] = worse_ref[...]
     pack_sides(comps, m_ref, where_ref, ax_ref, radup_ref, raddn_ref)
 
 
-def second_sides(
-    comps, where_ref, part_ref, bottom_ref, ax_ref, radlo_ref, radhi_ref, edge_ref, base_ref, full_ref
-):
-    hrad = put_columns(radlo_ref[...], radhi_ref[...])
-    rad = edge_ref[2]
-    for c in range(comps):
-        spots = slice(8 * c, 8 * c + 8)
-        halo = rad * hrad[spots]
-        base_ref[spots] = part_ref[spots] + halo
-        full_ref[spots] = bottom_ref[spots] + halo
-    for ref in (base_ref, full_ref):
-        add_axial(comps, 1.0, where_ref, edge_ref[1], ax_ref, ref)
-
-
-def second_top(comps, full_ref, above_ref, edge_ref, bad_ref, low_ref, high_ref, out_ref, again_ref):
+def second_rest(comps, where_ref, bottom_ref, above_ref, ax_ref, edge_ref, bad_ref, low_ref, high_ref, out_ref, again_ref):
     again_ref[0] = (jnp.max(bad_ref[...] + above_ref[5 * comps // 2 :]) > 0.0).astype(jnp.int32)
-    out_ref[...] = full_ref[...]
+    out_ref[...] = bottom_ref[...]
+    add_axial(comps, 1.0, where_ref, edge_ref[1], ax_ref, out_ref)
     add_azimuthal(comps, decode(comps, above_ref, low_ref, high_ref), edge_ref[0], 4, out_ref)
 
 
@@ -428,8 +426,10 @@
 
 
 def sides(ax, radup, raddn):
-    ax = lax.ppermute(ax, "axial", [(0, 1), (1, 0)])
-    return ax, shift(radup, "rad", 1, False), shift(raddn, "rad", -1, False)
+    radlo, radhi = shift(radup, "rad", 1, False), shift(raddn, "rad", -1, False)
+    for row, came in enumerate((radlo, radhi)):
+        ax = lax.dynamic_update_slice(ax, came[:, :128], (ax.shape[0] - 8 + row, 0))
+    return lax.ppermute(ax, "axial", [(0, 1), (1, 0)]), radlo, radhi
 
 
 def shards(adjoint_final, state_start, state_middle, speeds, flags, zones, growth_rate, transfer_rate, nucleation_rate):
@@ -457,7 +457,7 @@
         functools.partial(first_rest, comps),
         "svvv",
         "vvvv",
-        [(half + 8, 128), (rows + 8, 128), (1, cells + 128), (1, cells + 128)],
+        [(half + 8, 128), (rows + 16, 128), (1, cells + 128), (1, cells + 128)],
         2_000_000,
         where,
         a,
@@ -465,22 +465,23 @@
         flags2,
     )
     below = shift(up, "azim", 1, True)
-    edges = sides(*edges)
-    part, *lower_tables = call(
+    ax, *edges = sides(*edges)
+    part, rad, *lower_tables = call(
         functools.partial(first_local, sections),
-        "vvvvvsss",
-        "vvvvv",
-        [(cells, 128)] + 2 * tables,
+        "vvvvvvvsss",
+        "vvvvvv",
+        [(cells, 128), (8, 128)] + 2 * tables,
         8_000_000,
         a,
         state_middle.reshape(comps, 8, 128),
+        *edges,
         speeds2,
         flags2,
         *rates,
     )
     part, edge, up, bad, *upper_tables = call(
         functools.partial(first_top, comps),
-        "s" + "v" * 8,
+        "s" + "v" * 7,
         "v" * 8,
         [(cells, 128), (4, 8, 128), (message, 128), (8, 128)] + 2 * tables,
         4_000_000,
@@ -488,7 +489,8 @@
         part,
         a,
         above,
-        *edges,
+        ax,
+        rad,
         speeds2,
         flags2,
     )
@@ -497,7 +499,7 @@
         functools.partial(first_bottom, comps),
         "s" + "v" * 6,
         "v" * 6,
-        [(cells, 128), (message + 8, 128), (rows, 128), (1, cells), (1, cells), (8, 128)],
+        [(cells, 128), (message + 8, 128), (rows + 8, 128), (1, cells), (1, cells), (8, 128)],
         10_000,
         where,
         part,
@@ -507,10 +509,10 @@
         *lower_tables[:2],
     )
     next_above = shift(dn, "azim", -1, True)
-    edges = sides(*edges)
+    ax, *edges = sides(*edges)
     part, bottom = call(
         functools.partial(second_local, sections),
-        "v" * 10 + "sss",
+        "v" * 12 + "sss",
         "vv",
         [(cells, 128), (cells, 128)],
         300_000_000,
@@ -518,33 +520,23 @@
         a,
         state_start.reshape(comps, 8, 128),
         next_below,
+        *edges,
         edge,
         *lower_tables[2:],
         speeds2,
         flags2,
         *rates,
     )
-    base, full = call(
-        functools.partial(second_sides, comps),
-        "s" + "v" * 6,
-        "vv",
-        [(cells, 128), (cells, 128)],
-        10_000,
-        where,
-        part,
-        bottom,
-        *edges,
-        edge,
-    )
-
     out, again = call(
-        functools.partial(second_top, comps),
-        "vvvvvv",
+        functools.partial(second_rest, comps),
+        "s" + "v" * 7,
         "vs",
         [(cells, 128), jax.ShapeDtypeStruct((1,), jnp.int32)],
         1_000_000,
-        full,
+        where,
+        bottom,
         next_above,
+        ax,
         edge,
         bad,
         *upper_tables[:2],
@@ -553,7 +545,10 @@
     def whole():
         rows_ = m.reshape(comps, 2, 4, 128)
         halo = jnp.stack([shift(rows_[:, 1], "azim", 1, True), shift(rows_[:, 0], "azim", -1, True)], axis=1)
-        return base + (edge[0].reshape(1, 2, 4, 128) * halo).reshape(cells, 128)
+        azimuthal = edge[0].reshape(1, 2, 4, 128) * halo
+        outer = jnp.arange(4).reshape(1, 1, 4, 1) == 3 * (1 - where[0])
+        axial = jnp.where(outer, edge[1, :2].reshape(1, 2, 1, 128) * ax[:rows].reshape(comps, 2, 1, 128), 0.0)
+        return (part.reshape(comps, 2, 4, 128) + axial + azimuthal).reshape(cells, 128)
 
     again = again[0]
     if lax.axis_size("azim") != 4:

time: 42.2 us -> 46.1 us (1.092)
  waiting for transfers between devices: 5.6 us -> 8.09 us
  Pallas kernels: 9.49 us -> 10.6 us
  other arithmetic: 1.1 us -> 1.85 us
  starting transfers between devices: 23.3 us -> 22.7 us
    ppermute x2, waiting for transfers between devices: 0.01 us -> 1.9 us  [sides(): return (lax.ppermute(ax, 'axial', [(0, 1), (1, 0)]), radlo, radhi)]
    pallas_call x7 -> x6, Pallas kernels: 9.49 us -> 10.6 us  [call(): pl.pallas_call(body, in_specs=[SPACES[s] for s in ins], out_specs=[SPACES...]
    add x1, other arithmetic: 1.1 us -> 1.85 us  [shards(): dn = dn + lax.pad(speeds, 0.0, after) * lax.pad(flags, 0, after).astype(f32)]
    ppermute x8, starting transfers between devices: 20.8 us -> 20.1 us  [shift(): return lax.ppermute(x, axis, pairs)]
    ppermute x8, waiting for transfers between devices: 5.6 us -> 6.19 us  [shift(): return lax.ppermute(x, axis, pairs)]
    unnamed x20 -> x24, local copies, waits for them, and re-layouts: 1.55 us -> 1.57 us
  transfers between devices with their start and end apart: 10 -> 10, of which waited for: 3 -> 5; matrix products, arithmetic and copies ran while one was open for 0% -> 0% of each run, Pallas kernels for 20% -> 21%
where the time goes in v10:
time: 46.1 us; the launch traced here: 45.8 us
  starting transfers between devices  22.7 us (49%)
  Pallas kernels  10.6 us (23%)
  waiting for transfers between devices  8.09 us (18%)
  other arithmetic  1.85 us (4%)
  local copies, waits for them, and re-layouts  1.71 us (4%)
  between operations  0.84 us (2%)
    ppermute x8, starting transfers between devices, shift(): return lax.ppermute(x, axis, pairs)  20.1 us
    pallas_call x6, Pallas kernels, call(): pl.pallas_call(body, in_specs=[SPACES[s] for s in ins], out_specs=[SPACES...  10.6 us
    ppermute x8, waiting for transfers between devices, shift(): return lax.ppermute(x, axis, pairs)  6.19 us
    ppermute x2, starting transfers between devices, sides(): return (lax.ppermute(ax, 'axial', [(0, 1), (1, 0)]), radlo, radhi)  2.59 us
    ppermute x2, waiting for transfers between devices, sides(): return (lax.ppermute(ax, 'axial', [(0, 1), (1, 0)]), radlo, radhi)  1.9 us
    add x1, other arithmetic, shards(): dn = dn + lax.pad(speeds, 0.0, after) * lax.pad(flags, 0, after).astype(f32)  1.85 us
    unnamed x24, local copies, waits for them, and re-layouts  1.57 us
  transfers between devices with their start and end apart: 10, of which 5 were waited for; matrix products, arithmetic and copies ran while one was open for 0% of the time, Pallas kernels for 21%

profile of v10, /device:TPU:1, one launch (start us, length us, event | category | flops | bytes accessed | tf_op | source)
XLA Modules:
  0.0 45.8 jit_solution(7040619984672737557)
XLA Ops:
  0.0 0.0 copy-start
  0.0 0.0 copy-start.4
  0.0 1.8 %fusion = f32[194,1,4,128]{3,2,1,0:T(4,128)} fusion(f32[192,2,4,128]{3,2,1,0:T(4,128)} %bitcast.30, f32[3,2,4,128]{3,2,1,0:T(4,128)} %param.14, s32[3,2,4,128]{3,2,1,0:T(4,128)} %param.15), kind=kLoop, calls=%fused_computation.10 | loop fusion | flops 297984 | bytes 1208320 | tf_op jit(solution)/shard_map/add | solution.py:454
  1.9 0.0 copy-start.3
  1.9 4.2 %collective-permute-start.4 = (f32[776,128]{1,0:T(8,128)}, f32[776,128]{1,0:T(8,128)S(1)}, u32[]{:S(2)}, u32[]{:S(2)}) collective-permute-start(f32[776,128]{1,0:T(8,128)} %bitcast.19), channel_id=1, source_target_pairs={{0,24},{8,0},{16,8},{24,16},{1,25},{9,1},{17,9},{25,17},{2,26},{10... | collective-permute-start | bytes 1191944 | tf_op jit(solution)/shard_map/ppermute | solution.py:425
  6.0 0.0 copy-done
  6.0 0.0 copy-done.4
  6.0 0.0 copy-done.3
  6.0 0.0 copy-start.1
  6.0 0.8 %shard_map.93 = (f32[776,128]{1,0:T(8,128)S(1)}, f32[400,128]{1,0:T(8,128)S(1)}, f32[1,1664]{1,0:T(1,128)S(1)}, f32[1,1664]{1,0:T(1,128)S(1)}) custom-call(s32[1]{0:T(128)} %bitcast.12.where_ref, f32[1536,128]{1,0:T(8,128)S(1)} %bitcast.31, f32[3,8,128]{2,1,0:T(8,128)S(1)} %bitcast.37, s32[3,8,128]{2,1,0:T(8,128)S(1)} %bitcast.41), custom_call_target="tpu_custom_call" | custom-call | flops 2000000 | bytes 200000 | tf_op jit(solution)/shard_map/pallas_call | solution.py:412
  6.9 0.1 collective-permute-start.6
  6.9 4.0 %collective-permute-start.2 = (f32[1,1664]{1,0:T(1,128)S(1)}, f32[1,1664]{1,0:T(1,128)S(1)}, u32[]{:S(2)}, u32[]{:S(2)}) collective-permute-start(f32[1,1664]{1,0:T(1,128)S(1)} %get-tuple-element.52), channel_id=1, source_target_pairs={{0,2},{2,4},{4,6},{1,3},{3,5},{5,7},{8,10},{10,12},{12,14},{9,11},... | collective-permute-start | bytes 19976 | tf_op jit(solution)/shard_map/ppermute | solution.py:425
  10.9 1.9 %collective-permute-start.3 = (f32[1,1664]{1,0:T(1,128)S(1)}, f32[1,1664]{1,0:T(1,128)S(1)}, u32[]{:S(2)}, u32[]{:S(2)}) collective-permute-start(f32[1,1664]{1,0:T(1,128)S(1)} %get-tuple-element.53), channel_id=1, source_target_pairs={{2,0},{4,2},{6,4},{3,1},{5,3},{7,5},{10,8},{12,10},{14,12},{11,9},... | collective-permute-start | bytes 19976 | tf_op jit(solution)/shard_map/ppermute | solution.py:425
  12.8 0.0 collective-permute-done.2.radlo_ref
  12.9 0.0 copy-start.5
  12.9 3.0 %collective-permute-done.3.radhi_ref = f32[1,1664]{1,0:T(1,128)S(1)} collective-permute-done((f32[1,1664]{1,0:T(1,128)S(1)}, f32[1,1664]{1,0:T(1,128)S(1)}, u32[]{:S(2)}, u32[]{:S(2)}) %collective-permute-start.3) | collective-permute-done | bytes 6688 | tf_op jit(solution)/shard_map/ppermute | solution.py:425
  15.9 1.3 %collective-permute-start.5 = (f32[400,128]{1,0:T(8,128)S(1)}, f32[400,128]{1,0:T(8,128)S(1)}, u32[]{:S(2)}, u32[]{:S(2)}) collective-permute-start(f32[400,128]{1,0:T(8,128)S(1)} %dynamic_update_slice.13), channel_id=1, source_target_pairs={{0,1},{1,0},{2,3},{3,2},{4,5},{5,4},{6,7},{7,6},{8,9},{9,8},{10,11... | collective-permute-start | bytes 614408 | tf_op jit(solution)/shard_map/ppermute | solution.py:432
  17.2 0.0 copy-start.6
  17.2 0.0 copy-start.7
  17.2 0.0 copy-start.8
  17.2 0.0 copy-done.1
  17.2 0.0 copy-done.5
  17.2 0.6 %copy-done.6 = f32[48]{0:T(128)S(1)} copy-done((f32[48]{0:T(128)S(1)}, f32[48]{0:T(128)}, u32[]{:S(2)}) %copy-start.6) | copy-done | bytes 216
  17.8 0.0 copy-done.7
  17.9 0.0 copy-done.8
  17.9 2.0 %shard_map.94 = (f32[1536,128]{1,0:T(8,128)S(1)}, f32[8,128]{1,0:T(8,128)S(1)}, bf16[256,512]{1,0:T(8,128)(2,1)S(1)}, bf16[256,512]{1,0:T(8,128)(2,1)S(1)}, bf16...) custom-call(f32[1536,128]{1,0:T(8,128)S(1)} %bitcast.32, bf16[192,8,128]{2,1,0:T(8,128)(2,1)S(1)} %bitcast.35, ...), custom_call_target="tpu_custom_call" | custom-call | flops 8000000 | bytes 800000 | tf_op jit(solution)/shard_map/pallas_call | solution.py:412
  19.9 1.7 %collective-permute-done.5.ax_ref = f32[400,128]{1,0:T(8,128)S(1)} collective-permute-done((f32[400,128]{1,0:T(8,128)S(1)}, f32[400,128]{1,0:T(8,128)S(1)}, u32[]{:S(2)}, u32[]{:S(2)}) %collective-permute-start.5) | collective-permute-done | bytes 204832 | tf_op jit(solution)/shard_map/ppermute | solution.py:432
  21.6 0.0 collective-permute-done.4.above_ref
  21.6 1.7 %shard_map.95 = (f32[1536,128]{1,0:T(8,128)S(1)}, f32[4,8,128]{2,1,0:T(8,128)S(1)}, f32[480,128]{1,0:T(8,128)}, f32[8,128]{1,0:T(8,128)S(1)}, bf16[256,512]{1,0:...) custom-call(s32[1]{0:T(128)} %bitcast.12.where_ref, ...), custom_call_target="tpu_custom_call" | custom-call | flops 4000000 | bytes 400000 | tf_op jit(solution)/shard_map/pallas_call | solution.py:412
  23.4 0.0 collective-permute-start.7
  23.4 0.1 collective-permute-done.6.below_ref
  23.5 1.4 %shard_map.96 = (f32[1536,128]{1,0:T(8,128)}, f32[488,128]{1,0:T(8,128)S(1)}, f32[392,128]{1,0:T(8,128)S(1)}, f32[1,1536]{1,0:T(1,128)S(1)}, f32[1,1536]{1,0:T(1,128)S(1)}, /*index=5*/f32[8,128]{1,0:T(8,128)S(1)}) custom-call(s32[1]{0:T(128)} %bitcast.12.where_ref, f32[1536,128]{1,0:T(8,128)S(1)} %get-tuple-element.57.part_ref, ...), custom_call_target="tpu_custom_call" | custom-call | flops 10000 | bytes 1000 | tf_op jit(solution)/shard_map/pallas_call | solution.py:412
  24.9 3.4 %collective-permute-start.10 = (f32[488,128]{1,0:T(8,128)S(1)}, f32[488,128]{1,0:T(8,128)S(1)}, u32[]{:S(2)}, u32[]{:S(2)}) collective-permute-start(f32[488,128]{1,0:T(8,128)S(1)} %get-tuple-element.70), channel_id=1, source_target_pairs={{0,24},{8,0},{16,8},{24,16},{1,25},{9,1},{17,9},{25,17},{2,26},{10... | collective-permute-start | bytes 749576 | tf_op jit(solution)/shard_map/ppermute | solution.py:425
  28.3 4.7 %collective-permute-start.8 = (f32[1,1536]{1,0:T(1,128)S(1)}, f32[1,1536]{1,0:T(1,128)S(1)}, u32[]{:S(2)}, u32[]{:S(2)}) collective-permute-start(f32[1,1536]{1,0:T(1,128)S(1)} %get-tuple-element.65), channel_id=1, source_target_pairs={{0,2},{2,4},{4,6},{1,3},{3,5},{5,7},{8,10},{10,12},{12,14},{9,11},... | collective-permute-start | bytes 18440 | tf_op jit(solution)/shard_map/ppermute | solution.py:425
  33.0 1.9 %collective-permute-start.9 = (f32[1,1536]{1,0:T(1,128)S(1)}, f32[1,1536]{1,0:T(1,128)S(1)}, u32[]{:S(2)}, u32[]{:S(2)}) collective-permute-start(f32[1,1536]{1,0:T(1,128)S(1)} %get-tuple-element.66), channel_id=1, source_target_pairs={{2,0},{4,2},{6,4},{3,1},{5,3},{7,5},{10,8},{12,10},{14,12},{11,9},... | collective-permute-start | bytes 18440 | tf_op jit(solution)/shard_map/ppermute | solution.py:425
  34.9 0.0 collective-permute-done.8.radlo_ref
  35.0 3.1 %collective-permute-done.9.radhi_ref = f32[1,1536]{1,0:T(1,128)S(1)} collective-permute-done((f32[1,1536]{1,0:T(1,128)S(1)}, f32[1,1536]{1,0:T(1,128)S(1)}, u32[]{:S(2)}, u32[]{:S(2)}) %collective-permute-start.9) | collective-permute-done | bytes 6176 | tf_op jit(solution)/shard_map/ppermute | solution.py:425
  38.1 1.3 %collective-permute-start.11 = (f32[392,128]{1,0:T(8,128)S(1)}, f32[392,128]{1,0:T(8,128)S(1)}, u32[]{:S(2)}, u32[]{:S(2)}) collective-permute-start(f32[392,128]{1,0:T(8,128)S(1)} %dynamic_update_slice.15), channel_id=1, source_target_pairs={{0,1},{1,0},{2,3},{3,2},{4,5},{5,4},{6,7},{7,6},{8,9},{9,8},{10,11... | collective-permute-start | bytes 602120 | tf_op jit(solution)/shard_map/ppermute | solution.py:432
  39.4 0.0 collective-permute-done.7.below_ref
  39.4 0.0 copy-done.2
  39.4 3.7 %shard_map.97 = (f32[1536,128]{1,0:T(8,128)}, f32[1536,128]{1,0:T(8,128)S(1)}) custom-call(f32[1536,128]{1,0:T(8,128)} %get-tuple-element.63.m_ref, f32[1536,128]{1,0:T(8,128)S(1)} %bitcast.34, bf16[192,8,128]{2,1,0:T(8,128)(2,1)S(1)} %bitcast.36, f32[480,128]{1,0:T(8,128)S(1)} %collective-permute-done.7.below_ref, ...), custom_call_target="tpu_custom_call" | custom-call | flops 300000000 | bytes 30000000 | tf_op jit(solution)/shard_map/pallas_call | solution.py:412
  43.1 0.2 collective-permute-done.11.ax_ref
  43.4 0.0 collective-permute-done.10.above_ref
  43.4 0.8 %shard_map.98 = (f32[1536,128]{1,0:T(8,128)S(1)}, s32[1]{0:T(128)}) custom-call(s32[1]{0:T(128)} %bitcast.12.where_ref, f32[1536,128]{1,0:T(8,128)S(1)} %get-tuple-element.69.bottom_ref, f32[488,128]{1,0:T(8,128)S(1)} %collective-permute-done.10.above_ref, f32[392,128]{1,0:T(8,128)S(1)} %collective-permute-done.11.ax_ref, ...), custom_call_target="tpu_custom_call" | custom-call | flops 1000000 | bytes 100000 | tf_op jit(solution)/shard_map/pallas_call | solution.py:412
  44.9 0.0 copy-done.9
  44.9 0.0 copy-done.10
  44.9 0.0 copy-start.11
  44.9 0.9 %copy-done.11 = f32[4,48,2,4,128]{4,3,2,1,0:T(4,128)} copy-done((f32[4,48,2,4,128]{4,3,2,1,0:T(4,128)}, f32[4,48,2,4,128]{4,3,2,1,0:T(4,128)S(1)}, u32[]{:S(2)}) %copy-start.11) | copy-done | bytes 786456
  (12 shorter events, 0.1 us)
Async XLA Ops:
  0.0 6.0 %copy-start = (f32[4,48,2,4,128]{4,3,2,1,0:T(4,128)S(1)}, f32[4,48,2,4,128]{4,3,2,1,0:T(4,128)}, u32[]{:S(2)}) copy-start(f32[4,48,2,4,128]{4,3,2,1,0:T(4,128)} %param.11) | copy-start | bytes 2359300
  0.0 6.0 %copy-start.4 = (s32[3,2,4,128]{3,2,1,0:T(4,128)S(1)}, s32[3,2,4,128]{3,2,1,0:T(4,128)}, u32[]{:S(2)}) copy-start(s32[3,2,4,128]{3,2,1,0:T(4,128)} %param.15) | copy-start | bytes 36868
  1.9 4.2 %copy-start.3 = (f32[3,2,4,128]{3,2,1,0:T(4,128)S(1)}, f32[3,2,4,128]{3,2,1,0:T(4,128)}, u32[]{:S(2)}) copy-start(f32[3,2,4,128]{3,2,1,0:T(4,128)} %param.14) | copy-start | bytes 36868
  1.9 19.8 %collective-permute-start.4 = (f32[776,128]{1,0:T(8,128)}, f32[776,128]{1,0:T(8,128)S(1)}, u32[]{:S(2)}, u32[]{:S(2)}) collective-permute-start(f32[776,128]{1,0:T(8,128)} %bitcast.19), channel_id=1, source_target_pairs={{0,24},{8,0},{16,8},{24,16},{1,25},{9,1},{17,9},{25,17},{2,26},{10... | collective-permute-start | bytes 1191944 | tf_op jit(solution)/shard_map/ppermute | solution.py:425
  6.0 11.2 %copy-start.1 = (bf16[4,48,2,4,128]{4,3,2,1,0:T(4,128)(2,1)S(1)}, bf16[4,48,2,4,128]{4,3,2,1,0:T(4,128)(2,1)}, u32[]{:S(2)}) copy-start(bf16[4,48,2,4,128]{4,3,2,1,0:T(4,128)(2,1)} %param.13) | copy-start | bytes 1179652
  6.9 16.6 %collective-permute-start.6 = (f32[776,128]{1,0:T(8,128)S(1)}, f32[776,128]{1,0:T(8,128)S(1)}, u32[]{:S(2)}, u32[]{:S(2)}) collective-permute-start(f32[776,128]{1,0:T(8,128)S(1)} %get-tuple-element.58), channel_id=1, source_target_pairs={{0,8},{8,16},{16,24},{24,0},{1,9},{9,17},{17,25},{25,1},{2,10},{10... | collective-permute-start | bytes 1191944 | tf_op jit(solution)/shard_map/ppermute | solution.py:425
  6.9 5.9 %collective-permute-start.2 = (f32[1,1664]{1,0:T(1,128)S(1)}, f32[1,1664]{1,0:T(1,128)S(1)}, u32[]{:S(2)}, u32[]{:S(2)}) collective-permute-start(f32[1,1664]{1,0:T(1,128)S(1)} %get-tuple-element.52), channel_id=1, source_target_pairs={{0,2},{2,4},{4,6},{1,3},{3,5},{5,7},{8,10},{10,12},{12,14},{9,11},... | collective-permute-start | bytes 19976 | tf_op jit(solution)/shard_map/ppermute | solution.py:425
  10.9 5.0 %collective-permute-start.3 = (f32[1,1664]{1,0:T(1,128)S(1)}, f32[1,1664]{1,0:T(1,128)S(1)}, u32[]{:S(2)}, u32[]{:S(2)}) collective-permute-start(f32[1,1664]{1,0:T(1,128)S(1)} %get-tuple-element.53), channel_id=1, source_target_pairs={{2,0},{4,2},{6,4},{3,1},{5,3},{7,5},{10,8},{12,10},{14,12},{11,9},... | collective-permute-start | bytes 19976 | tf_op jit(solution)/shard_map/ppermute | solution.py:425
  12.9 4.3 %copy-start.5 = (s32[2,4,128]{2,1,0:T(4,128)S(1)}, s32[2,4,128]{2,1,0:T(4,128)}, u32[]{:S(2)}) copy-start(s32[2,4,128]{2,1,0:T(4,128)} %param.16) | copy-start | bytes 12292
  15.9 5.7 %collective-permute-start.5 = (f32[400,128]{1,0:T(8,128)S(1)}, f32[400,128]{1,0:T(8,128)S(1)}, u32[]{:S(2)}, u32[]{:S(2)}) collective-permute-start(f32[400,128]{1,0:T(8,128)S(1)} %dynamic_update_slice.13), channel_id=1, source_target_pairs={{0,1},{1,0},{2,3},{3,2},{4,5},{5,4},{6,7},{7,6},{8,9},{9,8},{10,11... | collective-permute-start | bytes 614408 | tf_op jit(solution)/shard_map/ppermute | solution.py:432
  17.2 0.7 %copy-start.6 = (f32[48]{0:T(128)S(1)}, f32[48]{0:T(128)}, u32[]{:S(2)}) copy-start(f32[48]{0:T(128)} %growth_ref.3) | copy-start | bytes 580
  17.2 0.7 %copy-start.7 = (f32[48]{0:T(128)S(1)}, f32[48]{0:T(128)}, u32[]{:S(2)}) copy-start(f32[48]{0:T(128)} %transfer_ref.3) | copy-start | bytes 580
  17.2 0.7 %copy-start.8 = (f32[4]{0:T(128)S(1)}, f32[4]{0:T(128)}, u32[]{:S(2)}) copy-start(f32[4]{0:T(128)} %rate_ref.3) | copy-start | bytes 52
  23.4 16.0 %collective-permute-start.7 = (f32[480,128]{1,0:T(8,128)}, f32[480,128]{1,0:T(8,128)S(1)}, u32[]{:S(2)}, u32[]{:S(2)}) collective-permute-start(f32[480,128]{1,0:T(8,128)} %get-tuple-element.64), channel_id=1, source_target_pairs={{0,8},{8,16},{16,24},{24,0},{1,9},{9,17},{17,25},{25,1},{2,10},{10... | collective-permute-start | bytes 737288 | tf_op jit(solution)/shard_map/ppermute | solution.py:425
  23.5 15.9 %copy-start.2 = (bf16[4,48,2,4,128]{4,3,2,1,0:T(4,128)(2,1)S(1)}, bf16[4,48,2,4,128]{4,3,2,1,0:T(4,128)(2,1)}, u32[]{:S(2)}) copy-start(bf16[4,48,2,4,128]{4,3,2,1,0:T(4,128)(2,1)} %param.12) | copy-start | bytes 1179652
  24.9 18.4 %collective-permute-start.10 = (f32[488,128]{1,0:T(8,128)S(1)}, f32[488,128]{1,0:T(8,128)S(1)}, u32[]{:S(2)}, u32[]{:S(2)}) collective-permute-start(f32[488,128]{1,0:T(8,128)S(1)} %get-tuple-element.70), channel_id=1, source_target_pairs={{0,24},{8,0},{16,8},{24,16},{1,25},{9,1},{17,9},{25,17},{2,26},{10... | collective-permute-start | bytes 749576 | tf_op jit(solution)/shard_map/ppermute | solution.py:425
  28.3 6.6 %collective-permute-start.8 = (f32[1,1536]{1,0:T(1,128)S(1)}, f32[1,1536]{1,0:T(1,128)S(1)}, u32[]{:S(2)}, u32[]{:S(2)}) collective-permute-start(f32[1,1536]{1,0:T(1,128)S(1)} %get-tuple-element.65), channel_id=1, source_target_pairs={{0,2},{2,4},{4,6},{1,3},{3,5},{5,7},{8,10},{10,12},{12,14},{9,11},... | collective-permute-start | bytes 18440 | tf_op jit(solution)/shard_map/ppermute | solution.py:425
  33.0 5.1 %collective-permute-start.9 = (f32[1,1536]{1,0:T(1,128)S(1)}, f32[1,1536]{1,0:T(1,128)S(1)}, u32[]{:S(2)}, u32[]{:S(2)}) collective-permute-start(f32[1,1536]{1,0:T(1,128)S(1)} %get-tuple-element.66), channel_id=1, source_target_pairs={{2,0},{4,2},{6,4},{3,1},{5,3},{7,5},{10,8},{12,10},{14,12},{11,9},... | collective-permute-start | bytes 18440 | tf_op jit(solution)/shard_map/ppermute | solution.py:425
  38.1 5.2 %collective-permute-start.11 = (f32[392,128]{1,0:T(8,128)S(1)}, f32[392,128]{1,0:T(8,128)S(1)}, u32[]{:S(2)}, u32[]{:S(2)}) collective-permute-start(f32[392,128]{1,0:T(8,128)S(1)} %dynamic_update_slice.15), channel_id=1, source_target_pairs={{0,1},{1,0},{2,3},{3,2},{4,5},{5,4},{6,7},{7,6},{8,9},{9,8},{10,11... | collective-permute-start | bytes 602120 | tf_op jit(solution)/shard_map/ppermute | solution.py:432
  43.4 1.5 %copy-start.9 = (f32[1536,128]{1,0:T(8,128)S(1)}, f32[1536,128]{1,0:T(8,128)}, u32[]{:S(2)}) copy-start(f32[1536,128]{1,0:T(8,128)} %get-tuple-element.63.m_ref) | copy-start | bytes 2359300
  43.4 1.5 %copy-start.10 = (f32[1536,128]{1,0:T(8,128)S(1)}, f32[1536,128]{1,0:T(8,128)}, u32[]{:S(2)}) copy-start(f32[1536,128]{1,0:T(8,128)} %get-tuple-element.77) | copy-start | bytes 2359300
  44.9 0.9 %copy-start.11 = (f32[4,48,2,4,128]{4,3,2,1,0:T(4,128)}, f32[4,48,2,4,128]{4,3,2,1,0:T(4,128)S(1)}, u32[]{:S(2)}) copy-start(f32[4,48,2,4,128]{4,3,2,1,0:T(4,128)S(1)} %get-tuple-element.105) | copy-start | bytes 2359300

commit v11 on v9

--- a/solution.py
+++ b/solution.py
@@ -151,7 +151,7 @@
         out_ref[spots] = out_ref[spots] + coefficient[first_row + z : first_row + z + 1] * halo[:, 128 * z : 128 * z + 128]
 
 
-def pack_sides(comps, x_ref, where_ref, ax_ref, radup_ref, raddn_ref):
+def pack_sides(comps, last, x_ref, where_ref, rad_ref, ax_ref, radup_ref, raddn_ref):
     @pl.when(where_ref[0] == 0)
     def _():
         ax_ref[0 : 2 * comps] = x_ref[pl.ds(3, 2 * comps, stride=4)]
@@ -161,8 +161,8 @@
         ax_ref[0 : 2 * comps] = x_ref[pl.ds(0, 2 * comps, stride=4)]
 
     ends = columns(x_ref[...])
-    radup_ref[:, 0 : 8 * comps] = ends[0:1]
-    raddn_ref[:, 0 : 8 * comps] = ends[1:2]
+    radup_ref[:, 0 : 8 * comps] = jnp.where(rad_ref[0] < last, ends[0:1], 0.0)
+    raddn_ref[:, 0 : 8 * comps] = jnp.where(rad_ref[0] > 0, ends[1:2], 0.0)
 
 
 def columns(x):
@@ -180,16 +180,16 @@
     return lax.dot_general(both, place, (((0,), (0,)), ((), ())), precision=exact, preferred_element_type=f32)
 
 
-def first_rest(comps, where_ref, a_ref, speeds_ref, flags_ref, up_ref, ax_ref, radup_ref, raddn_ref):
+def first_rest(comps, last, where_ref, rad_ref, a_ref, speeds_ref, flags_ref, up_ref, ax_ref, radup_ref, raddn_ref):
     p, _ = faces(speeds_ref, flags_ref)
     for c in range(comps):
         up_ref[4 * c : 4 * c + 4] = a_ref[8 * c + 4 : 8 * c + 8]
     up_ref[4 * comps :] = p[0]
-    pack_sides(comps, a_ref, where_ref, ax_ref, radup_ref, raddn_ref)
+    pack_sides(comps, last, a_ref, where_ref, rad_ref, ax_ref, radup_ref, raddn_ref)
     ax_ref[2 * comps : 2 * comps + 8] = pair_rows(p[1], 0, 4)
     radup_ref[:, 8 * comps :] = jnp.zeros((1, 128), f32)
     raddn_ref[:, 8 * comps :] = jnp.zeros((1, 128), f32)
-    raddn_ref[:, 8 * comps : 8 * comps + 8] = columns(p[2])[1:2]
+    raddn_ref[:, 8 * comps : 8 * comps + 8] = jnp.where(rad_ref[0] > 0, columns(p[2])[1:2], 0.0)
 
 
 def source(sections, x_ref, u_ref, growth_ref, transfer_ref, zones_ref, rate_ref, finish):
@@ -360,7 +360,9 @@
 
 def first_bottom(
     comps,
+    last,
     where_ref,
+    rad_ref,
     part_ref,
     below_ref,
     edge_ref,
@@ -380,7 +382,7 @@
     encode(comps, m_ref, 0, low_ref, high_ref, dn_ref)
     worse_ref[...] = bad_ref[...] + crowded(below_ref[4 * comps :])
     dn_ref[5 * comps // 2 :] = worse_ref[...]
-    pack_sides(comps, m_ref, where_ref, ax_ref, radup_ref, raddn_ref)
+    pack_sides(comps, last, m_ref, where_ref, rad_ref, ax_ref, radup_ref, raddn_ref)
 
 
 def second_sides(
@@ -429,7 +431,7 @@
 
 def sides(ax, radup, raddn):
     ax = lax.ppermute(ax, "axial", [(0, 1), (1, 0)])
-    return ax, shift(radup, "rad", 1, False), shift(raddn, "rad", -1, False)
+    return ax, shift(radup, "rad", 1, True), shift(raddn, "rad", -1, True)
 
 
 def shards(adjoint_final, state_start, state_middle, speeds, flags, zones, growth_rate, transfer_rate, nucleation_rate):
@@ -444,6 +446,8 @@
     speeds2 = speeds.reshape(3, 8, 128)
     flags2 = flags.reshape(3, 8, 128)
     where = lax.axis_index("axial").reshape(1)
+    place = (where, lax.axis_index("rad").reshape(1))
+    last = lax.axis_size("rad") - 1
     rates = (zones.reshape(8, 128), growth_rate, transfer_rate, nucleation_rate)
     message = 5 * comps // 2
     tables = [jax.ShapeDtypeStruct((256, 512), bf16)] * 2
@@ -454,12 +458,12 @@
     dn = dn + lax.pad(speeds, 0.0, after) * lax.pad(flags, 0, after).astype(f32)
     above = shift(dn.reshape(half + 8, 128), "azim", -1, True)
     up, *edges = call(
-        functools.partial(first_rest, comps),
-        "svvv",
+        functools.partial(first_rest, comps, last),
+        "ssvvv",
         "vvvv",
         [(half + 8, 128), (rows + 8, 128), (1, cells + 128), (1, cells + 128)],
         2_000_000,
-        where,
+        *place,
         a,
         speeds2,
         flags2,
@@ -494,12 +498,12 @@
     )
     next_below = shift(up, "azim", 1, True)
     m, dn, *edges, bad = call(
-        functools.partial(first_bottom, comps),
-        "s" + "v" * 6,
+        functools.partial(first_bottom, comps, last),
+        "ss" + "v" * 6,
         "v" * 6,
         [(cells, 128), (message + 8, 128), (rows, 128), (1, cells), (1, cells), (8, 128)],
         10_000,
-        where,
+        *place,
         part,
         below,
         edge,

time: 42.2 us -> 38.4 us (0.910)
  the two profiles are of different devices: /device:TPU:1 before, /device:TPU:0 now
where the time goes in v11:
time: 38.4 us; the launch traced here: 38.3 us
  starting transfers between devices  14.2 us (37%)
  waiting for transfers between devices  11.1 us (29%)
  Pallas kernels  9.48 us (25%)
  local copies, waits for them, and re-layouts  1.57 us (4%)
  other arithmetic  1.1 us (3%)
  between operations  0.81 us (2%)
    ppermute x8, starting transfers between devices, shift(): return lax.ppermute(x, axis, pairs)  11.1 us
    pallas_call x7, Pallas kernels, call(): pl.pallas_call(body, in_specs=[SPACES[s] for s in ins], out_specs=[SPACES...  9.48 us
    ppermute x8, waiting for transfers between devices, shift(): return lax.ppermute(x, axis, pairs)  9.23 us
    ppermute x2, starting transfers between devices, sides(): ax = lax.ppermute(ax, 'axial', [(0, 1), (1, 0)])  3.13 us
    ppermute x2, waiting for transfers between devices, sides(): ax = lax.ppermute(ax, 'axial', [(0, 1), (1, 0)])  1.83 us
    unnamed x20, local copies, waits for them, and re-layouts  1.57 us
    add x1, other arithmetic, shards(): dn = dn + lax.pad(speeds, 0.0, after) * lax.pad(flags, 0, after).astype(f32)  1.1 us
  transfers between devices with their start and end apart: 10, of which 4 were waited for; matrix products, arithmetic and copies ran while one was open for 0% of the time, Pallas kernels for 22%

profile of v11, /device:TPU:0, one launch (start us, length us, event | category | flops | bytes accessed | tf_op | source)
XLA Modules:
  0.0 38.3 jit_solution(3601073820836569360)
XLA Ops:
  0.0 0.0 copy-start
  0.0 0.0 copy-start.4
  0.0 1.1 %fusion = f32[194,1,4,128]{3,2,1,0:T(4,128)S(1)} fusion(f32[192,2,4,128]{3,2,1,0:T(4,128)} %bitcast.26, f32[3,2,4,128]{3,2,1,0:T(4,128)} %param.14, s32[3,2,4,128]{3,2,1,0:T(4,128)} %param.15), kind=kLoop, calls=%fused_computation.6 | loop fusion | flops 297984 | bytes 1208320 | tf_op jit(solution)/shard_map/add | solution.py:458
  1.1 0.0 copy-start.3
  1.1 5.1 %collective-permute-start.2 = (f32[776,128]{1,0:T(8,128)S(1)}, f32[776,128]{1,0:T(8,128)S(1)}, u32[]{:S(2)}, u32[]{:S(2)}) collective-permute-start(f32[776,128]{1,0:T(8,128)S(1)} %bitcast.45), channel_id=1, source_target_pairs={{0,24},{8,0},{16,8},{24,16},{1,25},{9,1},{17,9},{25,17},{2,26},{10... | collective-permute-start | bytes 1191944 | tf_op jit(solution)/shard_map/ppermute | solution.py:429
  6.2 0.0 copy-done
  6.2 0.0 copy-done.4
  6.2 0.0 copy-done.3
  6.2 0.0 copy-start.1
  6.2 0.9 %shard_map.94 = (f32[776,128]{1,0:T(8,128)S(1)}, f32[392,128]{1,0:T(8,128)S(1)}, f32[1,1664]{1,0:T(1,128)S(1)}, f32[1,1664]{1,0:T(1,128)S(1)}) custom-call(s32[1]{0:T(128)} %bitcast.9.where_ref, s32[1]{0:T(128)} %bitcast.10.rad_ref, f32[1536,128]{1,0:T(8,128)S(1)} %bitcast.27, f32[3,8,128]{2,1,0:T(8,128)S(1)} %bitcast.33, s32[3,8,128]{2,1,0:T(8,128)S(1)} %bitcast.37), custom_call_target="tpu_custom_call" | custom-call | flops 2000000 | bytes 200000 | tf_op jit(solution)/shard_map/pallas_call | solution.py:416
  7.1 0.1 collective-permute-start.6
  7.2 0.0 copy-start.5
  7.2 1.6 %collective-permute-start.3 = (f32[392,128]{1,0:T(8,128)S(1)}, f32[392,128]{1,0:T(8,128)S(1)}, u32[]{:S(2)}, u32[]{:S(2)}) collective-permute-start(f32[392,128]{1,0:T(8,128)S(1)} %get-tuple-element.48), channel_id=1, source_target_pairs={{0,1},{1,0},{2,3},{3,2},{4,5},{5,4},{6,7},{7,6},{8,9},{9,8},{10,11... | collective-permute-start | bytes 602120 | tf_op jit(solution)/shard_map/ppermute | solution.py:433
  8.8 0.0 collective-permute-start.4
  8.8 1.7 %collective-permute-start.5 = (f32[1,1664]{1,0:T(1,128)S(1)}, f32[1,1664]{1,0:T(1,128)S(1)}, u32[]{:S(2)}, u32[]{:S(2)}) collective-permute-start(f32[1,1664]{1,0:T(1,128)S(1)} %get-tuple-element.50), channel_id=1, source_target_pairs={{0,6},{2,0},{4,2},{6,4},{1,7},{3,1},{5,3},{7,5},{8,14},{10,8},{12,... | collective-permute-start | bytes 19976 | tf_op jit(solution)/shard_map/ppermute | solution.py:429
  10.5 0.0 copy-start.6
  10.5 0.0 copy-start.7
  10.5 0.0 copy-start.8
  10.5 0.0 copy-done.1
  10.5 0.0 copy-done.5
  10.5 0.6 %copy-done.6 = f32[48]{0:T(128)S(1)} copy-done((f32[48]{0:T(128)S(1)}, f32[48]{0:T(128)}, u32[]{:S(2)}) %copy-start.6) | copy-done | bytes 216
  11.2 0.0 copy-done.7
  11.2 0.0 copy-done.8
  11.2 1.6 %shard_map.93 = (f32[1536,128]{1,0:T(8,128)S(1)}, bf16[256,512]{1,0:T(8,128)(2,1)S(1)}, bf16[256,512]{1,0:T(8,128)(2,1)S(1)}, bf16[256,512]{1,0:T(8,128)(2,1)S(1)}, bf16[256,512]{1,0:T(8,128)(2,1)S(1)}) custom-call(f32[1536,128]{1,0:T(8,128)S(1)} %bitcast.28, bf16[192,8,128]{2,1,0:T(8,128)(2,1)S(1)} %bitcast.31, f32[3,8,128]{2,1,0:T(8,128)S(1)} %bitcast.34, ...), custom_call_target="tpu_custom_call" | custom-call | flops 8000000 | bytes 800000 | tf_op jit(solution)/shard_map/pallas_call | solution.py:416
  12.8 0.0 collective-permute-done.4.radlo_ref
  12.8 0.0 collective-permute-done.5.radhi_ref
  12.8 0.9 %collective-permute-done.3.ax_ref = f32[392,128]{1,0:T(8,128)S(1)} collective-permute-done((f32[392,128]{1,0:T(8,128)S(1)}, f32[392,128]{1,0:T(8,128)S(1)}, u32[]{:S(2)}, u32[]{:S(2)}) %collective-permute-start.3) | collective-permute-done | bytes 200736 | tf_op jit(solution)/shard_map/ppermute | solution.py:433
  13.7 2.1 %collective-permute-done.2.above_ref = f32[776,128]{1,0:T(8,128)S(1)} collective-permute-done((f32[776,128]{1,0:T(8,128)S(1)}, f32[776,128]{1,0:T(8,128)S(1)}, u32[]{:S(2)}, u32[]{:S(2)}) %collective-permute-start.2) | collective-permute-done | bytes 397344 | tf_op jit(solution)/shard_map/ppermute | solution.py:429
  15.8 2.3 %shard_map.95 = (f32[1536,128]{1,0:T(8,128)S(1)}, f32[4,8,128]{2,1,0:T(8,128)S(1)}, f32[480,128]{1,0:T(8,128)S(1)}, f32[8,128]{1,0:T(8,128)S(1)}, bf16[256,512]{...) custom-call(s32[1]{0:T(128)} %bitcast.9.where_ref, ...), custom_call_target="tpu_custom_call" | custom-call | flops 4000000 | bytes 400000 | tf_op jit(solution)/shard_map/pallas_call | solution.py:416
  18.1 0.1 collective-permute-start.7
  18.2 7.1 %collective-permute-done.6.below_ref = f32[776,128]{1,0:T(8,128)S(1)} collective-permute-done((f32[776,128]{1,0:T(8,128)S(1)}, f32[776,128]{1,0:T(8,128)S(1)}, u32[]{:S(2)}, u32[]{:S(2)}) %collective-permute-start.6) | collective-permute-done | bytes 397344 | tf_op jit(solution)/shard_map/ppermute | solution.py:429
  25.2 0.0 copy-start.2
  25.3 1.2 %shard_map.96 = (f32[1536,128]{1,0:T(8,128)S(1)}, f32[488,128]{1,0:T(8,128)S(1)}, f32[384,128]{1,0:T(8,128)S(1)}, f32[1,1536]{1,0:T(1,128)S(1)}, f32[1,1536]{1,0:T(1,128)S(1)}, /*index=5*/f32[8,128]{1,0:T(8,128)S(1)}) custom-call(s32[1]{0:T(128)} %bitcast.9.where_ref, s32[1]{0:T(128)} %bitcast.10.rad_ref, f32[1536,128]{1,0:T(8,128)S(1)} %get-tuple-element.51.part_ref, ...), custom_call_target="tpu_custom_call" | custom-call | flops 10000 | bytes 1000 | tf_op jit(solution)/shard_map/pallas_call | solution.py:416
  26.5 2.4 %collective-permute-start.11 = (f32[488,128]{1,0:T(8,128)S(1)}, f32[488,128]{1,0:T(8,128)S(1)}, u32[]{:S(2)}, u32[]{:S(2)}) collective-permute-start(f32[488,128]{1,0:T(8,128)S(1)} %get-tuple-element.67), channel_id=1, source_target_pairs={{0,24},{8,0},{16,8},{24,16},{1,25},{9,1},{17,9},{25,17},{2,26},{10... | collective-permute-start | bytes 749576 | tf_op jit(solution)/shard_map/ppermute | solution.py:429
  28.9 1.5 %collective-permute-start.8 = (f32[384,128]{1,0:T(8,128)S(1)}, f32[384,128]{1,0:T(8,128)S(1)}, u32[]{:S(2)}, u32[]{:S(2)}) collective-permute-start(f32[384,128]{1,0:T(8,128)S(1)} %get-tuple-element.63), channel_id=1, source_target_pairs={{0,1},{1,0},{2,3},{3,2},{4,5},{5,4},{6,7},{7,6},{8,9},{9,8},{10,11... | collective-permute-start | bytes 589832 | tf_op jit(solution)/shard_map/ppermute | solution.py:433
  30.5 0.0 collective-permute-start.9
  30.5 1.7 %collective-permute-start.10 = (f32[1,1536]{1,0:T(1,128)S(1)}, f32[1,1536]{1,0:T(1,128)S(1)}, u32[]{:S(2)}, u32[]{:S(2)}) collective-permute-start(f32[1,1536]{1,0:T(1,128)S(1)} %get-tuple-element.65), channel_id=1, source_target_pairs={{0,6},{2,0},{4,2},{6,4},{1,7},{3,1},{5,3},{7,5},{8,14},{10,8},{12,... | collective-permute-start | bytes 18440 | tf_op jit(solution)/shard_map/ppermute | solution.py:429
  32.2 0.0 collective-permute-done.7.below_ref
  32.2 0.0 copy-done.2
  32.2 1.6 %shard_map.97 = (f32[1536,128]{1,0:T(8,128)S(1)}, f32[1536,128]{1,0:T(8,128)S(1)}) custom-call(f32[1536,128]{1,0:T(8,128)S(1)} %get-tuple-element.57.m_ref, f32[1536,128]{1,0:T(8,128)S(1)} %bitcast.30, bf16[192,8,128]{2,1,0:T(8,128)(2,1)S(1)} %bitcast.32, f32[480,128]{1,0:T(8,128)S(1)} %collective-permute-done.7.below_ref, ...), custom_call_target="tpu_custom_call" | custom-call | flops 300000000 | bytes 30000000 | tf_op jit(solution)/shard_map/pallas_call | solution.py:416
  33.8 0.0 collective-permute-done.9.radlo_ref
  33.8 0.0 collective-permute-done.10.radhi_ref
  33.8 1.0 %collective-permute-done.8.ax_ref = f32[384,128]{1,0:T(8,128)S(1)} collective-permute-done((f32[384,128]{1,0:T(8,128)S(1)}, f32[384,128]{1,0:T(8,128)S(1)}, u32[]{:S(2)}, u32[]{:S(2)}) %collective-permute-start.8) | collective-permute-done | bytes 196640 | tf_op jit(solution)/shard_map/ppermute | solution.py:433
  34.8 0.9 %shard_map.98 = (f32[1536,128]{1,0:T(8,128)S(1)}, f32[1536,128]{1,0:T(8,128)S(1)}) custom-call(s32[1]{0:T(128)} %bitcast.9.where_ref, f32[1536,128]{1,0:T(8,128)S(1)} %get-tuple-element.61.part_ref, f32[1536,128]{1,0:T(8,128)S(1)} %get-tuple-element.62.bottom_ref, f32[384,128]{1,0:T(8,128)S(1)} %collective-permute-done.8.ax_ref, ...), custom_call_target="tpu_custom_call" | custom-call | flops 10000 | bytes 1000 | tf_op jit(solution)/shard_map/pallas_call | solution.py:416
  35.8 0.0 collective-permute-done.11.above_ref
  35.8 0.9 %shard_map.99 = (f32[1536,128]{1,0:T(8,128)S(1)}, s32[1]{0:T(128)}) custom-call(f32[1536,128]{1,0:T(8,128)S(1)} %get-tuple-element.66.full_ref, f32[488,128]{1,0:T(8,128)S(1)} %collective-permute-done.11.above_ref, f32[4,8,128]{2,1,0:T(8,128)S(1)} %get-tuple-element.53.edge_ref, f32[8,128]{1,0:T(8,128)S(1)} %get-tuple-element.68.bad_ref, ...), custom_call_target="tpu_custom_call" | custom-call | flops 1000000 | bytes 100000 | tf_op jit(solution)/shard_map/pallas_call | solution.py:416
  37.4 0.0 copy-start.9
  37.4 0.9 %copy-done.9 = f32[4,48,2,4,128]{4,3,2,1,0:T(4,128)} copy-done((f32[4,48,2,4,128]{4,3,2,1,0:T(4,128)}, f32[4,48,2,4,128]{4,3,2,1,0:T(4,128)S(1)}, u32[]{:S(2)}) %copy-start.9) | copy-done | bytes 786456
  (1 shorter events, 0.0 us)
Async XLA Ops:
  0.0 6.2 %copy-start = (f32[4,48,2,4,128]{4,3,2,1,0:T(4,128)S(1)}, f32[4,48,2,4,128]{4,3,2,1,0:T(4,128)}, u32[]{:S(2)}) copy-start(f32[4,48,2,4,128]{4,3,2,1,0:T(4,128)} %param.11) | copy-start | bytes 2359300
  0.0 6.2 %copy-start.4 = (s32[3,2,4,128]{3,2,1,0:T(4,128)S(1)}, s32[3,2,4,128]{3,2,1,0:T(4,128)}, u32[]{:S(2)}) copy-start(s32[3,2,4,128]{3,2,1,0:T(4,128)} %param.15) | copy-start | bytes 36868
  1.1 5.1 %copy-start.3 = (f32[3,2,4,128]{3,2,1,0:T(4,128)S(1)}, f32[3,2,4,128]{3,2,1,0:T(4,128)}, u32[]{:S(2)}) copy-start(f32[3,2,4,128]{3,2,1,0:T(4,128)} %param.14) | copy-start | bytes 36868
  1.1 14.7 %collective-permute-start.2 = (f32[776,128]{1,0:T(8,128)S(1)}, f32[776,128]{1,0:T(8,128)S(1)}, u32[]{:S(2)}, u32[]{:S(2)}) collective-permute-start(f32[776,128]{1,0:T(8,128)S(1)} %bitcast.45), channel_id=1, source_target_pairs={{0,24},{8,0},{16,8},{24,16},{1,25},{9,1},{17,9},{25,17},{2,26},{10... | collective-permute-start | bytes 1191944 | tf_op jit(solution)/shard_map/ppermute | solution.py:429
  6.2 4.3 %copy-start.1 = (bf16[4,48,2,4,128]{4,3,2,1,0:T(4,128)(2,1)S(1)}, bf16[4,48,2,4,128]{4,3,2,1,0:T(4,128)(2,1)}, u32[]{:S(2)}) copy-start(bf16[4,48,2,4,128]{4,3,2,1,0:T(4,128)(2,1)} %param.13) | copy-start | bytes 1179652
  7.1 18.2 %collective-permute-start.6 = (f32[776,128]{1,0:T(8,128)S(1)}, f32[776,128]{1,0:T(8,128)S(1)}, u32[]{:S(2)}, u32[]{:S(2)}) collective-permute-start(f32[776,128]{1,0:T(8,128)S(1)} %get-tuple-element.52), channel_id=1, source_target_pairs={{0,8},{8,16},{16,24},{24,0},{1,9},{9,17},{17,25},{25,1},{2,10},{10... | collective-permute-start | bytes 1191944 | tf_op jit(solution)/shard_map/ppermute | solution.py:429
  7.2 3.4 %copy-start.5 = (s32[2,4,128]{2,1,0:T(4,128)S(1)}, s32[2,4,128]{2,1,0:T(4,128)}, u32[]{:S(2)}) copy-start(s32[2,4,128]{2,1,0:T(4,128)} %param.16) | copy-start | bytes 12292
  7.2 6.5 %collective-permute-start.3 = (f32[392,128]{1,0:T(8,128)S(1)}, f32[392,128]{1,0:T(8,128)S(1)}, u32[]{:S(2)}, u32[]{:S(2)}) collective-permute-start(f32[392,128]{1,0:T(8,128)S(1)} %get-tuple-element.48), channel_id=1, source_target_pairs={{0,1},{1,0},{2,3},{3,2},{4,5},{5,4},{6,7},{7,6},{8,9},{9,8},{10,11... | collective-permute-start | bytes 602120 | tf_op jit(solution)/shard_map/ppermute | solution.py:433
  8.8 4.0 %collective-permute-start.4 = (f32[1,1664]{1,0:T(1,128)S(1)}, f32[1,1664]{1,0:T(1,128)S(1)}, u32[]{:S(2)}, u32[]{:S(2)}) collective-permute-start(f32[1,1664]{1,0:T(1,128)S(1)} %get-tuple-element.49), channel_id=1, source_target_pairs={{0,2},{2,4},{4,6},{6,0},{1,3},{3,5},{5,7},{7,1},{8,10},{10,12},{12... | collective-permute-start | bytes 19976 | tf_op jit(solution)/shard_map/ppermute | solution.py:429
  8.8 4.1 %collective-permute-start.5 = (f32[1,1664]{1,0:T(1,128)S(1)}, f32[1,1664]{1,0:T(1,128)S(1)}, u32[]{:S(2)}, u32[]{:S(2)}) collective-permute-start(f32[1,1664]{1,0:T(1,128)S(1)} %get-tuple-element.50), channel_id=1, source_target_pairs={{0,6},{2,0},{4,2},{6,4},{1,7},{3,1},{5,3},{7,5},{8,14},{10,8},{12,... | collective-permute-start | bytes 19976 | tf_op jit(solution)/shard_map/ppermute | solution.py:429
  10.5 0.7 %copy-start.6 = (f32[48]{0:T(128)S(1)}, f32[48]{0:T(128)}, u32[]{:S(2)}) copy-start(f32[48]{0:T(128)} %growth_ref.3) | copy-start | bytes 580
  10.5 0.7 %copy-start.7 = (f32[48]{0:T(128)S(1)}, f32[48]{0:T(128)}, u32[]{:S(2)}) copy-start(f32[48]{0:T(128)} %transfer_ref.3) | copy-start | bytes 580
  10.5 0.7 %copy-start.8 = (f32[4]{0:T(128)S(1)}, f32[4]{0:T(128)}, u32[]{:S(2)}) copy-start(f32[4]{0:T(128)} %rate_ref.3) | copy-start | bytes 52
  18.1 14.1 %collective-permute-start.7 = (f32[480,128]{1,0:T(8,128)S(1)}, f32[480,128]{1,0:T(8,128)S(1)}, u32[]{:S(2)}, u32[]{:S(2)}) collective-permute-start(f32[480,128]{1,0:T(8,128)S(1)} %get-tuple-element.58), channel_id=1, source_target_pairs={{0,8},{8,16},{16,24},{24,0},{1,9},{9,17},{17,25},{25,1},{2,10},{10... | collective-permute-start | bytes 737288 | tf_op jit(solution)/shard_map/ppermute | solution.py:429
  25.2 7.0 %copy-start.2 = (bf16[4,48,2,4,128]{4,3,2,1,0:T(4,128)(2,1)S(1)}, bf16[4,48,2,4,128]{4,3,2,1,0:T(4,128)(2,1)}, u32[]{:S(2)}) copy-start(bf16[4,48,2,4,128]{4,3,2,1,0:T(4,128)(2,1)} %param.12) | copy-start | bytes 1179652
  26.5 9.3 %collective-permute-start.11 = (f32[488,128]{1,0:T(8,128)S(1)}, f32[488,128]{1,0:T(8,128)S(1)}, u32[]{:S(2)}, u32[]{:S(2)}) collective-permute-start(f32[488,128]{1,0:T(8,128)S(1)} %get-tuple-element.67), channel_id=1, source_target_pairs={{0,24},{8,0},{16,8},{24,16},{1,25},{9,1},{17,9},{25,17},{2,26},{10... | collective-permute-start | bytes 749576 | tf_op jit(solution)/shard_map/ppermute | solution.py:429
  28.9 5.9 %collective-permute-start.8 = (f32[384,128]{1,0:T(8,128)S(1)}, f32[384,128]{1,0:T(8,128)S(1)}, u32[]{:S(2)}, u32[]{:S(2)}) collective-permute-start(f32[384,128]{1,0:T(8,128)S(1)} %get-tuple-element.63), channel_id=1, source_target_pairs={{0,1},{1,0},{2,3},{3,2},{4,5},{5,4},{6,7},{7,6},{8,9},{9,8},{10,11... | collective-permute-start | bytes 589832 | tf_op jit(solution)/shard_map/ppermute | solution.py:433
  30.5 3.4 %collective-permute-start.9 = (f32[1,1536]{1,0:T(1,128)S(1)}, f32[1,1536]{1,0:T(1,128)S(1)}, u32[]{:S(2)}, u32[]{:S(2)}) collective-permute-start(f32[1,1536]{1,0:T(1,128)S(1)} %get-tuple-element.64), channel_id=1, source_target_pairs={{0,2},{2,4},{4,6},{6,0},{1,3},{3,5},{5,7},{7,1},{8,10},{10,12},{12... | collective-permute-start | bytes 18440 | tf_op jit(solution)/shard_map/ppermute | solution.py:429
  30.5 3.4 %collective-permute-start.10 = (f32[1,1536]{1,0:T(1,128)S(1)}, f32[1,1536]{1,0:T(1,128)S(1)}, u32[]{:S(2)}, u32[]{:S(2)}) collective-permute-start(f32[1,1536]{1,0:T(1,128)S(1)} %get-tuple-element.65), channel_id=1, source_target_pairs={{0,6},{2,0},{4,2},{6,4},{1,7},{3,1},{5,3},{7,5},{8,14},{10,8},{12,... | collective-permute-start | bytes 18440 | tf_op jit(solution)/shard_map/ppermute | solution.py:429
  37.4 0.9 %copy-start.9 = (f32[4,48,2,4,128]{4,3,2,1,0:T(4,128)}, f32[4,48,2,4,128]{4,3,2,1,0:T(4,128)S(1)}, u32[]{:S(2)}) copy-start(f32[4,48,2,4,128]{4,3,2,1,0:T(4,128)S(1)} %get-tuple-element.103) | copy-start | bytes 2359300

commit v12 on v11

--- a/solution.py
+++ b/solution.py
@@ -385,24 +385,45 @@
     pack_sides(comps, last, m_ref, where_ref, rad_ref, ax_ref, radup_ref, raddn_ref)
 
 
-def second_sides(
-    comps, where_ref, part_ref, bottom_ref, ax_ref, radlo_ref, radhi_ref, edge_ref, base_ref, full_ref
+def second_rest(
+    comps,
+    parts,
+    where_ref,
+    bottom_ref,
+    above_ref,
+    ax_ref,
+    radlo_ref,
+    radhi_ref,
+    edge_ref,
+    bad_ref,
+    low_ref,
+    high_ref,
+    out_ref,
+    again_ref,
+    done_ref,
+    sems,
 ):
+    again_ref[0] = (jnp.max(bad_ref[...] + above_ref[5 * comps // 2 :]) > 0.0).astype(jnp.int32)
     hrad = put_columns(radlo_ref[...], radhi_ref[...])
-    rad = edge_ref[2]
+    halo = decode(comps, above_ref, low_ref, high_ref)
+    azim, rad = edge_ref[0], edge_ref[2]
     for c in range(comps):
         spots = slice(8 * c, 8 * c + 8)
-        halo = rad * hrad[spots]
-        base_ref[spots] = part_ref[spots] + halo
-        full_ref[spots] = bottom_ref[spots] + halo
-    for ref in (base_ref, full_ref):
-        add_axial(comps, 1.0, where_ref, edge_ref[1], ax_ref, ref)
-
-
-def second_top(comps, full_ref, above_ref, edge_ref, bad_ref, low_ref, high_ref, out_ref, again_ref):
-    again_ref[0] = (jnp.max(bad_ref[...] + above_ref[5 * comps // 2 :]) > 0.0).astype(jnp.int32)
-    out_ref[...] = full_ref[...]
-    add_azimuthal(comps, decode(comps, above_ref, low_ref, high_ref), edge_ref[0], 4, out_ref)
+        done_ref[spots] = bottom_ref[spots] + rad * hrad[spots]
+    add_axial(comps, 1.0, where_ref, edge_ref[1], ax_ref, done_ref)
+    size = comps // parts
+    made = []
+    for i in range(parts):
+        for z in range(4):
+            some = pl.ds(8 * size * i + 4 + z, size, stride=8)
+            done_ref[some] = (
+                done_ref[some] + azim[4 + z : 5 + z] * halo[size * i : size * i + size, 128 * z : 128 * z + 128]
+            )
+        spots = pl.ds(8 * size * i, 8 * size)
+        made.append(pltpu.make_async_copy(done_ref.at[spots], out_ref.at[spots], sems.at[i]))
+        made[-1].start()
+    for copy in made:
+        copy.wait()
 
 
 SPACES = {
@@ -412,12 +433,13 @@
 }
 
 
-def call(body, ins, outs, shapes, cost, *operands):
+def call(body, ins, outs, shapes, cost, *operands, scratch=()):
     return pl.pallas_call(
         body,
         in_specs=[SPACES[s] for s in ins],
         out_specs=[SPACES[s] for s in outs],
-        out_shape=[s if isinstance(s, jax.ShapeDtypeStruct) else jax.ShapeDtypeStruct(s, f32) for s in shapes],
+        out_shape=[jax.ShapeDtypeStruct(s, f32) if isinstance(s, tuple) else s for s in shapes],
+        scratch_shapes=scratch,
         cost_estimate=pl.CostEstimate(flops=cost, bytes_accessed=cost // 10, transcendentals=0),
         compiler_params=pltpu.CompilerParams(vmem_limit_bytes=32 * 1024 * 1024),
     )(*operands)
@@ -511,7 +533,7 @@
         *lower_tables[:2],
     )
     next_above = shift(dn, "azim", -1, True)
-    edges = sides(*edges)
+    ax, radlo, radhi = sides(*edges)
     part, bottom = call(
         functools.partial(second_local, sections),
         "v" * 10 + "sss",
@@ -528,41 +550,39 @@
         flags2,
         *rates,
     )
-    base, full = call(
-        functools.partial(second_sides, comps),
-        "s" + "v" * 6,
-        "vv",
-        [(cells, 128), (cells, 128)],
-        10_000,
+    out, again = call(
+        functools.partial(second_rest, comps, 4),
+        "s" + "v" * 9,
+        "hs",
+        [pltpu.HBM((cells, 128), f32), jax.ShapeDtypeStruct((1,), jnp.int32)],
+        1_000_000,
         where,
-        part,
         bottom,
-        *edges,
-        edge,
-    )
-
-    out, again = call(
-        functools.partial(second_top, comps),
-        "vvvvvv",
-        "vs",
-        [(cells, 128), jax.ShapeDtypeStruct((1,), jnp.int32)],
-        1_000_000,
-        full,
         next_above,
+        ax,
+        radlo,
+        radhi,
         edge,
         bad,
         *upper_tables[:2],
+        scratch=[pltpu.VMEM((cells, 128), f32), pltpu.SemaphoreType.DMA((4,))],
     )
 
     def whole():
         rows_ = m.reshape(comps, 2, 4, 128)
         halo = jnp.stack([shift(rows_[:, 1], "azim", 1, True), shift(rows_[:, 0], "azim", -1, True)], axis=1)
-        return base + (edge[0].reshape(1, 2, 4, 128) * halo).reshape(cells, 128)
+        azimuthal = (edge[0].reshape(1, 2, 4, 128) * halo).reshape(comps, 8, 128)
+        row, lane = jnp.arange(8).reshape(1, 8, 1), jnp.arange(128).reshape(1, 1, 128)
+        two = jnp.repeat(ax.reshape(comps, 2, 128) * edge[1, :2], 4, axis=1)
+        axial = jnp.where(row % 4 == 3 * (1 - where[0]), two, 0.0)
+        lower, upper = radlo.reshape(comps, 8, 1), radhi.reshape(comps, 8, 1)
+        radial = edge[2] * jnp.where(lane == 0, lower, jnp.where(lane == 127, upper, 0.0))
+        return part + (azimuthal + axial + radial).reshape(cells, 128)
 
     again = again[0]
     if lax.axis_size("azim") != 4:
         again = lax.pmax(again.astype(f32), "azim").astype(jnp.int32)
-    return lax.cond(again > 0, whole, lambda: out).reshape(shape)
+    return lax.switch(again, (lambda: out, whole)).reshape(shape)
 
 
 def solution(mesh):

time: 38.4 us -> 38.3 us (level)
  local copies, waits for them, and re-layouts: 1.57 us -> 0.7 us
  Pallas kernels: 9.48 us -> 10.3 us
    unnamed x20 -> x18, local copies, waits for them, and re-layouts: 1.57 us -> 0.7 us
    pallas_call x7 -> x6, Pallas kernels: 9.48 us -> 10.3 us  [call(): pl.pallas_call(body, in_specs=[SPACES[s] for s in ins], out_specs=[SPACES...]
  transfers between devices with their start and end apart: 10 -> 10, of which waited for: 4 -> 4; matrix products, arithmetic and copies ran while one was open for 0% -> 0% of each run, Pallas kernels for 22% -> 20%
where the time goes in v12:
time: 38.3 us; the launch traced here: 38.2 us
  starting transfers between devices  14.2 us (37%)
  waiting for transfers between devices  11 us (29%)
  Pallas kernels  10.3 us (27%)
  other arithmetic  1.1 us (3%)
  between operations  0.8 us (2%)
  local copies, waits for them, and re-layouts  0.7 us (2%)
    ppermute x8, starting transfers between devices, shift(): return lax.ppermute(x, axis, pairs)  11.1 us
    pallas_call x6, Pallas kernels, call(): pl.pallas_call(body, in_specs=[SPACES[s] for s in ins], out_specs=[SPACES...  10.3 us
    ppermute x8, waiting for transfers between devices, shift(): return lax.ppermute(x, axis, pairs)  9.23 us
    ppermute x2, starting transfers between devices, sides(): ax = lax.ppermute(ax, 'axial', [(0, 1), (1, 0)])  3.13 us
    ppermute x2, waiting for transfers between devices, sides(): ax = lax.ppermute(ax, 'axial', [(0, 1), (1, 0)])  1.81 us
    add x1, other arithmetic, shards(): dn = dn + lax.pad(speeds, 0.0, after) * lax.pad(flags, 0, after).astype(f32)  1.1 us
  transfers between devices with their start and end apart: 10, of which 4 were waited for; matrix products, arithmetic and copies ran while one was open for 0% of the time, Pallas kernels for 20%

profile of v12, /device:TPU:0, one launch (start us, length us, event | category | flops | bytes accessed | tf_op | source)
XLA Modules:
  0.0 38.2 jit_solution(5002005884743424898)
XLA Ops:
  0.0 0.0 copy-start
  0.0 0.0 copy-start.4
  0.0 1.1 %fusion.4 = f32[194,1,4,128]{3,2,1,0:T(4,128)S(1)} fusion(f32[192,2,4,128]{3,2,1,0:T(4,128)} %bitcast.48, f32[3,2,4,128]{3,2,1,0:T(4,128)} %param.14, s32[3,2,4,128]{3,2,1,0:T(4,128)} %param.15), kind=kLoop, calls=%fused_computation.19 | loop fusion | flops 297984 | bytes 1208320 | tf_op jit(solution)/shard_map/add | solution.py:480
  1.1 0.0 copy-start.3
  1.1 5.1 %collective-permute-start.2 = (f32[776,128]{1,0:T(8,128)S(1)}, f32[776,128]{1,0:T(8,128)S(1)}, u32[]{:S(2)}, u32[]{:S(2)}) collective-permute-start(f32[776,128]{1,0:T(8,128)S(1)} %bitcast.70), channel_id=1, source_target_pairs={{0,24},{8,0},{16,8},{24,16},{1,25},{9,1},{17,9},{25,17},{2,26},{10... | collective-permute-start | bytes 1191944 | tf_op jit(solution)/shard_map/ppermute | solution.py:451
  6.2 0.0 copy-done
  6.2 0.0 copy-done.4
  6.2 0.0 copy-done.3
  6.2 0.0 copy-start.1
  6.2 0.9 %shard_map.94 = (f32[776,128]{1,0:T(8,128)S(1)}, f32[392,128]{1,0:T(8,128)S(1)}, f32[1,1664]{1,0:T(1,128)S(1)}, f32[1,1664]{1,0:T(1,128)S(1)}) custom-call(s32[1]{0:T(128)} %bitcast.15.where_ref, s32[1]{0:T(128)} %bitcast.16.rad_ref, f32[1536,128]{1,0:T(8,128)S(1)} %bitcast.49, f32[3,8,128]{2,1,0:T(8,128)S(1)} %bitcast.55, s32[3,8,128]{2,1,0:T(8,128)S(1)} %bitcast.59), custom_call_target="tpu_custom_call" | custom-call | flops 2000000 | bytes 200000 | tf_op jit(solution)/shard_map/pallas_call | solution.py:437
  7.1 0.1 collective-permute-start.6
  7.2 0.0 copy-start.5
  7.2 1.6 %collective-permute-start.3 = (f32[392,128]{1,0:T(8,128)S(1)}, f32[392,128]{1,0:T(8,128)S(1)}, u32[]{:S(2)}, u32[]{:S(2)}) collective-permute-start(f32[392,128]{1,0:T(8,128)S(1)} %get-tuple-element.58), channel_id=1, source_target_pairs={{0,1},{1,0},{2,3},{3,2},{4,5},{5,4},{6,7},{7,6},{8,9},{9,8},{10,11... | collective-permute-start | bytes 602120 | tf_op jit(solution)/shard_map/ppermute | solution.py:455
  8.8 0.0 collective-permute-start.4
  8.8 1.7 %collective-permute-start.5 = (f32[1,1664]{1,0:T(1,128)S(1)}, f32[1,1664]{1,0:T(1,128)S(1)}, u32[]{:S(2)}, u32[]{:S(2)}) collective-permute-start(f32[1,1664]{1,0:T(1,128)S(1)} %get-tuple-element.60), channel_id=1, source_target_pairs={{0,6},{2,0},{4,2},{6,4},{1,7},{3,1},{5,3},{7,5},{8,14},{10,8},{12,... | collective-permute-start | bytes 19976 | tf_op jit(solution)/shard_map/ppermute | solution.py:451
  10.5 0.0 copy-start.6
  10.5 0.0 copy-start.7
  10.5 0.0 copy-start.8
  10.5 0.0 copy-done.1
  10.5 0.0 copy-done.5
  10.5 0.6 %copy-done.6 = f32[48]{0:T(128)S(1)} copy-done((f32[48]{0:T(128)S(1)}, f32[48]{0:T(128)}, u32[]{:S(2)}) %copy-start.6) | copy-done | bytes 216
  11.2 0.0 copy-done.7
  11.2 0.0 copy-done.8
  11.2 1.6 %shard_map.93 = (f32[1536,128]{1,0:T(8,128)S(1)}, bf16[256,512]{1,0:T(8,128)(2,1)S(1)}, bf16[256,512]{1,0:T(8,128)(2,1)S(1)}, bf16[256,512]{1,0:T(8,128)(2,1)S(1)}, bf16[256,512]{1,0:T(8,128)(2,1)S(1)}) custom-call(f32[1536,128]{1,0:T(8,128)S(1)} %bitcast.50, bf16[192,8,128]{2,1,0:T(8,128)(2,1)S(1)} %bitcast.53, f32[3,8,128]{2,1,0:T(8,128)S(1)} %bitcast.56, ...), custom_call_target="tpu_custom_call" | custom-call | flops 8000000 | bytes 800000 | tf_op jit(solution)/shard_map/pallas_call | solution.py:437
  12.8 0.0 collective-permute-done.4.radlo_ref
  12.8 0.0 collective-permute-done.5.radhi_ref
  12.8 0.9 %collective-permute-done.3.ax_ref = f32[392,128]{1,0:T(8,128)S(1)} collective-permute-done((f32[392,128]{1,0:T(8,128)S(1)}, f32[392,128]{1,0:T(8,128)S(1)}, u32[]{:S(2)}, u32[]{:S(2)}) %collective-permute-start.3) | collective-permute-done | bytes 200736 | tf_op jit(solution)/shard_map/ppermute | solution.py:455
  13.7 2.1 %collective-permute-done.2.above_ref = f32[776,128]{1,0:T(8,128)S(1)} collective-permute-done((f32[776,128]{1,0:T(8,128)S(1)}, f32[776,128]{1,0:T(8,128)S(1)}, u32[]{:S(2)}, u32[]{:S(2)}) %collective-permute-start.2) | collective-permute-done | bytes 397344 | tf_op jit(solution)/shard_map/ppermute | solution.py:451
  15.8 2.3 %shard_map.95 = (f32[1536,128]{1,0:T(8,128)S(1)}, f32[4,8,128]{2,1,0:T(8,128)S(1)}, f32[480,128]{1,0:T(8,128)S(1)}, f32[8,128]{1,0:T(8,128)S(1)}, bf16[256,512]{...) custom-call(s32[1]{0:T(128)} %bitcast.15.where_ref, ...), custom_call_target="tpu_custom_call" | custom-call | flops 4000000 | bytes 400000 | tf_op jit(solution)/shard_map/pallas_call | solution.py:437
  18.1 0.1 collective-permute-start.7
  18.2 7.1 %collective-permute-done.6.below_ref = f32[776,128]{1,0:T(8,128)S(1)} collective-permute-done((f32[776,128]{1,0:T(8,128)S(1)}, f32[776,128]{1,0:T(8,128)S(1)}, u32[]{:S(2)}, u32[]{:S(2)}) %collective-permute-start.6) | collective-permute-done | bytes 397344 | tf_op jit(solution)/shard_map/ppermute | solution.py:451
  25.2 0.0 copy-start.2
  25.3 1.3 %shard_map.96 = (f32[1536,128]{1,0:T(8,128)S(1)}, f32[488,128]{1,0:T(8,128)S(1)}, f32[384,128]{1,0:T(8,128)S(1)}, f32[1,1536]{1,0:T(1,128)S(1)}, f32[1,1536]{1,0:T(1,128)S(1)}, /*index=5*/f32[8,128]{1,0:T(8,128)S(1)}) custom-call(s32[1]{0:T(128)} %bitcast.15.where_ref, s32[1]{0:T(128)} %bitcast.16.rad_ref, f32[1536,128]{1,0:T(8,128)S(1)} %get-tuple-element.61.part_ref, ...), custom_call_target="tpu_custom_call" | custom-call | flops 10000 | bytes 1000 | tf_op jit(solution)/shard_map/pallas_call | solution.py:437
  26.5 2.4 %collective-permute-start.8 = (f32[488,128]{1,0:T(8,128)S(1)}, f32[488,128]{1,0:T(8,128)S(1)}, u32[]{:S(2)}, u32[]{:S(2)}) collective-permute-start(f32[488,128]{1,0:T(8,128)S(1)} %get-tuple-element.72), channel_id=1, source_target_pairs={{0,24},{8,0},{16,8},{24,16},{1,25},{9,1},{17,9},{25,17},{2,26},{10... | collective-permute-start | bytes 749576 | tf_op jit(solution)/shard_map/ppermute | solution.py:451
  28.9 1.5 %collective-permute-start.9 = (f32[384,128]{1,0:T(8,128)S(1)}, f32[384,128]{1,0:T(8,128)S(1)}, u32[]{:S(2)}, u32[]{:S(2)}) collective-permute-start(f32[384,128]{1,0:T(8,128)S(1)} %get-tuple-element.73), channel_id=1, source_target_pairs={{0,1},{1,0},{2,3},{3,2},{4,5},{5,4},{6,7},{7,6},{8,9},{9,8},{10,11... | collective-permute-start | bytes 589832 | tf_op jit(solution)/shard_map/ppermute | solution.py:455
  30.5 0.0 collective-permute-start.10
  30.5 1.7 %collective-permute-start.11 = (f32[1,1536]{1,0:T(1,128)S(1)}, f32[1,1536]{1,0:T(1,128)S(1)}, u32[]{:S(2)}, u32[]{:S(2)}) collective-permute-start(f32[1,1536]{1,0:T(1,128)S(1)} %get-tuple-element.75), channel_id=1, source_target_pairs={{0,6},{2,0},{4,2},{6,4},{1,7},{3,1},{5,3},{7,5},{8,14},{10,8},{12,... | collective-permute-start | bytes 18440 | tf_op jit(solution)/shard_map/ppermute | solution.py:451
  32.2 0.0 collective-permute-done.7.below_ref
  32.2 0.0 copy-done.2
  32.2 1.6 %shard_map.97 = (f32[1536,128]{1,0:T(8,128)S(1)}, f32[1536,128]{1,0:T(8,128)S(1)}) custom-call(f32[1536,128]{1,0:T(8,128)S(1)} %get-tuple-element.67.m_ref, f32[1536,128]{1,0:T(8,128)S(1)} %bitcast.52, bf16[192,8,128]{2,1,0:T(8,128)(2,1)S(1)} %bitcast.54, f32[480,128]{1,0:T(8,128)S(1)} %collective-permute-done.7.below_ref, ...), custom_call_target="tpu_custom_call" | custom-call | flops 300000000 | bytes 30000000 | tf_op jit(solution)/shard_map/pallas_call | solution.py:437
  33.8 0.0 collective-permute-done.10.radlo_ref
  33.9 0.0 collective-permute-done.11.radhi_ref
  33.9 0.9 %collective-permute-done.9.ax_ref = f32[384,128]{1,0:T(8,128)S(1)} collective-permute-done((f32[384,128]{1,0:T(8,128)S(1)}, f32[384,128]{1,0:T(8,128)S(1)}, u32[]{:S(2)}, u32[]{:S(2)}) %collective-permute-start.9) | collective-permute-done | bytes 196640 | tf_op jit(solution)/shard_map/ppermute | solution.py:455
  34.8 0.0 collective-permute-done.8.above_ref
  34.8 2.6 %shard_map.98 = (f32[1536,128]{1,0:T(8,128)}, s32[1]{0:T(128)}) custom-call(s32[1]{0:T(128)} %bitcast.15.where_ref, f32[1536,128]{1,0:T(8,128)S(1)} %get-tuple-element.71.bottom_ref, f32[488,128]{1,0:T(8,128)S(1)} %collective-permute-done.8.above_ref, f32[384,128]{1,0:T(8,128)S(1)} %collective-permute-done.9.ax_ref, ...), custom_call_target="tpu_custom_call" | custom-call | flops 1000000 | bytes 100000 | tf_op jit(solution)/shard_map/pallas_call | solution.py:437
  (1 shorter events, 0.0 us)
Async XLA Ops:
  0.0 6.2 %copy-start = (f32[4,48,2,4,128]{4,3,2,1,0:T(4,128)S(1)}, f32[4,48,2,4,128]{4,3,2,1,0:T(4,128)}, u32[]{:S(2)}) copy-start(f32[4,48,2,4,128]{4,3,2,1,0:T(4,128)} %param.11) | copy-start | bytes 2359300
  0.0 6.2 %copy-start.4 = (s32[3,2,4,128]{3,2,1,0:T(4,128)S(1)}, s32[3,2,4,128]{3,2,1,0:T(4,128)}, u32[]{:S(2)}) copy-start(s32[3,2,4,128]{3,2,1,0:T(4,128)} %param.15) | copy-start | bytes 36868
  1.1 5.1 %copy-start.3 = (f32[3,2,4,128]{3,2,1,0:T(4,128)S(1)}, f32[3,2,4,128]{3,2,1,0:T(4,128)}, u32[]{:S(2)}) copy-start(f32[3,2,4,128]{3,2,1,0:T(4,128)} %param.14) | copy-start | bytes 36868
  1.1 14.7 %collective-permute-start.2 = (f32[776,128]{1,0:T(8,128)S(1)}, f32[776,128]{1,0:T(8,128)S(1)}, u32[]{:S(2)}, u32[]{:S(2)}) collective-permute-start(f32[776,128]{1,0:T(8,128)S(1)} %bitcast.70), channel_id=1, source_target_pairs={{0,24},{8,0},{16,8},{24,16},{1,25},{9,1},{17,9},{25,17},{2,26},{10... | collective-permute-start | bytes 1191944 | tf_op jit(solution)/shard_map/ppermute | solution.py:451
  6.2 4.3 %copy-start.1 = (bf16[4,48,2,4,128]{4,3,2,1,0:T(4,128)(2,1)S(1)}, bf16[4,48,2,4,128]{4,3,2,1,0:T(4,128)(2,1)}, u32[]{:S(2)}) copy-start(bf16[4,48,2,4,128]{4,3,2,1,0:T(4,128)(2,1)} %param.13) | copy-start | bytes 1179652
  7.1 18.2 %collective-permute-start.6 = (f32[776,128]{1,0:T(8,128)S(1)}, f32[776,128]{1,0:T(8,128)S(1)}, u32[]{:S(2)}, u32[]{:S(2)}) collective-permute-start(f32[776,128]{1,0:T(8,128)S(1)} %get-tuple-element.62), channel_id=1, source_target_pairs={{0,8},{8,16},{16,24},{24,0},{1,9},{9,17},{17,25},{25,1},{2,10},{10... | collective-permute-start | bytes 1191944 | tf_op jit(solution)/shard_map/ppermute | solution.py:451
  7.2 3.4 %copy-start.5 = (s32[2,4,128]{2,1,0:T(4,128)S(1)}, s32[2,4,128]{2,1,0:T(4,128)}, u32[]{:S(2)}) copy-start(s32[2,4,128]{2,1,0:T(4,128)} %param.16) | copy-start | bytes 12292
  7.2 6.5 %collective-permute-start.3 = (f32[392,128]{1,0:T(8,128)S(1)}, f32[392,128]{1,0:T(8,128)S(1)}, u32[]{:S(2)}, u32[]{:S(2)}) collective-permute-start(f32[392,128]{1,0:T(8,128)S(1)} %get-tuple-element.58), channel_id=1, source_target_pairs={{0,1},{1,0},{2,3},{3,2},{4,5},{5,4},{6,7},{7,6},{8,9},{9,8},{10,11... | collective-permute-start | bytes 602120 | tf_op jit(solution)/shard_map/ppermute | solution.py:455
  8.8 4.0 %collective-permute-start.4 = (f32[1,1664]{1,0:T(1,128)S(1)}, f32[1,1664]{1,0:T(1,128)S(1)}, u32[]{:S(2)}, u32[]{:S(2)}) collective-permute-start(f32[1,1664]{1,0:T(1,128)S(1)} %get-tuple-element.59), channel_id=1, source_target_pairs={{0,2},{2,4},{4,6},{6,0},{1,3},{3,5},{5,7},{7,1},{8,10},{10,12},{12... | collective-permute-start | bytes 19976 | tf_op jit(solution)/shard_map/ppermute | solution.py:451
  8.8 4.1 %collective-permute-start.5 = (f32[1,1664]{1,0:T(1,128)S(1)}, f32[1,1664]{1,0:T(1,128)S(1)}, u32[]{:S(2)}, u32[]{:S(2)}) collective-permute-start(f32[1,1664]{1,0:T(1,128)S(1)} %get-tuple-element.60), channel_id=1, source_target_pairs={{0,6},{2,0},{4,2},{6,4},{1,7},{3,1},{5,3},{7,5},{8,14},{10,8},{12,... | collective-permute-start | bytes 19976 | tf_op jit(solution)/shard_map/ppermute | solution.py:451
  10.5 0.7 %copy-start.6 = (f32[48]{0:T(128)S(1)}, f32[48]{0:T(128)}, u32[]{:S(2)}) copy-start(f32[48]{0:T(128)} %growth_ref.3) | copy-start | bytes 580
  10.5 0.7 %copy-start.7 = (f32[48]{0:T(128)S(1)}, f32[48]{0:T(128)}, u32[]{:S(2)}) copy-start(f32[48]{0:T(128)} %transfer_ref.3) | copy-start | bytes 580
  10.5 0.7 %copy-start.8 = (f32[4]{0:T(128)S(1)}, f32[4]{0:T(128)}, u32[]{:S(2)}) copy-start(f32[4]{0:T(128)} %rate_ref.3) | copy-start | bytes 52
  18.1 14.1 %collective-permute-start.7 = (f32[480,128]{1,0:T(8,128)S(1)}, f32[480,128]{1,0:T(8,128)S(1)}, u32[]{:S(2)}, u32[]{:S(2)}) collective-permute-start(f32[480,128]{1,0:T(8,128)S(1)} %get-tuple-element.68), channel_id=1, source_target_pairs={{0,8},{8,16},{16,24},{24,0},{1,9},{9,17},{17,25},{25,1},{2,10},{10... | collective-permute-start | bytes 737288 | tf_op jit(solution)/shard_map/ppermute | solution.py:451
  25.2 7.0 %copy-start.2 = (bf16[4,48,2,4,128]{4,3,2,1,0:T(4,128)(2,1)S(1)}, bf16[4,48,2,4,128]{4,3,2,1,0:T(4,128)(2,1)}, u32[]{:S(2)}) copy-start(bf16[4,48,2,4,128]{4,3,2,1,0:T(4,128)(2,1)} %param.12) | copy-start | bytes 1179652
  26.5 8.3 %collective-permute-start.8 = (f32[488,128]{1,0:T(8,128)S(1)}, f32[488,128]{1,0:T(8,128)S(1)}, u32[]{:S(2)}, u32[]{:S(2)}) collective-permute-start(f32[488,128]{1,0:T(8,128)S(1)} %get-tuple-element.72), channel_id=1, source_target_pairs={{0,24},{8,0},{16,8},{24,16},{1,25},{9,1},{17,9},{25,17},{2,26},{10... | collective-permute-start | bytes 749576 | tf_op jit(solution)/shard_map/ppermute | solution.py:451
  28.9 5.9 %collective-permute-start.9 = (f32[384,128]{1,0:T(8,128)S(1)}, f32[384,128]{1,0:T(8,128)S(1)}, u32[]{:S(2)}, u32[]{:S(2)}) collective-permute-start(f32[384,128]{1,0:T(8,128)S(1)} %get-tuple-element.73), channel_id=1, source_target_pairs={{0,1},{1,0},{2,3},{3,2},{4,5},{5,4},{6,7},{7,6},{8,9},{9,8},{10,11... | collective-permute-start | bytes 589832 | tf_op jit(solution)/shard_map/ppermute | solution.py:455
  30.5 3.4 %collective-permute-start.10 = (f32[1,1536]{1,0:T(1,128)S(1)}, f32[1,1536]{1,0:T(1,128)S(1)}, u32[]{:S(2)}, u32[]{:S(2)}) collective-permute-start(f32[1,1536]{1,0:T(1,128)S(1)} %get-tuple-element.74), channel_id=1, source_target_pairs={{0,2},{2,4},{4,6},{6,0},{1,3},{3,5},{5,7},{7,1},{8,10},{10,12},{12... | collective-permute-start | bytes 18440 | tf_op jit(solution)/shard_map/ppermute | solution.py:451
  30.5 3.4 %collective-permute-start.11 = (f32[1,1536]{1,0:T(1,128)S(1)}, f32[1,1536]{1,0:T(1,128)S(1)}, u32[]{:S(2)}, u32[]{:S(2)}) collective-permute-start(f32[1,1536]{1,0:T(1,128)S(1)} %get-tuple-element.75), channel_id=1, source_target_pairs={{0,6},{2,0},{4,2},{6,4},{1,7},{3,1},{5,3},{7,5},{8,14},{10,8},{12,... | collective-permute-start | bytes 18440 | tf_op jit(solution)/shard_map/ppermute | solution.py:451

commit v13 on v12

--- a/solution.py
+++ b/solution.py
@@ -385,15 +385,21 @@
     pack_sides(comps, last, m_ref, where_ref, rad_ref, ax_ref, radup_ref, raddn_ref)
 
 
+def second_radial(comps, bottom_ref, radlo_ref, radhi_ref, edge_ref, full_ref):
+    hrad = put_columns(radlo_ref[...], radhi_ref[...])
+    rad = edge_ref[2]
+    for c in range(comps):
+        spots = slice(8 * c, 8 * c + 8)
+        full_ref[spots] = bottom_ref[spots] + rad * hrad[spots]
+
+
 def second_rest(
     comps,
     parts,
     where_ref,
-    bottom_ref,
+    full_ref,
     above_ref,
     ax_ref,
-    radlo_ref,
-    radhi_ref,
     edge_ref,
     bad_ref,
     low_ref,
@@ -404,12 +410,9 @@
     sems,
 ):
     again_ref[0] = (jnp.max(bad_ref[...] + above_ref[5 * comps // 2 :]) > 0.0).astype(jnp.int32)
-    hrad = put_columns(radlo_ref[...], radhi_ref[...])
     halo = decode(comps, above_ref, low_ref, high_ref)
-    azim, rad = edge_ref[0], edge_ref[2]
-    for c in range(comps):
-        spots = slice(8 * c, 8 * c + 8)
-        done_ref[spots] = bottom_ref[spots] + rad * hrad[spots]
+    azim = edge_ref[0]
+    done_ref[...] = full_ref[...]
     add_axial(comps, 1.0, where_ref, edge_ref[1], ax_ref, done_ref)
     size = comps // parts
     made = []
@@ -550,18 +553,27 @@
         flags2,
         *rates,
     )
+    (full,) = call(
+        functools.partial(second_radial, comps),
+        "v" * 4,
+        "v",
+        [(cells, 128)],
+        1_000_000,
+        bottom,
+        radlo,
+        radhi,
+        edge,
+    )
     out, again = call(
         functools.partial(second_rest, comps, 4),
-        "s" + "v" * 9,
+        "s" + "v" * 7,
         "hs",
         [pltpu.HBM((cells, 128), f32), jax.ShapeDtypeStruct((1,), jnp.int32)],
         1_000_000,
         where,
-        bottom,
+        full,
         next_above,
         ax,
-        radlo,
-        radhi,
         edge,
         bad,
         *upper_tables[:2],

time: 38.3 us -> 38.5 us (level)
    pallas_call x6 -> x7, Pallas kernels: 10.3 us -> 10.4 us  [call(): pl.pallas_call(body, in_specs=[SPACES[s] for s in ins], out_specs=[SPACES...]
  transfers between devices with their start and end apart: 10 -> 10, of which waited for: 4 -> 4; matrix products, arithmetic and copies ran while one was open for 0% -> 0% of each run, Pallas kernels for 20% -> 22%
where the time goes in v13:
time: 38.5 us; the launch traced here: 38.3 us
  starting transfers between devices  14.2 us (37%)
  waiting for transfers between devices  11.1 us (29%)
  Pallas kernels  10.4 us (27%)
  other arithmetic  1.1 us (3%)
  between operations  0.82 us (2%)
  local copies, waits for them, and re-layouts  0.7 us (2%)
    ppermute x8, starting transfers between devices, shift(): return lax.ppermute(x, axis, pairs)  11.1 us
    pallas_call x7, Pallas kernels, call(): pl.pallas_call(body, in_specs=[SPACES[s] for s in ins], out_specs=[SPACES...  10.4 us
    ppermute x8, waiting for transfers between devices, shift(): return lax.ppermute(x, axis, pairs)  9.23 us
    ppermute x2, starting transfers between devices, sides(): ax = lax.ppermute(ax, 'axial', [(0, 1), (1, 0)])  3.13 us
    ppermute x2, waiting for transfers between devices, sides(): ax = lax.ppermute(ax, 'axial', [(0, 1), (1, 0)])  1.82 us
    add x1, other arithmetic, shards(): dn = dn + lax.pad(speeds, 0.0, after) * lax.pad(flags, 0, after).astype(f32)  1.1 us
  transfers between devices with their start and end apart: 10, of which 4 were waited for; matrix products, arithmetic and copies ran while one was open for 0% of the time, Pallas kernels for 22%

profile of v13, /device:TPU:0, one launch (start us, length us, event | category | flops | bytes accessed | tf_op | source)
XLA Modules:
  0.0 38.3 jit_solution(17102531268684823096)
XLA Ops:
  0.0 0.0 copy-start
  0.0 0.0 copy-start.4
  0.0 1.1 %fusion.4 = f32[194,1,4,128]{3,2,1,0:T(4,128)S(1)} fusion(f32[192,2,4,128]{3,2,1,0:T(4,128)} %bitcast.48, f32[3,2,4,128]{3,2,1,0:T(4,128)} %param.14, s32[3,2,4,128]{3,2,1,0:T(4,128)} %param.15), kind=kLoop, calls=%fused_computation.19 | loop fusion | flops 297984 | bytes 1208320 | tf_op jit(solution)/shard_map/add | solution.py:483
  1.1 0.0 copy-start.3
  1.1 5.1 %collective-permute-start.2 = (f32[776,128]{1,0:T(8,128)S(1)}, f32[776,128]{1,0:T(8,128)S(1)}, u32[]{:S(2)}, u32[]{:S(2)}) collective-permute-start(f32[776,128]{1,0:T(8,128)S(1)} %bitcast.70), channel_id=1, source_target_pairs={{0,24},{8,0},{16,8},{24,16},{1,25},{9,1},{17,9},{25,17},{2,26},{10... | collective-permute-start | bytes 1191944 | tf_op jit(solution)/shard_map/ppermute | solution.py:454
  6.2 0.0 copy-done
  6.2 0.0 copy-done.4
  6.2 0.0 copy-done.3
  6.2 0.0 copy-start.1
  6.2 0.9 %shard_map.94 = (f32[776,128]{1,0:T(8,128)S(1)}, f32[392,128]{1,0:T(8,128)S(1)}, f32[1,1664]{1,0:T(1,128)S(1)}, f32[1,1664]{1,0:T(1,128)S(1)}) custom-call(s32[1]{0:T(128)} %bitcast.15.where_ref, s32[1]{0:T(128)} %bitcast.16.rad_ref, f32[1536,128]{1,0:T(8,128)S(1)} %bitcast.49, f32[3,8,128]{2,1,0:T(8,128)S(1)} %bitcast.55, s32[3,8,128]{2,1,0:T(8,128)S(1)} %bitcast.59), custom_call_target="tpu_custom_call" | custom-call | flops 2000000 | bytes 200000 | tf_op jit(solution)/shard_map/pallas_call | solution.py:440
  7.1 0.1 collective-permute-start.6
  7.2 0.0 copy-start.5
  7.2 1.6 %collective-permute-start.3 = (f32[392,128]{1,0:T(8,128)S(1)}, f32[392,128]{1,0:T(8,128)S(1)}, u32[]{:S(2)}, u32[]{:S(2)}) collective-permute-start(f32[392,128]{1,0:T(8,128)S(1)} %get-tuple-element.58), channel_id=1, source_target_pairs={{0,1},{1,0},{2,3},{3,2},{4,5},{5,4},{6,7},{7,6},{8,9},{9,8},{10,11... | collective-permute-start | bytes 602120 | tf_op jit(solution)/shard_map/ppermute | solution.py:458
  8.8 0.0 collective-permute-start.4
  8.8 1.7 %collective-permute-start.5 = (f32[1,1664]{1,0:T(1,128)S(1)}, f32[1,1664]{1,0:T(1,128)S(1)}, u32[]{:S(2)}, u32[]{:S(2)}) collective-permute-start(f32[1,1664]{1,0:T(1,128)S(1)} %get-tuple-element.60), channel_id=1, source_target_pairs={{0,6},{2,0},{4,2},{6,4},{1,7},{3,1},{5,3},{7,5},{8,14},{10,8},{12,... | collective-permute-start | bytes 19976 | tf_op jit(solution)/shard_map/ppermute | solution.py:454
  10.5 0.0 copy-start.6
  10.5 0.0 copy-start.7
  10.5 0.0 copy-start.8
  10.5 0.0 copy-done.1
  10.5 0.0 copy-done.5
  10.5 0.6 %copy-done.6 = f32[48]{0:T(128)S(1)} copy-done((f32[48]{0:T(128)S(1)}, f32[48]{0:T(128)}, u32[]{:S(2)}) %copy-start.6) | copy-done | bytes 216
  11.2 0.0 copy-done.7
  11.2 0.0 copy-done.8
  11.2 1.6 %shard_map.93 = (f32[1536,128]{1,0:T(8,128)S(1)}, bf16[256,512]{1,0:T(8,128)(2,1)S(1)}, bf16[256,512]{1,0:T(8,128)(2,1)S(1)}, bf16[256,512]{1,0:T(8,128)(2,1)S(1)}, bf16[256,512]{1,0:T(8,128)(2,1)S(1)}) custom-call(f32[1536,128]{1,0:T(8,128)S(1)} %bitcast.50, bf16[192,8,128]{2,1,0:T(8,128)(2,1)S(1)} %bitcast.53, f32[3,8,128]{2,1,0:T(8,128)S(1)} %bitcast.56, ...), custom_call_target="tpu_custom_call" | custom-call | flops 8000000 | bytes 800000 | tf_op jit(solution)/shard_map/pallas_call | solution.py:440
  12.8 0.0 collective-permute-done.4.radlo_ref
  12.8 0.0 collective-permute-done.5.radhi_ref
  12.8 0.9 %collective-permute-done.3.ax_ref = f32[392,128]{1,0:T(8,128)S(1)} collective-permute-done((f32[392,128]{1,0:T(8,128)S(1)}, f32[392,128]{1,0:T(8,128)S(1)}, u32[]{:S(2)}, u32[]{:S(2)}) %collective-permute-start.3) | collective-permute-done | bytes 200736 | tf_op jit(solution)/shard_map/ppermute | solution.py:458
  13.7 2.1 %collective-permute-done.2.above_ref = f32[776,128]{1,0:T(8,128)S(1)} collective-permute-done((f32[776,128]{1,0:T(8,128)S(1)}, f32[776,128]{1,0:T(8,128)S(1)}, u32[]{:S(2)}, u32[]{:S(2)}) %collective-permute-start.2) | collective-permute-done | bytes 397344 | tf_op jit(solution)/shard_map/ppermute | solution.py:454
  15.8 2.3 %shard_map.95 = (f32[1536,128]{1,0:T(8,128)S(1)}, f32[4,8,128]{2,1,0:T(8,128)S(1)}, f32[480,128]{1,0:T(8,128)S(1)}, f32[8,128]{1,0:T(8,128)S(1)}, bf16[256,512]{...) custom-call(s32[1]{0:T(128)} %bitcast.15.where_ref, ...), custom_call_target="tpu_custom_call" | custom-call | flops 4000000 | bytes 400000 | tf_op jit(solution)/shard_map/pallas_call | solution.py:440
  18.1 0.1 collective-permute-start.7
  18.2 7.1 %collective-permute-done.6.below_ref = f32[776,128]{1,0:T(8,128)S(1)} collective-permute-done((f32[776,128]{1,0:T(8,128)S(1)}, f32[776,128]{1,0:T(8,128)S(1)}, u32[]{:S(2)}, u32[]{:S(2)}) %collective-permute-start.6) | collective-permute-done | bytes 397344 | tf_op jit(solution)/shard_map/ppermute | solution.py:454
  25.2 0.0 copy-start.2
  25.3 1.3 %shard_map.96 = (f32[1536,128]{1,0:T(8,128)S(1)}, f32[488,128]{1,0:T(8,128)S(1)}, f32[384,128]{1,0:T(8,128)S(1)}, f32[1,1536]{1,0:T(1,128)S(1)}, f32[1,1536]{1,0:T(1,128)S(1)}, /*index=5*/f32[8,128]{1,0:T(8,128)S(1)}) custom-call(s32[1]{0:T(128)} %bitcast.15.where_ref, s32[1]{0:T(128)} %bitcast.16.rad_ref, f32[1536,128]{1,0:T(8,128)S(1)} %get-tuple-element.61.part_ref, ...), custom_call_target="tpu_custom_call" | custom-call | flops 10000 | bytes 1000 | tf_op jit(solution)/shard_map/pallas_call | solution.py:440
  26.5 2.4 %collective-permute-start.10 = (f32[488,128]{1,0:T(8,128)S(1)}, f32[488,128]{1,0:T(8,128)S(1)}, u32[]{:S(2)}, u32[]{:S(2)}) collective-permute-start(f32[488,128]{1,0:T(8,128)S(1)} %get-tuple-element.74), channel_id=1, source_target_pairs={{0,24},{8,0},{16,8},{24,16},{1,25},{9,1},{17,9},{25,17},{2,26},{10... | collective-permute-start | bytes 749576 | tf_op jit(solution)/shard_map/ppermute | solution.py:454
  28.9 1.5 %collective-permute-start.11 = (f32[384,128]{1,0:T(8,128)S(1)}, f32[384,128]{1,0:T(8,128)S(1)}, u32[]{:S(2)}, u32[]{:S(2)}) collective-permute-start(f32[384,128]{1,0:T(8,128)S(1)} %get-tuple-element.75), channel_id=1, source_target_pairs={{0,1},{1,0},{2,3},{3,2},{4,5},{5,4},{6,7},{7,6},{8,9},{9,8},{10,11... | collective-permute-start | bytes 589832 | tf_op jit(solution)/shard_map/ppermute | solution.py:458
  30.5 0.0 collective-permute-start.8
  30.5 1.7 %collective-permute-start.9 = (f32[1,1536]{1,0:T(1,128)S(1)}, f32[1,1536]{1,0:T(1,128)S(1)}, u32[]{:S(2)}, u32[]{:S(2)}) collective-permute-start(f32[1,1536]{1,0:T(1,128)S(1)} %get-tuple-element.73), channel_id=1, source_target_pairs={{0,6},{2,0},{4,2},{6,4},{1,7},{3,1},{5,3},{7,5},{8,14},{10,8},{12,... | collective-permute-start | bytes 18440 | tf_op jit(solution)/shard_map/ppermute | solution.py:454
  32.2 0.0 collective-permute-done.7.below_ref
  32.2 0.0 copy-done.2
  32.2 1.6 %shard_map.97 = (f32[1536,128]{1,0:T(8,128)S(1)}, f32[1536,128]{1,0:T(8,128)S(1)}) custom-call(f32[1536,128]{1,0:T(8,128)S(1)} %get-tuple-element.67.m_ref, f32[1536,128]{1,0:T(8,128)S(1)} %bitcast.52, bf16[192,8,128]{2,1,0:T(8,128)(2,1)S(1)} %bitcast.54, f32[480,128]{1,0:T(8,128)S(1)} %collective-permute-done.7.below_ref, ...), custom_call_target="tpu_custom_call" | custom-call | flops 300000000 | bytes 30000000 | tf_op jit(solution)/shard_map/pallas_call | solution.py:440
  33.8 0.0 collective-permute-done.8.radlo_ref
  33.8 0.0 collective-permute-done.9.radhi_ref
  33.9 1.0 %collective-permute-done.11.ax_ref = f32[384,128]{1,0:T(8,128)S(1)} collective-permute-done((f32[384,128]{1,0:T(8,128)S(1)}, f32[384,128]{1,0:T(8,128)S(1)}, u32[]{:S(2)}, u32[]{:S(2)}) %collective-permute-start.11) | collective-permute-done | bytes 196640 | tf_op jit(solution)/shard_map/ppermute | solution.py:458
  34.8 0.8 %shard_map.98.full_ref = f32[1536,128]{1,0:T(8,128)S(1)} custom-call(f32[1536,128]{1,0:T(8,128)S(1)} %get-tuple-element.71.bottom_ref, f32[1,1536]{1,0:T(1,128)S(1)} %collective-permute-done.8.radlo_ref, f32[1,1536]{1,0:T(1,128)S(1)} %collective-permute-done.9.radhi_ref, f32[4,8,128]{2,1,0:T(8,128)S(1)} %get-tuple-element.63.edge_ref), custom_call_target="tpu_custom_call" | custom-call | flops 1000000 | bytes 100000 | tf_op jit(solution)/shard_map/pallas_call | solution.py:440
  35.7 0.0 collective-permute-done.10.above_ref
  35.7 2.0 %shard_map.99 = (f32[1536,128]{1,0:T(8,128)}, s32[1]{0:T(128)}) custom-call(s32[1]{0:T(128)} %bitcast.15.where_ref, f32[1536,128]{1,0:T(8,128)S(1)} %shard_map.98.full_ref, f32[488,128]{1,0:T(8,128)S(1)} %collective-permute-done.10.above_ref, f32[384,128]{1,0:T(8,128)S(1)} %collective-permute-done.11.ax_ref, f32[4,8,128]{2,1,0:T(8,128)S(1)} %get-tuple-element.63.edge_ref, ...), custom_call_target="tpu_custom_call" | custom-call | flops 1000000 | bytes 100000 | tf_op jit(solution)/shard_map/pallas_call | solution.py:440
  (1 shorter events, 0.0 us)
Async XLA Ops:
  0.0 6.2 %copy-start = (f32[4,48,2,4,128]{4,3,2,1,0:T(4,128)S(1)}, f32[4,48,2,4,128]{4,3,2,1,0:T(4,128)}, u32[]{:S(2)}) copy-start(f32[4,48,2,4,128]{4,3,2,1,0:T(4,128)} %param.11) | copy-start | bytes 2359300
  0.0 6.2 %copy-start.4 = (s32[3,2,4,128]{3,2,1,0:T(4,128)S(1)}, s32[3,2,4,128]{3,2,1,0:T(4,128)}, u32[]{:S(2)}) copy-start(s32[3,2,4,128]{3,2,1,0:T(4,128)} %param.15) | copy-start | bytes 36868
  1.1 5.1 %copy-start.3 = (f32[3,2,4,128]{3,2,1,0:T(4,128)S(1)}, f32[3,2,4,128]{3,2,1,0:T(4,128)}, u32[]{:S(2)}) copy-start(f32[3,2,4,128]{3,2,1,0:T(4,128)} %param.14) | copy-start | bytes 36868
  1.1 14.7 %collective-permute-start.2 = (f32[776,128]{1,0:T(8,128)S(1)}, f32[776,128]{1,0:T(8,128)S(1)}, u32[]{:S(2)}, u32[]{:S(2)}) collective-permute-start(f32[776,128]{1,0:T(8,128)S(1)} %bitcast.70), channel_id=1, source_target_pairs={{0,24},{8,0},{16,8},{24,16},{1,25},{9,1},{17,9},{25,17},{2,26},{10... | collective-permute-start | bytes 1191944 | tf_op jit(solution)/shard_map/ppermute | solution.py:454
  6.2 4.3 %copy-start.1 = (bf16[4,48,2,4,128]{4,3,2,1,0:T(4,128)(2,1)S(1)}, bf16[4,48,2,4,128]{4,3,2,1,0:T(4,128)(2,1)}, u32[]{:S(2)}) copy-start(bf16[4,48,2,4,128]{4,3,2,1,0:T(4,128)(2,1)} %param.13) | copy-start | bytes 1179652
  7.1 18.2 %collective-permute-start.6 = (f32[776,128]{1,0:T(8,128)S(1)}, f32[776,128]{1,0:T(8,128)S(1)}, u32[]{:S(2)}, u32[]{:S(2)}) collective-permute-start(f32[776,128]{1,0:T(8,128)S(1)} %get-tuple-element.62), channel_id=1, source_target_pairs={{0,8},{8,16},{16,24},{24,0},{1,9},{9,17},{17,25},{25,1},{2,10},{10... | collective-permute-start | bytes 1191944 | tf_op jit(solution)/shard_map/ppermute | solution.py:454
  7.2 3.4 %copy-start.5 = (s32[2,4,128]{2,1,0:T(4,128)S(1)}, s32[2,4,128]{2,1,0:T(4,128)}, u32[]{:S(2)}) copy-start(s32[2,4,128]{2,1,0:T(4,128)} %param.16) | copy-start | bytes 12292
  7.2 6.5 %collective-permute-start.3 = (f32[392,128]{1,0:T(8,128)S(1)}, f32[392,128]{1,0:T(8,128)S(1)}, u32[]{:S(2)}, u32[]{:S(2)}) collective-permute-start(f32[392,128]{1,0:T(8,128)S(1)} %get-tuple-element.58), channel_id=1, source_target_pairs={{0,1},{1,0},{2,3},{3,2},{4,5},{5,4},{6,7},{7,6},{8,9},{9,8},{10,11... | collective-permute-start | bytes 602120 | tf_op jit(solution)/shard_map/ppermute | solution.py:458
  8.8 4.0 %collective-permute-start.4 = (f32[1,1664]{1,0:T(1,128)S(1)}, f32[1,1664]{1,0:T(1,128)S(1)}, u32[]{:S(2)}, u32[]{:S(2)}) collective-permute-start(f32[1,1664]{1,0:T(1,128)S(1)} %get-tuple-element.59), channel_id=1, source_target_pairs={{0,2},{2,4},{4,6},{6,0},{1,3},{3,5},{5,7},{7,1},{8,10},{10,12},{12... | collective-permute-start | bytes 19976 | tf_op jit(solution)/shard_map/ppermute | solution.py:454
  8.8 4.1 %collective-permute-start.5 = (f32[1,1664]{1,0:T(1,128)S(1)}, f32[1,1664]{1,0:T(1,128)S(1)}, u32[]{:S(2)}, u32[]{:S(2)}) collective-permute-start(f32[1,1664]{1,0:T(1,128)S(1)} %get-tuple-element.60), channel_id=1, source_target_pairs={{0,6},{2,0},{4,2},{6,4},{1,7},{3,1},{5,3},{7,5},{8,14},{10,8},{12,... | collective-permute-start | bytes 19976 | tf_op jit(solution)/shard_map/ppermute | solution.py:454
  10.5 0.7 %copy-start.6 = (f32[48]{0:T(128)S(1)}, f32[48]{0:T(128)}, u32[]{:S(2)}) copy-start(f32[48]{0:T(128)} %growth_ref.3) | copy-start | bytes 580
  10.5 0.7 %copy-start.7 = (f32[48]{0:T(128)S(1)}, f32[48]{0:T(128)}, u32[]{:S(2)}) copy-start(f32[48]{0:T(128)} %transfer_ref.3) | copy-start | bytes 580
  10.5 0.7 %copy-start.8 = (f32[4]{0:T(128)S(1)}, f32[4]{0:T(128)}, u32[]{:S(2)}) copy-start(f32[4]{0:T(128)} %rate_ref.3) | copy-start | bytes 52
  18.1 14.1 %collective-permute-start.7 = (f32[480,128]{1,0:T(8,128)S(1)}, f32[480,128]{1,0:T(8,128)S(1)}, u32[]{:S(2)}, u32[]{:S(2)}) collective-permute-start(f32[480,128]{1,0:T(8,128)S(1)} %get-tuple-element.68), channel_id=1, source_target_pairs={{0,8},{8,16},{16,24},{24,0},{1,9},{9,17},{17,25},{25,1},{2,10},{10... | collective-permute-start | bytes 737288 | tf_op jit(solution)/shard_map/ppermute | solution.py:454
  25.2 7.0 %copy-start.2 = (bf16[4,48,2,4,128]{4,3,2,1,0:T(4,128)(2,1)S(1)}, bf16[4,48,2,4,128]{4,3,2,1,0:T(4,128)(2,1)}, u32[]{:S(2)}) copy-start(bf16[4,48,2,4,128]{4,3,2,1,0:T(4,128)(2,1)} %param.12) | copy-start | bytes 1179652
  26.5 9.2 %collective-permute-start.10 = (f32[488,128]{1,0:T(8,128)S(1)}, f32[488,128]{1,0:T(8,128)S(1)}, u32[]{:S(2)}, u32[]{:S(2)}) collective-permute-start(f32[488,128]{1,0:T(8,128)S(1)} %get-tuple-element.74), channel_id=1, source_target_pairs={{0,24},{8,0},{16,8},{24,16},{1,25},{9,1},{17,9},{25,17},{2,26},{10... | collective-permute-start | bytes 749576 | tf_op jit(solution)/shard_map/ppermute | solution.py:454
  28.9 5.9 %collective-permute-start.11 = (f32[384,128]{1,0:T(8,128)S(1)}, f32[384,128]{1,0:T(8,128)S(1)}, u32[]{:S(2)}, u32[]{:S(2)}) collective-permute-start(f32[384,128]{1,0:T(8,128)S(1)} %get-tuple-element.75), channel_id=1, source_target_pairs={{0,1},{1,0},{2,3},{3,2},{4,5},{5,4},{6,7},{7,6},{8,9},{9,8},{10,11... | collective-permute-start | bytes 589832 | tf_op jit(solution)/shard_map/ppermute | solution.py:458
  30.5 3.4 %collective-permute-start.8 = (f32[1,1536]{1,0:T(1,128)S(1)}, f32[1,1536]{1,0:T(1,128)S(1)}, u32[]{:S(2)}, u32[]{:S(2)}) collective-permute-start(f32[1,1536]{1,0:T(1,128)S(1)} %get-tuple-element.72), channel_id=1, source_target_pairs={{0,2},{2,4},{4,6},{6,0},{1,3},{3,5},{5,7},{7,1},{8,10},{10,12},{12... | collective-permute-start | bytes 18440 | tf_op jit(solution)/shard_map/ppermute | solution.py:454
  30.5 3.4 %collective-permute-start.9 = (f32[1,1536]{1,0:T(1,128)S(1)}, f32[1,1536]{1,0:T(1,128)S(1)}, u32[]{:S(2)}, u32[]{:S(2)}) collective-permute-start(f32[1,1536]{1,0:T(1,128)S(1)} %get-tuple-element.73), channel_id=1, source_target_pairs={{0,6},{2,0},{4,2},{6,4},{1,7},{3,1},{5,3},{7,5},{8,14},{10,8},{12,... | collective-permute-start | bytes 18440 | tf_op jit(solution)/shard_map/ppermute | solution.py:454

commit v14 on v13

--- a/solution.py
+++ b/solution.py
@@ -558,7 +558,7 @@
         "v" * 4,
         "v",
         [(cells, 128)],
-        1_000_000,
+        1_000,
         bottom,
         radlo,
         radhi,

time: 38.5 us -> 38.4 us (level)
  the two profiles are of different devices: /device:TPU:0 before, /device:TPU:1 now
where the time goes in v14:
time: 38.4 us; the launch traced here: 38.2 us
  starting transfers between devices  15.8 us (41%)
  Pallas kernels  10.4 us (27%)
  waiting for transfers between devices  9.38 us (24%)
  other arithmetic  1.1 us (3%)
  between operations  0.82 us (2%)
  local copies, waits for them, and re-layouts  0.69 us (2%)
    ppermute x8, starting transfers between devices, shift(): return lax.ppermute(x, axis, pairs)  13.2 us
    pallas_call x7, Pallas kernels, call(): pl.pallas_call(body, in_specs=[SPACES[s] for s in ins], out_specs=[SPACES...  10.4 us
    ppermute x8, waiting for transfers between devices, shift(): return lax.ppermute(x, axis, pairs)  9.38 us
    ppermute x2, starting transfers between devices, sides(): ax = lax.ppermute(ax, 'axial', [(0, 1), (1, 0)])  2.56 us
    add x1, other arithmetic, shards(): dn = dn + lax.pad(speeds, 0.0, after) * lax.pad(flags, 0, after).astype(f32)  1.1 us
  transfers between devices with their start and end apart: 10, of which 3 were waited for; matrix products, arithmetic and copies ran while one was open for 0% of the time, Pallas kernels for 22%

profile of v14, /device:TPU:1, one launch (start us, length us, event | category | flops | bytes accessed | tf_op | source)
XLA Modules:
  0.0 38.2 jit_solution(16160289261157295693)
XLA Ops:
  0.0 0.0 copy-start
  0.0 0.0 copy-start.4
  0.0 1.1 %fusion.4 = f32[194,1,4,128]{3,2,1,0:T(4,128)S(1)} fusion(f32[192,2,4,128]{3,2,1,0:T(4,128)} %bitcast.48, f32[3,2,4,128]{3,2,1,0:T(4,128)} %param.14, s32[3,2,4,128]{3,2,1,0:T(4,128)} %param.15), kind=kLoop, calls=%fused_computation.19 | loop fusion | flops 297984 | bytes 1208320 | tf_op jit(solution)/shard_map/add | solution.py:483
  1.1 0.0 copy-start.3
  1.1 4.2 %collective-permute-start.2 = (f32[776,128]{1,0:T(8,128)S(1)}, f32[776,128]{1,0:T(8,128)S(1)}, u32[]{:S(2)}, u32[]{:S(2)}) collective-permute-start(f32[776,128]{1,0:T(8,128)S(1)} %bitcast.70), channel_id=1, source_target_pairs={{0,24},{8,0},{16,8},{24,16},{1,25},{9,1},{17,9},{25,17},{2,26},{10... | collective-permute-start | bytes 1191944 | tf_op jit(solution)/shard_map/ppermute | solution.py:454
  5.3 0.0 copy-done
  5.3 0.0 copy-done.4
  5.3 0.0 copy-done.3
  5.3 0.0 copy-start.1
  5.3 0.9 %shard_map.94 = (f32[776,128]{1,0:T(8,128)S(1)}, f32[392,128]{1,0:T(8,128)S(1)}, f32[1,1664]{1,0:T(1,128)S(1)}, f32[1,1664]{1,0:T(1,128)S(1)}) custom-call(s32[1]{0:T(128)} %bitcast.15.where_ref, s32[1]{0:T(128)} %bitcast.16.rad_ref, f32[1536,128]{1,0:T(8,128)S(1)} %bitcast.49, f32[3,8,128]{2,1,0:T(8,128)S(1)} %bitcast.55, s32[3,8,128]{2,1,0:T(8,128)S(1)} %bitcast.59), custom_call_target="tpu_custom_call" | custom-call | flops 2000000 | bytes 200000 | tf_op jit(solution)/shard_map/pallas_call | solution.py:440
  6.2 0.1 collective-permute-start.6
  6.3 0.0 copy-start.5
  6.3 1.3 %collective-permute-start.3 = (f32[392,128]{1,0:T(8,128)S(1)}, f32[392,128]{1,0:T(8,128)S(1)}, u32[]{:S(2)}, u32[]{:S(2)}) collective-permute-start(f32[392,128]{1,0:T(8,128)S(1)} %get-tuple-element.58), channel_id=1, source_target_pairs={{0,1},{1,0},{2,3},{3,2},{4,5},{5,4},{6,7},{7,6},{8,9},{9,8},{10,11... | collective-permute-start | bytes 602120 | tf_op jit(solution)/shard_map/ppermute | solution.py:458
  7.6 2.3 %collective-permute-start.4 = (f32[1,1664]{1,0:T(1,128)S(1)}, f32[1,1664]{1,0:T(1,128)S(1)}, u32[]{:S(2)}, u32[]{:S(2)}) collective-permute-start(f32[1,1664]{1,0:T(1,128)S(1)} %get-tuple-element.59), channel_id=1, source_target_pairs={{0,2},{2,4},{4,6},{6,0},{1,3},{3,5},{5,7},{7,1},{8,10},{10,12},{12... | collective-permute-start | bytes 19976 | tf_op jit(solution)/shard_map/ppermute | solution.py:454
  9.9 0.0 collective-permute-start.5
  9.9 0.0 copy-start.6
  9.9 0.0 copy-start.7
  9.9 0.0 copy-start.8
  9.9 0.0 copy-done.1
  9.9 0.0 copy-done.5
  9.9 0.6 %copy-done.6 = f32[48]{0:T(128)S(1)} copy-done((f32[48]{0:T(128)S(1)}, f32[48]{0:T(128)}, u32[]{:S(2)}) %copy-start.6) | copy-done | bytes 216
  10.6 0.0 copy-done.7
  10.6 0.0 copy-done.8
  10.6 1.6 %shard_map.93 = (f32[1536,128]{1,0:T(8,128)S(1)}, bf16[256,512]{1,0:T(8,128)(2,1)S(1)}, bf16[256,512]{1,0:T(8,128)(2,1)S(1)}, bf16[256,512]{1,0:T(8,128)(2,1)S(1)}, bf16[256,512]{1,0:T(8,128)(2,1)S(1)}) custom-call(f32[1536,128]{1,0:T(8,128)S(1)} %bitcast.50, bf16[192,8,128]{2,1,0:T(8,128)(2,1)S(1)} %bitcast.53, f32[3,8,128]{2,1,0:T(8,128)S(1)} %bitcast.56, ...), custom_call_target="tpu_custom_call" | custom-call | flops 8000000 | bytes 800000 | tf_op jit(solution)/shard_map/pallas_call | solution.py:440
  12.2 0.0 collective-permute-done.4.radlo_ref
  12.2 1.0 %collective-permute-done.5.radhi_ref = f32[1,1664]{1,0:T(1,128)S(1)} collective-permute-done((f32[1,1664]{1,0:T(1,128)S(1)}, f32[1,1664]{1,0:T(1,128)S(1)}, u32[]{:S(2)}, u32[]{:S(2)}) %collective-permute-start.5) | collective-permute-done | bytes 6688 | tf_op jit(solution)/shard_map/ppermute | solution.py:454
  13.3 0.0 collective-permute-done.3.ax_ref
  13.3 0.0 collective-permute-done.2.above_ref
  13.3 2.3 %shard_map.95 = (f32[1536,128]{1,0:T(8,128)S(1)}, f32[4,8,128]{2,1,0:T(8,128)S(1)}, f32[480,128]{1,0:T(8,128)S(1)}, f32[8,128]{1,0:T(8,128)S(1)}, bf16[256,512]{...) custom-call(s32[1]{0:T(128)} %bitcast.15.where_ref, ...), custom_call_target="tpu_custom_call" | custom-call | flops 4000000 | bytes 400000 | tf_op jit(solution)/shard_map/pallas_call | solution.py:440
  15.6 0.1 collective-permute-start.7
  15.7 6.9 %collective-permute-done.6.below_ref = f32[776,128]{1,0:T(8,128)S(1)} collective-permute-done((f32[776,128]{1,0:T(8,128)S(1)}, f32[776,128]{1,0:T(8,128)S(1)}, u32[]{:S(2)}, u32[]{:S(2)}) %collective-permute-start.6) | collective-permute-done | bytes 397344 | tf_op jit(solution)/shard_map/ppermute | solution.py:454
  22.6 0.0 copy-start.2
  22.6 1.3 %shard_map.96 = (f32[1536,128]{1,0:T(8,128)S(1)}, f32[488,128]{1,0:T(8,128)S(1)}, f32[384,128]{1,0:T(8,128)S(1)}, f32[1,1536]{1,0:T(1,128)S(1)}, f32[1,1536]{1,0:T(1,128)S(1)}, /*index=5*/f32[8,128]{1,0:T(8,128)S(1)}) custom-call(s32[1]{0:T(128)} %bitcast.15.where_ref, s32[1]{0:T(128)} %bitcast.16.rad_ref, f32[1536,128]{1,0:T(8,128)S(1)} %get-tuple-element.61.part_ref, ...), custom_call_target="tpu_custom_call" | custom-call | flops 10000 | bytes 1000 | tf_op jit(solution)/shard_map/pallas_call | solution.py:440
  23.9 3.7 %collective-permute-start.10 = (f32[488,128]{1,0:T(8,128)S(1)}, f32[488,128]{1,0:T(8,128)S(1)}, u32[]{:S(2)}, u32[]{:S(2)}) collective-permute-start(f32[488,128]{1,0:T(8,128)S(1)} %get-tuple-element.74), channel_id=1, source_target_pairs={{0,24},{8,0},{16,8},{24,16},{1,25},{9,1},{17,9},{25,17},{2,26},{10... | collective-permute-start | bytes 749576 | tf_op jit(solution)/shard_map/ppermute | solution.py:454
  27.6 1.3 %collective-permute-start.11 = (f32[384,128]{1,0:T(8,128)S(1)}, f32[384,128]{1,0:T(8,128)S(1)}, u32[]{:S(2)}, u32[]{:S(2)}) collective-permute-start(f32[384,128]{1,0:T(8,128)S(1)} %get-tuple-element.75), channel_id=1, source_target_pairs={{0,1},{1,0},{2,3},{3,2},{4,5},{5,4},{6,7},{7,6},{8,9},{9,8},{10,11... | collective-permute-start | bytes 589832 | tf_op jit(solution)/shard_map/ppermute | solution.py:458
  28.8 2.8 %collective-permute-start.8 = (f32[1,1536]{1,0:T(1,128)S(1)}, f32[1,1536]{1,0:T(1,128)S(1)}, u32[]{:S(2)}, u32[]{:S(2)}) collective-permute-start(f32[1,1536]{1,0:T(1,128)S(1)} %get-tuple-element.72), channel_id=1, source_target_pairs={{0,2},{2,4},{4,6},{6,0},{1,3},{3,5},{5,7},{7,1},{8,10},{10,12},{12... | collective-permute-start | bytes 18440 | tf_op jit(solution)/shard_map/ppermute | solution.py:454
  31.6 0.0 collective-permute-start.9
  31.6 0.0 collective-permute-done.7.below_ref
  31.6 0.0 copy-done.2
  31.6 1.6 %shard_map.97 = (f32[1536,128]{1,0:T(8,128)S(1)}, f32[1536,128]{1,0:T(8,128)S(1)}) custom-call(f32[1536,128]{1,0:T(8,128)S(1)} %get-tuple-element.67.m_ref, f32[1536,128]{1,0:T(8,128)S(1)} %bitcast.52, bf16[192,8,128]{2,1,0:T(8,128)(2,1)S(1)} %bitcast.54, f32[480,128]{1,0:T(8,128)S(1)} %collective-permute-done.7.below_ref, ...), custom_call_target="tpu_custom_call" | custom-call | flops 300000000 | bytes 30000000 | tf_op jit(solution)/shard_map/pallas_call | solution.py:440
  33.3 0.0 collective-permute-done.8.radlo_ref
  33.3 1.4 %collective-permute-done.9.radhi_ref = f32[1,1536]{1,0:T(1,128)S(1)} collective-permute-done((f32[1,1536]{1,0:T(1,128)S(1)}, f32[1,1536]{1,0:T(1,128)S(1)}, u32[]{:S(2)}, u32[]{:S(2)}) %collective-permute-start.9) | collective-permute-done | bytes 6176 | tf_op jit(solution)/shard_map/ppermute | solution.py:454
  34.7 0.8 %shard_map.98.full_ref = f32[1536,128]{1,0:T(8,128)S(1)} custom-call(f32[1536,128]{1,0:T(8,128)S(1)} %get-tuple-element.71.bottom_ref, f32[1,1536]{1,0:T(1,128)S(1)} %collective-permute-done.8.radlo_ref, f32[1,1536]{1,0:T(1,128)S(1)} %collective-permute-done.9.radhi_ref, f32[4,8,128]{2,1,0:T(8,128)S(1)} %get-tuple-element.63.edge_ref), custom_call_target="tpu_custom_call" | custom-call | flops 1000 | bytes 100 | tf_op jit(solution)/shard_map/pallas_call | solution.py:440
  35.5 0.0 collective-permute-done.11.ax_ref
  35.5 0.0 collective-permute-done.10.above_ref
  35.5 2.0 %shard_map.99 = (f32[1536,128]{1,0:T(8,128)}, s32[1]{0:T(128)}) custom-call(s32[1]{0:T(128)} %bitcast.15.where_ref, f32[1536,128]{1,0:T(8,128)S(1)} %shard_map.98.full_ref, f32[488,128]{1,0:T(8,128)S(1)} %collective-permute-done.10.above_ref, f32[384,128]{1,0:T(8,128)S(1)} %collective-permute-done.11.ax_ref, f32[4,8,128]{2,1,0:T(8,128)S(1)} %get-tuple-element.63.edge_ref, ...), custom_call_target="tpu_custom_call" | custom-call | flops 1000000 | bytes 100000 | tf_op jit(solution)/shard_map/pallas_call | solution.py:440
  (1 shorter events, 0.0 us)
Async XLA Ops:
  0.0 5.3 %copy-start = (f32[4,48,2,4,128]{4,3,2,1,0:T(4,128)S(1)}, f32[4,48,2,4,128]{4,3,2,1,0:T(4,128)}, u32[]{:S(2)}) copy-start(f32[4,48,2,4,128]{4,3,2,1,0:T(4,128)} %param.11) | copy-start | bytes 2359300
  0.0 5.3 %copy-start.4 = (s32[3,2,4,128]{3,2,1,0:T(4,128)S(1)}, s32[3,2,4,128]{3,2,1,0:T(4,128)}, u32[]{:S(2)}) copy-start(s32[3,2,4,128]{3,2,1,0:T(4,128)} %param.15) | copy-start | bytes 36868
  1.1 4.2 %copy-start.3 = (f32[3,2,4,128]{3,2,1,0:T(4,128)S(1)}, f32[3,2,4,128]{3,2,1,0:T(4,128)}, u32[]{:S(2)}) copy-start(f32[3,2,4,128]{3,2,1,0:T(4,128)} %param.14) | copy-start | bytes 36868
  1.1 12.2 %collective-permute-start.2 = (f32[776,128]{1,0:T(8,128)S(1)}, f32[776,128]{1,0:T(8,128)S(1)}, u32[]{:S(2)}, u32[]{:S(2)}) collective-permute-start(f32[776,128]{1,0:T(8,128)S(1)} %bitcast.70), channel_id=1, source_target_pairs={{0,24},{8,0},{16,8},{24,16},{1,25},{9,1},{17,9},{25,17},{2,26},{10... | collective-permute-start | bytes 1191944 | tf_op jit(solution)/shard_map/ppermute | solution.py:454
  5.3 4.6 %copy-start.1 = (bf16[4,48,2,4,128]{4,3,2,1,0:T(4,128)(2,1)S(1)}, bf16[4,48,2,4,128]{4,3,2,1,0:T(4,128)(2,1)}, u32[]{:S(2)}) copy-start(bf16[4,48,2,4,128]{4,3,2,1,0:T(4,128)(2,1)} %param.13) | copy-start | bytes 1179652
  6.2 16.4 %collective-permute-start.6 = (f32[776,128]{1,0:T(8,128)S(1)}, f32[776,128]{1,0:T(8,128)S(1)}, u32[]{:S(2)}, u32[]{:S(2)}) collective-permute-start(f32[776,128]{1,0:T(8,128)S(1)} %get-tuple-element.62), channel_id=1, source_target_pairs={{0,8},{8,16},{16,24},{24,0},{1,9},{9,17},{17,25},{25,1},{2,10},{10... | collective-permute-start | bytes 1191944 | tf_op jit(solution)/shard_map/ppermute | solution.py:454
  6.3 3.7 %copy-start.5 = (s32[2,4,128]{2,1,0:T(4,128)S(1)}, s32[2,4,128]{2,1,0:T(4,128)}, u32[]{:S(2)}) copy-start(s32[2,4,128]{2,1,0:T(4,128)} %param.16) | copy-start | bytes 12292
  6.3 7.0 %collective-permute-start.3 = (f32[392,128]{1,0:T(8,128)S(1)}, f32[392,128]{1,0:T(8,128)S(1)}, u32[]{:S(2)}, u32[]{:S(2)}) collective-permute-start(f32[392,128]{1,0:T(8,128)S(1)} %get-tuple-element.58), channel_id=1, source_target_pairs={{0,1},{1,0},{2,3},{3,2},{4,5},{5,4},{6,7},{7,6},{8,9},{9,8},{10,11... | collective-permute-start | bytes 602120 | tf_op jit(solution)/shard_map/ppermute | solution.py:458
  7.6 4.6 %collective-permute-start.4 = (f32[1,1664]{1,0:T(1,128)S(1)}, f32[1,1664]{1,0:T(1,128)S(1)}, u32[]{:S(2)}, u32[]{:S(2)}) collective-permute-start(f32[1,1664]{1,0:T(1,128)S(1)} %get-tuple-element.59), channel_id=1, source_target_pairs={{0,2},{2,4},{4,6},{6,0},{1,3},{3,5},{5,7},{7,1},{8,10},{10,12},{12... | collective-permute-start | bytes 19976 | tf_op jit(solution)/shard_map/ppermute | solution.py:454
  9.9 3.4 %collective-permute-start.5 = (f32[1,1664]{1,0:T(1,128)S(1)}, f32[1,1664]{1,0:T(1,128)S(1)}, u32[]{:S(2)}, u32[]{:S(2)}) collective-permute-start(f32[1,1664]{1,0:T(1,128)S(1)} %get-tuple-element.60), channel_id=1, source_target_pairs={{0,6},{2,0},{4,2},{6,4},{1,7},{3,1},{5,3},{7,5},{8,14},{10,8},{12,... | collective-permute-start | bytes 19976 | tf_op jit(solution)/shard_map/ppermute | solution.py:454
  9.9 0.7 %copy-start.6 = (f32[48]{0:T(128)S(1)}, f32[48]{0:T(128)}, u32[]{:S(2)}) copy-start(f32[48]{0:T(128)} %growth_ref.3) | copy-start | bytes 580
  9.9 0.7 %copy-start.7 = (f32[48]{0:T(128)S(1)}, f32[48]{0:T(128)}, u32[]{:S(2)}) copy-start(f32[48]{0:T(128)} %transfer_ref.3) | copy-start | bytes 580
  9.9 0.7 %copy-start.8 = (f32[4]{0:T(128)S(1)}, f32[4]{0:T(128)}, u32[]{:S(2)}) copy-start(f32[4]{0:T(128)} %rate_ref.3) | copy-start | bytes 52
  15.6 16.1 %collective-permute-start.7 = (f32[480,128]{1,0:T(8,128)S(1)}, f32[480,128]{1,0:T(8,128)S(1)}, u32[]{:S(2)}, u32[]{:S(2)}) collective-permute-start(f32[480,128]{1,0:T(8,128)S(1)} %get-tuple-element.68), channel_id=1, source_target_pairs={{0,8},{8,16},{16,24},{24,0},{1,9},{9,17},{17,25},{25,1},{2,10},{10... | collective-permute-start | bytes 737288 | tf_op jit(solution)/shard_map/ppermute | solution.py:454
  22.6 9.0 %copy-start.2 = (bf16[4,48,2,4,128]{4,3,2,1,0:T(4,128)(2,1)S(1)}, bf16[4,48,2,4,128]{4,3,2,1,0:T(4,128)(2,1)}, u32[]{:S(2)}) copy-start(bf16[4,48,2,4,128]{4,3,2,1,0:T(4,128)(2,1)} %param.12) | copy-start | bytes 1179652
  23.9 11.7 %collective-permute-start.10 = (f32[488,128]{1,0:T(8,128)S(1)}, f32[488,128]{1,0:T(8,128)S(1)}, u32[]{:S(2)}, u32[]{:S(2)}) collective-permute-start(f32[488,128]{1,0:T(8,128)S(1)} %get-tuple-element.74), channel_id=1, source_target_pairs={{0,24},{8,0},{16,8},{24,16},{1,25},{9,1},{17,9},{25,17},{2,26},{10... | collective-permute-start | bytes 749576 | tf_op jit(solution)/shard_map/ppermute | solution.py:454
  27.6 8.0 %collective-permute-start.11 = (f32[384,128]{1,0:T(8,128)S(1)}, f32[384,128]{1,0:T(8,128)S(1)}, u32[]{:S(2)}, u32[]{:S(2)}) collective-permute-start(f32[384,128]{1,0:T(8,128)S(1)} %get-tuple-element.75), channel_id=1, source_target_pairs={{0,1},{1,0},{2,3},{3,2},{4,5},{5,4},{6,7},{7,6},{8,9},{9,8},{10,11... | collective-permute-start | bytes 589832 | tf_op jit(solution)/shard_map/ppermute | solution.py:458
  28.8 4.4 %collective-permute-start.8 = (f32[1,1536]{1,0:T(1,128)S(1)}, f32[1,1536]{1,0:T(1,128)S(1)}, u32[]{:S(2)}, u32[]{:S(2)}) collective-permute-start(f32[1,1536]{1,0:T(1,128)S(1)} %get-tuple-element.72), channel_id=1, source_target_pairs={{0,2},{2,4},{4,6},{6,0},{1,3},{3,5},{5,7},{7,1},{8,10},{10,12},{12... | collective-permute-start | bytes 18440 | tf_op jit(solution)/shard_map/ppermute | solution.py:454
  31.6 3.1 %collective-permute-start.9 = (f32[1,1536]{1,0:T(1,128)S(1)}, f32[1,1536]{1,0:T(1,128)S(1)}, u32[]{:S(2)}, u32[]{:S(2)}) collective-permute-start(f32[1,1536]{1,0:T(1,128)S(1)} %get-tuple-element.73), channel_id=1, source_target_pairs={{0,6},{2,0},{4,2},{6,4},{1,7},{3,1},{5,3},{7,5},{8,14},{10,8},{12,... | collective-permute-start | bytes 18440 | tf_op jit(solution)/shard_map/ppermute | solution.py:454

commit v15 on v14

--- a/solution.py
+++ b/solution.py
@@ -180,11 +180,13 @@
     return lax.dot_general(both, place, (((0,), (0,)), ((), ())), precision=exact, preferred_element_type=f32)
 
 
-def first_rest(comps, last, where_ref, rad_ref, a_ref, speeds_ref, flags_ref, up_ref, ax_ref, radup_ref, raddn_ref):
+def first_rest(comps, last, where_ref, rad_ref, a_ref, speeds_ref, flags_ref, up_ref, up2_ref, ax_ref, radup_ref, raddn_ref):
     p, _ = faces(speeds_ref, flags_ref)
-    for c in range(comps):
+    half = comps // 2
+    for c in range(half):
         up_ref[4 * c : 4 * c + 4] = a_ref[8 * c + 4 : 8 * c + 8]
-    up_ref[4 * comps :] = p[0]
+        up2_ref[4 * c : 4 * c + 4] = a_ref[8 * (c + half) + 4 : 8 * (c + half) + 8]
+    up_ref[4 * half :] = p[0]
     pack_sides(comps, last, a_ref, where_ref, rad_ref, ax_ref, radup_ref, raddn_ref)
     ax_ref[2 * comps : 2 * comps + 8] = pair_rows(p[1], 0, 4)
     radup_ref[:, 8 * comps :] = jnp.zeros((1, 128), f32)
@@ -316,6 +318,7 @@
     part_ref,
     a_ref,
     above_ref,
+    below_ref,
     ax_ref,
     radlo_ref,
     radhi_ref,
@@ -335,7 +338,8 @@
     upper = above_ref[4 * comps :]
     make_tables(upper, True, up_low_ref, up_high_ref)
     make_tables(upper, False, dn_low_ref, dn_high_ref)
-    bad_ref[...] = crowded(p[0]) + crowded(upper)
+    bad_ref[...] = crowded(p[0]) + crowded(upper) + crowded(below_ref[2 * comps :])
+    low = jnp.where(row >= 4, 0.0, q[0])
     hrad = put_columns(radlo_ref[...], radhi_ref[...])
     lower_half = where_ref[0] == 0
     p_azim = jnp.where(row >= 4, pltpu.roll(upper, 4, 0), 0.0)
@@ -351,9 +355,10 @@
     edge_ref[3] = centre
     for c in range(comps):
         spots = slice(8 * c, 8 * c + 8)
-        m_ref[spots] = part_ref[spots] + 0.5 * (
-            p_azim * from_above(c, above_ref) + rad * hrad[spots] - centre * a_ref[spots]
-        )
+        halo = p_azim * from_above(c, above_ref)
+        if c < comps // 2:
+            halo = halo + low * from_below(c, below_ref)
+        m_ref[spots] = part_ref[spots] + 0.5 * (halo + rad * hrad[spots] - centre * a_ref[spots])
     add_axial(comps, 0.5, where_ref, axial, ax_ref, m_ref)
     encode(comps, m_ref, 4, up_low_ref, up_high_ref, up_ref)
 
@@ -374,14 +379,14 @@
     ax_ref,
     radup_ref,
     raddn_ref,
-    worse_ref,
 ):
     azim = jnp.where(rows_of() >= 4, 0.0, 0.5 * edge_ref[0])
     for c in range(comps):
-        m_ref[8 * c : 8 * c + 8] = part_ref[8 * c : 8 * c + 8] + azim * from_below(c, below_ref)
+        m_ref[8 * c : 8 * c + 8] = part_ref[8 * c : 8 * c + 8]
+        if c >= comps // 2:
+            m_ref[8 * c : 8 * c + 8] = m_ref[8 * c : 8 * c + 8] + azim * from_below(c - comps // 2, below_ref)
     encode(comps, m_ref, 0, low_ref, high_ref, dn_ref)
-    worse_ref[...] = bad_ref[...] + crowded(below_ref[4 * comps :])
-    dn_ref[5 * comps // 2 :] = worse_ref[...]
+    dn_ref[5 * comps // 2 :] = bad_ref[...]
     pack_sides(comps, last, m_ref, where_ref, rad_ref, ax_ref, radup_ref, raddn_ref)
 
 
@@ -409,7 +414,6 @@
     done_ref,
     sems,
 ):
-    again_ref[0] = (jnp.max(bad_ref[...] + above_ref[5 * comps // 2 :]) > 0.0).astype(jnp.int32)
     halo = decode(comps, above_ref, low_ref, high_ref)
     azim = edge_ref[0]
     done_ref[...] = full_ref[...]
@@ -425,6 +429,7 @@
         spots = pl.ds(8 * size * i, 8 * size)
         made.append(pltpu.make_async_copy(done_ref.at[spots], out_ref.at[spots], sems.at[i]))
         made[-1].start()
+    again_ref[0] = (jnp.max(bad_ref[...] + above_ref[5 * comps // 2 :]) > 0.0).astype(jnp.int32)
     for copy in made:
         copy.wait()
 
@@ -482,18 +487,18 @@
     dn = lax.pad(adjoint_final.reshape(comps, 2, 4, 128), 0.0, keep)
     dn = dn + lax.pad(speeds, 0.0, after) * lax.pad(flags, 0, after).astype(f32)
     above = shift(dn.reshape(half + 8, 128), "azim", -1, True)
-    up, *edges = call(
+    up, up2, *edges = call(
         functools.partial(first_rest, comps, last),
         "ssvvv",
-        "vvvv",
-        [(half + 8, 128), (rows + 8, 128), (1, cells + 128), (1, cells + 128)],
+        "vvvvv",
+        [(half // 2 + 8, 128), (half // 2, 128), (rows + 8, 128), (1, cells + 128), (1, cells + 128)],
         2_000_000,
         *place,
         a,
         speeds2,
         flags2,
     )
-    below = shift(up, "azim", 1, True)
+    below, below2 = shift(up, "azim", 1, True), shift(up2, "azim", 1, True)
     edges = sides(*edges)
     part, *lower_tables = call(
         functools.partial(first_local, sections),
@@ -509,7 +514,7 @@
     )
     part, edge, up, bad, *upper_tables = call(
         functools.partial(first_top, comps),
-        "s" + "v" * 8,
+        "s" + "v" * 9,
         "v" * 8,
         [(cells, 128), (4, 8, 128), (message, 128), (8, 128)] + 2 * tables,
         4_000_000,
@@ -517,20 +522,21 @@
         part,
         a,
         above,
+        below,
         *edges,
         speeds2,
         flags2,
     )
     next_below = shift(up, "azim", 1, True)
-    m, dn, *edges, bad = call(
+    m, dn, *edges = call(
         functools.partial(first_bottom, comps, last),
         "ss" + "v" * 6,
-        "v" * 6,
-        [(cells, 128), (message + 8, 128), (rows, 128), (1, cells), (1, cells), (8, 128)],
+        "v" * 5,
+        [(cells, 128), (message + 8, 128), (rows, 128), (1, cells), (1, cells)],
         10_000,
         *place,
         part,
-        below,
+        below2,
         edge,
         bad,
         *lower_tables[:2],

time: 38.4 us -> 39.4 us (1.026)
  the two profiles are of different devices: /device:TPU:1 before, /device:TPU:0 now
where the time goes in v15:
time: 39.4 us; the launch traced here: 39.2 us
  starting transfers between devices  14.2 us (36%)
  waiting for transfers between devices  12.1 us (31%)
  Pallas kernels  10.3 us (26%)
  other arithmetic  1.1 us (3%)
  between operations  0.83 us (2%)
  local copies, waits for them, and re-layouts  0.68 us (2%)
    ppermute x9, waiting for transfers between devices, shift(): return lax.ppermute(x, axis, pairs)  12.1 us
    ppermute x9, starting transfers between devices, shift(): return lax.ppermute(x, axis, pairs)  11.1 us
    pallas_call x7, Pallas kernels, call(): pl.pallas_call(body, in_specs=[SPACES[s] for s in ins], out_specs=[SPACES...  10.3 us
    ppermute x2, starting transfers between devices, sides(): ax = lax.ppermute(ax, 'axial', [(0, 1), (1, 0)])  3.12 us
    add x1, other arithmetic, shards(): dn = dn + lax.pad(speeds, 0.0, after) * lax.pad(flags, 0, after).astype(f32)  1.1 us
  transfers between devices with their start and end apart: 11, of which 4 were waited for; matrix products, arithmetic and copies ran while one was open for 0% of the time, Pallas kernels for 21%

profile of v15, /device:TPU:0, one launch (start us, length us, event | category | flops | bytes accessed | tf_op | source)
XLA Modules:
  0.0 39.2 jit_solution(16611527790994806152)
XLA Ops:
  0.0 0.0 copy-start
  0.0 0.0 copy-start.4
  0.0 1.1 %fusion.4 = f32[194,1,4,128]{3,2,1,0:T(4,128)S(1)} fusion(f32[192,2,4,128]{3,2,1,0:T(4,128)} %bitcast.48, f32[3,2,4,128]{3,2,1,0:T(4,128)} %param.14, s32[3,2,4,128]{3,2,1,0:T(4,128)} %param.15), kind=kLoop, calls=%fused_computation.19 | loop fusion | flops 297984 | bytes 1208320 | tf_op jit(solution)/shard_map/add | solution.py:488
  1.1 0.0 copy-start.3
  1.1 5.1 %collective-permute-start.2 = (f32[776,128]{1,0:T(8,128)S(1)}, f32[776,128]{1,0:T(8,128)S(1)}, u32[]{:S(2)}, u32[]{:S(2)}) collective-permute-start(f32[776,128]{1,0:T(8,128)S(1)} %bitcast.70), channel_id=1, source_target_pairs={{0,24},{8,0},{16,8},{24,16},{1,25},{9,1},{17,9},{25,17},{2,26},{10... | collective-permute-start | bytes 1191944 | tf_op jit(solution)/shard_map/ppermute | solution.py:459
  6.2 0.0 copy-done
  6.2 0.0 copy-done.4
  6.2 0.0 copy-done.3
  6.2 0.0 copy-start.1
  6.2 0.9 %shard_map.94 = (f32[392,128]{1,0:T(8,128)S(1)}, f32[384,128]{1,0:T(8,128)S(1)}, f32[392,128]{1,0:T(8,128)S(1)}, f32[1,1664]{1,0:T(1,128)S(1)}, f32[1,1664]{1,0:T(1,128)S(1)}) custom-call(s32[1]{0:T(128)} %bitcast.15.where_ref, s32[1]{0:T(128)} %bitcast.16.rad_ref, f32[1536,128]{1,0:T(8,128)S(1)} %bitcast.49, f32[3,8,128]{2,1,0:T(8,128)S(1)} %bitcast.55, ...), custom_call_target="tpu_custom_call" | custom-call | flops 2000000 | bytes 200000 | tf_op jit(solution)/shard_map/pallas_call | solution.py:445
  7.1 0.1 collective-permute-start.3
  7.2 1.6 %collective-permute-start.4 = (f32[392,128]{1,0:T(8,128)S(1)}, f32[392,128]{1,0:T(8,128)S(1)}, u32[]{:S(2)}, u32[]{:S(2)}) collective-permute-start(f32[392,128]{1,0:T(8,128)S(1)} %get-tuple-element.59), channel_id=1, source_target_pairs={{0,1},{1,0},{2,3},{3,2},{4,5},{5,4},{6,7},{7,6},{8,9},{9,8},{10,11... | collective-permute-start | bytes 602120 | tf_op jit(solution)/shard_map/ppermute | solution.py:463
  8.7 0.0 copy-start.5
  8.7 0.1 collective-permute-start.7
  8.9 0.0 collective-permute-start.5
  8.9 3.1 %collective-permute-done.5.radlo_ref = f32[1,1664]{1,0:T(1,128)S(1)} collective-permute-done((f32[1,1664]{1,0:T(1,128)S(1)}, f32[1,1664]{1,0:T(1,128)S(1)}, u32[]{:S(2)}, u32[]{:S(2)}) %collective-permute-start.5) | collective-permute-done | bytes 6688 | tf_op jit(solution)/shard_map/ppermute | solution.py:459
  11.9 0.0 collective-permute-start.6
  11.9 0.0 copy-start.6
  12.0 0.0 copy-start.7
  12.0 0.0 copy-start.8
  12.0 0.0 copy-done.1
  12.0 0.0 copy-done.5
  12.0 0.6 %copy-done.6 = f32[48]{0:T(128)S(1)} copy-done((f32[48]{0:T(128)S(1)}, f32[48]{0:T(128)}, u32[]{:S(2)}) %copy-start.6) | copy-done | bytes 216
  12.6 0.0 copy-done.7
  12.6 0.0 copy-done.8
  12.6 1.6 %shard_map.93 = (f32[1536,128]{1,0:T(8,128)S(1)}, bf16[256,512]{1,0:T(8,128)(2,1)S(1)}, bf16[256,512]{1,0:T(8,128)(2,1)S(1)}, bf16[256,512]{1,0:T(8,128)(2,1)S(1)}, bf16[256,512]{1,0:T(8,128)(2,1)S(1)}) custom-call(f32[1536,128]{1,0:T(8,128)S(1)} %bitcast.50, bf16[192,8,128]{2,1,0:T(8,128)(2,1)S(1)} %bitcast.53, f32[3,8,128]{2,1,0:T(8,128)S(1)} %bitcast.56, ...), custom_call_target="tpu_custom_call" | custom-call | flops 8000000 | bytes 800000 | tf_op jit(solution)/shard_map/pallas_call | solution.py:445
  14.2 0.0 collective-permute-done.6.radhi_ref
  14.3 6.8 %collective-permute-done.3.below_ref = f32[392,128]{1,0:T(8,128)S(1)} collective-permute-done((f32[392,128]{1,0:T(8,128)S(1)}, f32[392,128]{1,0:T(8,128)S(1)}, u32[]{:S(2)}, u32[]{:S(2)}) %collective-permute-start.3) | collective-permute-done | bytes 200736 | tf_op jit(solution)/shard_map/ppermute | solution.py:459
  21.0 0.0 collective-permute-done.4.ax_ref
  21.0 0.0 collective-permute-done.2.above_ref
  21.0 2.2 %shard_map.95 = (f32[1536,128]{1,0:T(8,128)S(1)}, f32[4,8,128]{2,1,0:T(8,128)S(1)}, f32[480,128]{1,0:T(8,128)S(1)}, f32[8,128]{1,0:T(8,128)S(1)}, bf16[256,512]{...) custom-call(s32[1]{0:T(128)} %bitcast.15.where_ref, ...), custom_call_target="tpu_custom_call" | custom-call | flops 4000000 | bytes 400000 | tf_op jit(solution)/shard_map/pallas_call | solution.py:445
  23.3 1.6 %collective-permute-start.8 = (f32[480,128]{1,0:T(8,128)S(1)}, f32[480,128]{1,0:T(8,128)S(1)}, u32[]{:S(2)}, u32[]{:S(2)}) collective-permute-start(f32[480,128]{1,0:T(8,128)S(1)} %get-tuple-element.69), channel_id=1, source_target_pairs={{0,8},{8,16},{16,24},{24,0},{1,9},{9,17},{17,25},{25,1},{2,10},{10... | collective-permute-start | bytes 737288 | tf_op jit(solution)/shard_map/ppermute | solution.py:459
  24.9 0.0 collective-permute-done.7.below_ref
  24.9 0.0 copy-start.2
  24.9 1.2 %shard_map.96 = (f32[1536,128]{1,0:T(8,128)S(1)}, f32[488,128]{1,0:T(8,128)S(1)}, f32[384,128]{1,0:T(8,128)S(1)}, f32[1,1536]{1,0:T(1,128)S(1)}, f32[1,1536]{1,0:T(1,128)S(1)}) custom-call(s32[1]{0:T(128)} %bitcast.15.where_ref, s32[1]{0:T(128)} %bitcast.16.rad_ref, f32[1536,128]{1,0:T(8,128)S(1)} %get-tuple-element.62.part_ref, ...), custom_call_target="tpu_custom_call" | custom-call | flops 10000 | bytes 1000 | tf_op jit(solution)/shard_map/pallas_call | solution.py:445
  26.2 2.4 %collective-permute-start.11 = (f32[488,128]{1,0:T(8,128)S(1)}, f32[488,128]{1,0:T(8,128)S(1)}, u32[]{:S(2)}, u32[]{:S(2)}) collective-permute-start(f32[488,128]{1,0:T(8,128)S(1)} %get-tuple-element.75), channel_id=1, source_target_pairs={{0,24},{8,0},{16,8},{24,16},{1,25},{9,1},{17,9},{25,17},{2,26},{10... | collective-permute-start | bytes 749576 | tf_op jit(solution)/shard_map/ppermute | solution.py:459
  28.5 1.5 %collective-permute-start.12 = (f32[384,128]{1,0:T(8,128)S(1)}, f32[384,128]{1,0:T(8,128)S(1)}, u32[]{:S(2)}, u32[]{:S(2)}) collective-permute-start(f32[384,128]{1,0:T(8,128)S(1)} %get-tuple-element.76), channel_id=1, source_target_pairs={{0,1},{1,0},{2,3},{3,2},{4,5},{5,4},{6,7},{7,6},{8,9},{9,8},{10,11... | collective-permute-start | bytes 589832 | tf_op jit(solution)/shard_map/ppermute | solution.py:463
  30.1 0.0 collective-permute-start.9
  30.1 1.7 %collective-permute-start.10 = (f32[1,1536]{1,0:T(1,128)S(1)}, f32[1,1536]{1,0:T(1,128)S(1)}, u32[]{:S(2)}, u32[]{:S(2)}) collective-permute-start(f32[1,1536]{1,0:T(1,128)S(1)} %get-tuple-element.74), channel_id=1, source_target_pairs={{0,6},{2,0},{4,2},{6,4},{1,7},{3,1},{5,3},{7,5},{8,14},{10,8},{12,... | collective-permute-start | bytes 18440 | tf_op jit(solution)/shard_map/ppermute | solution.py:459
  31.8 1.7 %collective-permute-done.8.below_ref = f32[480,128]{1,0:T(8,128)S(1)} collective-permute-done((f32[480,128]{1,0:T(8,128)S(1)}, f32[480,128]{1,0:T(8,128)S(1)}, u32[]{:S(2)}, u32[]{:S(2)}) %collective-permute-start.8) | collective-permute-done | bytes 245792 | tf_op jit(solution)/shard_map/ppermute | solution.py:459
  33.5 0.0 copy-done.2
  33.5 1.6 %shard_map.97 = (f32[1536,128]{1,0:T(8,128)S(1)}, f32[1536,128]{1,0:T(8,128)S(1)}) custom-call(f32[1536,128]{1,0:T(8,128)S(1)} %get-tuple-element.68.m_ref, f32[1536,128]{1,0:T(8,128)S(1)} %bitcast.52, bf16[192,8,128]{2,1,0:T(8,128)(2,1)S(1)} %bitcast.54, f32[480,128]{1,0:T(8,128)S(1)} %collective-permute-done.8.below_ref, ...), custom_call_target="tpu_custom_call" | custom-call | flops 300000000 | bytes 30000000 | tf_op jit(solution)/shard_map/pallas_call | solution.py:445
  35.1 0.0 collective-permute-done.9.radlo_ref
  35.1 0.0 collective-permute-done.10.radhi_ref
  35.1 0.8 %shard_map.98.full_ref = f32[1536,128]{1,0:T(8,128)S(1)} custom-call(f32[1536,128]{1,0:T(8,128)S(1)} %get-tuple-element.72.bottom_ref, f32[1,1536]{1,0:T(1,128)S(1)} %collective-permute-done.9.radlo_ref, f32[1,1536]{1,0:T(1,128)S(1)} %collective-permute-done.10.radhi_ref, f32[4,8,128]{2,1,0:T(8,128)S(1)} %get-tuple-element.64.edge_ref), custom_call_target="tpu_custom_call" | custom-call | flops 1000 | bytes 100 | tf_op jit(solution)/shard_map/pallas_call | solution.py:445
  36.0 0.0 collective-permute-done.12.ax_ref
  36.0 0.6 %collective-permute-done.11.above_ref = f32[488,128]{1,0:T(8,128)S(1)} collective-permute-done((f32[488,128]{1,0:T(8,128)S(1)}, f32[488,128]{1,0:T(8,128)S(1)}, u32[]{:S(2)}, u32[]{:S(2)}) %collective-permute-start.11) | collective-permute-done | bytes 249888 | tf_op jit(solution)/shard_map/ppermute | solution.py:459
  36.6 2.0 %shard_map.99 = (f32[1536,128]{1,0:T(8,128)}, s32[1]{0:T(128)}) custom-call(s32[1]{0:T(128)} %bitcast.15.where_ref, f32[1536,128]{1,0:T(8,128)S(1)} %shard_map.98.full_ref, f32[488,128]{1,0:T(8,128)S(1)} %collective-permute-done.11.above_ref, f32[384,128]{1,0:T(8,128)S(1)} %collective-permute-done.12.ax_ref, f32[4,8,128]{2,1,0:T(8,128)S(1)} %get-tuple-element.64.edge_ref, ...), custom_call_target="tpu_custom_call" | custom-call | flops 1000000 | bytes 100000 | tf_op jit(solution)/shard_map/pallas_call | solution.py:445
  (1 shorter events, 0.0 us)
Async XLA Ops:
  0.0 6.2 %copy-start = (f32[4,48,2,4,128]{4,3,2,1,0:T(4,128)S(1)}, f32[4,48,2,4,128]{4,3,2,1,0:T(4,128)}, u32[]{:S(2)}) copy-start(f32[4,48,2,4,128]{4,3,2,1,0:T(4,128)} %param.11) | copy-start | bytes 2359300
  0.0 6.2 %copy-start.4 = (s32[3,2,4,128]{3,2,1,0:T(4,128)S(1)}, s32[3,2,4,128]{3,2,1,0:T(4,128)}, u32[]{:S(2)}) copy-start(s32[3,2,4,128]{3,2,1,0:T(4,128)} %param.15) | copy-start | bytes 36868
  1.1 5.1 %copy-start.3 = (f32[3,2,4,128]{3,2,1,0:T(4,128)S(1)}, f32[3,2,4,128]{3,2,1,0:T(4,128)}, u32[]{:S(2)}) copy-start(f32[3,2,4,128]{3,2,1,0:T(4,128)} %param.14) | copy-start | bytes 36868
  1.1 19.9 %collective-permute-start.2 = (f32[776,128]{1,0:T(8,128)S(1)}, f32[776,128]{1,0:T(8,128)S(1)}, u32[]{:S(2)}, u32[]{:S(2)}) collective-permute-start(f32[776,128]{1,0:T(8,128)S(1)} %bitcast.70), channel_id=1, source_target_pairs={{0,24},{8,0},{16,8},{24,16},{1,25},{9,1},{17,9},{25,17},{2,26},{10... | collective-permute-start | bytes 1191944 | tf_op jit(solution)/shard_map/ppermute | solution.py:459
  6.2 5.7 %copy-start.1 = (bf16[4,48,2,4,128]{4,3,2,1,0:T(4,128)(2,1)S(1)}, bf16[4,48,2,4,128]{4,3,2,1,0:T(4,128)(2,1)}, u32[]{:S(2)}) copy-start(bf16[4,48,2,4,128]{4,3,2,1,0:T(4,128)(2,1)} %param.13) | copy-start | bytes 1179652
  7.1 13.9 %collective-permute-start.3 = (f32[392,128]{1,0:T(8,128)S(1)}, f32[392,128]{1,0:T(8,128)S(1)}, u32[]{:S(2)}, u32[]{:S(2)}) collective-permute-start(f32[392,128]{1,0:T(8,128)S(1)} %get-tuple-element.58), channel_id=1, source_target_pairs={{0,8},{8,16},{16,24},{24,0},{1,9},{9,17},{17,25},{25,1},{2,10},{10... | collective-permute-start | bytes 602120 | tf_op jit(solution)/shard_map/ppermute | solution.py:459
  7.2 13.9 %collective-permute-start.4 = (f32[392,128]{1,0:T(8,128)S(1)}, f32[392,128]{1,0:T(8,128)S(1)}, u32[]{:S(2)}, u32[]{:S(2)}) collective-permute-start(f32[392,128]{1,0:T(8,128)S(1)} %get-tuple-element.59), channel_id=1, source_target_pairs={{0,1},{1,0},{2,3},{3,2},{4,5},{5,4},{6,7},{7,6},{8,9},{9,8},{10,11... | collective-permute-start | bytes 602120 | tf_op jit(solution)/shard_map/ppermute | solution.py:463
  8.7 3.2 %copy-start.5 = (s32[2,4,128]{2,1,0:T(4,128)S(1)}, s32[2,4,128]{2,1,0:T(4,128)}, u32[]{:S(2)}) copy-start(s32[2,4,128]{2,1,0:T(4,128)} %param.16) | copy-start | bytes 12292
  8.7 16.2 %collective-permute-start.7 = (f32[384,128]{1,0:T(8,128)S(1)}, f32[384,128]{1,0:T(8,128)S(1)}, u32[]{:S(2)}, u32[]{:S(2)}) collective-permute-start(f32[384,128]{1,0:T(8,128)S(1)} %get-tuple-element.63), channel_id=1, source_target_pairs={{0,8},{8,16},{16,24},{24,0},{1,9},{9,17},{17,25},{25,1},{2,10},{10... | collective-permute-start | bytes 589832 | tf_op jit(solution)/shard_map/ppermute | solution.py:459
  8.9 3.1 %collective-permute-start.5 = (f32[1,1664]{1,0:T(1,128)S(1)}, f32[1,1664]{1,0:T(1,128)S(1)}, u32[]{:S(2)}, u32[]{:S(2)}) collective-permute-start(f32[1,1664]{1,0:T(1,128)S(1)} %get-tuple-element.60), channel_id=1, source_target_pairs={{0,2},{2,4},{4,6},{6,0},{1,3},{3,5},{5,7},{7,1},{8,10},{10,12},{12... | collective-permute-start | bytes 19976 | tf_op jit(solution)/shard_map/ppermute | solution.py:459
  11.9 2.3 %collective-permute-start.6 = (f32[1,1664]{1,0:T(1,128)S(1)}, f32[1,1664]{1,0:T(1,128)S(1)}, u32[]{:S(2)}, u32[]{:S(2)}) collective-permute-start(f32[1,1664]{1,0:T(1,128)S(1)} %get-tuple-element.61), channel_id=1, source_target_pairs={{0,6},{2,0},{4,2},{6,4},{1,7},{3,1},{5,3},{7,5},{8,14},{10,8},{12,... | collective-permute-start | bytes 19976 | tf_op jit(solution)/shard_map/ppermute | solution.py:459
  11.9 0.7 %copy-start.6 = (f32[48]{0:T(128)S(1)}, f32[48]{0:T(128)}, u32[]{:S(2)}) copy-start(f32[48]{0:T(128)} %growth_ref.3) | copy-start | bytes 580
  12.0 0.7 %copy-start.7 = (f32[48]{0:T(128)S(1)}, f32[48]{0:T(128)}, u32[]{:S(2)}) copy-start(f32[48]{0:T(128)} %transfer_ref.3) | copy-start | bytes 580
  12.0 0.7 %copy-start.8 = (f32[4]{0:T(128)S(1)}, f32[4]{0:T(128)}, u32[]{:S(2)}) copy-start(f32[4]{0:T(128)} %rate_ref.3) | copy-start | bytes 52
  23.3 10.2 %collective-permute-start.8 = (f32[480,128]{1,0:T(8,128)S(1)}, f32[480,128]{1,0:T(8,128)S(1)}, u32[]{:S(2)}, u32[]{:S(2)}) collective-permute-start(f32[480,128]{1,0:T(8,128)S(1)} %get-tuple-element.69), channel_id=1, source_target_pairs={{0,8},{8,16},{16,24},{24,0},{1,9},{9,17},{17,25},{25,1},{2,10},{10... | collective-permute-start | bytes 737288 | tf_op jit(solution)/shard_map/ppermute | solution.py:459
  24.9 8.6 %copy-start.2 = (bf16[4,48,2,4,128]{4,3,2,1,0:T(4,128)(2,1)S(1)}, bf16[4,48,2,4,128]{4,3,2,1,0:T(4,128)(2,1)}, u32[]{:S(2)}) copy-start(bf16[4,48,2,4,128]{4,3,2,1,0:T(4,128)(2,1)} %param.12) | copy-start | bytes 1179652
  26.2 10.4 %collective-permute-start.11 = (f32[488,128]{1,0:T(8,128)S(1)}, f32[488,128]{1,0:T(8,128)S(1)}, u32[]{:S(2)}, u32[]{:S(2)}) collective-permute-start(f32[488,128]{1,0:T(8,128)S(1)} %get-tuple-element.75), channel_id=1, source_target_pairs={{0,24},{8,0},{16,8},{24,16},{1,25},{9,1},{17,9},{25,17},{2,26},{10... | collective-permute-start | bytes 749576 | tf_op jit(solution)/shard_map/ppermute | solution.py:459
  28.5 7.5 %collective-permute-start.12 = (f32[384,128]{1,0:T(8,128)S(1)}, f32[384,128]{1,0:T(8,128)S(1)}, u32[]{:S(2)}, u32[]{:S(2)}) collective-permute-start(f32[384,128]{1,0:T(8,128)S(1)} %get-tuple-element.76), channel_id=1, source_target_pairs={{0,1},{1,0},{2,3},{3,2},{4,5},{5,4},{6,7},{7,6},{8,9},{9,8},{10,11... | collective-permute-start | bytes 589832 | tf_op jit(solution)/shard_map/ppermute | solution.py:463
  30.1 5.1 %collective-permute-start.9 = (f32[1,1536]{1,0:T(1,128)S(1)}, f32[1,1536]{1,0:T(1,128)S(1)}, u32[]{:S(2)}, u32[]{:S(2)}) collective-permute-start(f32[1,1536]{1,0:T(1,128)S(1)} %get-tuple-element.73), channel_id=1, source_target_pairs={{0,2},{2,4},{4,6},{6,0},{1,3},{3,5},{5,7},{7,1},{8,10},{10,12},{12... | collective-permute-start | bytes 18440 | tf_op jit(solution)/shard_map/ppermute | solution.py:459
  30.1 5.1 %collective-permute-start.10 = (f32[1,1536]{1,0:T(1,128)S(1)}, f32[1,1536]{1,0:T(1,128)S(1)}, u32[]{:S(2)}, u32[]{:S(2)}) collective-permute-start(f32[1,1536]{1,0:T(1,128)S(1)} %get-tuple-element.74), channel_id=1, source_target_pairs={{0,6},{2,0},{4,2},{6,4},{1,7},{3,1},{5,3},{7,5},{8,14},{10,8},{12,... | collective-permute-start | bytes 18440 | tf_op jit(solution)/shard_map/ppermute | solution.py:459

commit v16 on v14

--- a/solution.py
+++ b/solution.py
@@ -12,7 +12,6 @@
 nucleus_moments = (1.0, 0.5, 0.25, 0.125)
 f32 = jnp.float32
 bf16 = jnp.bfloat16
-exact = lax.Precision.HIGHEST
 
 slots = 320
 extra = slots - 256
@@ -167,8 +166,11 @@
 
 def columns(x):
     row, lane = rows_of(), lanes_of()
-    take = jnp.where(((row == 0) & (lane == 127)) | ((row == 1) & (lane == 0)), 1.0, 0.0)
-    return lax.dot_general(take, x, (((1,), (1,)), ((), ())), precision=exact, preferred_element_type=f32)
+    take = jnp.where(((row == 0) & (lane == 127)) | ((row == 1) & (lane == 0)), 1.0, 0.0).astype(bf16)
+    high, middle, low = (
+        lax.dot_general(take, part, (((1,), (1,)), ((), ())), preferred_element_type=f32) for part in pieces(x)
+    )
+    return high + (middle + low)
 
 
 def put_columns(lower, upper):
@@ -177,7 +179,9 @@
     which = lax.broadcasted_iota(jnp.int32, (8, n), 0)
     both = jnp.where(which == 0, lower, jnp.where(which == 1, upper, 0.0))
     place = jnp.where(((row == 0) & (lane == 0)) | ((row == 1) & (lane == 127)), 1.0, 0.0)
-    return lax.dot_general(both, place, (((0,), (0,)), ((), ())), precision=exact, preferred_element_type=f32)
+    parts = jnp.concatenate([part.astype(f32) for part in pieces(both)], axis=0).astype(bf16)
+    places = jnp.concatenate([place] * 3, axis=0).astype(bf16)
+    return lax.dot_general(parts, places, (((0,), (0,)), ((), ())), preferred_element_type=f32)
 
 
 def first_rest(comps, last, where_ref, rad_ref, a_ref, speeds_ref, flags_ref, up_ref, ax_ref, radup_ref, raddn_ref):

time: 38.4 us -> 37.6 us (0.979)
  the two profiles are of different devices: /device:TPU:1 before, /device:TPU:0 now
where the time goes in v16:
time: 37.6 us; the launch traced here: 37.4 us
  starting transfers between devices  14.2 us (38%)
  waiting for transfers between devices  12 us (32%)
  Pallas kernels  8.59 us (23%)
  other arithmetic  1.1 us (3%)
  between operations  0.8 us (2%)
  local copies, waits for them, and re-layouts  0.7 us (2%)
    ppermute x8, starting transfers between devices, shift(): return lax.ppermute(x, axis, pairs)  11.1 us
    ppermute x8, waiting for transfers between devices, shift(): return lax.ppermute(x, axis, pairs)  10.7 us
    pallas_call x7, Pallas kernels, call(): pl.pallas_call(body, in_specs=[SPACES[s] for s in ins], out_specs=[SPACES...  8.59 us
    ppermute x2, starting transfers between devices, sides(): ax = lax.ppermute(ax, 'axial', [(0, 1), (1, 0)])  3.13 us
    ppermute x2, waiting for transfers between devices, sides(): ax = lax.ppermute(ax, 'axial', [(0, 1), (1, 0)])  1.26 us
    add x1, other arithmetic, shards(): dn = dn + lax.pad(speeds, 0.0, after) * lax.pad(flags, 0, after).astype(f32)  1.1 us
  transfers between devices with their start and end apart: 10, of which 5 were waited for; matrix products, arithmetic and copies ran while one was open for 0% of the time, Pallas kernels for 18%

profile of v16, /device:TPU:0, one launch (start us, length us, event | category | flops | bytes accessed | tf_op | source)
XLA Modules:
  0.0 37.4 jit_solution(3135850105716111067)
XLA Ops:
  0.0 0.0 copy-start
  0.0 0.0 copy-start.4
  0.0 1.1 %fusion.4 = f32[194,1,4,128]{3,2,1,0:T(4,128)S(1)} fusion(f32[192,2,4,128]{3,2,1,0:T(4,128)} %bitcast.48, f32[3,2,4,128]{3,2,1,0:T(4,128)} %param.14, s32[3,2,4,128]{3,2,1,0:T(4,128)} %param.15), kind=kLoop, calls=%fused_computation.19 | loop fusion | flops 297984 | bytes 1208320 | tf_op jit(solution)/shard_map/add | solution.py:487
  1.1 0.0 copy-start.3
  1.1 5.1 %collective-permute-start.2 = (f32[776,128]{1,0:T(8,128)S(1)}, f32[776,128]{1,0:T(8,128)S(1)}, u32[]{:S(2)}, u32[]{:S(2)}) collective-permute-start(f32[776,128]{1,0:T(8,128)S(1)} %bitcast.70), channel_id=1, source_target_pairs={{0,24},{8,0},{16,8},{24,16},{1,25},{9,1},{17,9},{25,17},{2,26},{10... | collective-permute-start | bytes 1191944 | tf_op jit(solution)/shard_map/ppermute | solution.py:458
  6.2 0.0 copy-done
  6.2 0.0 copy-done.4
  6.2 0.0 copy-done.3
  6.2 0.0 copy-start.1
  6.2 0.6 %shard_map.94 = (f32[776,128]{1,0:T(8,128)S(1)}, f32[392,128]{1,0:T(8,128)S(1)}, f32[1,1664]{1,0:T(1,128)S(1)}, f32[1,1664]{1,0:T(1,128)S(1)}) custom-call(s32[1]{0:T(128)} %bitcast.15.where_ref, s32[1]{0:T(128)} %bitcast.16.rad_ref, f32[1536,128]{1,0:T(8,128)S(1)} %bitcast.49, f32[3,8,128]{2,1,0:T(8,128)S(1)} %bitcast.55, s32[3,8,128]{2,1,0:T(8,128)S(1)} %bitcast.59), custom_call_target="tpu_custom_call" | custom-call | flops 2000000 | bytes 200000 | tf_op jit(solution)/shard_map/pallas_call | solution.py:444
  6.8 0.1 collective-permute-start.6
  6.9 0.0 copy-start.5
  6.9 1.6 %collective-permute-start.3 = (f32[392,128]{1,0:T(8,128)S(1)}, f32[392,128]{1,0:T(8,128)S(1)}, u32[]{:S(2)}, u32[]{:S(2)}) collective-permute-start(f32[392,128]{1,0:T(8,128)S(1)} %get-tuple-element.58), channel_id=1, source_target_pairs={{0,1},{1,0},{2,3},{3,2},{4,5},{5,4},{6,7},{7,6},{8,9},{9,8},{10,11... | collective-permute-start | bytes 602120 | tf_op jit(solution)/shard_map/ppermute | solution.py:462
  8.5 0.0 collective-permute-start.4
  8.5 1.7 %collective-permute-start.5 = (f32[1,1664]{1,0:T(1,128)S(1)}, f32[1,1664]{1,0:T(1,128)S(1)}, u32[]{:S(2)}, u32[]{:S(2)}) collective-permute-start(f32[1,1664]{1,0:T(1,128)S(1)} %get-tuple-element.60), channel_id=1, source_target_pairs={{0,6},{2,0},{4,2},{6,4},{1,7},{3,1},{5,3},{7,5},{8,14},{10,8},{12,... | collective-permute-start | bytes 19976 | tf_op jit(solution)/shard_map/ppermute | solution.py:458
  10.2 0.0 copy-start.6
  10.2 0.0 copy-start.7
  10.2 0.0 copy-start.8
  10.2 0.0 copy-done.1
  10.2 0.0 copy-done.5
  10.3 0.6 %copy-done.6 = f32[48]{0:T(128)S(1)} copy-done((f32[48]{0:T(128)S(1)}, f32[48]{0:T(128)}, u32[]{:S(2)}) %copy-start.6) | copy-done | bytes 216
  10.9 0.0 copy-done.7
  10.9 0.0 copy-done.8
  10.9 1.6 %shard_map.93 = (f32[1536,128]{1,0:T(8,128)S(1)}, bf16[256,512]{1,0:T(8,128)(2,1)S(1)}, bf16[256,512]{1,0:T(8,128)(2,1)S(1)}, bf16[256,512]{1,0:T(8,128)(2,1)S(1)}, bf16[256,512]{1,0:T(8,128)(2,1)S(1)}) custom-call(f32[1536,128]{1,0:T(8,128)S(1)} %bitcast.50, bf16[192,8,128]{2,1,0:T(8,128)(2,1)S(1)} %bitcast.53, f32[3,8,128]{2,1,0:T(8,128)S(1)} %bitcast.56, ...), custom_call_target="tpu_custom_call" | custom-call | flops 8000000 | bytes 800000 | tf_op jit(solution)/shard_map/pallas_call | solution.py:444
  12.5 0.0 collective-permute-done.4.radlo_ref
  12.5 0.0 collective-permute-done.5.radhi_ref
  12.5 0.9 %collective-permute-done.3.ax_ref = f32[392,128]{1,0:T(8,128)S(1)} collective-permute-done((f32[392,128]{1,0:T(8,128)S(1)}, f32[392,128]{1,0:T(8,128)S(1)}, u32[]{:S(2)}, u32[]{:S(2)}) %collective-permute-start.3) | collective-permute-done | bytes 200736 | tf_op jit(solution)/shard_map/ppermute | solution.py:462
  13.4 2.4 %collective-permute-done.2.above_ref = f32[776,128]{1,0:T(8,128)S(1)} collective-permute-done((f32[776,128]{1,0:T(8,128)S(1)}, f32[776,128]{1,0:T(8,128)S(1)}, u32[]{:S(2)}, u32[]{:S(2)}) %collective-permute-start.2) | collective-permute-done | bytes 397344 | tf_op jit(solution)/shard_map/ppermute | solution.py:458
  15.8 1.5 %shard_map.95 = (f32[1536,128]{1,0:T(8,128)S(1)}, f32[4,8,128]{2,1,0:T(8,128)S(1)}, f32[480,128]{1,0:T(8,128)S(1)}, f32[8,128]{1,0:T(8,128)S(1)}, bf16[256,512]{...) custom-call(s32[1]{0:T(128)} %bitcast.15.where_ref, ...), custom_call_target="tpu_custom_call" | custom-call | flops 4000000 | bytes 400000 | tf_op jit(solution)/shard_map/pallas_call | solution.py:444
  17.4 0.0 collective-permute-start.7
  17.4 7.9 %collective-permute-done.6.below_ref = f32[776,128]{1,0:T(8,128)S(1)} collective-permute-done((f32[776,128]{1,0:T(8,128)S(1)}, f32[776,128]{1,0:T(8,128)S(1)}, u32[]{:S(2)}, u32[]{:S(2)}) %collective-permute-start.6) | collective-permute-done | bytes 397344 | tf_op jit(solution)/shard_map/ppermute | solution.py:458
  25.2 0.0 copy-start.2
  25.3 1.0 %shard_map.96 = (f32[1536,128]{1,0:T(8,128)S(1)}, f32[488,128]{1,0:T(8,128)S(1)}, f32[384,128]{1,0:T(8,128)S(1)}, f32[1,1536]{1,0:T(1,128)S(1)}, f32[1,1536]{1,0:T(1,128)S(1)}, /*index=5*/f32[8,128]{1,0:T(8,128)S(1)}) custom-call(s32[1]{0:T(128)} %bitcast.15.where_ref, s32[1]{0:T(128)} %bitcast.16.rad_ref, f32[1536,128]{1,0:T(8,128)S(1)} %get-tuple-element.61.part_ref, ...), custom_call_target="tpu_custom_call" | custom-call | flops 10000 | bytes 1000 | tf_op jit(solution)/shard_map/pallas_call | solution.py:444
  26.2 2.4 %collective-permute-start.10 = (f32[488,128]{1,0:T(8,128)S(1)}, f32[488,128]{1,0:T(8,128)S(1)}, u32[]{:S(2)}, u32[]{:S(2)}) collective-permute-start(f32[488,128]{1,0:T(8,128)S(1)} %get-tuple-element.74), channel_id=1, source_target_pairs={{0,24},{8,0},{16,8},{24,16},{1,25},{9,1},{17,9},{25,17},{2,26},{10... | collective-permute-start | bytes 749576 | tf_op jit(solution)/shard_map/ppermute | solution.py:458
  28.7 1.5 %collective-permute-start.11 = (f32[384,128]{1,0:T(8,128)S(1)}, f32[384,128]{1,0:T(8,128)S(1)}, u32[]{:S(2)}, u32[]{:S(2)}) collective-permute-start(f32[384,128]{1,0:T(8,128)S(1)} %get-tuple-element.75), channel_id=1, source_target_pairs={{0,1},{1,0},{2,3},{3,2},{4,5},{5,4},{6,7},{7,6},{8,9},{9,8},{10,11... | collective-permute-start | bytes 589832 | tf_op jit(solution)/shard_map/ppermute | solution.py:462
  30.2 0.0 collective-permute-start.8
  30.2 1.7 %collective-permute-start.9 = (f32[1,1536]{1,0:T(1,128)S(1)}, f32[1,1536]{1,0:T(1,128)S(1)}, u32[]{:S(2)}, u32[]{:S(2)}) collective-permute-start(f32[1,1536]{1,0:T(1,128)S(1)} %get-tuple-element.73), channel_id=1, source_target_pairs={{0,6},{2,0},{4,2},{6,4},{1,7},{3,1},{5,3},{7,5},{8,14},{10,8},{12,... | collective-permute-start | bytes 18440 | tf_op jit(solution)/shard_map/ppermute | solution.py:458
  32.0 0.0 collective-permute-done.7.below_ref
  32.0 0.0 copy-done.2
  32.0 1.6 %shard_map.97 = (f32[1536,128]{1,0:T(8,128)S(1)}, f32[1536,128]{1,0:T(8,128)S(1)}) custom-call(f32[1536,128]{1,0:T(8,128)S(1)} %get-tuple-element.67.m_ref, f32[1536,128]{1,0:T(8,128)S(1)} %bitcast.52, bf16[192,8,128]{2,1,0:T(8,128)(2,1)S(1)} %bitcast.54, f32[480,128]{1,0:T(8,128)S(1)} %collective-permute-done.7.below_ref, ...), custom_call_target="tpu_custom_call" | custom-call | flops 300000000 | bytes 30000000 | tf_op jit(solution)/shard_map/pallas_call | solution.py:444
  33.6 0.0 collective-permute-done.8.radlo_ref
  33.6 0.0 collective-permute-done.9.radhi_ref
  33.6 0.3 shard_map.98.full_ref
  33.9 0.4 %collective-permute-done.11.ax_ref = f32[384,128]{1,0:T(8,128)S(1)} collective-permute-done((f32[384,128]{1,0:T(8,128)S(1)}, f32[384,128]{1,0:T(8,128)S(1)}, u32[]{:S(2)}, u32[]{:S(2)}) %collective-permute-start.11) | collective-permute-done | bytes 196640 | tf_op jit(solution)/shard_map/ppermute | solution.py:462
  34.3 0.4 %collective-permute-done.10.above_ref = f32[488,128]{1,0:T(8,128)S(1)} collective-permute-done((f32[488,128]{1,0:T(8,128)S(1)}, f32[488,128]{1,0:T(8,128)S(1)}, u32[]{:S(2)}, u32[]{:S(2)}) %collective-permute-start.10) | collective-permute-done | bytes 249888 | tf_op jit(solution)/shard_map/ppermute | solution.py:458
  34.7 2.0 %shard_map.99 = (f32[1536,128]{1,0:T(8,128)}, s32[1]{0:T(128)}) custom-call(s32[1]{0:T(128)} %bitcast.15.where_ref, f32[1536,128]{1,0:T(8,128)S(1)} %shard_map.98.full_ref, f32[488,128]{1,0:T(8,128)S(1)} %collective-permute-done.10.above_ref, f32[384,128]{1,0:T(8,128)S(1)} %collective-permute-done.11.ax_ref, f32[4,8,128]{2,1,0:T(8,128)S(1)} %get-tuple-element.63.edge_ref, ...), custom_call_target="tpu_custom_call" | custom-call | flops 1000000 | bytes 100000 | tf_op jit(solution)/shard_map/pallas_call | solution.py:444
  (1 shorter events, 0.0 us)
Async XLA Ops:
  0.0 6.2 %copy-start = (f32[4,48,2,4,128]{4,3,2,1,0:T(4,128)S(1)}, f32[4,48,2,4,128]{4,3,2,1,0:T(4,128)}, u32[]{:S(2)}) copy-start(f32[4,48,2,4,128]{4,3,2,1,0:T(4,128)} %param.11) | copy-start | bytes 2359300
  0.0 6.2 %copy-start.4 = (s32[3,2,4,128]{3,2,1,0:T(4,128)S(1)}, s32[3,2,4,128]{3,2,1,0:T(4,128)}, u32[]{:S(2)}) copy-start(s32[3,2,4,128]{3,2,1,0:T(4,128)} %param.15) | copy-start | bytes 36868
  1.1 5.1 %copy-start.3 = (f32[3,2,4,128]{3,2,1,0:T(4,128)S(1)}, f32[3,2,4,128]{3,2,1,0:T(4,128)}, u32[]{:S(2)}) copy-start(f32[3,2,4,128]{3,2,1,0:T(4,128)} %param.14) | copy-start | bytes 36868
  1.1 14.7 %collective-permute-start.2 = (f32[776,128]{1,0:T(8,128)S(1)}, f32[776,128]{1,0:T(8,128)S(1)}, u32[]{:S(2)}, u32[]{:S(2)}) collective-permute-start(f32[776,128]{1,0:T(8,128)S(1)} %bitcast.70), channel_id=1, source_target_pairs={{0,24},{8,0},{16,8},{24,16},{1,25},{9,1},{17,9},{25,17},{2,26},{10... | collective-permute-start | bytes 1191944 | tf_op jit(solution)/shard_map/ppermute | solution.py:458
  6.2 4.0 %copy-start.1 = (bf16[4,48,2,4,128]{4,3,2,1,0:T(4,128)(2,1)S(1)}, bf16[4,48,2,4,128]{4,3,2,1,0:T(4,128)(2,1)}, u32[]{:S(2)}) copy-start(bf16[4,48,2,4,128]{4,3,2,1,0:T(4,128)(2,1)} %param.13) | copy-start | bytes 1179652
  6.8 18.4 %collective-permute-start.6 = (f32[776,128]{1,0:T(8,128)S(1)}, f32[776,128]{1,0:T(8,128)S(1)}, u32[]{:S(2)}, u32[]{:S(2)}) collective-permute-start(f32[776,128]{1,0:T(8,128)S(1)} %get-tuple-element.62), channel_id=1, source_target_pairs={{0,8},{8,16},{16,24},{24,0},{1,9},{9,17},{17,25},{25,1},{2,10},{10... | collective-permute-start | bytes 1191944 | tf_op jit(solution)/shard_map/ppermute | solution.py:458
  6.9 3.4 %copy-start.5 = (s32[2,4,128]{2,1,0:T(4,128)S(1)}, s32[2,4,128]{2,1,0:T(4,128)}, u32[]{:S(2)}) copy-start(s32[2,4,128]{2,1,0:T(4,128)} %param.16) | copy-start | bytes 12292
  6.9 6.5 %collective-permute-start.3 = (f32[392,128]{1,0:T(8,128)S(1)}, f32[392,128]{1,0:T(8,128)S(1)}, u32[]{:S(2)}, u32[]{:S(2)}) collective-permute-start(f32[392,128]{1,0:T(8,128)S(1)} %get-tuple-element.58), channel_id=1, source_target_pairs={{0,1},{1,0},{2,3},{3,2},{4,5},{5,4},{6,7},{7,6},{8,9},{9,8},{10,11... | collective-permute-start | bytes 602120 | tf_op jit(solution)/shard_map/ppermute | solution.py:462
  8.5 4.0 %collective-permute-start.4 = (f32[1,1664]{1,0:T(1,128)S(1)}, f32[1,1664]{1,0:T(1,128)S(1)}, u32[]{:S(2)}, u32[]{:S(2)}) collective-permute-start(f32[1,1664]{1,0:T(1,128)S(1)} %get-tuple-element.59), channel_id=1, source_target_pairs={{0,2},{2,4},{4,6},{6,0},{1,3},{3,5},{5,7},{7,1},{8,10},{10,12},{12... | collective-permute-start | bytes 19976 | tf_op jit(solution)/shard_map/ppermute | solution.py:458
  8.5 4.1 %collective-permute-start.5 = (f32[1,1664]{1,0:T(1,128)S(1)}, f32[1,1664]{1,0:T(1,128)S(1)}, u32[]{:S(2)}, u32[]{:S(2)}) collective-permute-start(f32[1,1664]{1,0:T(1,128)S(1)} %get-tuple-element.60), channel_id=1, source_target_pairs={{0,6},{2,0},{4,2},{6,4},{1,7},{3,1},{5,3},{7,5},{8,14},{10,8},{12,... | collective-permute-start | bytes 19976 | tf_op jit(solution)/shard_map/ppermute | solution.py:458
  10.2 0.7 %copy-start.6 = (f32[48]{0:T(128)S(1)}, f32[48]{0:T(128)}, u32[]{:S(2)}) copy-start(f32[48]{0:T(128)} %growth_ref.3) | copy-start | bytes 580
  10.2 0.7 %copy-start.7 = (f32[48]{0:T(128)S(1)}, f32[48]{0:T(128)}, u32[]{:S(2)}) copy-start(f32[48]{0:T(128)} %transfer_ref.3) | copy-start | bytes 580
  10.2 0.7 %copy-start.8 = (f32[4]{0:T(128)S(1)}, f32[4]{0:T(128)}, u32[]{:S(2)}) copy-start(f32[4]{0:T(128)} %rate_ref.3) | copy-start | bytes 52
  17.4 14.6 %collective-permute-start.7 = (f32[480,128]{1,0:T(8,128)S(1)}, f32[480,128]{1,0:T(8,128)S(1)}, u32[]{:S(2)}, u32[]{:S(2)}) collective-permute-start(f32[480,128]{1,0:T(8,128)S(1)} %get-tuple-element.68), channel_id=1, source_target_pairs={{0,8},{8,16},{16,24},{24,0},{1,9},{9,17},{17,25},{25,1},{2,10},{10... | collective-permute-start | bytes 737288 | tf_op jit(solution)/shard_map/ppermute | solution.py:458
  25.2 6.7 %copy-start.2 = (bf16[4,48,2,4,128]{4,3,2,1,0:T(4,128)(2,1)S(1)}, bf16[4,48,2,4,128]{4,3,2,1,0:T(4,128)(2,1)}, u32[]{:S(2)}) copy-start(bf16[4,48,2,4,128]{4,3,2,1,0:T(4,128)(2,1)} %param.12) | copy-start | bytes 1179652
  26.2 8.5 %collective-permute-start.10 = (f32[488,128]{1,0:T(8,128)S(1)}, f32[488,128]{1,0:T(8,128)S(1)}, u32[]{:S(2)}, u32[]{:S(2)}) collective-permute-start(f32[488,128]{1,0:T(8,128)S(1)} %get-tuple-element.74), channel_id=1, source_target_pairs={{0,24},{8,0},{16,8},{24,16},{1,25},{9,1},{17,9},{25,17},{2,26},{10... | collective-permute-start | bytes 749576 | tf_op jit(solution)/shard_map/ppermute | solution.py:458
  28.7 5.7 %collective-permute-start.11 = (f32[384,128]{1,0:T(8,128)S(1)}, f32[384,128]{1,0:T(8,128)S(1)}, u32[]{:S(2)}, u32[]{:S(2)}) collective-permute-start(f32[384,128]{1,0:T(8,128)S(1)} %get-tuple-element.75), channel_id=1, source_target_pairs={{0,1},{1,0},{2,3},{3,2},{4,5},{5,4},{6,7},{7,6},{8,9},{9,8},{10,11... | collective-permute-start | bytes 589832 | tf_op jit(solution)/shard_map/ppermute | solution.py:462
  30.2 3.4 %collective-permute-start.8 = (f32[1,1536]{1,0:T(1,128)S(1)}, f32[1,1536]{1,0:T(1,128)S(1)}, u32[]{:S(2)}, u32[]{:S(2)}) collective-permute-start(f32[1,1536]{1,0:T(1,128)S(1)} %get-tuple-element.72), channel_id=1, source_target_pairs={{0,2},{2,4},{4,6},{6,0},{1,3},{3,5},{5,7},{7,1},{8,10},{10,12},{12... | collective-permute-start | bytes 18440 | tf_op jit(solution)/shard_map/ppermute | solution.py:458
  30.2 3.4 %collective-permute-start.9 = (f32[1,1536]{1,0:T(1,128)S(1)}, f32[1,1536]{1,0:T(1,128)S(1)}, u32[]{:S(2)}, u32[]{:S(2)}) collective-permute-start(f32[1,1536]{1,0:T(1,128)S(1)} %get-tuple-element.73), channel_id=1, source_target_pairs={{0,6},{2,0},{4,2},{6,4},{1,7},{3,1},{5,3},{7,5},{8,14},{10,8},{12,... | collective-permute-start | bytes 18440 | tf_op jit(solution)/shard_map/ppermute | solution.py:458

commit v17 on v16

--- a/solution.py
+++ b/solution.py
@@ -144,10 +144,9 @@
     return jnp.concatenate(found, axis=0)
 
 
-def add_azimuthal(comps, halo, coefficient, first_row, out_ref):
+def spread(comps, halo, first_row, out_ref):
     for z in range(4):
-        spots = pl.ds(first_row + z, comps, stride=8)
-        out_ref[spots] = out_ref[spots] + coefficient[first_row + z : first_row + z + 1] * halo[:, 128 * z : 128 * z + 128]
+        out_ref[pl.ds(first_row + z, comps, stride=8)] = halo[:, 128 * z : 128 * z + 128]
 
 
 def pack_sides(comps, last, x_ref, where_ref, rad_ref, ax_ref, radup_ref, raddn_ref):
@@ -282,6 +281,7 @@
     rate_ref,
     out_ref,
     bottom_ref,
+    halo_ref,
 ):
     local = Local(*faces(speeds_ref, flags_ref))
     local.centre = local.centre + (edge_ref[3] - 1.0)
@@ -290,8 +290,11 @@
         out_ref[8 * c : 8 * c + 8] = 0.5 * a_ref[8 * c : 8 * c + 8] + (local(x) + term)
 
     source(sections, m_ref, u_ref, growth_ref, transfer_ref, zones_ref, rate_ref, finish)
-    bottom_ref[...] = out_ref[...]
-    add_azimuthal(4 * sections, decode(4 * sections, below_ref, low_ref, high_ref), edge_ref[0], 0, bottom_ref)
+    spread(4 * sections, decode(4 * sections, below_ref, low_ref, high_ref), 0, halo_ref)
+    azim, bottom = edge_ref[0], rows_of() < 4
+    for c in range(4 * sections):
+        spots = slice(8 * c, 8 * c + 8)
+        bottom_ref[spots] = out_ref[spots] + jnp.where(bottom, azim * halo_ref[spots], 0.0)
 
 
 def from_below(c, below_ref):
@@ -410,21 +413,29 @@
     high_ref,
     out_ref,
     again_ref,
+    halo_ref,
+    side_ref,
     done_ref,
     sems,
 ):
     again_ref[0] = (jnp.max(bad_ref[...] + above_ref[5 * comps // 2 :]) > 0.0).astype(jnp.int32)
-    halo = decode(comps, above_ref, low_ref, high_ref)
-    azim = edge_ref[0]
-    done_ref[...] = full_ref[...]
-    add_axial(comps, 1.0, where_ref, edge_ref[1], ax_ref, done_ref)
+    spread(comps, decode(comps, above_ref, low_ref, high_ref), 4, halo_ref)
+    several = jnp.concatenate([edge_ref[1]] * (2 * comps // 8), axis=0)
+    for start, index in ((3, 0), (0, 1)):
+
+        @pl.when(where_ref[0] == index)
+        def _():
+            side_ref[pl.ds(start, 2 * comps, stride=4)] = several * ax_ref[0 : 2 * comps]
+
+    row = rows_of()
+    azim, top, side = edge_ref[0], row >= 4, row % 4 == jnp.where(where_ref[0] == 0, 3, 0)
     size = comps // parts
     made = []
     for i in range(parts):
-        for z in range(4):
-            some = pl.ds(8 * size * i + 4 + z, size, stride=8)
-            done_ref[some] = (
-                done_ref[some] + azim[4 + z : 5 + z] * halo[size * i : size * i + size, 128 * z : 128 * z + 128]
+        for c in range(size * i, size * i + size):
+            spots = slice(8 * c, 8 * c + 8)
+            done_ref[spots] = (
+                full_ref[spots] + jnp.where(top, azim * halo_ref[spots], 0.0) + jnp.where(side, side_ref[spots], 0.0)
             )
         spots = pl.ds(8 * size * i, 8 * size)
         made.append(pltpu.make_async_copy(done_ref.at[spots], out_ref.at[spots], sems.at[i]))
@@ -556,6 +567,7 @@
         speeds2,
         flags2,
         *rates,
+        scratch=[pltpu.VMEM((cells, 128), f32)],
     )
     (full,) = call(
         functools.partial(second_radial, comps),
@@ -581,7 +593,7 @@
         edge,
         bad,
         *upper_tables[:2],
-        scratch=[pltpu.VMEM((cells, 128), f32), pltpu.SemaphoreType.DMA((4,))],
+        scratch=[pltpu.VMEM((cells, 128), f32)] * 3 + [pltpu.SemaphoreType.DMA((4,))],
     )
 
     def whole():

time: 37.6 us -> 37.6 us (level)
  no operation moved by 1% of the time
where the time goes in v17:
time: 37.6 us; the launch traced here: 37.4 us
  starting transfers between devices  14.2 us (38%)
  waiting for transfers between devices  12 us (32%)
  Pallas kernels  8.59 us (23%)
  other arithmetic  1.1 us (3%)
  between operations  0.8 us (2%)
  local copies, waits for them, and re-layouts  0.7 us (2%)
    ppermute x8, starting transfers between devices, shift(): return lax.ppermute(x, axis, pairs)  11.1 us
    ppermute x8, waiting for transfers between devices, shift(): return lax.ppermute(x, axis, pairs)  10.7 us
    pallas_call x7, Pallas kernels, call(): pl.pallas_call(body, in_specs=[SPACES[s] for s in ins], out_specs=[SPACES...  8.59 us
    ppermute x2, starting transfers between devices, sides(): ax = lax.ppermute(ax, 'axial', [(0, 1), (1, 0)])  3.13 us
    ppermute x2, waiting for transfers between devices, sides(): ax = lax.ppermute(ax, 'axial', [(0, 1), (1, 0)])  1.26 us
    add x1, other arithmetic, shards(): dn = dn + lax.pad(speeds, 0.0, after) * lax.pad(flags, 0, after).astype(f32)  1.1 us
  transfers between devices with their start and end apart: 10, of which 5 were waited for; matrix products, arithmetic and copies ran while one was open for 0% of the time, Pallas kernels for 18%

profile of v17, /device:TPU:0, one launch (start us, length us, event | category | flops | bytes accessed | tf_op | source)
XLA Modules:
  0.0 37.4 jit_solution(17919313045190050422)
XLA Ops:
  0.0 0.0 copy-start
  0.0 0.0 copy-start.4
  0.0 1.1 %fusion.4 = f32[194,1,4,128]{3,2,1,0:T(4,128)S(1)} fusion(f32[192,2,4,128]{3,2,1,0:T(4,128)} %bitcast.48, f32[3,2,4,128]{3,2,1,0:T(4,128)} %param.14, s32[3,2,4,128]{3,2,1,0:T(4,128)} %param.15), kind=kLoop, calls=%fused_computation.19 | loop fusion | flops 297984 | bytes 1208320 | tf_op jit(solution)/shard_map/add | solution.py:498
  1.1 0.0 copy-start.3
  1.1 5.1 %collective-permute-start.2 = (f32[776,128]{1,0:T(8,128)S(1)}, f32[776,128]{1,0:T(8,128)S(1)}, u32[]{:S(2)}, u32[]{:S(2)}) collective-permute-start(f32[776,128]{1,0:T(8,128)S(1)} %bitcast.70), channel_id=1, source_target_pairs={{0,24},{8,0},{16,8},{24,16},{1,25},{9,1},{17,9},{25,17},{2,26},{10... | collective-permute-start | bytes 1191944 | tf_op jit(solution)/shard_map/ppermute | solution.py:469
  6.2 0.0 copy-done
  6.2 0.0 copy-done.4
  6.2 0.0 copy-done.3
  6.2 0.0 copy-start.1
  6.2 0.6 %shard_map.94 = (f32[776,128]{1,0:T(8,128)S(1)}, f32[392,128]{1,0:T(8,128)S(1)}, f32[1,1664]{1,0:T(1,128)S(1)}, f32[1,1664]{1,0:T(1,128)S(1)}) custom-call(s32[1]{0:T(128)} %bitcast.15.where_ref, s32[1]{0:T(128)} %bitcast.16.rad_ref, f32[1536,128]{1,0:T(8,128)S(1)} %bitcast.49, f32[3,8,128]{2,1,0:T(8,128)S(1)} %bitcast.55, s32[3,8,128]{2,1,0:T(8,128)S(1)} %bitcast.59), custom_call_target="tpu_custom_call" | custom-call | flops 2000000 | bytes 200000 | tf_op jit(solution)/shard_map/pallas_call | solution.py:455
  6.8 0.1 collective-permute-start.6
  6.9 0.0 copy-start.5
  6.9 1.6 %collective-permute-start.3 = (f32[392,128]{1,0:T(8,128)S(1)}, f32[392,128]{1,0:T(8,128)S(1)}, u32[]{:S(2)}, u32[]{:S(2)}) collective-permute-start(f32[392,128]{1,0:T(8,128)S(1)} %get-tuple-element.58), channel_id=1, source_target_pairs={{0,1},{1,0},{2,3},{3,2},{4,5},{5,4},{6,7},{7,6},{8,9},{9,8},{10,11... | collective-permute-start | bytes 602120 | tf_op jit(solution)/shard_map/ppermute | solution.py:473
  8.5 0.0 collective-permute-start.4
  8.5 1.7 %collective-permute-start.5 = (f32[1,1664]{1,0:T(1,128)S(1)}, f32[1,1664]{1,0:T(1,128)S(1)}, u32[]{:S(2)}, u32[]{:S(2)}) collective-permute-start(f32[1,1664]{1,0:T(1,128)S(1)} %get-tuple-element.60), channel_id=1, source_target_pairs={{0,6},{2,0},{4,2},{6,4},{1,7},{3,1},{5,3},{7,5},{8,14},{10,8},{12,... | collective-permute-start | bytes 19976 | tf_op jit(solution)/shard_map/ppermute | solution.py:469
  10.2 0.0 copy-start.6
  10.2 0.0 copy-start.7
  10.2 0.0 copy-start.8
  10.2 0.0 copy-done.1
  10.2 0.0 copy-done.5
  10.3 0.6 %copy-done.6 = f32[48]{0:T(128)S(1)} copy-done((f32[48]{0:T(128)S(1)}, f32[48]{0:T(128)}, u32[]{:S(2)}) %copy-start.6) | copy-done | bytes 216
  10.9 0.0 copy-done.7
  10.9 0.0 copy-done.8
  10.9 1.6 %shard_map.93 = (f32[1536,128]{1,0:T(8,128)S(1)}, bf16[256,512]{1,0:T(8,128)(2,1)S(1)}, bf16[256,512]{1,0:T(8,128)(2,1)S(1)}, bf16[256,512]{1,0:T(8,128)(2,1)S(1)}, bf16[256,512]{1,0:T(8,128)(2,1)S(1)}) custom-call(f32[1536,128]{1,0:T(8,128)S(1)} %bitcast.50, bf16[192,8,128]{2,1,0:T(8,128)(2,1)S(1)} %bitcast.53, f32[3,8,128]{2,1,0:T(8,128)S(1)} %bitcast.56, ...), custom_call_target="tpu_custom_call" | custom-call | flops 8000000 | bytes 800000 | tf_op jit(solution)/shard_map/pallas_call | solution.py:455
  12.5 0.0 collective-permute-done.4.radlo_ref
  12.5 0.0 collective-permute-done.5.radhi_ref
  12.5 0.9 %collective-permute-done.3.ax_ref = f32[392,128]{1,0:T(8,128)S(1)} collective-permute-done((f32[392,128]{1,0:T(8,128)S(1)}, f32[392,128]{1,0:T(8,128)S(1)}, u32[]{:S(2)}, u32[]{:S(2)}) %collective-permute-start.3) | collective-permute-done | bytes 200736 | tf_op jit(solution)/shard_map/ppermute | solution.py:473
  13.4 2.4 %collective-permute-done.2.above_ref = f32[776,128]{1,0:T(8,128)S(1)} collective-permute-done((f32[776,128]{1,0:T(8,128)S(1)}, f32[776,128]{1,0:T(8,128)S(1)}, u32[]{:S(2)}, u32[]{:S(2)}) %collective-permute-start.2) | collective-permute-done | bytes 397344 | tf_op jit(solution)/shard_map/ppermute | solution.py:469
  15.8 1.5 %shard_map.95 = (f32[1536,128]{1,0:T(8,128)S(1)}, f32[4,8,128]{2,1,0:T(8,128)S(1)}, f32[480,128]{1,0:T(8,128)S(1)}, f32[8,128]{1,0:T(8,128)S(1)}, bf16[256,512]{...) custom-call(s32[1]{0:T(128)} %bitcast.15.where_ref, ...), custom_call_target="tpu_custom_call" | custom-call | flops 4000000 | bytes 400000 | tf_op jit(solution)/shard_map/pallas_call | solution.py:455
  17.4 0.0 collective-permute-start.7
  17.4 7.9 %collective-permute-done.6.below_ref = f32[776,128]{1,0:T(8,128)S(1)} collective-permute-done((f32[776,128]{1,0:T(8,128)S(1)}, f32[776,128]{1,0:T(8,128)S(1)}, u32[]{:S(2)}, u32[]{:S(2)}) %collective-permute-start.6) | collective-permute-done | bytes 397344 | tf_op jit(solution)/shard_map/ppermute | solution.py:469
  25.2 0.0 copy-start.2
  25.3 1.0 %shard_map.96 = (f32[1536,128]{1,0:T(8,128)S(1)}, f32[488,128]{1,0:T(8,128)S(1)}, f32[384,128]{1,0:T(8,128)S(1)}, f32[1,1536]{1,0:T(1,128)S(1)}, f32[1,1536]{1,0:T(1,128)S(1)}, /*index=5*/f32[8,128]{1,0:T(8,128)S(1)}) custom-call(s32[1]{0:T(128)} %bitcast.15.where_ref, s32[1]{0:T(128)} %bitcast.16.rad_ref, f32[1536,128]{1,0:T(8,128)S(1)} %get-tuple-element.61.part_ref, ...), custom_call_target="tpu_custom_call" | custom-call | flops 10000 | bytes 1000 | tf_op jit(solution)/shard_map/pallas_call | solution.py:455
  26.2 2.4 %collective-permute-start.10 = (f32[488,128]{1,0:T(8,128)S(1)}, f32[488,128]{1,0:T(8,128)S(1)}, u32[]{:S(2)}, u32[]{:S(2)}) collective-permute-start(f32[488,128]{1,0:T(8,128)S(1)} %get-tuple-element.74), channel_id=1, source_target_pairs={{0,24},{8,0},{16,8},{24,16},{1,25},{9,1},{17,9},{25,17},{2,26},{10... | collective-permute-start | bytes 749576 | tf_op jit(solution)/shard_map/ppermute | solution.py:469
  28.7 1.5 %collective-permute-start.11 = (f32[384,128]{1,0:T(8,128)S(1)}, f32[384,128]{1,0:T(8,128)S(1)}, u32[]{:S(2)}, u32[]{:S(2)}) collective-permute-start(f32[384,128]{1,0:T(8,128)S(1)} %get-tuple-element.75), channel_id=1, source_target_pairs={{0,1},{1,0},{2,3},{3,2},{4,5},{5,4},{6,7},{7,6},{8,9},{9,8},{10,11... | collective-permute-start | bytes 589832 | tf_op jit(solution)/shard_map/ppermute | solution.py:473
  30.2 0.0 collective-permute-start.8
  30.2 1.7 %collective-permute-start.9 = (f32[1,1536]{1,0:T(1,128)S(1)}, f32[1,1536]{1,0:T(1,128)S(1)}, u32[]{:S(2)}, u32[]{:S(2)}) collective-permute-start(f32[1,1536]{1,0:T(1,128)S(1)} %get-tuple-element.73), channel_id=1, source_target_pairs={{0,6},{2,0},{4,2},{6,4},{1,7},{3,1},{5,3},{7,5},{8,14},{10,8},{12,... | collective-permute-start | bytes 18440 | tf_op jit(solution)/shard_map/ppermute | solution.py:469
  32.0 0.0 collective-permute-done.7.below_ref
  32.0 0.0 copy-done.2
  32.0 1.6 %shard_map.97 = (f32[1536,128]{1,0:T(8,128)S(1)}, f32[1536,128]{1,0:T(8,128)S(1)}) custom-call(f32[1536,128]{1,0:T(8,128)S(1)} %get-tuple-element.67.m_ref, f32[1536,128]{1,0:T(8,128)S(1)} %bitcast.52, bf16[192,8,128]{2,1,0:T(8,128)(2,1)S(1)} %bitcast.54, f32[480,128]{1,0:T(8,128)S(1)} %collective-permute-done.7.below_ref, ...), custom_call_target="tpu_custom_call" | custom-call | flops 300000000 | bytes 30000000 | tf_op jit(solution)/shard_map/pallas_call | solution.py:455
  33.6 0.0 collective-permute-done.8.radlo_ref
  33.6 0.0 collective-permute-done.9.radhi_ref
  33.6 0.3 shard_map.98.full_ref
  34.0 0.4 %collective-permute-done.11.ax_ref = f32[384,128]{1,0:T(8,128)S(1)} collective-permute-done((f32[384,128]{1,0:T(8,128)S(1)}, f32[384,128]{1,0:T(8,128)S(1)}, u32[]{:S(2)}, u32[]{:S(2)}) %collective-permute-start.11) | collective-permute-done | bytes 196640 | tf_op jit(solution)/shard_map/ppermute | solution.py:473
  34.3 0.4 %collective-permute-done.10.above_ref = f32[488,128]{1,0:T(8,128)S(1)} collective-permute-done((f32[488,128]{1,0:T(8,128)S(1)}, f32[488,128]{1,0:T(8,128)S(1)}, u32[]{:S(2)}, u32[]{:S(2)}) %collective-permute-start.10) | collective-permute-done | bytes 249888 | tf_op jit(solution)/shard_map/ppermute | solution.py:469
  34.7 2.0 %shard_map.99 = (f32[1536,128]{1,0:T(8,128)}, s32[1]{0:T(128)}) custom-call(s32[1]{0:T(128)} %bitcast.15.where_ref, f32[1536,128]{1,0:T(8,128)S(1)} %shard_map.98.full_ref, f32[488,128]{1,0:T(8,128)S(1)} %collective-permute-done.10.above_ref, f32[384,128]{1,0:T(8,128)S(1)} %collective-permute-done.11.ax_ref, f32[4,8,128]{2,1,0:T(8,128)S(1)} %get-tuple-element.63.edge_ref, ...), custom_call_target="tpu_custom_call" | custom-call | flops 1000000 | bytes 100000 | tf_op jit(solution)/shard_map/pallas_call | solution.py:455
  (1 shorter events, 0.0 us)
Async XLA Ops:
  0.0 6.2 %copy-start = (f32[4,48,2,4,128]{4,3,2,1,0:T(4,128)S(1)}, f32[4,48,2,4,128]{4,3,2,1,0:T(4,128)}, u32[]{:S(2)}) copy-start(f32[4,48,2,4,128]{4,3,2,1,0:T(4,128)} %param.11) | copy-start | bytes 2359300
  0.0 6.2 %copy-start.4 = (s32[3,2,4,128]{3,2,1,0:T(4,128)S(1)}, s32[3,2,4,128]{3,2,1,0:T(4,128)}, u32[]{:S(2)}) copy-start(s32[3,2,4,128]{3,2,1,0:T(4,128)} %param.15) | copy-start | bytes 36868
  1.1 5.1 %copy-start.3 = (f32[3,2,4,128]{3,2,1,0:T(4,128)S(1)}, f32[3,2,4,128]{3,2,1,0:T(4,128)}, u32[]{:S(2)}) copy-start(f32[3,2,4,128]{3,2,1,0:T(4,128)} %param.14) | copy-start | bytes 36868
  1.1 14.7 %collective-permute-start.2 = (f32[776,128]{1,0:T(8,128)S(1)}, f32[776,128]{1,0:T(8,128)S(1)}, u32[]{:S(2)}, u32[]{:S(2)}) collective-permute-start(f32[776,128]{1,0:T(8,128)S(1)} %bitcast.70), channel_id=1, source_target_pairs={{0,24},{8,0},{16,8},{24,16},{1,25},{9,1},{17,9},{25,17},{2,26},{10... | collective-permute-start | bytes 1191944 | tf_op jit(solution)/shard_map/ppermute | solution.py:469
  6.2 4.0 %copy-start.1 = (bf16[4,48,2,4,128]{4,3,2,1,0:T(4,128)(2,1)S(1)}, bf16[4,48,2,4,128]{4,3,2,1,0:T(4,128)(2,1)}, u32[]{:S(2)}) copy-start(bf16[4,48,2,4,128]{4,3,2,1,0:T(4,128)(2,1)} %param.13) | copy-start | bytes 1179652
  6.8 18.4 %collective-permute-start.6 = (f32[776,128]{1,0:T(8,128)S(1)}, f32[776,128]{1,0:T(8,128)S(1)}, u32[]{:S(2)}, u32[]{:S(2)}) collective-permute-start(f32[776,128]{1,0:T(8,128)S(1)} %get-tuple-element.62), channel_id=1, source_target_pairs={{0,8},{8,16},{16,24},{24,0},{1,9},{9,17},{17,25},{25,1},{2,10},{10... | collective-permute-start | bytes 1191944 | tf_op jit(solution)/shard_map/ppermute | solution.py:469
  6.9 3.4 %copy-start.5 = (s32[2,4,128]{2,1,0:T(4,128)S(1)}, s32[2,4,128]{2,1,0:T(4,128)}, u32[]{:S(2)}) copy-start(s32[2,4,128]{2,1,0:T(4,128)} %param.16) | copy-start | bytes 12292
  6.9 6.5 %collective-permute-start.3 = (f32[392,128]{1,0:T(8,128)S(1)}, f32[392,128]{1,0:T(8,128)S(1)}, u32[]{:S(2)}, u32[]{:S(2)}) collective-permute-start(f32[392,128]{1,0:T(8,128)S(1)} %get-tuple-element.58), channel_id=1, source_target_pairs={{0,1},{1,0},{2,3},{3,2},{4,5},{5,4},{6,7},{7,6},{8,9},{9,8},{10,11... | collective-permute-start | bytes 602120 | tf_op jit(solution)/shard_map/ppermute | solution.py:473
  8.5 4.0 %collective-permute-start.4 = (f32[1,1664]{1,0:T(1,128)S(1)}, f32[1,1664]{1,0:T(1,128)S(1)}, u32[]{:S(2)}, u32[]{:S(2)}) collective-permute-start(f32[1,1664]{1,0:T(1,128)S(1)} %get-tuple-element.59), channel_id=1, source_target_pairs={{0,2},{2,4},{4,6},{6,0},{1,3},{3,5},{5,7},{7,1},{8,10},{10,12},{12... | collective-permute-start | bytes 19976 | tf_op jit(solution)/shard_map/ppermute | solution.py:469
  8.5 4.1 %collective-permute-start.5 = (f32[1,1664]{1,0:T(1,128)S(1)}, f32[1,1664]{1,0:T(1,128)S(1)}, u32[]{:S(2)}, u32[]{:S(2)}) collective-permute-start(f32[1,1664]{1,0:T(1,128)S(1)} %get-tuple-element.60), channel_id=1, source_target_pairs={{0,6},{2,0},{4,2},{6,4},{1,7},{3,1},{5,3},{7,5},{8,14},{10,8},{12,... | collective-permute-start | bytes 19976 | tf_op jit(solution)/shard_map/ppermute | solution.py:469
  10.2 0.7 %copy-start.6 = (f32[48]{0:T(128)S(1)}, f32[48]{0:T(128)}, u32[]{:S(2)}) copy-start(f32[48]{0:T(128)} %growth_ref.3) | copy-start | bytes 580
  10.2 0.7 %copy-start.7 = (f32[48]{0:T(128)S(1)}, f32[48]{0:T(128)}, u32[]{:S(2)}) copy-start(f32[48]{0:T(128)} %transfer_ref.3) | copy-start | bytes 580
  10.2 0.7 %copy-start.8 = (f32[4]{0:T(128)S(1)}, f32[4]{0:T(128)}, u32[]{:S(2)}) copy-start(f32[4]{0:T(128)} %rate_ref.3) | copy-start | bytes 52
  17.4 14.6 %collective-permute-start.7 = (f32[480,128]{1,0:T(8,128)S(1)}, f32[480,128]{1,0:T(8,128)S(1)}, u32[]{:S(2)}, u32[]{:S(2)}) collective-permute-start(f32[480,128]{1,0:T(8,128)S(1)} %get-tuple-element.68), channel_id=1, source_target_pairs={{0,8},{8,16},{16,24},{24,0},{1,9},{9,17},{17,25},{25,1},{2,10},{10... | collective-permute-start | bytes 737288 | tf_op jit(solution)/shard_map/ppermute | solution.py:469
  25.2 6.7 %copy-start.2 = (bf16[4,48,2,4,128]{4,3,2,1,0:T(4,128)(2,1)S(1)}, bf16[4,48,2,4,128]{4,3,2,1,0:T(4,128)(2,1)}, u32[]{:S(2)}) copy-start(bf16[4,48,2,4,128]{4,3,2,1,0:T(4,128)(2,1)} %param.12) | copy-start | bytes 1179652
  26.2 8.5 %collective-permute-start.10 = (f32[488,128]{1,0:T(8,128)S(1)}, f32[488,128]{1,0:T(8,128)S(1)}, u32[]{:S(2)}, u32[]{:S(2)}) collective-permute-start(f32[488,128]{1,0:T(8,128)S(1)} %get-tuple-element.74), channel_id=1, source_target_pairs={{0,24},{8,0},{16,8},{24,16},{1,25},{9,1},{17,9},{25,17},{2,26},{10... | collective-permute-start | bytes 749576 | tf_op jit(solution)/shard_map/ppermute | solution.py:469
  28.7 5.7 %collective-permute-start.11 = (f32[384,128]{1,0:T(8,128)S(1)}, f32[384,128]{1,0:T(8,128)S(1)}, u32[]{:S(2)}, u32[]{:S(2)}) collective-permute-start(f32[384,128]{1,0:T(8,128)S(1)} %get-tuple-element.75), channel_id=1, source_target_pairs={{0,1},{1,0},{2,3},{3,2},{4,5},{5,4},{6,7},{7,6},{8,9},{9,8},{10,11... | collective-permute-start | bytes 589832 | tf_op jit(solution)/shard_map/ppermute | solution.py:473
  30.2 3.4 %collective-permute-start.8 = (f32[1,1536]{1,0:T(1,128)S(1)}, f32[1,1536]{1,0:T(1,128)S(1)}, u32[]{:S(2)}, u32[]{:S(2)}) collective-permute-start(f32[1,1536]{1,0:T(1,128)S(1)} %get-tuple-element.72), channel_id=1, source_target_pairs={{0,2},{2,4},{4,6},{6,0},{1,3},{3,5},{5,7},{7,1},{8,10},{10,12},{12... | collective-permute-start | bytes 18440 | tf_op jit(solution)/shard_map/ppermute | solution.py:469
  30.2 3.4 %collective-permute-start.9 = (f32[1,1536]{1,0:T(1,128)S(1)}, f32[1,1536]{1,0:T(1,128)S(1)}, u32[]{:S(2)}, u32[]{:S(2)}) collective-permute-start(f32[1,1536]{1,0:T(1,128)S(1)} %get-tuple-element.73), channel_id=1, source_target_pairs={{0,6},{2,0},{4,2},{6,4},{1,7},{3,1},{5,3},{7,5},{8,14},{10,8},{12,... | collective-permute-start | bytes 18440 | tf_op jit(solution)/shard_map/ppermute | solution.py:469

commit v18 on v16

--- a/solution.py
+++ b/solution.py
@@ -413,7 +413,7 @@
     done_ref,
     sems,
 ):
-    again_ref[0] = (jnp.max(bad_ref[...] + above_ref[5 * comps // 2 :]) > 0.0).astype(jnp.int32)
+    again_ref[...] = jnp.minimum(bad_ref[...] + above_ref[5 * comps // 2 :], 1.0).astype(jnp.int32)
     halo = decode(comps, above_ref, low_ref, high_ref)
     azim = edge_ref[0]
     done_ref[...] = full_ref[...]
@@ -571,8 +571,8 @@
     out, again = call(
         functools.partial(second_rest, comps, 4),
         "s" + "v" * 7,
-        "hs",
-        [pltpu.HBM((cells, 128), f32), jax.ShapeDtypeStruct((1,), jnp.int32)],
+        "hv",
+        [pltpu.HBM((cells, 128), f32), jax.ShapeDtypeStruct((8, 128), jnp.int32)],
         1_000_000,
         where,
         full,
@@ -595,7 +595,7 @@
         radial = edge[2] * jnp.where(lane == 0, lower, jnp.where(lane == 127, upper, 0.0))
         return part + (azimuthal + axial + radial).reshape(cells, 128)
 
-    again = again[0]
+    again = again[0, 0]
     if lax.axis_size("azim") != 4:
         again = lax.pmax(again.astype(f32), "azim").astype(jnp.int32)
     return lax.switch(again, (lambda: out, whole)).reshape(shape)

time: 37.6 us -> 37.5 us (level)
  Pallas kernels: 8.59 us -> 8.06 us
  local copies, waits for them, and re-layouts: 0.7 us -> 1.21 us
    pallas_call x7, Pallas kernels: 8.59 us -> 8.06 us  [call(): pl.pallas_call(body, in_specs=[SPACES[s] for s in ins], out_specs=[SPACES...]
    slice x0 -> x1, local copies, waits for them, and re-layouts: none -> 0.51 us  [shards(): again = again[0, 0]]
where the time goes in v18:
time: 37.5 us; the launch traced here: 37.3 us
  starting transfers between devices  14.2 us (38%)
  waiting for transfers between devices  12 us (32%)
  Pallas kernels  8.06 us (21%)
  local copies, waits for them, and re-layouts  1.21 us (3%)
  other arithmetic  1.1 us (3%)
  between operations  0.71 us (2%)
    ppermute x8, starting transfers between devices, shift(): return lax.ppermute(x, axis, pairs)  11.1 us
    ppermute x8, waiting for transfers between devices, shift(): return lax.ppermute(x, axis, pairs)  10.7 us
    pallas_call x7, Pallas kernels, call(): pl.pallas_call(body, in_specs=[SPACES[s] for s in ins], out_specs=[SPACES...  8.06 us
    ppermute x2, starting transfers between devices, sides(): ax = lax.ppermute(ax, 'axial', [(0, 1), (1, 0)])  3.13 us
    ppermute x2, waiting for transfers between devices, sides(): ax = lax.ppermute(ax, 'axial', [(0, 1), (1, 0)])  1.26 us
    add x1, other arithmetic, shards(): dn = dn + lax.pad(speeds, 0.0, after) * lax.pad(flags, 0, after).astype(f32)  1.1 us
  transfers between devices with their start and end apart: 10, of which 5 were waited for; matrix products, arithmetic and copies ran while one was open for 0% of the time, Pallas kernels for 18%

profile of v18, /device:TPU:0, one launch (start us, length us, event | category | flops | bytes accessed | tf_op | source)
XLA Modules:
  0.0 37.3 jit_solution(9775026847192261766)
XLA Ops:
  0.0 0.0 copy-start
  0.0 0.0 copy-start.4
  0.0 1.1 %fusion.4 = f32[194,1,4,128]{3,2,1,0:T(4,128)S(1)} fusion(f32[192,2,4,128]{3,2,1,0:T(4,128)} %bitcast.48, f32[3,2,4,128]{3,2,1,0:T(4,128)} %param.14, s32[3,2,4,128]{3,2,1,0:T(4,128)} %param.15), kind=kLoop, calls=%fused_computation.19 | loop fusion | flops 297984 | bytes 1208320 | tf_op jit(solution)/shard_map/add | solution.py:487
  1.1 0.0 copy-start.3
  1.1 5.1 %collective-permute-start.2 = (f32[776,128]{1,0:T(8,128)S(1)}, f32[776,128]{1,0:T(8,128)S(1)}, u32[]{:S(2)}, u32[]{:S(2)}) collective-permute-start(f32[776,128]{1,0:T(8,128)S(1)} %bitcast.70), channel_id=1, source_target_pairs={{0,24},{8,0},{16,8},{24,16},{1,25},{9,1},{17,9},{25,17},{2,26},{10... | collective-permute-start | bytes 1191944 | tf_op jit(solution)/shard_map/ppermute | solution.py:458
  6.2 0.0 copy-done
  6.2 0.0 copy-done.4
  6.2 0.0 copy-done.3
  6.2 0.0 copy-start.1
  6.2 0.6 %shard_map.94 = (f32[776,128]{1,0:T(8,128)S(1)}, f32[392,128]{1,0:T(8,128)S(1)}, f32[1,1664]{1,0:T(1,128)S(1)}, f32[1,1664]{1,0:T(1,128)S(1)}) custom-call(s32[1]{0:T(128)} %bitcast.15.where_ref, s32[1]{0:T(128)} %bitcast.16.rad_ref, f32[1536,128]{1,0:T(8,128)S(1)} %bitcast.49, f32[3,8,128]{2,1,0:T(8,128)S(1)} %bitcast.55, s32[3,8,128]{2,1,0:T(8,128)S(1)} %bitcast.59), custom_call_target="tpu_custom_call" | custom-call | flops 2000000 | bytes 200000 | tf_op jit(solution)/shard_map/pallas_call | solution.py:444
  6.8 0.1 collective-permute-start.6
  6.9 0.0 copy-start.5
  6.9 1.6 %collective-permute-start.3 = (f32[392,128]{1,0:T(8,128)S(1)}, f32[392,128]{1,0:T(8,128)S(1)}, u32[]{:S(2)}, u32[]{:S(2)}) collective-permute-start(f32[392,128]{1,0:T(8,128)S(1)} %get-tuple-element.58), channel_id=1, source_target_pairs={{0,1},{1,0},{2,3},{3,2},{4,5},{5,4},{6,7},{7,6},{8,9},{9,8},{10,11... | collective-permute-start | bytes 602120 | tf_op jit(solution)/shard_map/ppermute | solution.py:462
  8.5 0.0 collective-permute-start.4
  8.5 1.7 %collective-permute-start.5 = (f32[1,1664]{1,0:T(1,128)S(1)}, f32[1,1664]{1,0:T(1,128)S(1)}, u32[]{:S(2)}, u32[]{:S(2)}) collective-permute-start(f32[1,1664]{1,0:T(1,128)S(1)} %get-tuple-element.60), channel_id=1, source_target_pairs={{0,6},{2,0},{4,2},{6,4},{1,7},{3,1},{5,3},{7,5},{8,14},{10,8},{12,... | collective-permute-start | bytes 19976 | tf_op jit(solution)/shard_map/ppermute | solution.py:458
  10.2 0.0 copy-start.6
  10.2 0.0 copy-start.7
  10.2 0.0 copy-start.8
  10.2 0.0 copy-done.1
  10.2 0.0 copy-done.5
  10.3 0.6 %copy-done.6 = f32[48]{0:T(128)S(1)} copy-done((f32[48]{0:T(128)S(1)}, f32[48]{0:T(128)}, u32[]{:S(2)}) %copy-start.6) | copy-done | bytes 216
  10.9 0.0 copy-done.7
  10.9 0.0 copy-done.8
  10.9 1.6 %shard_map.93 = (f32[1536,128]{1,0:T(8,128)S(1)}, bf16[256,512]{1,0:T(8,128)(2,1)S(1)}, bf16[256,512]{1,0:T(8,128)(2,1)S(1)}, bf16[256,512]{1,0:T(8,128)(2,1)S(1)}, bf16[256,512]{1,0:T(8,128)(2,1)S(1)}) custom-call(f32[1536,128]{1,0:T(8,128)S(1)} %bitcast.50, bf16[192,8,128]{2,1,0:T(8,128)(2,1)S(1)} %bitcast.53, f32[3,8,128]{2,1,0:T(8,128)S(1)} %bitcast.56, ...), custom_call_target="tpu_custom_call" | custom-call | flops 8000000 | bytes 800000 | tf_op jit(solution)/shard_map/pallas_call | solution.py:444
  12.5 0.0 collective-permute-done.4.radlo_ref
  12.5 0.0 collective-permute-done.5.radhi_ref
  12.5 0.9 %collective-permute-done.3.ax_ref = f32[392,128]{1,0:T(8,128)S(1)} collective-permute-done((f32[392,128]{1,0:T(8,128)S(1)}, f32[392,128]{1,0:T(8,128)S(1)}, u32[]{:S(2)}, u32[]{:S(2)}) %collective-permute-start.3) | collective-permute-done | bytes 200736 | tf_op jit(solution)/shard_map/ppermute | solution.py:462
  13.4 2.4 %collective-permute-done.2.above_ref = f32[776,128]{1,0:T(8,128)S(1)} collective-permute-done((f32[776,128]{1,0:T(8,128)S(1)}, f32[776,128]{1,0:T(8,128)S(1)}, u32[]{:S(2)}, u32[]{:S(2)}) %collective-permute-start.2) | collective-permute-done | bytes 397344 | tf_op jit(solution)/shard_map/ppermute | solution.py:458
  15.8 1.5 %shard_map.95 = (f32[1536,128]{1,0:T(8,128)S(1)}, f32[4,8,128]{2,1,0:T(8,128)S(1)}, f32[480,128]{1,0:T(8,128)S(1)}, f32[8,128]{1,0:T(8,128)S(1)}, bf16[256,512]{...) custom-call(s32[1]{0:T(128)} %bitcast.15.where_ref, ...), custom_call_target="tpu_custom_call" | custom-call | flops 4000000 | bytes 400000 | tf_op jit(solution)/shard_map/pallas_call | solution.py:444
  17.4 0.0 collective-permute-start.7
  17.4 7.9 %collective-permute-done.6.below_ref = f32[776,128]{1,0:T(8,128)S(1)} collective-permute-done((f32[776,128]{1,0:T(8,128)S(1)}, f32[776,128]{1,0:T(8,128)S(1)}, u32[]{:S(2)}, u32[]{:S(2)}) %collective-permute-start.6) | collective-permute-done | bytes 397344 | tf_op jit(solution)/shard_map/ppermute | solution.py:458
  25.2 0.0 copy-start.2
  25.3 1.0 %shard_map.96 = (f32[1536,128]{1,0:T(8,128)S(1)}, f32[488,128]{1,0:T(8,128)S(1)}, f32[384,128]{1,0:T(8,128)S(1)}, f32[1,1536]{1,0:T(1,128)S(1)}, f32[1,1536]{1,0:T(1,128)S(1)}, /*index=5*/f32[8,128]{1,0:T(8,128)S(1)}) custom-call(s32[1]{0:T(128)} %bitcast.15.where_ref, s32[1]{0:T(128)} %bitcast.16.rad_ref, f32[1536,128]{1,0:T(8,128)S(1)} %get-tuple-element.61.part_ref, ...), custom_call_target="tpu_custom_call" | custom-call | flops 10000 | bytes 1000 | tf_op jit(solution)/shard_map/pallas_call | solution.py:444
  26.2 2.4 %collective-permute-start.10 = (f32[488,128]{1,0:T(8,128)S(1)}, f32[488,128]{1,0:T(8,128)S(1)}, u32[]{:S(2)}, u32[]{:S(2)}) collective-permute-start(f32[488,128]{1,0:T(8,128)S(1)} %get-tuple-element.74), channel_id=1, source_target_pairs={{0,24},{8,0},{16,8},{24,16},{1,25},{9,1},{17,9},{25,17},{2,26},{10... | collective-permute-start | bytes 749576 | tf_op jit(solution)/shard_map/ppermute | solution.py:458
  28.7 1.5 %collective-permute-start.11 = (f32[384,128]{1,0:T(8,128)S(1)}, f32[384,128]{1,0:T(8,128)S(1)}, u32[]{:S(2)}, u32[]{:S(2)}) collective-permute-start(f32[384,128]{1,0:T(8,128)S(1)} %get-tuple-element.75), channel_id=1, source_target_pairs={{0,1},{1,0},{2,3},{3,2},{4,5},{5,4},{6,7},{7,6},{8,9},{9,8},{10,11... | collective-permute-start | bytes 589832 | tf_op jit(solution)/shard_map/ppermute | solution.py:462
  30.2 0.0 collective-permute-start.8
  30.2 1.7 %collective-permute-start.9 = (f32[1,1536]{1,0:T(1,128)S(1)}, f32[1,1536]{1,0:T(1,128)S(1)}, u32[]{:S(2)}, u32[]{:S(2)}) collective-permute-start(f32[1,1536]{1,0:T(1,128)S(1)} %get-tuple-element.73), channel_id=1, source_target_pairs={{0,6},{2,0},{4,2},{6,4},{1,7},{3,1},{5,3},{7,5},{8,14},{10,8},{12,... | collective-permute-start | bytes 18440 | tf_op jit(solution)/shard_map/ppermute | solution.py:458
  32.0 0.0 collective-permute-done.7.below_ref
  32.0 0.0 copy-done.2
  32.0 1.6 %shard_map.97 = (f32[1536,128]{1,0:T(8,128)S(1)}, f32[1536,128]{1,0:T(8,128)S(1)}) custom-call(f32[1536,128]{1,0:T(8,128)S(1)} %get-tuple-element.67.m_ref, f32[1536,128]{1,0:T(8,128)S(1)} %bitcast.52, bf16[192,8,128]{2,1,0:T(8,128)(2,1)S(1)} %bitcast.54, f32[480,128]{1,0:T(8,128)S(1)} %collective-permute-done.7.below_ref, ...), custom_call_target="tpu_custom_call" | custom-call | flops 300000000 | bytes 30000000 | tf_op jit(solution)/shard_map/pallas_call | solution.py:444
  33.6 0.0 collective-permute-done.8.radlo_ref
  33.6 0.0 collective-permute-done.9.radhi_ref
  33.6 0.3 shard_map.98.full_ref
  33.9 0.4 %collective-permute-done.11.ax_ref = f32[384,128]{1,0:T(8,128)S(1)} collective-permute-done((f32[384,128]{1,0:T(8,128)S(1)}, f32[384,128]{1,0:T(8,128)S(1)}, u32[]{:S(2)}, u32[]{:S(2)}) %collective-permute-start.11) | collective-permute-done | bytes 196640 | tf_op jit(solution)/shard_map/ppermute | solution.py:462
  34.3 0.4 %collective-permute-done.10.above_ref = f32[488,128]{1,0:T(8,128)S(1)} collective-permute-done((f32[488,128]{1,0:T(8,128)S(1)}, f32[488,128]{1,0:T(8,128)S(1)}, u32[]{:S(2)}, u32[]{:S(2)}) %collective-permute-start.10) | collective-permute-done | bytes 249888 | tf_op jit(solution)/shard_map/ppermute | solution.py:458
  34.7 1.4 %shard_map.99 = (f32[1536,128]{1,0:T(8,128)}, s32[8,128]{1,0:T(8,128)S(1)}) custom-call(s32[1]{0:T(128)} %bitcast.15.where_ref, f32[1536,128]{1,0:T(8,128)S(1)} %shard_map.98.full_ref, f32[488,128]{1,0:T(8,128)S(1)} %collective-permute-done.10.above_ref, f32[384,128]{1,0:T(8,128)S(1)} %collective-permute-done.11.ax_ref, ...), custom_call_target="tpu_custom_call" | custom-call | flops 1000000 | bytes 100000 | tf_op jit(solution)/shard_map/pallas_call | solution.py:444
  36.2 0.5 %slice.21 = s32[1,1]{1,0:T(1,128)} slice(s32[8,128]{1,0:T(8,128)S(1)} %get-tuple-element.79), slice={[0:1], [0:1]} | slice | bytes 8 | tf_op jit(solution)/shard_map/slice | solution.py:598
  (1 shorter events, 0.0 us)
Async XLA Ops:
  0.0 6.2 %copy-start = (f32[4,48,2,4,128]{4,3,2,1,0:T(4,128)S(1)}, f32[4,48,2,4,128]{4,3,2,1,0:T(4,128)}, u32[]{:S(2)}) copy-start(f32[4,48,2,4,128]{4,3,2,1,0:T(4,128)} %param.11) | copy-start | bytes 2359300
  0.0 6.2 %copy-start.4 = (s32[3,2,4,128]{3,2,1,0:T(4,128)S(1)}, s32[3,2,4,128]{3,2,1,0:T(4,128)}, u32[]{:S(2)}) copy-start(s32[3,2,4,128]{3,2,1,0:T(4,128)} %param.15) | copy-start | bytes 36868
  1.1 5.1 %copy-start.3 = (f32[3,2,4,128]{3,2,1,0:T(4,128)S(1)}, f32[3,2,4,128]{3,2,1,0:T(4,128)}, u32[]{:S(2)}) copy-start(f32[3,2,4,128]{3,2,1,0:T(4,128)} %param.14) | copy-start | bytes 36868
  1.1 14.7 %collective-permute-start.2 = (f32[776,128]{1,0:T(8,128)S(1)}, f32[776,128]{1,0:T(8,128)S(1)}, u32[]{:S(2)}, u32[]{:S(2)}) collective-permute-start(f32[776,128]{1,0:T(8,128)S(1)} %bitcast.70), channel_id=1, source_target_pairs={{0,24},{8,0},{16,8},{24,16},{1,25},{9,1},{17,9},{25,17},{2,26},{10... | collective-permute-start | bytes 1191944 | tf_op jit(solution)/shard_map/ppermute | solution.py:458
  6.2 4.0 %copy-start.1 = (bf16[4,48,2,4,128]{4,3,2,1,0:T(4,128)(2,1)S(1)}, bf16[4,48,2,4,128]{4,3,2,1,0:T(4,128)(2,1)}, u32[]{:S(2)}) copy-start(bf16[4,48,2,4,128]{4,3,2,1,0:T(4,128)(2,1)} %param.13) | copy-start | bytes 1179652
  6.8 18.4 %collective-permute-start.6 = (f32[776,128]{1,0:T(8,128)S(1)}, f32[776,128]{1,0:T(8,128)S(1)}, u32[]{:S(2)}, u32[]{:S(2)}) collective-permute-start(f32[776,128]{1,0:T(8,128)S(1)} %get-tuple-element.62), channel_id=1, source_target_pairs={{0,8},{8,16},{16,24},{24,0},{1,9},{9,17},{17,25},{25,1},{2,10},{10... | collective-permute-start | bytes 1191944 | tf_op jit(solution)/shard_map/ppermute | solution.py:458
  6.9 3.4 %copy-start.5 = (s32[2,4,128]{2,1,0:T(4,128)S(1)}, s32[2,4,128]{2,1,0:T(4,128)}, u32[]{:S(2)}) copy-start(s32[2,4,128]{2,1,0:T(4,128)} %param.16) | copy-start | bytes 12292
  6.9 6.5 %collective-permute-start.3 = (f32[392,128]{1,0:T(8,128)S(1)}, f32[392,128]{1,0:T(8,128)S(1)}, u32[]{:S(2)}, u32[]{:S(2)}) collective-permute-start(f32[392,128]{1,0:T(8,128)S(1)} %get-tuple-element.58), channel_id=1, source_target_pairs={{0,1},{1,0},{2,3},{3,2},{4,5},{5,4},{6,7},{7,6},{8,9},{9,8},{10,11... | collective-permute-start | bytes 602120 | tf_op jit(solution)/shard_map/ppermute | solution.py:462
  8.5 4.0 %collective-permute-start.4 = (f32[1,1664]{1,0:T(1,128)S(1)}, f32[1,1664]{1,0:T(1,128)S(1)}, u32[]{:S(2)}, u32[]{:S(2)}) collective-permute-start(f32[1,1664]{1,0:T(1,128)S(1)} %get-tuple-element.59), channel_id=1, source_target_pairs={{0,2},{2,4},{4,6},{6,0},{1,3},{3,5},{5,7},{7,1},{8,10},{10,12},{12... | collective-permute-start | bytes 19976 | tf_op jit(solution)/shard_map/ppermute | solution.py:458
  8.5 4.1 %collective-permute-start.5 = (f32[1,1664]{1,0:T(1,128)S(1)}, f32[1,1664]{1,0:T(1,128)S(1)}, u32[]{:S(2)}, u32[]{:S(2)}) collective-permute-start(f32[1,1664]{1,0:T(1,128)S(1)} %get-tuple-element.60), channel_id=1, source_target_pairs={{0,6},{2,0},{4,2},{6,4},{1,7},{3,1},{5,3},{7,5},{8,14},{10,8},{12,... | collective-permute-start | bytes 19976 | tf_op jit(solution)/shard_map/ppermute | solution.py:458
  10.2 0.7 %copy-start.6 = (f32[48]{0:T(128)S(1)}, f32[48]{0:T(128)}, u32[]{:S(2)}) copy-start(f32[48]{0:T(128)} %growth_ref.3) | copy-start | bytes 580
  10.2 0.7 %copy-start.7 = (f32[48]{0:T(128)S(1)}, f32[48]{0:T(128)}, u32[]{:S(2)}) copy-start(f32[48]{0:T(128)} %transfer_ref.3) | copy-start | bytes 580
  10.2 0.7 %copy-start.8 = (f32[4]{0:T(128)S(1)}, f32[4]{0:T(128)}, u32[]{:S(2)}) copy-start(f32[4]{0:T(128)} %rate_ref.3) | copy-start | bytes 52
  17.4 14.6 %collective-permute-start.7 = (f32[480,128]{1,0:T(8,128)S(1)}, f32[480,128]{1,0:T(8,128)S(1)}, u32[]{:S(2)}, u32[]{:S(2)}) collective-permute-start(f32[480,128]{1,0:T(8,128)S(1)} %get-tuple-element.68), channel_id=1, source_target_pairs={{0,8},{8,16},{16,24},{24,0},{1,9},{9,17},{17,25},{25,1},{2,10},{10... | collective-permute-start | bytes 737288 | tf_op jit(solution)/shard_map/ppermute | solution.py:458
  25.2 6.7 %copy-start.2 = (bf16[4,48,2,4,128]{4,3,2,1,0:T(4,128)(2,1)S(1)}, bf16[4,48,2,4,128]{4,3,2,1,0:T(4,128)(2,1)}, u32[]{:S(2)}) copy-start(bf16[4,48,2,4,128]{4,3,2,1,0:T(4,128)(2,1)} %param.12) | copy-start | bytes 1179652
  26.2 8.5 %collective-permute-start.10 = (f32[488,128]{1,0:T(8,128)S(1)}, f32[488,128]{1,0:T(8,128)S(1)}, u32[]{:S(2)}, u32[]{:S(2)}) collective-permute-start(f32[488,128]{1,0:T(8,128)S(1)} %get-tuple-element.74), channel_id=1, source_target_pairs={{0,24},{8,0},{16,8},{24,16},{1,25},{9,1},{17,9},{25,17},{2,26},{10... | collective-permute-start | bytes 749576 | tf_op jit(solution)/shard_map/ppermute | solution.py:458
  28.7 5.7 %collective-permute-start.11 = (f32[384,128]{1,0:T(8,128)S(1)}, f32[384,128]{1,0:T(8,128)S(1)}, u32[]{:S(2)}, u32[]{:S(2)}) collective-permute-start(f32[384,128]{1,0:T(8,128)S(1)} %get-tuple-element.75), channel_id=1, source_target_pairs={{0,1},{1,0},{2,3},{3,2},{4,5},{5,4},{6,7},{7,6},{8,9},{9,8},{10,11... | collective-permute-start | bytes 589832 | tf_op jit(solution)/shard_map/ppermute | solution.py:462
  30.2 3.4 %collective-permute-start.8 = (f32[1,1536]{1,0:T(1,128)S(1)}, f32[1,1536]{1,0:T(1,128)S(1)}, u32[]{:S(2)}, u32[]{:S(2)}) collective-permute-start(f32[1,1536]{1,0:T(1,128)S(1)} %get-tuple-element.72), channel_id=1, source_target_pairs={{0,2},{2,4},{4,6},{6,0},{1,3},{3,5},{5,7},{7,1},{8,10},{10,12},{12... | collective-permute-start | bytes 18440 | tf_op jit(solution)/shard_map/ppermute | solution.py:458
  30.2 3.4 %collective-permute-start.9 = (f32[1,1536]{1,0:T(1,128)S(1)}, f32[1,1536]{1,0:T(1,128)S(1)}, u32[]{:S(2)}, u32[]{:S(2)}) collective-permute-start(f32[1,1536]{1,0:T(1,128)S(1)} %get-tuple-element.73), channel_id=1, source_target_pairs={{0,6},{2,0},{4,2},{6,4},{1,7},{3,1},{5,3},{7,5},{8,14},{10,8},{12,... | collective-permute-start | bytes 18440 | tf_op jit(solution)/shard_map/ppermute | solution.py:458
